TPU v7x, 32 devices: a whole 2x2x4 slice. The times are simulated.
32 devices in a mesh: seq: 16 (over z, y, x), fsdp: 2 (over core).
Axes of the slice: x: 2, y: 2, z: 4, core: 2. Of those that a mesh axis runs over, the one named last changes fastest.
Arguments:
- tokens: bfloat16 [2, 2, 2048, 1152], P('fsdp', None, 'seq'), may hold values from -6 to 6
- cotangent: bfloat16 [2, 2, 2048, 1152], P('fsdp', None, 'seq'), may hold values from -6 to 6
- lengths: int32 [2, 2, 8], P('fsdp'), may hold values from 0 to 2048, as said below
- deal_order: int32 [2, 16], P('fsdp'), may hold values from 0 to 15, each once within a row
- w_query: bfloat16 [1152, 1024], P('fsdp'), may hold values from -0.1875 to 0.1875
- w_key: bfloat16 [1152, 256], P('fsdp'), may hold values from -0.1875 to 0.1875
- w_value: bfloat16 [1152, 256], P('fsdp'), may hold values from -0.1875 to 0.1875
- w_out: bfloat16 [1024, 1152], P(None, 'fsdp'), may hold values from -0.1875 to 0.1875
- w_gate: bfloat16 [1152, 6912], P(None, 'fsdp'), may hold values from -0.1875 to 0.1875
- w_up: bfloat16 [1152, 6912], P(None, 'fsdp'), may hold values from -0.1875 to 0.1875
- w_down: bfloat16 [6912, 1152], P('fsdp'), may hold values from -0.078125 to 0.078125
- norm_gains: float32 [4, 1152], replicated, may hold values from 0.1 to 1.9
- head_gains: float32 [2, 256], replicated, may hold values from 0.1 to 1.9
Outputs:
- output: float32 [2, 2, 2048, 1152], P('fsdp', None, 'seq')
- input_grad: float32 [2, 2, 2048, 1152], P('fsdp', None, 'seq')
- query_grad: float32 [1152, 1024], P('fsdp', 'seq')
- key_grad: float32 [1152, 256], P('fsdp', 'seq')
- value_grad: float32 [1152, 256], P('fsdp', 'seq')
- out_grad: float32 [1024, 1152], P('seq', 'fsdp')
- gate_grad: float32 [1152, 6912], P('seq', 'fsdp')
- up_grad: float32 [1152, 6912], P('seq', 'fsdp')
- down_grad: float32 [6912, 1152], P('fsdp', 'seq')
- norm_gains_grad: float32 [4, 1152], replicated
- head_gains_grad: float32 [2, 256], replicated
Inputs may be any that keep to these rules, and one draw needn't show every extreme that they name: In every group one lane, drawn from the seed, holds a single sequence of 2048 tokens and zeros after it; in the other lanes all 8 lengths are positive. Each lane's lengths sum to 2048. `deal_order`: each row is a permutation of the block positions.
All inputs are finite; a program needn't handle non-finite values.
Results may differ from a plain program's by a relative error of at most 0.019.
Values may be sent and summed in bfloat16 or wider, within the bound.
No kernel may reach another device: no remote copies, remote signals or barrier semaphores. Data moves between devices by JAX's collectives and lax.ppermute only.
A program may use at most 256 MiB of HBM per device.

v0:
```python
import math

import jax
import jax.numpy as jnp
from jax import lax
from jax.sharding import PartitionSpec as P

HQ = 4
HD = 256
W = 512


EPSILON = 1e-06
ROPE_BASE = 10000.0


def from_partner(block, axis, distance):
    count = lax.axis_size(axis)
    route = []
    for low in range(count):
        high = low | 1 << distance
        if high != low and high < count:
            route += [(low, high), (high, low)]
    return lax.ppermute(block, axis, route)


def passed_along(value, axis, by):
    peers = lax.axis_size(axis)
    pairs = [(i, i + by) for i in range(peers) if 0 <= i + by < peers]
    return lax.ppermute(value, axis, pairs)


def rms_scale(values):
    return lax.rsqrt(jnp.mean(values * values, axis=-1, keepdims=True) + EPSILON)


def rms_forward(values, gain_vec):
    return values * rms_scale(values) * gain_vec


def rms_backward(values, gain_vec, grad_out):
    scale_rows = rms_scale(values)
    weighted = grad_out * gain_vec
    inner_mean = jnp.mean(weighted * values, axis=-1, keepdims=True)
    grad_in = scale_rows * weighted - values * (scale_rows * scale_rows * scale_rows) * inner_mean
    return (grad_in, grad_out * values * scale_rows)


def rope_tables(seq_pos, head_dim):
    half_dim = head_dim // 2
    frequency = jnp.exp(
        jnp.arange(half_dim, dtype=jnp.float32) * (-2.0 * math.log(ROPE_BASE) / head_dim)
    )
    angles = seq_pos.astype(jnp.float32)[..., None] * frequency
    return (jnp.cos(angles), jnp.sin(angles))


def rotate(values, cosine_table, sine_table):
    half_dim = values.shape[-1] // 2
    first_half = values[..., :half_dim]
    second_half = values[..., half_dim:]
    return jnp.concatenate(
        [
            first_half * cosine_table - second_half * sine_table,
            second_half * cosine_table + first_half * sine_table,
        ],
        axis=-1,
    )


def gelu_tanh(values):
    return jax.nn.gelu(values, approximate=True)


def sequence_info(lengths, stream_pos):
    seq_ends = jnp.cumsum(lengths, axis=-1)
    before = seq_ends[..., None, :] <= stream_pos[..., :, None]
    seq_ids = jnp.sum(before.astype(jnp.int32), axis=-1)
    starts = jnp.sum(jnp.where(before, lengths[..., None, :], 0), axis=-1)
    return (seq_ids, stream_pos - starts)


def route_flags(sort_keys, own_index, node_count):
    switches = []
    positions = jnp.arange(node_count, dtype=jnp.int32)
    block_span = 2
    while block_span <= node_count:
        half_span = block_span // 2
        while half_span >= 1:
            partner = jnp.bitwise_xor(positions, half_span)
            own_key = sort_keys
            peer_key = sort_keys[partner]
            rising = jnp.bitwise_and(positions, block_span) == 0
            lower_half = jnp.bitwise_and(positions, half_span) == 0
            take_peer = jnp.where(lower_half == rising, peer_key < own_key, peer_key > own_key)
            sort_keys = jnp.where(take_peer, peer_key, own_key)
            switches.append((half_span.bit_length() - 1, take_peer[own_index]))
            half_span = half_span // 2
        block_span = block_span * 2
    return switches


def shards(
    tokens,
    cotangent,
    lengths,
    deal_order,
    w_query,
    w_key,
    w_value,
    w_out,
    w_gate,
    w_up,
    w_down,
    norm_gains,
    head_gains,
):
    brain_float_type = jnp.bfloat16
    lane_count, lane_rows, model_width = (tokens.shape[1], tokens.shape[2], tokens.shape[3])
    row_count = lane_count * lane_rows
    head_count = HQ
    head_dim = HD
    window = W
    seq_count = lax.axis_size("seq")
    own_index = lax.axis_index("seq")
    deal_keys = deal_order[0]
    positions = jnp.arange(seq_count, dtype=jnp.int32)
    back_keys = jnp.sum(
        jnp.where(deal_keys[None, :] == positions[:, None], positions[None, :], 0), axis=1
    )
    payload = jnp.stack([tokens[0], cotangent[0]])
    for bit_number, take_peer in route_flags(deal_keys, own_index, seq_count):
        arrived = from_partner(payload, "seq", bit_number)
        payload = jnp.where(take_peer, arrived, payload)
    inputs = payload[0].astype(jnp.float32).reshape(row_count, model_width)
    upstream = payload[1].astype(jnp.float32).reshape(row_count, model_width)
    wq_full, wk_full, wv_full, wo_full, wg_full, wu_full, wd_full = (
        lax.all_gather(w_query, "fsdp", axis=0, tiled=True),
        lax.all_gather(w_key, "fsdp", axis=0, tiled=True),
        lax.all_gather(w_value, "fsdp", axis=0, tiled=True),
        lax.all_gather(w_out, "fsdp", axis=1, tiled=True),
        lax.all_gather(w_gate, "fsdp", axis=1, tiled=True),
        lax.all_gather(w_up, "fsdp", axis=1, tiled=True),
        lax.all_gather(w_down, "fsdp", axis=0, tiled=True),
    )
    lane_lengths = lengths[0]
    local_stream = own_index * lane_rows + jnp.arange(lane_rows, dtype=jnp.int32)
    query_ids, query_pos = sequence_info(
        lane_lengths, jnp.broadcast_to(local_stream, (lane_count, lane_rows))
    )
    gain_in, gain_mid, gain_ffn, gain_top = (
        norm_gains[0],
        norm_gains[1],
        norm_gains[2],
        norm_gains[3],
    )
    query_gain, key_gain = (head_gains[0], head_gains[1])
    attn_in = rms_forward(inputs, gain_in).astype(brain_float_type)
    query_proj = jnp.dot(attn_in, wq_full, preferred_element_type=jnp.float32).reshape(
        lane_count, lane_rows, head_count, head_dim
    )
    key_proj = jnp.dot(attn_in, wk_full, preferred_element_type=jnp.float32).reshape(
        lane_count, lane_rows, head_dim
    )
    value_proj = (
        jnp.dot(attn_in, wv_full, preferred_element_type=jnp.float32)
        .reshape(lane_count, lane_rows, head_dim)
        .astype(brain_float_type)
    )
    cosine_table, sine_table = rope_tables(query_pos, head_dim)
    query_rot = rotate(
        rms_forward(query_proj, query_gain), cosine_table[:, :, None, :], sine_table[:, :, None, :]
    ).astype(brain_float_type)
    key_rot = rotate(rms_forward(key_proj, key_gain), cosine_table, sine_table).astype(
        brain_float_type
    )
    kv_local = jnp.concatenate([key_rot, value_proj], axis=-1)
    hop_count = (window - 1 + lane_rows - 1) // lane_rows
    hop_sizes = [
        min(lane_rows, window - 1 - (distance - 1) * lane_rows)
        for distance in range(1, hop_count + 1)
    ]
    pieces = []
    stream_parts = []
    for distance in range(1, hop_count + 1):
        needed = hop_sizes[distance - 1]
        pieces.append(passed_along(kv_local[:, lane_rows - needed :], "seq", distance))
        stream_parts.append(
            (own_index - distance) * lane_rows
            + lane_rows
            - needed
            + jnp.arange(needed, dtype=jnp.int32)
        )
    kv_all = jnp.concatenate(pieces[::-1] + [kv_local], axis=1)
    key_stream = jnp.concatenate(stream_parts[::-1] + [local_stream])
    key_total = kv_all.shape[1]
    key_ids = sequence_info(lane_lengths, jnp.broadcast_to(key_stream, (lane_count, key_total)))[0]
    allowed = (
        (key_ids[:, None, :] == query_ids[:, :, None])
        & (key_stream[None, None, :] <= local_stream[None, :, None])
        & (local_stream[None, :, None] - key_stream[None, None, :] < window)
        & (key_stream[None, None, :] >= 0)
    )
    allowed = jnp.repeat(allowed, head_count, axis=1)
    flattened_query = query_rot.reshape(lane_count, lane_rows * head_count, head_dim)
    gathered_keys = kv_all[..., :head_dim]
    gathered_values = kv_all[..., head_dim:]
    score_scale = head_dim ** (-0.5)

    def scores_of():
        raw_scores = jnp.einsum(
            "nfi,nhi->nfh", flattened_query, gathered_keys, preferred_element_type=jnp.float32
        )
        return jnp.where(allowed, raw_scores * score_scale, -1e30)

    masked = scores_of()
    top_score = jnp.max(masked, axis=-1, keepdims=True)
    exponents = jnp.exp(masked - top_score)
    row_total = jnp.sum(exponents, axis=-1, keepdims=True)
    log_norm = top_score + jnp.log(row_total)
    probabilities_reduced = (exponents / row_total).astype(brain_float_type)
    attention_output = jnp.einsum(
        "ajm,amn->ajn", probabilities_reduced, gathered_values, preferred_element_type=jnp.float32
    )
    mixed_low = attention_output.reshape(row_count, head_count * head_dim).astype(brain_float_type)
    branch = jnp.dot(mixed_low, wo_full, preferred_element_type=jnp.float32)
    middle = inputs + rms_forward(branch, gain_mid)
    ffn_in = rms_forward(middle, gain_ffn).astype(brain_float_type)
    gate_proj = jnp.dot(ffn_in, wg_full, preferred_element_type=jnp.float32)
    upward = jnp.dot(ffn_in, wu_full, preferred_element_type=jnp.float32)
    activated, gelu_pull = jax.vjp(gelu_tanh, gate_proj)
    hidden = (activated * upward).astype(brain_float_type)
    ffn_out = jnp.dot(hidden, wd_full, preferred_element_type=jnp.float32)
    result = middle + rms_forward(ffn_out, gain_top)
    wq_full, wk_full, wv_full, wo_full, wg_full, wu_full, wd_full = (
        lax.all_gather(w_query, "fsdp", axis=0, tiled=True),
        lax.all_gather(w_key, "fsdp", axis=0, tiled=True),
        lax.all_gather(w_value, "fsdp", axis=0, tiled=True),
        lax.all_gather(w_out, "fsdp", axis=1, tiled=True),
        lax.all_gather(w_gate, "fsdp", axis=1, tiled=True),
        lax.all_gather(w_up, "fsdp", axis=1, tiled=True),
        lax.all_gather(w_down, "fsdp", axis=0, tiled=True),
    )
    grad_ffn_out, top_terms = rms_backward(ffn_out, gain_top, upstream)
    grad_ffn_low = grad_ffn_out.astype(brain_float_type)
    grad_wdown = jnp.einsum("rf,rd->fd", hidden, grad_ffn_low, preferred_element_type=jnp.float32)
    grad_hidden = jnp.einsum("rd,fd->rf", grad_ffn_low, wd_full, preferred_element_type=jnp.float32)
    grad_gate = gelu_pull(grad_hidden * upward)[0].astype(brain_float_type)
    grad_upward = (grad_hidden * activated).astype(brain_float_type)
    grad_wgate = jnp.einsum("rd,rf->df", ffn_in, grad_gate, preferred_element_type=jnp.float32)
    grad_wup = jnp.einsum("rd,rf->df", ffn_in, grad_upward, preferred_element_type=jnp.float32)
    grad_ffn_in = jnp.einsum(
        "rf,df->rd", grad_gate, wg_full, preferred_element_type=jnp.float32
    ) + jnp.einsum("rf,df->rd", grad_upward, wu_full, preferred_element_type=jnp.float32)
    grad_middle_norm, ffn_terms = rms_backward(middle, gain_ffn, grad_ffn_in)
    grad_middle = upstream + grad_middle_norm
    grad_branch, mid_terms = rms_backward(branch, gain_mid, grad_middle)
    grad_branch_low = grad_branch.astype(brain_float_type)
    grad_wout = jnp.einsum(
        "re,rd->ed", mixed_low, grad_branch_low, preferred_element_type=jnp.float32
    )
    mixed_gradient = (
        jnp.einsum("rd,ed->re", grad_branch_low, wo_full, preferred_element_type=jnp.float32)
        .astype(brain_float_type)
        .reshape(lane_count, lane_rows * head_count, head_dim)
    )
    recomputed_probabilities = jnp.exp(scores_of() - log_norm)
    grad_probs = jnp.einsum(
        "nfi,nhi->nfh", mixed_gradient, gathered_values, preferred_element_type=jnp.float32
    )
    inner_sum = jnp.sum(recomputed_probabilities * grad_probs, axis=-1, keepdims=True)
    raw_score_gradient = (recomputed_probabilities * (grad_probs - inner_sum) * score_scale).astype(
        brain_float_type
    )
    query_gradient = jnp.einsum(
        "ajm,amn->ajn", raw_score_gradient, gathered_keys, preferred_element_type=jnp.float32
    )
    grad_key_all = jnp.einsum(
        "xzo,xza->xoa", raw_score_gradient, flattened_query, preferred_element_type=jnp.float32
    )
    grad_value_all = jnp.einsum(
        "xzo,xza->xoa",
        recomputed_probabilities.astype(brain_float_type),
        mixed_gradient,
        preferred_element_type=jnp.float32,
    )
    grad_kv = jnp.concatenate([grad_key_all, grad_value_all], axis=-1)
    grad_local = grad_kv[:, key_total - lane_rows :]
    offset = 0
    for distance in range(hop_count, 0, -1):
        needed = hop_sizes[distance - 1]
        returned = passed_along(
            grad_kv[:, offset : offset + needed].astype(jnp.bfloat16), "seq", -distance
        ).astype(jnp.float32)
        grad_local = grad_local + jnp.pad(returned, ((0, 0), (lane_rows - needed, 0), (0, 0)))
        offset = offset + needed
    grad_value_low = (
        grad_local[..., head_dim:].reshape(row_count, head_dim).astype(brain_float_type)
    )
    key_normed_grad = rotate(grad_local[..., :head_dim], cosine_table, -sine_table)
    grad_key_proj, key_terms = rms_backward(key_proj, key_gain, key_normed_grad)
    grad_key_low = grad_key_proj.reshape(row_count, head_dim).astype(brain_float_type)
    query_normed_grad = rotate(
        query_gradient.reshape(lane_count, lane_rows, head_count, head_dim),
        cosine_table[:, :, None, :],
        -sine_table[:, :, None, :],
    )
    grad_query_proj, query_terms = rms_backward(query_proj, query_gain, query_normed_grad)
    grad_query_low = grad_query_proj.reshape(row_count, head_count * head_dim).astype(
        brain_float_type
    )
    grad_wq = jnp.einsum("rd,re->de", attn_in, grad_query_low, preferred_element_type=jnp.float32)
    grad_wk = jnp.einsum("rd,re->de", attn_in, grad_key_low, preferred_element_type=jnp.float32)
    grad_wv = jnp.einsum("rd,re->de", attn_in, grad_value_low, preferred_element_type=jnp.float32)
    grad_attn_in = jnp.einsum(
        "re,de->rd", grad_query_low, wq_full, preferred_element_type=jnp.float32
    )
    grad_attn_in = grad_attn_in + jnp.einsum(
        "re,de->rd", grad_key_low, wk_full, preferred_element_type=jnp.float32
    )
    grad_attn_in = grad_attn_in + jnp.einsum(
        "re,de->rd", grad_value_low, wv_full, preferred_element_type=jnp.float32
    )
    grad_input_norm, in_terms = rms_backward(inputs, gain_in, grad_attn_in)
    grad_inputs = grad_middle + grad_input_norm
    norm_terms = jnp.stack(
        [
            jnp.sum(in_terms, axis=0),
            jnp.sum(mid_terms, axis=0),
            jnp.sum(ffn_terms, axis=0),
            jnp.sum(top_terms, axis=0),
        ]
    )
    head_terms = jnp.stack([jnp.sum(query_terms, axis=(0, 1, 2)), jnp.sum(key_terms, axis=(0, 1))])
    norm_total, head_total = lax.psum((norm_terms, head_terms), ("seq", "fsdp"))
    sums_a = (
        lax.psum_scatter(
            grad_wq.astype(jnp.bfloat16), "fsdp", scatter_dimension=0, tiled=True
        ).astype(jnp.float32),
        lax.psum_scatter(
            grad_wk.astype(jnp.bfloat16), "fsdp", scatter_dimension=0, tiled=True
        ).astype(jnp.float32),
        lax.psum_scatter(
            grad_wv.astype(jnp.bfloat16), "fsdp", scatter_dimension=0, tiled=True
        ).astype(jnp.float32),
        lax.psum_scatter(
            grad_wout.astype(jnp.bfloat16), "fsdp", scatter_dimension=1, tiled=True
        ).astype(jnp.float32),
        lax.psum_scatter(
            grad_wgate.astype(jnp.bfloat16), "fsdp", scatter_dimension=1, tiled=True
        ).astype(jnp.float32),
        lax.psum_scatter(
            grad_wup.astype(jnp.bfloat16), "fsdp", scatter_dimension=1, tiled=True
        ).astype(jnp.float32),
        lax.psum_scatter(
            grad_wdown.astype(jnp.bfloat16), "fsdp", scatter_dimension=0, tiled=True
        ).astype(jnp.float32),
    )
    sums_b = (
        lax.psum_scatter(sums_a[0], "seq", scatter_dimension=1, tiled=True),
        lax.psum_scatter(sums_a[1], "seq", scatter_dimension=1, tiled=True),
        lax.psum_scatter(sums_a[2], "seq", scatter_dimension=1, tiled=True),
        lax.psum_scatter(sums_a[3], "seq", scatter_dimension=0, tiled=True),
        lax.psum_scatter(sums_a[4], "seq", scatter_dimension=0, tiled=True),
        lax.psum_scatter(sums_a[5], "seq", scatter_dimension=0, tiled=True),
        lax.psum_scatter(sums_a[6], "seq", scatter_dimension=1, tiled=True),
    )
    homeward = jnp.stack([result, grad_inputs]).reshape(2, lane_count, lane_rows, model_width)
    for bit_number, take_peer in route_flags(back_keys, own_index, seq_count):
        arrived = from_partner(homeward.astype(jnp.bfloat16), "seq", bit_number).astype(
            homeward.dtype
        )
        homeward = jnp.where(take_peer, arrived, homeward)
    return (
        homeward[0][None],
        homeward[1][None],
        sums_b[0],
        sums_b[1],
        sums_b[2],
        sums_b[3],
        sums_b[4],
        sums_b[5],
        sums_b[6],
        norm_total,
        head_total,
    )


def solution(mesh):
    in_specs = (
        P("fsdp", None, "seq", None),
        P("fsdp", None, "seq", None),
        P("fsdp", None, None),
        P("fsdp", None),
        P("fsdp", None),
        P("fsdp", None),
        P("fsdp", None),
        P(None, "fsdp"),
        P(None, "fsdp"),
        P(None, "fsdp"),
        P("fsdp", None),
        P(),
        P(),
    )
    out_specs = (
        P("fsdp", None, "seq", None),
        P("fsdp", None, "seq", None),
        P("fsdp", "seq"),
        P("fsdp", "seq"),
        P("fsdp", "seq"),
        P("seq", "fsdp"),
        P("seq", "fsdp"),
        P("seq", "fsdp"),
        P("fsdp", "seq"),
        P(),
        P(),
    )
    return jax.shard_map(shards, mesh=mesh, in_specs=in_specs, out_specs=out_specs, check_vma=False)
```

profile of v0, /device:TPU:0, one launch (start us, length us, event | category | flops | bytes accessed | tf_op | source)
XLA Modules:
  0.0 1918.0 jit_solution(12450446064073937651)
XLA Ops:
  11.2 3.0 collective-permute-start
  15.5 24.6 %collective-permute-done = bf16[2,2,128,1152]{3,2,1,0:T(8,128)(2,1)S(1)} collective-permute-done((bf16[2,2,128,1152]{3,2,1,0:T(8,128)(2,1)S(1)}, bf16[2,2,128,1152]{3,2,1,0:T(8,128)(2,1)S(1)}, u32[]{:S(2)}, u32[]{:S(2)}) %collective-permute-start) | collective-permute-done | bytes 1179680 | tf_op jit(solution)/shard_map/ppermute | solution.py:24
  44.7 23.5 %collective-permute-done.1 = bf16[2,2,128,1152]{3,2,1,0:T(8,128)(2,1)S(1)} collective-permute-done((bf16[2,2,128,1152]{3,2,1,0:T(8,128)(2,1)S(1)}, bf16[2,2,128,1152]{3,2,1,0:T(8,128)(2,1)S(1)}, u32[]{:S(2)}, u32[]{:S(2)}) %collective-permute-start.1) | collective-permute-done | bytes 1179680 | tf_op jit(solution)/shard_map/ppermute | solution.py:24
  72.4 22.9 %collective-permute-done.2 = bf16[2,2,128,1152]{3,2,1,0:T(8,128)(2,1)S(1)} collective-permute-done((bf16[2,2,128,1152]{3,2,1,0:T(8,128)(2,1)S(1)}, bf16[2,2,128,1152]{3,2,1,0:T(8,128)(2,1)S(1)}, u32[]{:S(2)}, u32[]{:S(2)}) %collective-permute-start.2) | collective-permute-done | bytes 1179680 | tf_op jit(solution)/shard_map/ppermute | solution.py:24
  99.8 21.6 %collective-permute-done.3 = bf16[2,2,128,1152]{3,2,1,0:T(8,128)(2,1)S(1)} collective-permute-done((bf16[2,2,128,1152]{3,2,1,0:T(8,128)(2,1)S(1)}, bf16[2,2,128,1152]{3,2,1,0:T(8,128)(2,1)S(1)}, u32[]{:S(2)}, u32[]{:S(2)}) %collective-permute-start.3) | collective-permute-done | bytes 1179680 | tf_op jit(solution)/shard_map/ppermute | solution.py:24
  125.0 21.6 %collective-permute-done.4 = bf16[2,2,128,1152]{3,2,1,0:T(8,128)(2,1)S(1)} collective-permute-done((bf16[2,2,128,1152]{3,2,1,0:T(8,128)(2,1)S(1)}, bf16[2,2,128,1152]{3,2,1,0:T(8,128)(2,1)S(1)}, u32[]{:S(2)}, u32[]{:S(2)}) %collective-permute-start.4) | collective-permute-done | bytes 1179680 | tf_op jit(solution)/shard_map/ppermute | solution.py:24
  149.9 21.1 %collective-permute-done.5 = bf16[2,2,128,1152]{3,2,1,0:T(8,128)(2,1)S(1)} collective-permute-done((bf16[2,2,128,1152]{3,2,1,0:T(8,128)(2,1)S(1)}, bf16[2,2,128,1152]{3,2,1,0:T(8,128)(2,1)S(1)}, u32[]{:S(2)}, u32[]{:S(2)}) %collective-permute-start.5) | collective-permute-done | bytes 1179680 | tf_op jit(solution)/shard_map/ppermute | solution.py:24
  175.5 45.4 %collective-permute-done.6 = bf16[2,2,128,1152]{3,2,1,0:T(8,128)(2,1)S(1)} collective-permute-done((bf16[2,2,128,1152]{3,2,1,0:T(8,128)(2,1)S(1)}, bf16[2,2,128,1152]{3,2,1,0:T(8,128)(2,1)S(1)}, u32[]{:S(2)}, u32[]{:S(2)}) %collective-permute-start.6) | collective-permute-done | bytes 1179680 | tf_op jit(solution)/shard_map/ppermute | solution.py:24
  226.7 24.1 %collective-permute-done.7 = bf16[2,2,128,1152]{3,2,1,0:T(8,128)(2,1)S(1)} collective-permute-done((bf16[2,2,128,1152]{3,2,1,0:T(8,128)(2,1)S(1)}, bf16[2,2,128,1152]{3,2,1,0:T(8,128)(2,1)S(1)}, u32[]{:S(2)}, u32[]{:S(2)}) %collective-permute-start.7) | collective-permute-done | bytes 1179680 | tf_op jit(solution)/shard_map/ppermute | solution.py:24
  254.8 23.9 %collective-permute-done.8 = bf16[2,2,128,1152]{3,2,1,0:T(8,128)(2,1)S(1)} collective-permute-done((bf16[2,2,128,1152]{3,2,1,0:T(8,128)(2,1)S(1)}, bf16[2,2,128,1152]{3,2,1,0:T(8,128)(2,1)S(1)}, u32[]{:S(2)}, u32[]{:S(2)}) %collective-permute-start.8) | collective-permute-done | bytes 1179680 | tf_op jit(solution)/shard_map/ppermute | solution.py:24
  284.1 2.3 all_gather.29
  286.5 3.8 all_gather.30
  291.5 4.5 copy.66
  295.9 9.8 collective-permute-done.9
  311.0 2.7 collective-permute-start.13
  313.7 5.1 collective-permute-start.12
  318.9 4.8 collective-permute-start.11
  323.6 2.8 collective-permute-start.10
  332.9 7.7 concatenate.40
  345.6 2.8 multiply_reduce_fusion.7
  350.9 12.4 fusion.138
  363.3 14.7 multiply_convert_fusion.1
  378.0 10.4 multiply_reduce_fusion.5
  391.0 24.6 %multiply_convert_fusion = (bf16[256,6912]{1,0:T(8,128)(2,1)}, bf16[256,6912]{1,0:T(8,128)(2,1)}) fusion(f32[256,6912]{1,0:T(8,128)} %fusion.138, f32[256,6912]{1,0:T(8,128)} %get-tuple-element.132, bf16[256,1152]{1,0:T(8,128)(2,1)S(1)} %fusion.39, bf16[6912,1152]{1,0:T(8,128)(2,1)} %all-gather.14.cloned.1.call-done), kind=kOutput, calls=%fused_computation.33 | convolution fusion | flops 4119330816 | bytes 37748736 | tf_op jit(solution)/shard_map/rd,fd->rf/dot_general | solution.py:247
  415.6 12.4 fusion.139
  427.9 13.2 multiply_reduce_fusion.1
  441.2 2.8 multiply_reduce_fusion.2
  452.1 12.0 fusion.15
  471.2 21.1 %collective-permute-done.14 = bf16[2,127,512]{2,1,0:T(8,128)(2,1)S(1)} collective-permute-done((bf16[2,127,512]{2,1,0:T(8,128)(2,1)S(1)}, bf16[2,127,512]{2,1,0:T(8,128)(2,1)S(1)}, u32[]{:S(2)}, u32[]{:S(2)}) %collective-permute-start.14) | collective-permute-done | bytes 260128 | tf_op jit(solution)/shard_map/ppermute | solution.py:30
  498.2 2.3 convolution_convert_fusion.3
  501.8 10.5 fusion.18
  522.0 10.3 convolution_convert_fusion
  532.2 20.3 %copy.97 = bf16[1152,6912]{0,1:T(8,128)(2,1)} copy(bf16[1152,6912]{1,0:T(8,128)(2,1)} %convolution_convert_fusion) | data formatting | bytes 31850496
  552.6 9.9 convolution_convert_fusion.1
  562.5 23.0 %copy.95 = bf16[1152,6912]{0,1:T(8,128)(2,1)} copy(bf16[1152,6912]{1,0:T(8,128)(2,1)} %convolution_convert_fusion.1) | data formatting | bytes 31850496
  586.5 11.0 convolution_convert_fusion.2
  601.9 3.0 copy.93
  605.0 3.0 copy.87
  608.0 12.2 copy.98
  620.2 12.9 convert_element_type.314
  633.2 12.7 copy.96
  645.9 9.9 convert_element_type.312
  666.8 28.5 %collective-permute-done.18 = bf16[2,2,128,1152]{3,2,1,0:T(8,128)(2,1)S(1)} collective-permute-done((bf16[2,2,128,1152]{3,2,1,0:T(8,128)(2,1)}, bf16[2,2,128,1152]{3,2,1,0:T(8,128)(2,1)S(1)}, u32[]{:S(2)}, u32[]{:S(2)}) %collective-permute-start.18) | collective-permute-done | bytes 1179680 | tf_op jit(solution)/shard_map/ppermute | solution.py:24
  698.7 24.8 %collective-permute-done.19 = bf16[2,2,128,1152]{3,2,1,0:T(8,128)(2,1)} collective-permute-done((bf16[2,2,128,1152]{3,2,1,0:T(8,128)(2,1)}, bf16[2,2,128,1152]{3,2,1,0:T(8,128)(2,1)}, u32[]{:S(2)}, u32[]{:S(2)}) %collective-permute-start.19) | collective-permute-done | bytes 1179680 | tf_op jit(solution)/shard_map/ppermute | solution.py:24
  723.5 4.0 fusion.21
  730.3 26.2 %collective-permute-done.20 = bf16[2,2,128,1152]{3,2,1,0:T(8,128)(2,1)} collective-permute-done((bf16[2,2,128,1152]{3,2,1,0:T(8,128)(2,1)}, bf16[2,2,128,1152]{3,2,1,0:T(8,128)(2,1)}, u32[]{:S(2)}, u32[]{:S(2)}) %collective-permute-start.20) | collective-permute-done | bytes 1179680 | tf_op jit(solution)/shard_map/ppermute | solution.py:24
  756.6 6.0 fusion.132
  762.6 10.0 collective-permute-start.21
  774.0 22.8 %collective-permute-done.21 = bf16[2,2,128,1152]{3,2,1,0:T(8,128)(2,1)S(1)} collective-permute-done((bf16[2,2,128,1152]{3,2,1,0:T(8,128)(2,1)}, bf16[2,2,128,1152]{3,2,1,0:T(8,128)(2,1)S(1)}, u32[]{:S(2)}, u32[]{:S(2)}) %collective-permute-start.21) | collective-permute-done | bytes 1179680 | tf_op jit(solution)/shard_map/ppermute | solution.py:24
  796.8 3.8 fusion.22
  802.1 30.6 %collective-permute-done.22 = bf16[2,2,128,1152]{3,2,1,0:T(8,128)(2,1)} collective-permute-done((bf16[2,2,128,1152]{3,2,1,0:T(8,128)(2,1)}, bf16[2,2,128,1152]{3,2,1,0:T(8,128)(2,1)}, u32[]{:S(2)}, u32[]{:S(2)}) %collective-permute-start.22) | collective-permute-done | bytes 1179680 | tf_op jit(solution)/shard_map/ppermute | solution.py:24
  832.6 4.8 fusion.131
  838.9 50.8 %collective-permute-done.23 = bf16[2,2,128,1152]{3,2,1,0:T(8,128)(2,1)S(1)} collective-permute-done((bf16[2,2,128,1152]{3,2,1,0:T(8,128)(2,1)}, bf16[2,2,128,1152]{3,2,1,0:T(8,128)(2,1)S(1)}, u32[]{:S(2)}, u32[]{:S(2)}) %collective-permute-start.23) | collective-permute-done | bytes 1179680 | tf_op jit(solution)/shard_map/ppermute | solution.py:24
  891.6 10.7 collective-permute-start.24
  903.7 66.7 %collective-permute-done.24 = bf16[2,2,128,1152]{3,2,1,0:T(8,128)(2,1)S(1)} collective-permute-done((bf16[2,2,128,1152]{3,2,1,0:T(8,128)(2,1)}, bf16[2,2,128,1152]{3,2,1,0:T(8,128)(2,1)S(1)}, u32[]{:S(2)}, u32[]{:S(2)}) %collective-permute-start.24) | collective-permute-done | bytes 1179680 | tf_op jit(solution)/shard_map/ppermute | solution.py:24
  971.5 4.0 fusion.130
  975.4 6.3 collective-permute-start.25
  983.2 33.9 %collective-permute-done.25 = bf16[2,2,128,1152]{3,2,1,0:T(8,128)(2,1)S(1)} collective-permute-done((bf16[2,2,128,1152]{3,2,1,0:T(8,128)(2,1)}, bf16[2,2,128,1152]{3,2,1,0:T(8,128)(2,1)S(1)}, u32[]{:S(2)}, u32[]{:S(2)}) %collective-permute-start.25) | collective-permute-done | bytes 1179680 | tf_op jit(solution)/shard_map/ppermute | solution.py:24
  1020.6 29.2 %collective-permute-done.26 = bf16[2,2,128,1152]{3,2,1,0:T(8,128)(2,1)} collective-permute-done((bf16[2,2,128,1152]{3,2,1,0:T(8,128)(2,1)}, bf16[2,2,128,1152]{3,2,1,0:T(8,128)(2,1)}, u32[]{:S(2)}, u32[]{:S(2)}) %collective-permute-start.26) | collective-permute-done | bytes 1179680 | tf_op jit(solution)/shard_map/ppermute | solution.py:24
  1049.7 4.0 fusion.54
  1062.8 76.2 %all-reduce.4 = (f32[4,1152]{1,0:T(4,128)}, f32[2,256]{1,0:T(2,128)}) all-reduce(f32[4,1152]{1,0:T(4,128)} %pad_maximum_fusion.8, f32[2,256]{1,0:T(2,128)S(1)} %pad_maximum_fusion.9), channel_id=1, replica_groups=mesh['seq'=16,'fsdp'=2] {'seq','fsdp'}, use_global_device_ids=true, to_apply=%region_38.39 | all-reduce | flops 5120 | bytes 40960 | tf_op jit(solution)/shard_map/psum | solution.py:335
  1139.1 4.0 convert_select_fusion
  1144.7 762.2 %all-reduce.6 = f32[3456,1152]{1,0:T(8,128)} all-reduce(bf16[3456,1152]{1,0:T(8,128)(2,1)} %reduce-scatter.39.cloned.1.call-done), channel_id=15, replica_groups=mesh['seq'=16,'fsdp'=2] {'seq'}, use_global_device_ids=true, to_apply=%region_33.34.clone | all-reduce | flops 3981312 | bytes 23887872
  1906.9 2.5 constant_dynamic-slice_fusion
  (484 shorter events, 146.6 us)
Async XLA Ops:
  7.2 284.3 %all-gather.6.cloned.1.call-start = ((), (), s32[]{:S(2)}) async-start(), calls=%async_computation.13 | async-start | bytes 3538944 | tf_op jit(solution)/shard_map/all_gather | solution.py:138
  7.9 337.7 %all-gather.8.cloned.1.call-start = ((), (), s32[]{:S(2)}) async-start(), calls=%async_computation.14 | async-start | bytes 3538944 | tf_op jit(solution)/shard_map/all_gather | solution.py:141
  8.7 342.2 %all-gather.10.cloned.1.call-start = ((), (), s32[]{:S(2)}) async-start(), calls=%async_computation.15 | async-start | bytes 23887872 | tf_op jit(solution)/shard_map/all_gather | solution.py:142
  9.4 353.9 %all-gather.12.cloned.1.call-start = ((), (), s32[]{:S(2)}) async-start(), calls=%async_computation.16 | async-start | bytes 23887872 | tf_op jit(solution)/shard_map/all_gather | solution.py:143
  10.0 368.0 %all-gather.14.cloned.1.call-start = ((), (), s32[]{:S(2)}) async-start(), calls=%async_computation.17 | async-start | bytes 23887872 | tf_op jit(solution)/shard_map/all_gather | solution.py:144
  11.2 29.0 %collective-permute-start = (bf16[2,2,128,1152]{3,2,1,0:T(8,128)(2,1)S(1)}, bf16[2,2,128,1152]{3,2,1,0:T(8,128)(2,1)S(1)}, u32[]{:S(2)}, u32[]{:S(2)}) collective-permute-start(bf16[2,2,128,1152]{3,2,1,0:T(8,128)(2,1)S(1)} %constant_dynamic-update-slice_fusion), channel_id=1, source_target_pairs={{0,2},{2,0},{4,6},{6,4},{8,10},{10,8},{12,14},{14,12},{16,18},{18,... | collective-permute-start | bytes 3538952 | tf_op jit(solution)/shard_map/ppermute | solution.py:24
  14.2 211.1 %copy-start.84 = (s32[1024]{0:T(1024)}, s32[1024]{0:T(1024)S(1)}, u32[]{:S(2)}) copy-start(s32[1024]{0:T(1024)S(1)} %get-tuple-element.141) | copy-start | bytes 12292
  14.2 211.8 %copy-start.83 = (s32[1024]{0:T(1024)}, s32[1024]{0:T(1024)S(1)}, u32[]{:S(2)}) copy-start(s32[1024]{0:T(1024)S(1)} %get-tuple-element.142) | copy-start | bytes 12292
  14.9 26.1 %copy-start.104 = (s32[16]{0:T(128)}, s32[16]{0:T(128)S(1)}, u32[]{:S(2)}) copy-start(s32[16]{0:T(128)S(1)} %gather_fusion.10) | copy-start | bytes 196
  40.9 27.2 %collective-permute-start.1 = (bf16[2,2,128,1152]{3,2,1,0:T(8,128)(2,1)S(1)}, bf16[2,2,128,1152]{3,2,1,0:T(8,128)(2,1)S(1)}, u32[]{:S(2)}, u32[]{:S(2)}) collective-permute-start(bf16[2,2,128,1152]{3,2,1,0:T(8,128)(2,1)S(1)} %broadcast_select_fusion), channel_id=1, source_target_pairs={{0,4},{4,0},{2,6},{6,2},{8,12},{12,8},{10,14},{14,10},{16,20},{20,... | collective-permute-start | bytes 3538952 | tf_op jit(solution)/shard_map/ppermute | solution.py:24
  44.1 24.9 %copy-start.101 = (s32[16]{0:T(128)}, s32[16]{0:T(128)S(1)}, u32[]{:S(2)}) copy-start(s32[16]{0:T(128)S(1)} %gather_fusion.11) | copy-start | bytes 196
  68.9 26.3 %collective-permute-start.2 = (bf16[2,2,128,1152]{3,2,1,0:T(8,128)(2,1)S(1)}, bf16[2,2,128,1152]{3,2,1,0:T(8,128)(2,1)S(1)}, u32[]{:S(2)}, u32[]{:S(2)}) collective-permute-start(bf16[2,2,128,1152]{3,2,1,0:T(8,128)(2,1)S(1)} %broadcast_select_fusion.1), channel_id=1, source_target_pairs={{0,2},{2,0},{4,6},{6,4},{8,10},{10,8},{12,14},{14,12},{16,18},{18,... | collective-permute-start | bytes 3538952 | tf_op jit(solution)/shard_map/ppermute | solution.py:24
  71.8 24.3 %copy-start.99 = (s32[16]{0:T(128)}, s32[16]{0:T(128)S(1)}, u32[]{:S(2)}) copy-start(s32[16]{0:T(128)S(1)} %gather_fusion.12) | copy-start | bytes 196
  96.0 25.4 %collective-permute-start.3 = (bf16[2,2,128,1152]{3,2,1,0:T(8,128)(2,1)S(1)}, bf16[2,2,128,1152]{3,2,1,0:T(8,128)(2,1)S(1)}, u32[]{:S(2)}, u32[]{:S(2)}) collective-permute-start(bf16[2,2,128,1152]{3,2,1,0:T(8,128)(2,1)S(1)} %broadcast_select_fusion.2), channel_id=1, source_target_pairs={{0,8},{8,0},{2,10},{10,2},{4,12},{12,4},{6,14},{14,6},{16,24},{24,... | collective-permute-start | bytes 3538952 | tf_op jit(solution)/shard_map/ppermute | solution.py:24
  97.9 23.5 %copy-start.90 = (s32[1024]{0:T(1024)}, s32[1024]{0:T(1024)S(1)}, u32[]{:S(2)}) copy-start(s32[1024]{0:T(1024)S(1)} %get-tuple-element.140) | copy-start | bytes 12292
  99.2 23.0 %copy-start.102 = (s32[16]{0:T(128)}, s32[16]{0:T(128)S(1)}, u32[]{:S(2)}) copy-start(s32[16]{0:T(128)S(1)} %gather_fusion.13) | copy-start | bytes 196
  122.2 24.5 %collective-permute-start.4 = (bf16[2,2,128,1152]{3,2,1,0:T(8,128)(2,1)S(1)}, bf16[2,2,128,1152]{3,2,1,0:T(8,128)(2,1)S(1)}, u32[]{:S(2)}, u32[]{:S(2)}) collective-permute-start(bf16[2,2,128,1152]{3,2,1,0:T(8,128)(2,1)S(1)} %broadcast_select_fusion.3), channel_id=1, source_target_pairs={{0,4},{4,0},{2,6},{6,2},{8,12},{12,8},{10,14},{14,10},{16,20},{20,... | collective-permute-start | bytes 3538952 | tf_op jit(solution)/shard_map/ppermute | solution.py:24
  124.4 23.0 %copy-start.103 = (s32[16]{0:T(128)}, s32[16]{0:T(128)S(1)}, u32[]{:S(2)}) copy-start(s32[16]{0:T(128)S(1)} %gather_fusion.14) | copy-start | bytes 196
  147.5 23.5 %collective-permute-start.5 = (bf16[2,2,128,1152]{3,2,1,0:T(8,128)(2,1)S(1)}, bf16[2,2,128,1152]{3,2,1,0:T(8,128)(2,1)S(1)}, u32[]{:S(2)}, u32[]{:S(2)}) collective-permute-start(bf16[2,2,128,1152]{3,2,1,0:T(8,128)(2,1)S(1)} %broadcast_select_fusion.4), channel_id=1, source_target_pairs={{0,2},{2,0},{4,6},{6,4},{8,10},{10,8},{12,14},{14,12},{16,18},{18,... | collective-permute-start | bytes 3538952 | tf_op jit(solution)/shard_map/ppermute | solution.py:24
  172.8 48.1 %collective-permute-start.6 = (bf16[2,2,128,1152]{3,2,1,0:T(8,128)(2,1)S(1)}, bf16[2,2,128,1152]{3,2,1,0:T(8,128)(2,1)S(1)}, u32[]{:S(2)}, u32[]{:S(2)}) collective-permute-start(bf16[2,2,128,1152]{3,2,1,0:T(8,128)(2,1)S(1)} %broadcast_select_fusion.5), channel_id=1, source_target_pairs={{0,16},{16,0},{2,18},{18,2},{4,20},{20,4},{6,22},{22,6},{8,24},{24... | collective-permute-start | bytes 3538952 | tf_op jit(solution)/shard_map/ppermute | solution.py:24
  222.9 28.0 %collective-permute-start.7 = (bf16[2,2,128,1152]{3,2,1,0:T(8,128)(2,1)S(1)}, bf16[2,2,128,1152]{3,2,1,0:T(8,128)(2,1)S(1)}, u32[]{:S(2)}, u32[]{:S(2)}) collective-permute-start(bf16[2,2,128,1152]{3,2,1,0:T(8,128)(2,1)S(1)} %broadcast_select_fusion.6), channel_id=1, source_target_pairs={{0,8},{8,0},{2,10},{10,2},{4,12},{12,4},{6,14},{14,6},{16,24},{24,... | collective-permute-start | bytes 3538952 | tf_op jit(solution)/shard_map/ppermute | solution.py:24
  223.9 373.7 %reduce-scatter.35.cloned.1.call-start = ((), (), s32[]{:S(2)}) async-start(), calls=%async_computation.20 | async-start | bytes 884736 | tf_op jit(solution)/shard_map/reduce_scatter | solution.py:343
  251.6 27.1 %collective-permute-start.8 = (bf16[2,2,128,1152]{3,2,1,0:T(8,128)(2,1)S(1)}, bf16[2,2,128,1152]{3,2,1,0:T(8,128)(2,1)S(1)}, u32[]{:S(2)}, u32[]{:S(2)}) collective-permute-start(bf16[2,2,128,1152]{3,2,1,0:T(8,128)(2,1)S(1)} %broadcast_select_fusion.7), channel_id=1, source_target_pairs={{0,4},{4,0},{2,6},{6,2},{8,12},{12,8},{10,14},{14,10},{16,20},{20,... | collective-permute-start | bytes 3538952 | tf_op jit(solution)/shard_map/ppermute | solution.py:24
  279.5 26.2 %collective-permute-start.9 = (bf16[2,2,128,1152]{3,2,1,0:T(8,128)(2,1)S(1)}, bf16[2,2,128,1152]{3,2,1,0:T(8,128)(2,1)S(1)}, u32[]{:S(2)}, u32[]{:S(2)}) collective-permute-start(bf16[2,2,128,1152]{3,2,1,0:T(8,128)(2,1)S(1)} %broadcast_select_fusion.8), channel_id=1, source_target_pairs={{0,2},{2,0},{4,6},{6,4},{8,10},{10,8},{12,14},{14,12},{16,18},{18,... | collective-permute-start | bytes 3538952 | tf_op jit(solution)/shard_map/ppermute | solution.py:24
  284.1 42.3 %copy-start.59 = (f32[1152]{0:T(1024)}, f32[1152]{0:T(1024)S(1)}, u32[]{:S(2)}) copy-start(f32[1152]{0:T(1024)S(1)} %get-tuple-element.69) | copy-start | bytes 13828
  291.5 36.8 %copy-start.71 = (f32[1,256]{1,0:T(1,128)}, f32[1,256]{1,0:T(1,128)S(1)}, u32[]{:S(2)}) copy-start(f32[1,256]{1,0:T(1,128)S(1)} %get-tuple-element.106) | copy-start | bytes 3076
  307.6 41.3 %copy-start.4 = (bf16[2,2,128,1152]{3,2,1,0:T(8,128)(2,1)}, bf16[2,2,128,1152]{3,2,1,0:T(8,128)(2,1)S(1)}, u32[]{:S(2)}) copy-start(bf16[2,2,128,1152]{3,2,1,0:T(8,128)(2,1)S(1)} %broadcast_select_fusion.9) | copy-start | bytes 3538948
  310.4 18.9 copy-start.40
  311.0 20.4 %collective-permute-start.13 = (bf16[2,128,512]{2,1,0:T(8,128)(2,1)S(1)}, bf16[2,128,512]{2,1,0:T(8,128)(2,1)S(1)}, u32[]{:S(2)}, u32[]{:S(2)}) collective-permute-start(bf16[2,128,512]{2,1,0:T(8,128)(2,1)S(1)} %pad_maximum_fusion.6), channel_id=1, source_target_pairs={{0,2},{2,4},{4,6},{6,8},{8,10},{10,12},{12,14},{14,16},{16,18},{18... | collective-permute-start | bytes 786440 | tf_op jit(solution)/shard_map/ppermute | solution.py:30
  313.7 17.7 collective-permute-start.12
  318.9 14.0 collective-permute-start.11
  323.6 7.8 collective-permute-start.10
  350.1 77.9 %copy-start.85 = (f32[256]{0:T(256)}, f32[256]{0:T(256)S(1)}, u32[]{:S(2)}) copy-start(f32[256]{0:T(256)S(1)} %get-tuple-element.120) | copy-start | bytes 3076
  391.0 24.6 %copy-start.25 = (bf16[256,1152]{1,0:T(8,128)(2,1)}, bf16[256,1152]{1,0:T(8,128)(2,1)S(1)}, u32[]{:S(2)}) copy-start(bf16[256,1152]{1,0:T(8,128)(2,1)S(1)} %fusion.39) | copy-start | bytes 1769476
  465.5 26.8 %copy-start.18 = (f32[2,639,256]{2,1,0:T(8,128)S(1)}, f32[2,639,256]{2,1,0:T(8,128)}, u32[]{:S(2)}) copy-start(f32[2,639,256]{2,1,0:T(8,128)} %fusion.15) | copy-start | bytes 3926020
  465.7 26.6 %collective-permute-start.15 = (bf16[2,128,512]{2,1,0:T(8,128)(2,1)S(1)}, bf16[2,128,512]{2,1,0:T(8,128)(2,1)S(1)}, u32[]{:S(2)}, u32[]{:S(2)}) collective-permute-start(bf16[2,128,512]{2,1,0:T(8,128)(2,1)S(1)} %get-tuple-element.88), channel_id=1, source_target_pairs={{6,0},{8,2},{10,4},{12,6},{14,8},{16,10},{18,12},{20,14},{22,16},{... | collective-permute-start | bytes 786440 | tf_op jit(solution)/shard_map/ppermute | solution.py:30
  467.2 25.1 %collective-permute-start.17 = (bf16[2,128,512]{2,1,0:T(8,128)(2,1)S(1)}, bf16[2,128,512]{2,1,0:T(8,128)(2,1)S(1)}, u32[]{:S(2)}, u32[]{:S(2)}) collective-permute-start(bf16[2,128,512]{2,1,0:T(8,128)(2,1)S(1)} %get-tuple-element.89), channel_id=1, source_target_pairs={{2,0},{4,2},{6,4},{8,6},{10,8},{12,10},{14,12},{16,14},{18,16},{20... | collective-permute-start | bytes 786440 | tf_op jit(solution)/shard_map/ppermute | solution.py:30
  468.5 23.8 %collective-permute-start.16 = (bf16[2,128,512]{2,1,0:T(8,128)(2,1)S(1)}, bf16[2,128,512]{2,1,0:T(8,128)(2,1)S(1)}, u32[]{:S(2)}, u32[]{:S(2)}) collective-permute-start(bf16[2,128,512]{2,1,0:T(8,128)(2,1)S(1)} %get-tuple-element.90), channel_id=1, source_target_pairs={{4,0},{6,2},{8,4},{10,6},{12,8},{14,10},{16,12},{18,14},{20,16},{2... | collective-permute-start | bytes 786440 | tf_op jit(solution)/shard_map/ppermute | solution.py:30
  469.8 23.6 %copy-start.13 = (bf16[1,2,128,1152]{3,2,1,0:T(8,128)(2,1)S(1)}, bf16[1,2,128,1152]{3,2,1,0:T(8,128)(2,1)}, u32[]{:S(2)}) copy-start(bf16[1,2,128,1152]{3,2,1,0:T(8,128)(2,1)} %copy-done.12) | copy-start | bytes 1769476
  469.8 22.5 %collective-permute-start.14 = (bf16[2,127,512]{2,1,0:T(8,128)(2,1)S(1)}, bf16[2,127,512]{2,1,0:T(8,128)(2,1)S(1)}, u32[]{:S(2)}, u32[]{:S(2)}) collective-permute-start(bf16[2,127,512]{2,1,0:T(8,128)(2,1)S(1)} %slice.168), channel_id=1, source_target_pairs={{8,0},{10,2},{12,4},{14,6},{16,8},{18,10},{20,12},{22,14},{24,16},... | collective-permute-start | bytes 780296 | tf_op jit(solution)/shard_map/ppermute | solution.py:30
  494.6 105.1 %reduce-scatter.33.cloned.1.call-start = ((), (), s32[]{:S(2)}) async-start(), calls=%async_computation.19 | async-start | bytes 884736 | tf_op jit(solution)/shard_map/reduce_scatter | solution.py:340
  498.1 103.8 %reduce-scatter.37.cloned.1.call-start = ((), (), s32[]{:S(2)}) async-start(), calls=%async_computation.21 | async-start | bytes 3538944 | tf_op jit(solution)/shard_map/reduce_scatter | solution.py:346
  500.5 104.5 %reduce-scatter.31.cloned.1.call-start = ((), (), s32[]{:S(2)}) async-start(), calls=%async_computation.18 | async-start | bytes 3538944 | tf_op jit(solution)/shard_map/reduce_scatter | solution.py:337
  520.9 87.1 %reduce-scatter.51.cloned.1.call-start = ((), (), s32[]{:S(2)}) async-start(), calls=%async_computation.28 | async-start | bytes 23887872
  552.6 80.6 %reduce-scatter.49.cloned.1.call-start = ((), (), s32[]{:S(2)}) async-start(), calls=%async_computation.27 | async-start | bytes 23887872
  585.5 559.2 %reduce-scatter.39.cloned.1.call-start = ((), (), s32[]{:S(2)}) async-start(), calls=%async_computation.22 | async-start | bytes 23887872 | tf_op jit(solution)/shard_map/reduce_scatter | solution.py:355
  597.5 1313.4 %reduce-scatter.45.cloned.1.call-start = ((), (), s32[]{:S(2)}) async-start(), calls=%async_computation.25 | async-start | bytes 696320
  599.6 1311.3 %reduce-scatter.43.cloned.1.call-start = ((), (), s32[]{:S(2)}) async-start(), calls=%async_computation.24 | async-start | bytes 696320
  601.8 1309.1 %reduce-scatter.47.cloned.1.call-start = ((), (), s32[]{:S(2)}) async-start(), calls=%async_computation.26 | async-start | bytes 2785280
  604.9 1306.0 %reduce-scatter.41.cloned.1.call-start = ((), (), s32[]{:S(2)}) async-start(), calls=%async_computation.23 | async-start | bytes 2785280
  607.9 1303.0 %reduce-scatter.55.cloned.1.call-start = ((), (), s32[]{:S(2)}) async-start(), calls=%async_computation.30 | async-start | bytes 16920576
  633.1 1277.9 %reduce-scatter.53.cloned.1.call-start = ((), (), s32[]{:S(2)}) async-start(), calls=%async_computation.29 | async-start | bytes 16920576
  664.6 30.7 %collective-permute-start.18 = (bf16[2,2,128,1152]{3,2,1,0:T(8,128)(2,1)}, bf16[2,2,128,1152]{3,2,1,0:T(8,128)(2,1)S(1)}, u32[]{:S(2)}, u32[]{:S(2)}) collective-permute-start(bf16[2,2,128,1152]{3,2,1,0:T(8,128)(2,1)} %fusion.20), channel_id=1, source_target_pairs={{0,2},{2,0},{4,6},{6,4},{8,10},{10,8},{12,14},{14,12},{16,18},{18,... | collective-permute-start | bytes 3538952 | tf_op jit(solution)/shard_map/ppermute | solution.py:24
  697.2 26.3 %collective-permute-start.19 = (bf16[2,2,128,1152]{3,2,1,0:T(8,128)(2,1)}, bf16[2,2,128,1152]{3,2,1,0:T(8,128)(2,1)}, u32[]{:S(2)}, u32[]{:S(2)}) collective-permute-start(bf16[2,2,128,1152]{3,2,1,0:T(8,128)(2,1)} %fusion.87), channel_id=1, source_target_pairs={{0,4},{4,0},{2,6},{6,2},{8,12},{12,8},{10,14},{14,10},{16,20},{20,... | collective-permute-start | bytes 3538952 | tf_op jit(solution)/shard_map/ppermute | solution.py:24
  727.5 29.0 %collective-permute-start.20 = (bf16[2,2,128,1152]{3,2,1,0:T(8,128)(2,1)}, bf16[2,2,128,1152]{3,2,1,0:T(8,128)(2,1)}, u32[]{:S(2)}, u32[]{:S(2)}) collective-permute-start(bf16[2,2,128,1152]{3,2,1,0:T(8,128)(2,1)} %fusion.21), channel_id=1, source_target_pairs={{0,2},{2,0},{4,6},{6,4},{8,10},{10,8},{12,14},{14,12},{16,18},{18,... | collective-permute-start | bytes 3538952 | tf_op jit(solution)/shard_map/ppermute | solution.py:24
  762.6 34.2 %collective-permute-start.21 = (bf16[2,2,128,1152]{3,2,1,0:T(8,128)(2,1)}, bf16[2,2,128,1152]{3,2,1,0:T(8,128)(2,1)S(1)}, u32[]{:S(2)}, u32[]{:S(2)}) collective-permute-start(bf16[2,2,128,1152]{3,2,1,0:T(8,128)(2,1)} %get-tuple-element.79), channel_id=1, source_target_pairs={{0,8},{8,0},{2,10},{10,2},{4,12},{12,4},{6,14},{14,6},{16,24},{24,... | collective-permute-start | bytes 3538952 | tf_op jit(solution)/shard_map/ppermute | solution.py:24
  796.8 35.8 %copy-start.3 = (f32[2,2,128,1152]{3,2,1,0:T(8,128)S(1)}, f32[2,2,128,1152]{3,2,1,0:T(8,128)}, u32[]{:S(2)}) copy-start(f32[2,2,128,1152]{3,2,1,0:T(8,128)} %get-tuple-element.80) | copy-start | bytes 7077892
  800.6 32.1 %collective-permute-start.22 = (bf16[2,2,128,1152]{3,2,1,0:T(8,128)(2,1)}, bf16[2,2,128,1152]{3,2,1,0:T(8,128)(2,1)}, u32[]{:S(2)}, u32[]{:S(2)}) collective-permute-start(bf16[2,2,128,1152]{3,2,1,0:T(8,128)(2,1)} %fusion.22), channel_id=1, source_target_pairs={{0,4},{4,0},{2,6},{6,2},{8,12},{12,8},{10,14},{14,10},{16,20},{20,... | collective-permute-start | bytes 3538952 | tf_op jit(solution)/shard_map/ppermute | solution.py:24
  837.5 52.2 %collective-permute-start.23 = (bf16[2,2,128,1152]{3,2,1,0:T(8,128)(2,1)}, bf16[2,2,128,1152]{3,2,1,0:T(8,128)(2,1)S(1)}, u32[]{:S(2)}, u32[]{:S(2)}) collective-permute-start(bf16[2,2,128,1152]{3,2,1,0:T(8,128)(2,1)} %get-tuple-element.77), channel_id=1, source_target_pairs={{0,2},{2,0},{4,6},{6,4},{8,10},{10,8},{12,14},{14,12},{16,18},{18,... | collective-permute-start | bytes 3538952 | tf_op jit(solution)/shard_map/ppermute | solution.py:24
  891.6 78.9 %collective-permute-start.24 = (bf16[2,2,128,1152]{3,2,1,0:T(8,128)(2,1)}, bf16[2,2,128,1152]{3,2,1,0:T(8,128)(2,1)S(1)}, u32[]{:S(2)}, u32[]{:S(2)}) collective-permute-start(bf16[2,2,128,1152]{3,2,1,0:T(8,128)(2,1)} %fusion.23), channel_id=1, source_target_pairs={{0,16},{16,0},{2,18},{18,2},{4,20},{20,4},{6,22},{22,6},{8,24},{24... | collective-permute-start | bytes 3538952 | tf_op jit(solution)/shard_map/ppermute | solution.py:24
  975.4 41.7 %collective-permute-start.25 = (bf16[2,2,128,1152]{3,2,1,0:T(8,128)(2,1)}, bf16[2,2,128,1152]{3,2,1,0:T(8,128)(2,1)S(1)}, u32[]{:S(2)}, u32[]{:S(2)}) collective-permute-start(bf16[2,2,128,1152]{3,2,1,0:T(8,128)(2,1)} %get-tuple-element.75), channel_id=1, source_target_pairs={{0,8},{8,0},{2,10},{10,2},{4,12},{12,4},{6,14},{14,6},{16,24},{24,... | collective-permute-start | bytes 3538952 | tf_op jit(solution)/shard_map/ppermute | solution.py:24
  1019.2 30.6 %collective-permute-start.26 = (bf16[2,2,128,1152]{3,2,1,0:T(8,128)(2,1)}, bf16[2,2,128,1152]{3,2,1,0:T(8,128)(2,1)}, u32[]{:S(2)}, u32[]{:S(2)}) collective-permute-start(bf16[2,2,128,1152]{3,2,1,0:T(8,128)(2,1)} %fusion.24), channel_id=1, source_target_pairs={{0,4},{4,0},{2,6},{6,2},{8,12},{12,8},{10,14},{14,10},{16,20},{20,... | collective-permute-start | bytes 3538952 | tf_op jit(solution)/shard_map/ppermute | solution.py:24
  1020.0 33.8 %copy-start.100 = (s32[16]{0:T(128)}, s32[16]{0:T(128)S(1)}, u32[]{:S(2)}) copy-start(s32[16]{0:T(128)S(1)} %gather_fusion.8) | copy-start | bytes 196
  1053.8 85.3 %collective-permute-start.27 = (bf16[2,2,128,1152]{3,2,1,0:T(8,128)(2,1)}, bf16[2,2,128,1152]{3,2,1,0:T(8,128)(2,1)}, u32[]{:S(2)}, u32[]{:S(2)}) collective-permute-start(bf16[2,2,128,1152]{3,2,1,0:T(8,128)(2,1)} %fusion.54), channel_id=1, source_target_pairs={{0,2},{2,0},{4,6},{6,4},{8,10},{10,8},{12,14},{14,12},{16,18},{18,... | collective-permute-start | bytes 3538952 | tf_op jit(solution)/shard_map/ppermute | solution.py:24
  (87 other events, 248.0 us)
Sparse Core Ops, SparseCore 0:
  9.6 13.6 all-gather.5
  24.8 12.1 all-gather.7
  38.5 29.9 all-gather.9
  69.9 29.9 all-gather.11
  224.0 29.8 all-gather.13
  494.8 9.6 reduce-scatter.34
  507.4 9.2 reduce-scatter.32
  518.9 11.0 reduce-scatter.36
  532.3 11.0 reduce-scatter.30
  552.7 29.3 reduce-scatter.50
  585.6 30.1 reduce-scatter.48
  618.0 27.0 reduce-scatter.38
  648.0 78.7 reduce-scatter.44
  729.5 74.8 reduce-scatter.42
  807.2 90.8 reduce-scatter.46
  900.9 88.0 reduce-scatter.40
  996.3 323.9 reduce-scatter.54
  1327.4 442.7 reduce-scatter.52
where the time goes:
time: 1940 us; the launch traced here: 1920 us
  blocking collectives  845 us (44%)
  waiting for transfers between devices  576 us (30%)
  matrix products  164 us (8%)
  local copies, waits for them, and re-layouts  156 us (8%)
  other arithmetic  95 us (5%)
  starting transfers between devices  65 us (3%)
    unnamed x1, blocking collectives  762 us
    ppermute x20, waiting for transfers between devices, from_partner(): return lax.ppermute(block, axis, route)  552 us
    unnamed x223, local copies, waits for them, and re-layouts  102 us
    psum x1, blocking collectives, shards(): norm_total, head_total = lax.psum((norm_terms, head_terms), ('seq', 'fsdp'))  76.2 us
    ppermute x20, starting transfers between devices, from_partner(): return lax.ppermute(block, axis, route)  43.4 us
  transfers between devices with their start and end apart: 46, of which 20 were waited for; matrix products, arithmetic and copies ran while one was open for 16% of the time, Pallas kernels for 0%

commit v1 on v0

v1 whole, which is shorter than its diff:
```python
import math

import jax
import jax.numpy as jnp
from jax import lax
from jax.sharding import PartitionSpec as P

HQ = 4
HD = 256
W = 512
EPSILON = 1e-06
ROPE_BASE = 10000.0
SPLIT_BIT = 4

BF = jnp.bfloat16
F32 = jnp.float32


def swap(value, axis, mask):
    count = lax.axis_size(axis)
    return lax.ppermute(value, axis, [(i, i ^ mask) for i in range(count)])


def masks(count):
    return [1 << k for k in range(count.bit_length() - 1)]


def gather_cores(block):
    for mask in masks(lax.axis_size("fsdp")):
        block = jnp.concatenate([block, swap(block, "fsdp", mask)], axis=0)
    return block


def sum_cores(block):
    for mask in reversed(masks(lax.axis_size("fsdp"))):
        half = block.shape[0] // 2
        got = swap(block[half:].astype(BF), "fsdp", mask)
        block = block[:half].astype(F32) + got.astype(F32)
    return block


def flip(parts, index):
    count = parts.shape[0]
    for mask in masks(count):
        turned = jnp.stack([parts[j ^ mask] for j in range(count)])
        parts = jnp.where((index & mask) != 0, turned, parts)
    return parts


def rms_scale(values):
    return lax.rsqrt(jnp.mean(values * values, axis=-1, keepdims=True) + EPSILON)


def rms_forward(values, gain_vec):
    return values * rms_scale(values) * gain_vec


def rms_backward(values, gain_vec, grad_out):
    scale_rows = rms_scale(values)
    weighted = grad_out * gain_vec
    inner_mean = jnp.mean(weighted * values, axis=-1, keepdims=True)
    grad_in = scale_rows * weighted - values * (scale_rows * scale_rows * scale_rows) * inner_mean
    return (grad_in, grad_out * values * scale_rows)


def rope_tables(seq_pos, head_dim):
    half_dim = head_dim // 2
    frequency = jnp.exp(
        jnp.arange(half_dim, dtype=F32) * (-2.0 * math.log(ROPE_BASE) / head_dim)
    )
    angles = seq_pos.astype(F32)[..., None] * frequency
    return (jnp.cos(angles), jnp.sin(angles))


def rotate(values, cosine_table, sine_table):
    half_dim = values.shape[-1] // 2
    first_half = values[..., :half_dim]
    second_half = values[..., half_dim:]
    return jnp.concatenate(
        [
            first_half * cosine_table - second_half * sine_table,
            second_half * cosine_table + first_half * sine_table,
        ],
        axis=-1,
    )


def gelu_tanh(values):
    return jax.nn.gelu(values, approximate=True)


def sequence_info(lengths, stream_pos):
    seq_ends = jnp.cumsum(lengths, axis=-1)
    before = seq_ends[..., None, :] <= stream_pos[..., :, None]
    seq_ids = jnp.sum(before.astype(jnp.int32), axis=-1)
    starts = jnp.sum(jnp.where(before, lengths[..., None, :], 0), axis=-1)
    return (seq_ids, stream_pos - starts)


def dot(a, b):
    return jnp.dot(a, b, preferred_element_type=F32)


def dot_tn(a, b):
    return lax.dot_general(a, b, (((0,), (0,)), ((), ())), preferred_element_type=F32)


def dot_nt(a, b):
    return lax.dot_general(a, b, (((1,), (1,)), ((), ())), preferred_element_type=F32)


def pick(table, source):
    return jnp.take(source, table, axis=0)


def pick_sum(hops, table, valid, source):
    terms = jnp.take(source, table, axis=0).astype(F32) * valid.astype(F32)[:, None, None]
    count = table.shape[0] // hops
    return jnp.sum(terms.reshape((count, hops) + source.shape[1:]), axis=1).astype(source.dtype)


def halve(block, order, own, keep_bits=()):
    count = block.shape[0]
    bits = masks(count)[::-1]
    shape = block.shape[1:]
    block = block.reshape((2,) * len(bits) + shape)
    left = list(bits)
    for mask in order:
        axis = left.index(mask)
        mine = ((own & mask) != 0).astype(jnp.int32)
        sent = lax.dynamic_index_in_dim(block, 1 - mine, axis, keepdims=False)
        kept = lax.dynamic_index_in_dim(block, mine, axis, keepdims=False)
        got = swap(sent.astype(BF), "seq", mask)
        block = kept.astype(F32) + got.astype(F32)
        left.remove(mask)
        if mask != order[-1] or left:
            block = block.astype(BF)
    return block.reshape((2 ** len(left),) + shape)


def shards(
    tokens,
    cotangent,
    lengths,
    deal_order,
    w_query,
    w_key,
    w_value,
    w_out,
    w_gate,
    w_up,
    w_down,
    norm_gains,
    head_gains,
):
    lanes, rows, width = tokens.shape[1:]
    total = lanes * rows
    seq_count = lax.axis_size("seq")
    cores = lax.axis_size("fsdp")
    own = lax.axis_index("seq")
    core = lax.axis_index("fsdp")
    window = W
    hops = (window - 1 + rows - 1) // rows
    chunk = total // seq_count

    deal = deal_order[0]
    places = jnp.arange(seq_count, dtype=jnp.int32)
    back = jnp.sum(jnp.where(deal[None, :] == places[:, None], places[None, :], 0), axis=1)
    place = deal[own]
    steps = jnp.arange(1, hops + 1, dtype=jnp.int32)
    wanted = deal[:, None] - steps[None, :]
    fetch_table = back[jnp.maximum(wanted, 0)].reshape(-1)
    readers = deal[:, None] + steps[None, :]
    reader_ok = (readers < seq_count).astype(jnp.int32).reshape(-1)
    reader_table = (
        back[jnp.minimum(readers, seq_count - 1)] * hops + (steps[None, :] - 1)
    ).reshape(-1)

    inputs = tokens[0].astype(F32).reshape(total, width)
    upstream = cotangent[0].astype(F32).reshape(total, width)

    w_in = jnp.concatenate([w_query, w_key, w_value], axis=1)
    peers_in = gather_cores(w_in).reshape((cores,) + w_in.shape)
    w_in_full = flip(peers_in, core).reshape(width, w_in.shape[1])
    peers_out = gather_cores(w_out).reshape((cores,) + w_out.shape)
    peers_out = flip(peers_out, core)
    w_out_full = jnp.concatenate([peers_out[j] for j in range(cores)], axis=1)
    q_width = HQ * HD

    gain_in, gain_mid, gain_ffn, gain_top = (norm_gains[i] for i in range(4))
    query_gain, key_gain = (head_gains[0], head_gains[1])

    local_stream = place * rows + jnp.arange(rows, dtype=jnp.int32)
    query_ids, query_pos = sequence_info(lengths[0], jnp.broadcast_to(local_stream, (lanes, rows)))
    cosine, sine = rope_tables(query_pos, HD)

    attn_in = rms_forward(inputs, gain_in).astype(BF)
    kv_proj = dot(attn_in, w_in_full[:, q_width:])
    key_proj = kv_proj[:, :HD].reshape(lanes, rows, HD)
    value_proj = kv_proj[:, HD:].reshape(lanes, rows, HD).astype(BF)
    key_rot = rotate(rms_forward(key_proj, key_gain), cosine, sine).astype(BF)
    kv_local = jnp.concatenate([key_rot, value_proj], axis=-1)

    spread = lax.all_to_all(
        kv_local.reshape(seq_count, chunk, 2 * HD), "seq", 0, 0, tiled=True
    )
    picked = pick(fetch_table, spread).reshape(seq_count, hops * chunk, 2 * HD)
    arrived = lax.all_to_all(picked, "seq", 0, 0, tiled=True)
    earlier = (
        arrived.reshape(seq_count, hops, chunk, 2 * HD)
        .transpose(1, 0, 2, 3)
        .reshape(hops, lanes, rows, 2 * HD)
    )

    query_proj = dot(attn_in, w_in_full[:, :q_width]).reshape(lanes, rows, HQ, HD)
    query_rot = rotate(
        rms_forward(query_proj, query_gain), cosine[:, :, None, :], sine[:, :, None, :]
    ).astype(BF)

    hidden_cols = w_gate.shape[1]
    share = hidden_cols // 2
    part = ((own & SPLIT_BIT) != 0).astype(jnp.int32)
    gate_share = lax.dynamic_slice_in_dim(w_gate, part * share, share, 1)
    up_share = lax.dynamic_slice_in_dim(w_up, part * share, share, 1)
    down_share = lax.dynamic_slice_in_dim(w_down, part * share, share, 0)

    kv_all = jnp.concatenate([earlier[d] for d in range(hops - 1, -1, -1)] + [kv_local], axis=1)
    key_total = kv_all.shape[1]
    key_stream = (place - hops) * rows + jnp.arange(key_total, dtype=jnp.int32)
    key_ids = sequence_info(lengths[0], jnp.broadcast_to(key_stream, (lanes, key_total)))[0]
    allowed = (
        (key_ids[:, None, :] == query_ids[:, :, None])
        & (key_stream[None, None, :] <= local_stream[None, :, None])
        & (local_stream[None, :, None] - key_stream[None, None, :] < window)
        & (key_stream[None, None, :] >= 0)
    )
    allowed = jnp.repeat(allowed, HQ, axis=1)
    flat_query = query_rot.reshape(lanes, rows * HQ, HD)
    all_keys = kv_all[..., :HD]
    all_values = kv_all[..., HD:]
    score_scale = HD ** (-0.5)

    raw_scores = jnp.einsum("nfi,nhi->nfh", flat_query, all_keys, preferred_element_type=F32)
    masked = jnp.where(allowed, raw_scores * score_scale, -1e30)
    top_score = jnp.max(masked, axis=-1, keepdims=True)
    exponents = jnp.exp(masked - top_score)
    soft = exponents / jnp.sum(exponents, axis=-1, keepdims=True)
    probs_low = soft.astype(BF)
    mixed_low = (
        jnp.einsum("ajm,amn->ajn", probs_low, all_values, preferred_element_type=F32)
        .reshape(total, q_width)
        .astype(BF)
    )
    branch = dot(mixed_low, w_out_full)
    middle = inputs + rms_forward(branch, gain_mid)
    ffn_in = rms_forward(middle, gain_ffn).astype(BF)

    far_in = swap(ffn_in, "seq", SPLIT_BIT)
    near_all = gather_cores(ffn_in)
    far_all = gather_cores(far_in)

    def ffn_forward(rows_in):
        gate = dot(rows_in, gate_share)
        upward = dot(rows_in, up_share)
        hid = (gelu_tanh(gate) * upward).astype(BF)
        return gate, upward, hid, dot(hid, down_share)

    near = ffn_forward(near_all)
    far = ffn_forward(far_all)

    def sum_group(near_part, far_part):
        far_sum = sum_cores(far_part)
        got = swap(far_sum.astype(BF), "seq", SPLIT_BIT)
        return sum_cores(near_part) + got.astype(F32)

    ffn_out = sum_group(near[3], far[3])
    result = middle + rms_forward(ffn_out, gain_top)

    grad_ffn_out, top_terms = rms_backward(ffn_out, gain_top, upstream)
    grad_low = grad_ffn_out.astype(BF)
    far_grad = swap(grad_low, "seq", SPLIT_BIT)
    near_grads = gather_cores(grad_low)
    far_grads = gather_cores(far_grad)

    def ffn_backward(saved, grads):
        gate, upward, hid, _ = saved
        d_hidden = dot_nt(grads, down_share)
        activated, pull = jax.vjp(gelu_tanh, gate)
        d_gate = pull(d_hidden * upward)[0].astype(BF)
        d_up = (d_hidden * activated).astype(BF)
        return d_gate, d_up, dot_nt(d_gate, gate_share) + dot_nt(d_up, up_share)

    near_back = ffn_backward(near, near_grads)
    far_back = ffn_backward(far, far_grads)

    grad_ffn_in = sum_group(near_back[2], far_back[2])

    def weight_terms(left_near, left_far, right_near, right_far):
        left = jnp.concatenate([left_near, left_far], axis=0)
        right = jnp.concatenate([right_near, right_far], axis=0)
        out = dot_tn(left, right).astype(BF)
        return out.reshape(seq_count, width // seq_count, share)

    others = [m for m in masks(seq_count) if m != SPLIT_BIT]

    def owned(terms, order):
        block = halve(terms, order, own)
        mine = lax.dynamic_index_in_dim(block, part, 0, keepdims=False)
        sent = lax.dynamic_index_in_dim(block, 1 - part, 0, keepdims=False)
        got = swap(sent.astype(BF), "seq", SPLIT_BIT).astype(F32)
        mine = mine.astype(F32)
        return jnp.where(
            part == 0,
            jnp.concatenate([mine, got], axis=1),
            jnp.concatenate([got, mine], axis=1),
        )

    swapped = [others[1], others[0]] + others[2:]
    down_terms = weight_terms(near_grads, far_grads, near[2], far[2])
    down_grad = owned(down_terms, others).T
    gate_terms = weight_terms(near_all, far_all, near_back[0], far_back[0])
    gate_grad = owned(gate_terms, swapped)
    up_terms = weight_terms(near_all, far_all, near_back[1], far_back[1])
    up_grad = owned(up_terms, others)

    grad_middle_norm, ffn_terms = rms_backward(middle, gain_ffn, grad_ffn_in)
    grad_middle = upstream + grad_middle_norm
    grad_branch, mid_terms = rms_backward(branch, gain_mid, grad_middle)
    grad_branch_low = grad_branch.astype(BF)
    grad_mixed = dot_nt(grad_branch_low, w_out_full).astype(BF).reshape(lanes, rows * HQ, HD)

    grad_probs = jnp.einsum("nfi,nhi->nfh", grad_mixed, all_values, preferred_element_type=F32)
    inner_sum = jnp.sum(soft * grad_probs, axis=-1, keepdims=True)
    grad_raw = (soft * (grad_probs - inner_sum) * score_scale).astype(BF)
    grad_query = jnp.einsum("ajm,amn->ajn", grad_raw, all_keys, preferred_element_type=F32)
    grad_keys = jnp.einsum("xzo,xza->xoa", grad_raw, flat_query, preferred_element_type=F32)
    grad_values = jnp.einsum("xzo,xza->xoa", probs_low, grad_mixed, preferred_element_type=F32)
    grad_kv = jnp.concatenate([grad_keys, grad_values], axis=-1)

    outward = (
        jnp.stack(
            [
                grad_kv[:, (hops - d) * rows : (hops - d + 1) * rows].reshape(total, 2 * HD)
                for d in range(1, hops + 1)
            ]
        )
        .astype(BF)
        .reshape(hops, seq_count, chunk, 2 * HD)
        .transpose(1, 0, 2, 3)
        .reshape(seq_count, hops * chunk, 2 * HD)
    )
    collected = lax.all_to_all(outward, "seq", 0, 0, tiled=True)
    summed = pick_sum(
        hops, reader_table, reader_ok, collected.reshape(seq_count * hops, chunk, 2 * HD)
    )
    returned = lax.all_to_all(summed, "seq", 0, 0, tiled=True)
    grad_local = grad_kv[:, hops * rows :] + returned.reshape(lanes, rows, 2 * HD).astype(F32)

    grad_value_low = grad_local[..., HD:].reshape(total, HD).astype(BF)
    key_normed_grad = rotate(grad_local[..., :HD], cosine, -sine)
    grad_key_proj, key_terms = rms_backward(key_proj, key_gain, key_normed_grad)
    grad_key_low = grad_key_proj.reshape(total, HD).astype(BF)
    query_normed_grad = rotate(
        grad_query.reshape(lanes, rows, HQ, HD), cosine[:, :, None, :], -sine[:, :, None, :]
    )
    grad_query_proj, query_terms = rms_backward(query_proj, query_gain, query_normed_grad)
    grad_query_low = grad_query_proj.reshape(total, q_width).astype(BF)

    grad_kv_low = jnp.concatenate([grad_key_low, grad_value_low], axis=1)
    grad_attn_in = dot_nt(grad_query_low, w_in_full[:, :q_width]) + dot_nt(
        grad_kv_low, w_in_full[:, q_width:]
    )
    grad_input_norm, in_terms = rms_backward(inputs, gain_in, grad_attn_in)
    grad_inputs = grad_middle + grad_input_norm

    def by_peer(values):
        columns = values.reshape(total, cores, width // cores).transpose(1, 0, 2)
        return flip(columns, core)

    def peer_terms(left, right):
        return jnp.concatenate([dot_tn(left, right[j]) for j in range(cores)], axis=0)

    in_peers = by_peer(attn_in)
    branch_peers = by_peer(grad_branch_low)
    narrow = width // cores
    out_terms = sum_cores(peer_terms(mixed_low, branch_peers).astype(BF)).astype(BF)
    query_terms_w = sum_cores(peer_terms(grad_query_low, in_peers).astype(BF)).astype(BF)
    every = masks(seq_count)
    out_grad = halve(
        out_terms.reshape(seq_count, q_width // seq_count, narrow), every, own
    ).reshape(q_width // seq_count, narrow)
    query_grad = (
        halve(query_terms_w.reshape(seq_count, q_width // seq_count, narrow), swapped + [SPLIT_BIT], own)
        .reshape(q_width // seq_count, narrow)
        .T
    )

    kv_terms = sum_cores(peer_terms(grad_kv_low, in_peers).astype(BF)).astype(BF)
    kv_rows = HD // seq_count
    kv_terms = (
        kv_terms.reshape(2, seq_count, kv_rows, narrow)
        .transpose(1, 0, 2, 3)
        .reshape(seq_count, 2 * kv_rows, narrow)
    )
    gains = jnp.concatenate(
        [
            jnp.sum(in_terms, axis=0),
            jnp.sum(mid_terms, axis=0),
            jnp.sum(ffn_terms, axis=0),
            jnp.sum(top_terms, axis=0),
            jnp.sum(query_terms, axis=(0, 1, 2)),
            jnp.sum(key_terms, axis=(0, 1)),
        ]
    )
    for mask in masks(cores):
        gains = gains + swap(gains, "fsdp", mask)
    gain_size = gains.shape[0]
    gain_rows = -(-gain_size // narrow)
    gains = jnp.pad(gains, (0, gain_rows * narrow - gain_size)).reshape(gain_rows, narrow)
    high = lax.reduce_precision(gains, 8, 7)
    low = gains - high
    tail = jnp.concatenate(
        [
            kv_terms,
            jnp.broadcast_to(high.astype(BF), (seq_count, gain_rows, narrow)),
            jnp.broadcast_to(low.astype(BF), (seq_count, gain_rows, narrow)),
        ],
        axis=1,
    )
    tail = jnp.sum(lax.all_to_all(tail, "seq", 0, 0, tiled=True).astype(F32), axis=0)
    key_grad = tail[:kv_rows].T
    value_grad = tail[kv_rows : 2 * kv_rows].T
    gains = tail[2 * kv_rows : 2 * kv_rows + gain_rows] + tail[2 * kv_rows + gain_rows :]
    gains = gains.reshape(-1)[:gain_size]
    norm_total = gains[: 4 * width].reshape(4, width)
    head_total = gains[4 * width :].reshape(2, HD)

    return (
        result.reshape(1, lanes, rows, width),
        grad_inputs.reshape(1, lanes, rows, width),
        query_grad,
        key_grad,
        value_grad,
        out_grad,
        gate_grad,
        up_grad,
        down_grad,
        norm_total,
        head_total,
    )


def solution(mesh):
    in_specs = (
        P("fsdp", None, "seq", None),
        P("fsdp", None, "seq", None),
        P("fsdp", None, None),
        P("fsdp", None),
        P("fsdp", None),
        P("fsdp", None),
        P("fsdp", None),
        P(None, "fsdp"),
        P(None, "fsdp"),
        P(None, "fsdp"),
        P("fsdp", None),
        P(),
        P(),
    )
    out_specs = (
        P("fsdp", None, "seq", None),
        P("fsdp", None, "seq", None),
        P("fsdp", "seq"),
        P("fsdp", "seq"),
        P("fsdp", "seq"),
        P("seq", "fsdp"),
        P("seq", "fsdp"),
        P("seq", "fsdp"),
        P("fsdp", "seq"),
        P(),
        P(),
    )
    return jax.shard_map(shards, mesh=mesh, in_specs=in_specs, out_specs=out_specs, check_vma=False)
```

time: 1940 us -> 546 us (0.28)
  blocking collectives: 845 us -> 0 us
  waiting for transfers between devices: 576 us -> 141 us
  local copies, waits for them, and re-layouts: 156 us -> 99.8 us
    unnamed x1 -> x0, blocking collectives: 762 us -> none
    ppermute x28 -> x38, waiting for transfers between devices: 573 us -> 105 us  [swap(): return lax.ppermute(value, axis, [(i, i ^ mask) for i in range(count)])]
    unnamed x223 -> x317, local copies, waits for them, and re-layouts: 102 us -> 17.7 us
    psum x1 -> x0, blocking collectives: 76.2 us -> none  [shards(): norm_total, head_total = lax.psum((norm_terms, head_terms), ('seq', 'fsdp'))]
    all_to_all x0 -> x5, waiting for transfers between devices: none -> 35.8 us  [the longest x1 16.7 us: shards(): lax.all_to_all(tail, 'seq', 0, 0, tiled=True).astype(F32)]
    convert_element_type x2 -> x11, local copies, waits for them, and re-layouts: 0.72 us -> 30.9 us  [the longest x3 19.4 us: weight_terms(): out = dot_tn(left, right).astype(BF)]
    ppermute x28 -> x38, starting transfers between devices: 64.3 us -> 35.8 us  [swap(): return lax.ppermute(value, axis, [(i, i ^ mask) for i in range(count)])]
    convert_element_type x19 -> x32, other arithmetic: 58.7 us -> 31.3 us  [the longest x15 18 us: halve(): block = block.astype(BF)]
  transfers between devices with their start and end apart: 46 -> 43, of which waited for: 20 -> 13; matrix products, arithmetic and copies ran while one was open for 16% -> 52% of each run, Pallas kernels for 0% -> 0%
where the time goes in v1:
time: 546 us; the launch traced here: 537 us
  matrix products  150 us (27%)
  waiting for transfers between devices  141 us (26%)
  local copies, waits for them, and re-layouts  99.8 us (18%)
  other arithmetic  80.9 us (15%)
  starting transfers between devices  61.1 us (11%)
    ppermute x38, waiting for transfers between devices, swap(): return lax.ppermute(value, axis, [(i, i ^ mask) for i in range(count)])  105 us
    dot_general x9, matrix products, dot_nt(): lax.dot_general(a, b, (((1,), (1,)), ((), ())), preferred_element_type=F32)  45.4 us
    dot_general x9, matrix products, dot(): return jnp.dot(a, b, preferred_element_type=F32)  40 us
    ppermute x38, starting transfers between devices, swap(): return lax.ppermute(value, axis, [(i, i ^ mask) for i in range(count)])  35.8 us
    dot_general x9, matrix products, dot_tn(): lax.dot_general(a, b, (((0,), (0,)), ((), ())), preferred_element_type=F32)  30.5 us
    convert_element_type x3, local copies, waits for them, and re-layouts, weight_terms(): out = dot_tn(left, right).astype(BF)  19.4 us
    convert_element_type x15, other arithmetic, halve(): block = block.astype(BF)  18 us
    unnamed x317, local copies, waits for them, and re-layouts  17.7 us
  transfers between devices with their start and end apart: 43, of which 13 were waited for; matrix products, arithmetic and copies ran while one was open for 52% of the time, Pallas kernels for 0%

profile of v1, /device:TPU:0, one launch (start us, length us, event | category | flops | bytes accessed | tf_op | source)
XLA Modules:
  0.0 537.0 jit_solution(17898288561940603524)
XLA Ops:
  15.8 2.4 maximum_select_fusion
  24.8 8.3 %all-to-all-start = ((bf16[16,16,512]{2,1,0:T(8,128)(2,1)}), bf16[16,16,512]{2,1,0:T(8,128)(2,1)S(1)}, u32[]{:S(2)}, u32[]{:S(2)}) async-start(bf16[16,16,512]{2,1,0:T(8,128)(2,1)} %pad_maximum_fusion.20), calls=%async_computation | async-start | bytes 524288 | tf_op jit(solution)/shard_map/all_to_all | solution.py:204
  37.0 6.3 %all-to-all-done = bf16[16,16,512]{2,1,0:T(8,128)(2,1)S(1)} async-done(((bf16[16,16,512]{2,1,0:T(8,128)(2,1)}), bf16[16,16,512]{2,1,0:T(8,128)(2,1)S(1)}, u32[]{:S(2)}, u32[]{:S(2)}) %all-to-all-start) | async-done | bytes 262176 | tf_op jit(solution)/shard_map/all_to_all | solution.py:204
  45.0 2.4 bitcast_select_fusion.1
  47.4 4.3 all-to-all-start.1
  54.9 2.7 copy.69
  57.7 2.7 multiply_reduce_fusion.11
  62.2 12.8 %all-to-all-done.1 = bf16[16,64,512]{2,1,0:T(8,128)(2,1)} async-done(((bf16[16,64,512]{2,1,0:T(8,128)(2,1)}), bf16[16,64,512]{2,1,0:T(8,128)(2,1)}, u32[]{:S(2)}, u32[]{:S(2)}) %all-to-all-start.1) | async-done | bytes 1048608 | tf_op jit(solution)/shard_map/all_to_all | solution.py:208
  76.5 2.6 fusion.216
  79.1 3.6 convolution_convert_fusion.9
  83.1 2.4 multiply_reduce_fusion.8
  87.9 3.1 collective-permute-start.4
  95.5 7.1 %collective-permute-done.4 = bf16[256,1152]{1,0:T(8,128)(2,1)} collective-permute-done((bf16[256,1152]{1,0:T(8,128)(2,1)S(1)}, bf16[256,1152]{1,0:T(8,128)(2,1)}, u32[]{:S(2)}, u32[]{:S(2)}) %collective-permute-start.4) | collective-permute-done | bytes 589856 | tf_op jit(solution)/shard_map/ppermute | solution.py:21
  103.9 8.5 %fusion.40 = f32[512,1728]{0,1:T(8,128)} fusion(bf16[1152,3456]{1,0:T(8,128)(2,1)} %param.21, s32[]{:T(128)S(6)} %mul.841, bf16[256,1152]{1,0:T(8,128)(2,1)S(1)} %collective-permute-done.2, bf16[256,1152]{1,0:T(8,128)(2,1)S(1)} %multiply_convert_fusion.6), kind=kOutput, calls=%fused_computation.68 | convolution fusion | flops 2040791040 | bytes 8847364 | tf_op jit(solution)/shard_map/dot_general | solution.py:101
  113.3 4.3 fusion.38
  117.6 6.6 %multiply_convert_fusion.2 = (bf16[512,1728]{0,1:T(8,128)(2,1)S(1)}, f32[512,1728]{0,1:T(8,128)}) fusion(f32[512,1728]{0,1:T(8,128)S(1)} %fusion.38, bf16[512,1152]{1,0:T(8,128)(2,1)S(1)} %constant_dynamic-update-slice_fusion.7, bf16[1152,3456]{1,0:T(8,128)(2,1)S(1)} %bitcast.364, s32[]{:T(128)S(6)} %mul.841), kind=kOutput, calls=%fused_computation.46 | convolution fusion | flops 2047279104 | bytes 14155780 | tf_op jit(solution)/shard_map/dot_general | solution.py:101
  124.3 2.7 fusion.48
  127.6 9.8 %multiply_convert_fusion.3 = (bf16[512,1728]{0,1:T(8,128)(2,1)S(1)}, f32[512,1728]{0,1:T(8,128)}) fusion(f32[512,1728]{0,1:T(8,128)S(1)} %copy-done.128, bf16[1152,3456]{1,0:T(8,128)(2,1)S(1)} %bitcast.364, s32[]{:T(128)S(6)} %mul.841, bf16[256,1152]{1,0:T(8,128)(2,1)S(1)} %collective-permute-done.2, bf16[256,1152]{1,0:T(8,128)(2,1)S(1)} %multiply_convert_fusion.6), kind=kOutput, calls=%fused_computation.47 | convolution fusion | flops 2049638400 | bytes 14155780 | tf_op jit(solution)/shard_map/dot_general | solution.py:101
  137.4 2.7 fusion.50
  147.0 3.2 copy.103
  152.4 5.7 %collective-permute-done.7 = bf16[256,1152]{1,0:T(8,128)(2,1)} collective-permute-done((bf16[256,1152]{1,0:T(8,128)(2,1)}, bf16[256,1152]{1,0:T(8,128)(2,1)}, u32[]{:S(2)}, u32[]{:S(2)}) %collective-permute-start.7) | collective-permute-done | bytes 589856 | tf_op jit(solution)/shard_map/ppermute | solution.py:21
  166.0 9.0 %multiply_convert_fusion.1 = (bf16[512,1728]{0,1:T(8,128)(2,1)}, bf16[512,1728]{0,1:T(8,128)(2,1)}) fusion(f32[512,1728]{0,1:T(8,128)S(1)} %copy-done.129, f32[512,1728]{0,1:T(8,128)S(1)} %copy-done.130, bf16[3456,1152]{1,0:T(8,128)(2,1)} %param.23, s32[]{:T(128)S(6)} %mul.841, bf16[256,1152]{1,0:T(8,128)(2,1)S(1)} %collective-permute-done.8, ...), kind=kOutput, calls=%fused_computation.45 | convolution fusion | flops 2062024704 | bytes 15777796 | tf_op jit(solution)/shard_map/dot_general | solution.py:109
  175.1 5.5 %fusion.36 = f32[512,1152]{1,0:T(8,128)S(1)} fusion(bf16[512,1728]{0,1:T(8,128)(2,1)} %get-tuple-element.35, bf16[1152,3456]{1,0:T(8,128)(2,1)S(1)} %bitcast.362, s32[]{:T(128)S(6)} %mul.841), kind=kOutput, calls=%fused_computation.64 | convolution fusion | flops 2038431744 | bytes 8257540 | tf_op jit(solution)/shard_map/dot_general | solution.py:109
  180.9 6.5 %convolution_add_fusion.1 = f32[512,1152]{1,0:T(8,128)S(1)} fusion(f32[512,1152]{1,0:T(8,128)S(1)} %fusion.36, bf16[512,1728]{0,1:T(8,128)(2,1)S(1)} %copy-done.131, bf16[1152,3456]{1,0:T(8,128)(2,1)} %param.22, s32[]{:T(128)S(6)} %mul.841), kind=kOutput, calls=%fused_computation.49 | convolution fusion | flops 2039021568 | bytes 10616836 | tf_op jit(solution)/shard_map/dot_general | solution.py:109
  190.1 7.8 %multiply_convert_fusion = (bf16[512,1728]{0,1:T(8,128)(2,1)S(1)}, bf16[512,1728]{0,1:T(8,128)(2,1)}) fusion(f32[512,1728]{0,1:T(8,128)S(1)} %copy-done.127, f32[512,1728]{0,1:T(8,128)} %get-tuple-element.113, bf16[3456,1152]{1,0:T(8,128)(2,1)S(1)} %bitcast.358, s32[]{:T(128)S(6)} %mul.841, bf16[256,1152]{1,0:T(8,128)(2,1)S(1)} %collective-permute-done.11, ...), kind=kOutput, calls=%fused_computation.44 | convolution fusion | flops 2062024704 | bytes 15777796 | tf_op jit(solution)/shard_map/dot_general | solution.py:109
  197.9 6.0 %fusion.34 = f32[512,1152]{1,0:T(8,128)S(1)} fusion(bf16[512,1728]{0,1:T(8,128)(2,1)} %get-tuple-element.37, bf16[1152,3456]{1,0:T(8,128)(2,1)S(1)} %bitcast.362, s32[]{:T(128)S(6)} %mul.841), kind=kOutput, calls=%fused_computation.62 | convolution fusion | flops 2038431744 | bytes 8257540 | tf_op jit(solution)/shard_map/dot_general | solution.py:109
  203.9 6.3 %convolution_add_fusion = f32[512,1152]{1,0:T(8,128)S(1)} fusion(f32[512,1152]{1,0:T(8,128)S(1)} %fusion.34, bf16[512,1728]{0,1:T(8,128)(2,1)S(1)} %get-tuple-element.36, bf16[1152,3456]{1,0:T(8,128)(2,1)} %param.22, s32[]{:T(128)S(6)} %mul.841), kind=kOutput, calls=%fused_computation.48 | convolution fusion | flops 2039021568 | bytes 10616836 | tf_op jit(solution)/shard_map/dot_general | solution.py:109
  212.9 7.8 %convolution_convert_fusion.2 = bf16[1152,1728]{0,1:T(8,128)(2,1)} fusion(bf16[512,1728]{0,1:T(8,128)(2,1)S(1)} %copy-done.135, bf16[512,1728]{0,1:T(8,128)(2,1)S(1)} %copy-done.134, bf16[256,1152]{1,0:T(8,128)(2,1)S(1)} %copy-done.60, bf16[256,1152]{1,0:T(8,128)(2,1)} %collective-permute-done.4, bf16[256,1152]{1,0:T(8,128)(2,1)S(1)} %copy-done.118, ...), kind=kOutput, calls=%fused_computation.8 | convolution fusion | flops 4095369216 | bytes 9879552 | tf_op jit(solution)/shard_map/dot_general | solution.py:105
  220.6 6.5 %copy.91 = bf16[1152,1728]{1,0:T(8,128)(2,1)} copy(bf16[1152,1728]{0,1:T(8,128)(2,1)} %convolution_convert_fusion.2) | data formatting | bytes 7962624 | tf_op jit(solution)/shard_map/convert_element_type | solution.py:301
  227.1 3.3 dynamic-slice_bitcast_fusion
  232.4 8.3 %convolution_convert_fusion.1 = bf16[1152,1728]{0,1:T(8,128)(2,1)} fusion(bf16[512,1728]{0,1:T(8,128)(2,1)} %copy-done.133, bf16[512,1728]{0,1:T(8,128)(2,1)S(1)} %copy-done.132, bf16[256,1152]{1,0:T(8,128)(2,1)S(1)} %copy-done.61, bf16[256,1152]{1,0:T(8,128)(2,1)} %collective-permute-done.4, bf16[256,1152]{1,0:T(8,128)(2,1)S(1)} %copy-done.119, ...), kind=kOutput, calls=%fused_computation.7 | convolution fusion | flops 4095369216 | bytes 9879552 | tf_op jit(solution)/shard_map/dot_general | solution.py:105
  240.7 6.4 %copy.92 = bf16[1152,1728]{1,0:T(8,128)(2,1)} copy(bf16[1152,1728]{0,1:T(8,128)(2,1)} %convolution_convert_fusion.1) | data formatting | bytes 7962624 | tf_op jit(solution)/shard_map/convert_element_type | solution.py:301
  247.1 4.0 constant_dynamic-slice_fusion.3
  253.6 2.3 fusion.89
  256.8 6.2 %convolution_convert_fusion = bf16[1152,1728]{0,1:T(8,128)(2,1)} fusion(bf16[512,1728]{0,1:T(8,128)(2,1)S(1)} %copy-done.137, bf16[512,1728]{0,1:T(8,128)(2,1)S(1)} %copy-done.139, bf16[256,1152]{1,0:T(8,128)(2,1)S(1)} %copy-done.125, bf16[256,1152]{1,0:T(8,128)(2,1)S(1)} %copy-done.123, bf16[256,1152]{1,0:T(8,128)(2,1)S(1)} %copy-done.121, ...), kind=kOutput, calls=%fused_computation.6 | convolution fusion | flops 4095369216 | bytes 9879552 | tf_op jit(solution)/shard_map/dot_general | solution.py:105
  263.0 6.5 %copy.95 = bf16[1152,1728]{1,0:T(8,128)(2,1)} copy(bf16[1152,1728]{0,1:T(8,128)(2,1)} %convolution_convert_fusion) | data formatting | bytes 7962624 | tf_op jit(solution)/shard_map/convert_element_type | solution.py:301
  269.6 3.8 constant_dynamic-slice_fusion.1
  275.7 2.3 multiply_reduce_fusion.2
  278.1 2.7 multiply_reduce_fusion.3
  286.0 2.1 fusion.129
  288.0 3.9 fusion.120
  291.9 12.1 %fusion.67 = f32[2,640,256]{2,1,0:T(8,128)} fusion(f32[2,512,640]{2,1,0:T(8,128)} %fusion.129, bf16[2,512,128]{2,1,0:T(8,128)(2,1)S(1)} %bitcast.339, bf16[2,512,128]{2,1,0:T(8,128)(2,1)} %bitcast.343, f32[2,512,640]{2,1,0:T(8,128)} %get-tuple-element.109, f32[2,512]{1,0:T(2,128)S(1)} %copy-done.141), kind=kOutput, calls=%fused_computation.113 | convolution fusion | flops 341182080 | bytes 7081984 | tf_op jit(solution)/shard_map/xzo,xza->xoa/dot_general | solution.py:336
  304.0 10.4 %fusion.70 = f32[2,512,256]{2,1,0:T(8,128)} fusion(f32[2,512,640]{2,1,0:T(8,128)} %fusion.129, bf16[2,640,512]{2,1,0:T(8,128)(2,1)} %copy-done.52, f32[2,512,640]{2,1,0:T(8,128)} %get-tuple-element.109, f32[2,512]{1,0:T(2,128)S(1)} %copy-done.141), kind=kOutput, calls=%fused_computation.114 | convolution fusion | flops 340133504 | bytes 12197888 | tf_op jit(solution)/shard_map/ajm,amn->ajn/dot_general | solution.py:335
  317.4 4.6 all-to-all-start.2
  329.0 2.1 fusion.4
  334.1 2.1 fusion.3
  338.7 14.7 %collective-permute-done.34 = bf16[2,2,2,72,1728]{4,3,1,0,2:T(8,128)(2,1)} collective-permute-done((bf16[2,2,2,72,1728]{4,3,1,0,2:T(8,128)(2,1)}, bf16[2,2,2,72,1728]{4,3,1,0,2:T(8,128)(2,1)}, u32[]{:S(2)}, u32[]{:S(2)}) %collective-permute-start.34) | collective-permute-done | bytes 1990688 | tf_op jit(solution)/shard_map/ppermute | solution.py:21
  353.4 3.4 fusion.2
  358.2 2.5 copy.86
  362.7 3.0 add_convert_fusion
  365.7 2.5 copy.90
  371.3 2.1 collective-permute-start.35
  373.4 8.0 %collective-permute-done.15 = bf16[2,2,2,64,576]{4,3,2,1,0:T(8,128)(2,1)} collective-permute-done((bf16[2,2,2,64,576]{4,3,2,1,0:T(8,128)(2,1)}, bf16[2,2,2,64,576]{4,3,2,1,0:T(8,128)(2,1)}, u32[]{:S(2)}, u32[]{:S(2)}) %collective-permute-start.15) | collective-permute-done | bytes 589856 | tf_op jit(solution)/shard_map/ppermute | solution.py:21
  384.4 7.9 %collective-permute-done.22 = bf16[2,2,2,64,576]{4,3,2,1,0:T(8,128)(2,1)S(1)} collective-permute-done((bf16[2,2,2,64,576]{4,3,2,1,0:T(8,128)(2,1)S(1)}, bf16[2,2,2,64,576]{4,3,2,1,0:T(8,128)(2,1)S(1)}, u32[]{:S(2)}, u32[]{:S(2)}) %collective-permute-start.22) | collective-permute-done | bytes 589856 | tf_op jit(solution)/shard_map/ppermute | solution.py:21
  401.1 2.4 collective-permute-done.35
  405.5 2.1 collective-permute-start.36
  410.7 4.0 all-to-all-start.3
  415.9 3.0 collective-permute-start.17
  421.6 55.1 %collective-permute-done.17 = bf16[2,64,576]{2,1,0:T(8,128)(2,1)S(1)} collective-permute-done((bf16[2,64,576]{2,1,0:T(8,128)(2,1)S(1)}, bf16[2,64,576]{2,1,0:T(8,128)(2,1)S(1)}, u32[]{:S(2)}, u32[]{:S(2)}) %collective-permute-start.17) | collective-permute-done | bytes 147488 | tf_op jit(solution)/shard_map/ppermute | solution.py:21
  476.9 2.3 collective-permute-start.25
  479.3 2.2 collective-permute-done.18
  503.7 4.1 all-to-all-start.4
  507.9 2.7 fusion.106
  517.6 16.7 %all-to-all-done.4 = bf16[16,50,576]{2,1,0:T(8,128)(2,1)S(1)} async-done(((bf16[16,50,576]{2,1,0:T(8,128)(2,1)}), bf16[16,50,576]{2,1,0:T(8,128)(2,1)S(1)}, u32[]{:S(2)}, u32[]{:S(2)}) %all-to-all-start.4) | async-done | bytes 921632 | tf_op jit(solution)/shard_map/all_to_all | solution.py:430
  (562 shorter events, 152.0 us)
Async XLA Ops:
  2.2 11.8 %collective-permute-start = (bf16[576,1536]{1,0:T(8,128)(2,1)S(1)}, bf16[576,1536]{1,0:T(8,128)(2,1)}, u32[]{:S(2)}, u32[]{:S(2)}) collective-permute-start(bf16[576,1536]{1,0:T(8,128)(2,1)S(1)} %constant_dynamic-update-slice_fusion), channel_id=1, source_target_pairs={{0,1},{1,0},{2,3},{3,2},{4,5},{5,4},{6,7},{7,6},{8,9},{9,8},{10,11... | collective-permute-start | bytes 5308424 | tf_op jit(solution)/shard_map/ppermute | solution.py:21
  2.7 30.5 %collective-permute-start.1 = (bf16[1024,576]{0,1:T(8,128)(2,1)}, bf16[1024,576]{0,1:T(8,128)(2,1)}, u32[]{:S(2)}, u32[]{:S(2)}) collective-permute-start(bf16[1024,576]{0,1:T(8,128)(2,1)} %param.20), channel_id=1, source_target_pairs={{0,1},{1,0},{2,3},{3,2},{4,5},{5,4},{6,7},{7,6},{8,9},{9,8},{10,11... | collective-permute-start | bytes 3538952 | tf_op jit(solution)/shard_map/ppermute | solution.py:21
  2.8 19.4 %copy-start.112 = (f32[128]{0:T(128)}, f32[128]{0:T(128)S(1)}, u32[]{:S(2)}) copy-start(f32[128]{0:T(128)S(1)} %multiply_exponential_fusion) | copy-start | bytes 1540
  23.5 38.1 %copy-start.45 = (f32[2,128,128]{2,1,0:T(8,128)}, f32[2,128,128]{2,1,0:T(8,128)S(1)}, u32[]{:S(2)}) copy-start(f32[2,128,128]{2,1,0:T(8,128)S(1)} %get-tuple-element.90) | copy-start | bytes 393220
  24.8 18.4 %all-to-all-start = ((bf16[16,16,512]{2,1,0:T(8,128)(2,1)}), bf16[16,16,512]{2,1,0:T(8,128)(2,1)S(1)}, u32[]{:S(2)}, u32[]{:S(2)}) async-start(bf16[16,16,512]{2,1,0:T(8,128)(2,1)} %pad_maximum_fusion.20), calls=%async_computation | async-start | bytes 524288 | tf_op jit(solution)/shard_map/all_to_all | solution.py:204
  47.4 27.6 %all-to-all-start.1 = ((bf16[16,64,512]{2,1,0:T(8,128)(2,1)}), bf16[16,64,512]{2,1,0:T(8,128)(2,1)}, u32[]{:S(2)}, u32[]{:S(2)}) async-start(bf16[16,64,512]{2,1,0:T(8,128)(2,1)} %bitcast_select_fusion.1), calls=%async_computation.1 | async-start | bytes 2097152 | tf_op jit(solution)/shard_map/all_to_all | solution.py:208
  62.0 14.5 %copy-start.68 = (bf16[2,128,4,128]{3,2,1,0:T(4,128)(2,1)}, bf16[2,128,4,128]{3,2,1,0:T(4,128)(2,1)S(1)}, u32[]{:S(2)}) copy-start(bf16[2,128,4,128]{3,2,1,0:T(4,128)(2,1)S(1)} %copy.71) | copy-start | bytes 786436
  62.0 14.4 %copy-start.63 = (bf16[2,128,128]{2,1,0:T(8,128)(2,1)S(1)}, bf16[2,128,128]{2,1,0:T(8,128)(2,1)}, u32[]{:S(2)}) copy-start(bf16[2,128,128]{2,1,0:T(8,128)(2,1)} %copy-done.62) | copy-start | bytes 196612
  62.2 14.3 %copy-start.70 = (bf16[2,128,4,128]{3,2,1,0:T(4,128)(2,1)}, bf16[2,128,4,128]{3,2,1,0:T(4,128)(2,1)S(1)}, u32[]{:S(2)}) copy-start(bf16[2,128,4,128]{3,2,1,0:T(4,128)(2,1)S(1)} %copy.70) | copy-start | bytes 786436
  87.9 39.8 %copy-start.56 = (bf16[256,1152]{1,0:T(8,128)(2,1)}, bf16[256,1152]{1,0:T(8,128)(2,1)S(1)}, u32[]{:S(2)}) copy-start(bf16[256,1152]{1,0:T(8,128)(2,1)S(1)} %multiply_convert_fusion.6) | copy-start | bytes 1769476
  87.9 14.7 %collective-permute-start.4 = (bf16[256,1152]{1,0:T(8,128)(2,1)S(1)}, bf16[256,1152]{1,0:T(8,128)(2,1)}, u32[]{:S(2)}, u32[]{:S(2)}) collective-permute-start(bf16[256,1152]{1,0:T(8,128)(2,1)S(1)} %multiply_convert_fusion.6), channel_id=1, source_target_pairs={{0,8},{2,10},{4,12},{6,14},{8,0},{10,2},{12,4},{14,6},{16,24},{18,... | collective-permute-start | bytes 1769480 | tf_op jit(solution)/shard_map/ppermute | solution.py:21
  92.8 11.0 %collective-permute-start.2 = (bf16[256,1152]{1,0:T(8,128)(2,1)S(1)}, bf16[256,1152]{1,0:T(8,128)(2,1)S(1)}, u32[]{:S(2)}, u32[]{:S(2)}) collective-permute-start(bf16[256,1152]{1,0:T(8,128)(2,1)S(1)} %multiply_convert_fusion.6), channel_id=1, source_target_pairs={{0,1},{1,0},{2,3},{3,2},{4,5},{5,4},{6,7},{7,6},{8,9},{9,8},{10,11... | collective-permute-start | bytes 1769480 | tf_op jit(solution)/shard_map/ppermute | solution.py:21
  102.6 9.8 %collective-permute-start.5 = (bf16[256,1152]{1,0:T(8,128)(2,1)}, bf16[256,1152]{1,0:T(8,128)(2,1)S(1)}, u32[]{:S(2)}, u32[]{:S(2)}) collective-permute-start(bf16[256,1152]{1,0:T(8,128)(2,1)} %collective-permute-done.4), channel_id=1, source_target_pairs={{0,1},{1,0},{2,3},{3,2},{4,5},{5,4},{6,7},{7,6},{8,9},{9,8},{10,11... | collective-permute-start | bytes 1769480 | tf_op jit(solution)/shard_map/ppermute | solution.py:21
  102.6 10.7 %slice-start.4 = ((s8[7962624]{0:T(1024)(128)(4,1)}), s8[4194304]{0:T(1024)(128)(4,1)S(1)}, s32[]{:S(2)}) async-start(s8[7962624]{0:T(1024)(128)(4,1)} %bitcast.359), calls=%async_computation.9 | async-start | bytes 8388608
  103.9 23.7 %copy-start.117 = (bf16[256,1152]{1,0:T(8,128)(2,1)}, bf16[256,1152]{1,0:T(8,128)(2,1)S(1)}, u32[]{:S(2)}) copy-start(bf16[256,1152]{1,0:T(8,128)(2,1)S(1)} %collective-permute-done.2) | copy-start | bytes 1769476
  103.9 13.7 %slice-start.8 = ((s8[7962624]{0:T(1024)(128)(4,1)}), s8[4194304]{0:T(1024)(128)(4,1)S(1)}, s32[]{:S(2)}) async-start(s8[7962624]{0:T(1024)(128)(4,1)} %bitcast.363), calls=%async_computation.13 | async-start | bytes 8388608
  113.3 11.0 %slice-start = ((s8[7962624]{0:T(1024)(128)(4,1)}), s8[4194304]{0:T(1024)(128)(4,1)S(1)}, s32[]{:S(2)}) async-start(s8[7962624]{0:T(1024)(128)(4,1)} %bitcast.355), calls=%async_computation.5 | async-start | bytes 8388608
  127.0 14.1 %collective-permute-start.6 = (bf16[256,1152]{1,0:T(8,128)(2,1)S(1)}, bf16[256,1152]{1,0:T(8,128)(2,1)S(1)}, u32[]{:S(2)}, u32[]{:S(2)}) collective-permute-start(bf16[256,1152]{1,0:T(8,128)(2,1)S(1)} %slice.456), channel_id=1, source_target_pairs={{0,1},{1,0},{2,3},{3,2},{4,5},{5,4},{6,7},{7,6},{8,9},{9,8},{10,11... | collective-permute-start | bytes 1769480 | tf_op jit(solution)/shard_map/ppermute | solution.py:21
  141.1 11.3 %collective-permute-start.3 = (bf16[256,1152]{1,0:T(8,128)(2,1)}, bf16[256,1152]{1,0:T(8,128)(2,1)}, u32[]{:S(2)}, u32[]{:S(2)}) collective-permute-start(bf16[256,1152]{1,0:T(8,128)(2,1)} %slice.457), channel_id=1, source_target_pairs={{0,1},{1,0},{2,3},{3,2},{4,5},{5,4},{6,7},{7,6},{8,9},{9,8},{10,11... | collective-permute-start | bytes 1769480 | tf_op jit(solution)/shard_map/ppermute | solution.py:21
  142.1 16.0 %collective-permute-start.7 = (bf16[256,1152]{1,0:T(8,128)(2,1)}, bf16[256,1152]{1,0:T(8,128)(2,1)}, u32[]{:S(2)}, u32[]{:S(2)}) collective-permute-start(bf16[256,1152]{1,0:T(8,128)(2,1)} %fusion.91), channel_id=1, source_target_pairs={{0,8},{2,10},{4,12},{6,14},{8,0},{10,2},{12,4},{14,6},{16,24},{18,... | collective-permute-start | bytes 1769480 | tf_op jit(solution)/shard_map/ppermute | solution.py:21
  162.5 12.6 %copy-start.54 = (bf16[256,1152]{1,0:T(8,128)(2,1)}, bf16[256,1152]{1,0:T(8,128)(2,1)S(1)}, u32[]{:S(2)}) copy-start(bf16[256,1152]{1,0:T(8,128)(2,1)S(1)} %get-tuple-element.52) | copy-start | bytes 1769476
  162.5 3.5 collective-permute-start.8
  163.1 12.0 %slice-start.6 = ((s8[7962624]{0:T(1024)(128)(4,1)}), s8[4194304]{0:T(1024)(128)(4,1)S(1)}, s32[]{:S(2)}) async-start(s8[7962624]{0:T(1024)(128)(4,1)} %bitcast.361), calls=%async_computation.11 | async-start | bytes 8388608
  164.4 16.2 %collective-permute-start.10 = (bf16[256,1152]{1,0:T(8,128)(2,1)S(1)}, bf16[256,1152]{1,0:T(8,128)(2,1)S(1)}, u32[]{:S(2)}, u32[]{:S(2)}) collective-permute-start(bf16[256,1152]{1,0:T(8,128)(2,1)S(1)} %get-tuple-element.52), channel_id=1, source_target_pairs={{0,8},{2,10},{4,12},{6,14},{8,0},{10,2},{12,4},{14,6},{16,24},{18,... | collective-permute-start | bytes 1769480 | tf_op jit(solution)/shard_map/ppermute | solution.py:21
  175.1 14.9 %slice-start.2 = ((s8[7962624]{0:T(1024)(128)(4,1)}), s8[3768320]{0:T(1024)(128)(4,1)S(1)}, s32[]{:S(2)}) async-start(s8[7962624]{0:T(1024)(128)(4,1)} %bitcast.357), calls=%async_computation.7 | async-start | bytes 7536640
  180.6 9.4 %collective-permute-start.11 = (bf16[256,1152]{1,0:T(8,128)(2,1)S(1)}, bf16[256,1152]{1,0:T(8,128)(2,1)S(1)}, u32[]{:S(2)}, u32[]{:S(2)}) collective-permute-start(bf16[256,1152]{1,0:T(8,128)(2,1)S(1)} %collective-permute-done.10), channel_id=1, source_target_pairs={{0,1},{1,0},{2,3},{3,2},{4,5},{5,4},{6,7},{7,6},{8,9},{9,8},{10,11... | collective-permute-start | bytes 1769480 | tf_op jit(solution)/shard_map/ppermute | solution.py:21
  189.7 85.9 %collective-permute-start.9 = (bf16[256,1152]{1,0:T(8,128)(2,1)}, bf16[256,1152]{1,0:T(8,128)(2,1)}, u32[]{:S(2)}, u32[]{:S(2)}) collective-permute-start(bf16[256,1152]{1,0:T(8,128)(2,1)} %slice.455), channel_id=1, source_target_pairs={{0,1},{1,0},{2,3},{3,2},{4,5},{5,4},{6,7},{7,6},{8,9},{9,8},{10,11... | collective-permute-start | bytes 1769480 | tf_op jit(solution)/shard_map/ppermute | solution.py:21
  212.6 40.5 %collective-permute-start.12 = (bf16[256,1152]{1,0:T(8,128)(2,1)}, bf16[256,1152]{1,0:T(8,128)(2,1)}, u32[]{:S(2)}, u32[]{:S(2)}) collective-permute-start(bf16[256,1152]{1,0:T(8,128)(2,1)} %slice.454), channel_id=1, source_target_pairs={{0,1},{1,0},{2,3},{3,2},{4,5},{5,4},{6,7},{7,6},{8,9},{9,8},{10,11... | collective-permute-start | bytes 1769480 | tf_op jit(solution)/shard_map/ppermute | solution.py:21
  230.4 98.0 %collective-permute-start.26 = (bf16[2,2,2,72,1728]{4,3,2,1,0:T(8,128)(2,1)}, bf16[2,2,2,72,1728]{4,3,2,1,0:T(8,128)(2,1)}, u32[]{:S(2)}, u32[]{:S(2)}) collective-permute-start(bf16[2,2,2,72,1728]{4,3,2,1,0:T(8,128)(2,1)} %dynamic-slice_bitcast_fusion), channel_id=1, source_target_pairs={{0,4},{2,6},{4,0},{6,2},{8,12},{10,14},{12,8},{14,10},{16,20},{18,... | collective-permute-start | bytes 5971976 | tf_op jit(solution)/shard_map/ppermute | solution.py:21
  252.6 81.5 %collective-permute-start.30 = (bf16[2,2,2,72,1728]{4,3,1,0,2:T(8,128)(2,1)}, bf16[2,2,2,72,1728]{4,3,1,0,2:T(8,128)(2,1)}, u32[]{:S(2)}, u32[]{:S(2)}) collective-permute-start(bf16[2,2,2,72,1728]{4,3,1,0,2:T(8,128)(2,1)} %bitcast.289), channel_id=1, source_target_pairs={{0,2},{2,0},{4,6},{6,4},{8,10},{10,8},{12,14},{14,12},{16,18},{18,... | collective-permute-start | bytes 5971976 | tf_op jit(solution)/shard_map/ppermute | solution.py:21
  255.9 19.7 %collective-permute-start.13 = (bf16[256,1152]{1,0:T(8,128)(2,1)}, bf16[256,1152]{1,0:T(8,128)(2,1)}, u32[]{:S(2)}, u32[]{:S(2)}) collective-permute-start(bf16[256,1152]{1,0:T(8,128)(2,1)} %fusion.89), channel_id=1, source_target_pairs={{0,8},{2,10},{4,12},{6,14},{8,0},{10,2},{12,4},{14,6},{16,24},{18,... | collective-permute-start | bytes 1769480 | tf_op jit(solution)/shard_map/ppermute | solution.py:21
  274.8 78.6 %collective-permute-start.34 = (bf16[2,2,2,72,1728]{4,3,1,0,2:T(8,128)(2,1)}, bf16[2,2,2,72,1728]{4,3,1,0,2:T(8,128)(2,1)}, u32[]{:S(2)}, u32[]{:S(2)}) collective-permute-start(bf16[2,2,2,72,1728]{4,3,1,0,2:T(8,128)(2,1)} %bitcast.288), channel_id=1, source_target_pairs={{0,2},{2,0},{4,6},{6,4},{8,10},{10,8},{12,14},{14,12},{16,18},{18,... | collective-permute-start | bytes 5971976 | tf_op jit(solution)/shard_map/ppermute | solution.py:21
  291.9 22.8 %copy-start.19 = (f32[2,640,256]{2,1,0:T(8,128)}, f32[2,640,256]{2,1,0:T(8,128)S(1)}, u32[]{:S(2)}) copy-start(f32[2,640,256]{2,1,0:T(8,128)S(1)} %fusion.120) | copy-start | bytes 3932164
  317.4 90.2 %all-to-all-start.2 = ((bf16[16,64,512]{2,1,0:T(8,128)(2,1)}), bf16[16,64,512]{2,1,0:T(8,128)(2,1)}, u32[]{:S(2)}, u32[]{:S(2)}) async-start(bf16[16,64,512]{2,1,0:T(8,128)(2,1)} %bitcast.52), calls=%async_computation.2 | async-start | bytes 2097152 | tf_op jit(solution)/shard_map/all_to_all | solution.py:352
  325.6 31.2 %copy-start.23 = (bf16[32,8,4,256]{3,1,2,0:T(8,128)(2,1)}, bf16[32,8,4,256]{3,1,2,0:T(8,128)(2,1)S(1)}, u32[]{:S(2)}) copy-start(bf16[32,8,4,256]{3,1,2,0:T(8,128)(2,1)S(1)} %copy.109) | copy-start | bytes 1572868
  326.1 30.6 %collective-permute-start.14 = (bf16[1024,576]{0,1:T(8,128)(2,1)S(1)}, bf16[1024,576]{0,1:T(8,128)(2,1)S(1)}, u32[]{:S(2)}, u32[]{:S(2)}) collective-permute-start(bf16[1024,576]{0,1:T(8,128)(2,1)S(1)} %convolution_convert_fusion.5), channel_id=1, source_target_pairs={{0,1},{1,0},{2,3},{3,2},{4,5},{5,4},{6,7},{7,6},{8,9},{9,8},{10,11... | collective-permute-start | bytes 3538952 | tf_op jit(solution)/shard_map/ppermute | solution.py:21
  328.3 34.4 %collective-permute-start.21 = (bf16[1024,576]{0,1:T(8,128)(2,1)}, bf16[1024,576]{0,1:T(8,128)(2,1)}, u32[]{:S(2)}, u32[]{:S(2)}) collective-permute-start(bf16[1024,576]{0,1:T(8,128)(2,1)} %convolution_convert_fusion.3), channel_id=1, source_target_pairs={{0,1},{1,0},{2,3},{3,2},{4,5},{5,4},{6,7},{7,6},{8,9},{9,8},{10,11... | collective-permute-start | bytes 3538952 | tf_op jit(solution)/shard_map/ppermute | solution.py:21
  332.2 61.2 %collective-permute-start.27 = (bf16[2,2,72,1728]{3,2,1,0:T(8,128)(2,1)}, bf16[2,2,72,1728]{3,2,1,0:T(8,128)(2,1)}, u32[]{:S(2)}, u32[]{:S(2)}) collective-permute-start(bf16[2,2,72,1728]{3,2,1,0:T(8,128)(2,1)} %dynamic-slice_bitcast_fusion.3), channel_id=1, source_target_pairs={{0,2},{2,0},{4,6},{6,4},{8,10},{10,8},{12,14},{14,12},{16,18},{18,... | collective-permute-start | bytes 2985992 | tf_op jit(solution)/shard_map/ppermute | solution.py:21
  336.1 20.6 %copy-start.10 = (bf16[2,2,2,72,1728]{4,3,1,0,2:T(8,128)(2,1)}, bf16[2,2,2,72,1728]{4,3,1,0,2:T(8,128)(2,1)S(1)}, u32[]{:S(2)}) copy-start(bf16[2,2,2,72,1728]{4,3,1,0,2:T(8,128)(2,1)S(1)} %fusion.3) | copy-start | bytes 5971972
  336.1 17.2 %copy-start.14 = (bf16[2,2,2,1,72,1728]{5,4,3,2,1,0:T(8,128)(2,1)S(1)}, bf16[2,2,2,1,72,1728]{5,4,3,2,1,0:T(8,128)(2,1)}, u32[]{:S(2)}) copy-start(bf16[2,2,2,1,72,1728]{5,4,3,2,1,0:T(8,128)(2,1)} %get-tuple-element.38) | copy-start | bytes 5971972
  337.2 60.1 %collective-permute-start.31 = (bf16[2,2,72,1728]{3,2,1,0:T(8,128)(2,1)}, bf16[2,2,72,1728]{3,2,1,0:T(8,128)(2,1)}, u32[]{:S(2)}, u32[]{:S(2)}) collective-permute-start(bf16[2,2,72,1728]{3,2,1,0:T(8,128)(2,1)} %dynamic-slice_bitcast_fusion.2), channel_id=1, source_target_pairs={{0,4},{2,6},{4,0},{6,2},{8,12},{10,14},{12,8},{14,10},{16,20},{18,... | collective-permute-start | bytes 2985992 | tf_op jit(solution)/shard_map/ppermute | solution.py:21
  362.7 18.8 %collective-permute-start.15 = (bf16[2,2,2,64,576]{4,3,2,1,0:T(8,128)(2,1)}, bf16[2,2,2,64,576]{4,3,2,1,0:T(8,128)(2,1)}, u32[]{:S(2)}, u32[]{:S(2)}) collective-permute-start(bf16[2,2,2,64,576]{4,3,2,1,0:T(8,128)(2,1)} %dynamic-slice_bitcast_fusion.5), channel_id=1, source_target_pairs={{0,4},{2,6},{4,0},{6,2},{8,12},{10,14},{12,8},{14,10},{16,20},{18,... | collective-permute-start | bytes 1769480 | tf_op jit(solution)/shard_map/ppermute | solution.py:21
  368.2 13.3 %copy-start.17 = (bf16[1024,576]{1,0:T(8,128)(2,1)S(1)}, bf16[1024,576]{1,0:T(8,128)(2,1)}, u32[]{:S(2)}) copy-start(bf16[1024,576]{1,0:T(8,128)(2,1)} %copy.86) | copy-start | bytes 3538948
  369.4 22.8 %copy-start.18 = (bf16[1024,576]{1,0:T(8,128)(2,1)S(1)}, bf16[1024,576]{1,0:T(8,128)(2,1)}, u32[]{:S(2)}) copy-start(bf16[1024,576]{1,0:T(8,128)(2,1)} %copy.90) | copy-start | bytes 3538948
  369.4 22.8 %collective-permute-start.22 = (bf16[2,2,2,64,576]{4,3,2,1,0:T(8,128)(2,1)S(1)}, bf16[2,2,2,64,576]{4,3,2,1,0:T(8,128)(2,1)S(1)}, u32[]{:S(2)}, u32[]{:S(2)}) collective-permute-start(bf16[2,2,2,64,576]{4,3,2,1,0:T(8,128)(2,1)S(1)} %dynamic-slice_bitcast_fusion.4), channel_id=1, source_target_pairs={{0,2},{2,0},{4,6},{6,4},{8,10},{10,8},{12,14},{14,12},{16,18},{18,... | collective-permute-start | bytes 1769480 | tf_op jit(solution)/shard_map/ppermute | solution.py:21
  371.3 32.1 %collective-permute-start.35 = (bf16[2,2,72,1728]{3,2,1,0:T(8,128)(2,1)S(1)}, bf16[2,2,72,1728]{3,2,1,0:T(8,128)(2,1)S(1)}, u32[]{:S(2)}, u32[]{:S(2)}) collective-permute-start(bf16[2,2,72,1728]{3,2,1,0:T(8,128)(2,1)S(1)} %dynamic-slice_bitcast_fusion.1), channel_id=1, source_target_pairs={{0,4},{2,6},{4,0},{6,2},{8,12},{10,14},{12,8},{14,10},{16,20},{18,... | collective-permute-start | bytes 2985992 | tf_op jit(solution)/shard_map/ppermute | solution.py:21
  383.5 31.2 %collective-permute-start.16 = (bf16[2,2,64,576]{3,2,1,0:T(8,128)(2,1)}, bf16[2,2,64,576]{3,2,1,0:T(8,128)(2,1)}, u32[]{:S(2)}, u32[]{:S(2)}) collective-permute-start(bf16[2,2,64,576]{3,2,1,0:T(8,128)(2,1)} %dynamic-slice_bitcast_fusion.10), channel_id=1, source_target_pairs={{0,2},{2,0},{4,6},{6,4},{8,10},{10,8},{12,14},{14,12},{16,18},{18,... | collective-permute-start | bytes 884744 | tf_op jit(solution)/shard_map/ppermute | solution.py:21
  393.2 25.7 %collective-permute-start.23 = (bf16[2,2,64,576]{3,2,1,0:T(8,128)(2,1)}, bf16[2,2,64,576]{3,2,1,0:T(8,128)(2,1)}, u32[]{:S(2)}, u32[]{:S(2)}) collective-permute-start(bf16[2,2,64,576]{3,2,1,0:T(8,128)(2,1)} %dynamic-slice_bitcast_fusion.9), channel_id=1, source_target_pairs={{0,4},{2,6},{4,0},{6,2},{8,12},{10,14},{12,8},{14,10},{16,20},{18,... | collective-permute-start | bytes 884744 | tf_op jit(solution)/shard_map/ppermute | solution.py:21
  395.7 87.7 %collective-permute-start.28 = (bf16[2,72,1728]{2,1,0:T(8,128)(2,1)}, bf16[2,72,1728]{2,1,0:T(8,128)(2,1)}, u32[]{:S(2)}, u32[]{:S(2)}) collective-permute-start(bf16[2,72,1728]{2,1,0:T(8,128)(2,1)} %dynamic-slice_bitcast_fusion.8), channel_id=1, source_target_pairs={{0,16},{2,18},{4,20},{6,22},{8,24},{10,26},{12,28},{14,30},{16,0},... | collective-permute-start | bytes 1493000 | tf_op jit(solution)/shard_map/ppermute | solution.py:21
  399.7 87.4 %collective-permute-start.32 = (bf16[2,72,1728]{2,1,0:T(8,128)(2,1)}, bf16[2,72,1728]{2,1,0:T(8,128)(2,1)}, u32[]{:S(2)}, u32[]{:S(2)}) collective-permute-start(bf16[2,72,1728]{2,1,0:T(8,128)(2,1)} %dynamic-slice_bitcast_fusion.7), channel_id=1, source_target_pairs={{0,16},{2,18},{4,20},{6,22},{8,24},{10,26},{12,28},{14,30},{16,0},... | collective-permute-start | bytes 1493000 | tf_op jit(solution)/shard_map/ppermute | solution.py:21
  405.5 84.2 %collective-permute-start.36 = (bf16[2,72,1728]{2,1,0:T(8,128)(2,1)}, bf16[2,72,1728]{2,1,0:T(8,128)(2,1)}, u32[]{:S(2)}, u32[]{:S(2)}) collective-permute-start(bf16[2,72,1728]{2,1,0:T(8,128)(2,1)} %dynamic-slice_bitcast_fusion.6), channel_id=1, source_target_pairs={{0,16},{2,18},{4,20},{6,22},{8,24},{10,26},{12,28},{14,30},{16,0},... | collective-permute-start | bytes 1493000 | tf_op jit(solution)/shard_map/ppermute | solution.py:21
  410.7 82.8 %all-to-all-start.3 = ((bf16[16,16,512]{2,1,0:T(8,128)(2,1)}), bf16[16,16,512]{2,1,0:T(8,128)(2,1)S(1)}, u32[]{:S(2)}, u32[]{:S(2)}) async-start(bf16[16,16,512]{2,1,0:T(8,128)(2,1)} %multiply_reduce_fusion.1), calls=%async_computation.3 | async-start | bytes 524288 | tf_op jit(solution)/shard_map/all_to_all | solution.py:356
  414.7 68.7 %copy-start.30 = (bf16[2,2,72,1728]{3,2,1,0:T(8,128)(2,1)S(1)}, bf16[2,2,72,1728]{3,2,1,0:T(8,128)(2,1)}, u32[]{:S(2)}) copy-start(bf16[2,2,72,1728]{3,2,1,0:T(8,128)(2,1)} %copy-done.29) | copy-start | bytes 2985988
  415.9 60.8 %collective-permute-start.17 = (bf16[2,64,576]{2,1,0:T(8,128)(2,1)S(1)}, bf16[2,64,576]{2,1,0:T(8,128)(2,1)S(1)}, u32[]{:S(2)}, u32[]{:S(2)}) collective-permute-start(bf16[2,64,576]{2,1,0:T(8,128)(2,1)S(1)} %dynamic-slice_bitcast_fusion.15), channel_id=1, source_target_pairs={{0,16},{2,18},{4,20},{6,22},{8,24},{10,26},{12,28},{14,30},{16,0},... | collective-permute-start | bytes 442376 | tf_op jit(solution)/shard_map/ppermute | solution.py:21
  420.1 67.0 %copy-start.28 = (bf16[2,2,72,1728]{3,2,1,0:T(8,128)(2,1)S(1)}, bf16[2,2,72,1728]{3,2,1,0:T(8,128)(2,1)}, u32[]{:S(2)}) copy-start(bf16[2,2,72,1728]{3,2,1,0:T(8,128)(2,1)} %copy-done.27) | copy-start | bytes 2985988
  420.1 56.7 %collective-permute-start.24 = (bf16[2,64,576]{2,1,0:T(8,128)(2,1)S(1)}, bf16[2,64,576]{2,1,0:T(8,128)(2,1)S(1)}, u32[]{:S(2)}, u32[]{:S(2)}) collective-permute-start(bf16[2,64,576]{2,1,0:T(8,128)(2,1)S(1)} %dynamic-slice_bitcast_fusion.14), channel_id=1, source_target_pairs={{0,8},{2,10},{4,12},{6,14},{8,0},{10,2},{12,4},{14,6},{16,24},{18,... | collective-permute-start | bytes 442376 | tf_op jit(solution)/shard_map/ppermute | solution.py:21
  476.8 4.7 collective-permute-start.18
  476.9 5.8 %collective-permute-start.25 = (bf16[64,576]{1,0:T(8,128)(2,1)S(1)}, bf16[64,576]{1,0:T(8,128)(2,1)S(1)}, u32[]{:S(2)}, u32[]{:S(2)}) collective-permute-start(bf16[64,576]{1,0:T(8,128)(2,1)S(1)} %dynamic-slice_bitcast_fusion.16), channel_id=1, source_target_pairs={{0,16},{2,18},{4,20},{6,22},{8,24},{10,26},{12,28},{14,30},{16,0},... | collective-permute-start | bytes 221192 | tf_op jit(solution)/shard_map/ppermute | solution.py:21
  485.5 25.1 %collective-permute-start.29 = (bf16[72,1728]{1,0:T(8,128)(2,1)}, bf16[72,1728]{1,0:T(8,128)(2,1)}, u32[]{:S(2)}, u32[]{:S(2)}) collective-permute-start(bf16[72,1728]{1,0:T(8,128)(2,1)} %get-tuple-element.73), channel_id=1, source_target_pairs={{0,8},{2,10},{4,12},{6,14},{8,0},{10,2},{12,4},{14,6},{16,24},{18,... | collective-permute-start | bytes 746504 | tf_op jit(solution)/shard_map/ppermute | solution.py:21
  489.3 22.4 %collective-permute-start.33 = (bf16[72,1728]{1,0:T(8,128)(2,1)}, bf16[72,1728]{1,0:T(8,128)(2,1)}, u32[]{:S(2)}, u32[]{:S(2)}) collective-permute-start(bf16[72,1728]{1,0:T(8,128)(2,1)} %get-tuple-element.71), channel_id=1, source_target_pairs={{0,8},{2,10},{4,12},{6,14},{8,0},{10,2},{12,4},{14,6},{16,24},{18,... | collective-permute-start | bytes 746504 | tf_op jit(solution)/shard_map/ppermute | solution.py:21
  491.8 20.8 %collective-permute-start.37 = (bf16[72,1728]{1,0:T(8,128)(2,1)}, bf16[72,1728]{1,0:T(8,128)(2,1)}, u32[]{:S(2)}, u32[]{:S(2)}) collective-permute-start(bf16[72,1728]{1,0:T(8,128)(2,1)} %get-tuple-element.69), channel_id=1, source_target_pairs={{0,8},{2,10},{4,12},{6,14},{8,0},{10,2},{12,4},{14,6},{16,24},{18,... | collective-permute-start | bytes 746504 | tf_op jit(solution)/shard_map/ppermute | solution.py:21
  498.6 2.1 collective-permute-start.19
  498.7 1.9 collective-permute-start.20
  503.7 30.6 %all-to-all-start.4 = ((bf16[16,50,576]{2,1,0:T(8,128)(2,1)}), bf16[16,50,576]{2,1,0:T(8,128)(2,1)S(1)}, u32[]{:S(2)}, u32[]{:S(2)}) async-start(bf16[16,50,576]{2,1,0:T(8,128)(2,1)} %pad_maximum_fusion.10), calls=%async_computation.4 | async-start | bytes 2293760 | tf_op jit(solution)/shard_map/all_to_all | solution.py:430
  (131 other events, 536.8 us)

commit v2 on v1

--- a/solution.py
+++ b/solution.py
@@ -1,8 +1,11 @@
+import functools
 import math
 
 import jax
 import jax.numpy as jnp
 from jax import lax
+from jax.experimental import pallas as pl
+from jax.experimental.pallas import tpu as pltpu
 from jax.sharding import PartitionSpec as P
 
 HQ = 4
@@ -119,23 +122,182 @@
     return jnp.sum(terms.reshape((count, hops) + source.shape[1:]), axis=1).astype(source.dtype)
 
 
-def halve(block, order, own, keep_bits=()):
-    count = block.shape[0]
-    bits = masks(count)[::-1]
-    shape = block.shape[1:]
-    block = block.reshape((2,) * len(bits) + shape)
-    left = list(bits)
+def arrangement(order):
+    if not order:
+        return [0]
+    rest = arrangement(order[1:])
+    return [j | order[0] for j in rest] + rest
+
+
+def halve(first, rest, order):
     for mask in order:
-        axis = left.index(mask)
-        mine = ((own & mask) != 0).astype(jnp.int32)
-        sent = lax.dynamic_index_in_dim(block, 1 - mine, axis, keepdims=False)
-        kept = lax.dynamic_index_in_dim(block, mine, axis, keepdims=False)
-        got = swap(sent.astype(BF), "seq", mask)
-        block = kept.astype(F32) + got.astype(F32)
-        left.remove(mask)
-        if mask != order[-1] or left:
-            block = block.astype(BF)
-    return block.reshape((2 ** len(left),) + shape)
+        got = swap(first, "seq", mask)
+        total = rest.astype(F32) + got.astype(F32)
+        half = total.shape[0] // 2
+        first, rest = total[:half].astype(BF), total[half:].astype(BF)
+    return total
+
+
+def tiles(size):
+    tile = 256 if size % 256 == 0 else 128
+    return tile, size // tile
+
+
+def column_tiles(size):
+    return [(start, min(256, size - start)) for start in range(0, size, 256)]
+
+
+VMEM = pl.BlockSpec(memory_space=pltpu.VMEM)
+SMEM = pl.BlockSpec(memory_space=pltpu.SMEM)
+PARAMS = pltpu.CompilerParams(vmem_limit_bytes=56 * 1024 * 1024)
+ROOT = math.sqrt(2.0 / math.pi)
+CUBE = 0.044715
+
+
+def ffn_forward_kernel(n, *refs):
+    x_refs, (wg, wu, wd) = refs[:n], refs[n : n + 3]
+    hid, act, slope, keep, send, x_all = refs[n + 3 :]
+    rows = x_refs[0].shape[0]
+    for j in range(n):
+        x_all[j * rows : (j + 1) * rows, :] = x_refs[j][...]
+    tile, count = tiles(wg.shape[1])
+
+    @pl.loop(0, count)
+    def _(i):
+        cols = pl.ds(pl.multiple_of(i * tile, tile), tile)
+        g = dot(x_all[...], wg[:, cols])
+        u = dot(x_all[...], wu[:, cols])
+        square = g * g
+        t = jnp.tanh(g * (ROOT + ROOT * CUBE * square))
+        half = 0.5 * (1.0 + t)
+        a = g * half
+        d = half + a * (1.0 - t) * (ROOT + 3.0 * ROOT * CUBE * square)
+        hid[:, cols] = (a * u).astype(BF)
+        act[:, cols] = a.astype(BF)
+        slope[:, cols] = (u * d).astype(BF)
+
+    for start, size in column_tiles(wd.shape[1]):
+        out = dot(hid[...], wd[:, start : start + size])
+        half = out.shape[0] // 2
+        keep[:, start : start + size] = out[:half]
+        send[:, start : start + size] = out[half:].astype(BF)
+
+
+def ffn_forward(blocks, wg, wu, wd):
+    n, (rows, width), share = len(blocks), blocks[0].shape, wg.shape[1]
+    total = n * rows
+    return pl.pallas_call(
+        functools.partial(ffn_forward_kernel, n),
+        out_shape=[jax.ShapeDtypeStruct((total, share), BF)] * 3
+        + [
+            jax.ShapeDtypeStruct((total // 2, width), F32),
+            jax.ShapeDtypeStruct((total // 2, width), BF),
+        ],
+        in_specs=[VMEM] * (n + 3),
+        out_specs=[VMEM] * 5,
+        scratch_shapes=[pltpu.VMEM((total, width), BF)],
+        compiler_params=PARAMS,
+        cost_estimate=pl.CostEstimate(
+            flops=6 * total * width * share,
+            bytes_accessed=6 * width * share + 6 * total * share,
+            transcendentals=total * share,
+        ),
+    )(*blocks, wg, wu, wd)
+
+
+def ffn_backward_kernel(n, *refs):
+    g_refs, (act, slope, wg, wu, wd) = refs[:n], refs[n : n + 5]
+    d_gate, d_up, keep, send, g_all = refs[n + 5 :]
+    rows = g_refs[0].shape[0]
+    for j in range(n):
+        g_all[j * rows : (j + 1) * rows, :] = g_refs[j][...]
+    tile, count = tiles(wg.shape[1])
+
+    @pl.loop(0, count)
+    def _(i):
+        cols = pl.ds(pl.multiple_of(i * tile, tile), tile)
+        d = dot_nt(g_all[...], wd[cols, :])
+        d_gate[:, cols] = (d * slope[:, cols].astype(F32)).astype(BF)
+        d_up[:, cols] = (d * act[:, cols].astype(F32)).astype(BF)
+
+    for start, size in column_tiles(wg.shape[0]):
+        out = dot_nt(d_gate[...], wg[start : start + size, :])
+        out = out + dot_nt(d_up[...], wu[start : start + size, :])
+        half = out.shape[0] // 2
+        keep[:, start : start + size] = out[:half]
+        send[:, start : start + size] = out[half:].astype(BF)
+
+
+def ffn_backward(blocks, act, slope, wg, wu, wd):
+    n, (rows, width), share = len(blocks), blocks[0].shape, wg.shape[1]
+    total = n * rows
+    return pl.pallas_call(
+        functools.partial(ffn_backward_kernel, n),
+        out_shape=[jax.ShapeDtypeStruct((total, share), BF)] * 2
+        + [
+            jax.ShapeDtypeStruct((total // 2, width), F32),
+            jax.ShapeDtypeStruct((total // 2, width), BF),
+        ],
+        in_specs=[VMEM] * (n + 5),
+        out_specs=[VMEM] * 4,
+        scratch_shapes=[pltpu.VMEM((total, width), BF)],
+        compiler_params=PARAMS,
+        cost_estimate=pl.CostEstimate(
+            flops=6 * total * width * share,
+            bytes_accessed=6 * width * share + 8 * total * share,
+            transcendentals=0,
+        ),
+    )(*blocks, act, slope, wg, wu, wd)
+
+
+def weight_kernel(n, order, *refs):
+    own, left = refs[0], refs[1 : n + 1]
+    near, far = refs[n + 1 : n + 3]
+    first, rest, turned, out = refs[n + 3 :]
+    rows = left[0].shape[0]
+    for j in range(n):
+        turned[:, j * rows : (j + 1) * rows] = left[j][...].T
+    tile, count = tiles(near.shape[1])
+    half = near.shape[0]
+    block = first.shape[1]
+    me = own[0]
+
+    @pl.loop(0, count)
+    def _(i):
+        cols = pl.ds(pl.multiple_of(i * tile, tile), tile)
+        out[...] = dot(turned[:, :half], near[:, cols]) + dot(turned[:, half:], far[:, cols])
+        for k, j in enumerate(arrangement(order)):
+            source = pl.multiple_of((me ^ j) * block, 8)
+            target = first if k < first.shape[0] else rest
+            target[k % first.shape[0], :, cols] = out[pl.ds(source, block), :].astype(BF)
+
+
+def weight_terms(own, seq_count, order, left, near, far):
+    width, share = left[0].shape[1], near.shape[1]
+    block = width // seq_count
+    n = len(left)
+    if block % 8:
+        full = dot_tn(jnp.concatenate(left), jnp.concatenate([near, far])).astype(BF)
+        full = full.reshape(seq_count, block, share)
+        full = jnp.take(full, own ^ jnp.array(arrangement(order), jnp.int32), axis=0)
+        return full[: seq_count // 2], full[seq_count // 2 :]
+    tile, _ = tiles(share)
+    return pl.pallas_call(
+        functools.partial(weight_kernel, n, order),
+        out_shape=[jax.ShapeDtypeStruct((seq_count // 2, block, share), BF)] * 2,
+        in_specs=[SMEM] + [VMEM] * (n + 2),
+        out_specs=[VMEM] * 2,
+        scratch_shapes=[
+            pltpu.VMEM((width, n * left[0].shape[0]), BF),
+            pltpu.VMEM((width, tile), F32),
+        ],
+        compiler_params=PARAMS,
+        cost_estimate=pl.CostEstimate(
+            flops=2 * n * left[0].shape[0] * width * share,
+            bytes_accessed=2 * width * share + 2 * n * left[0].shape[0] * (width + share),
+            transcendentals=0,
+        ),
+    )(own.reshape(1), *left, near, far)
 
 
 def shards(
@@ -218,11 +380,15 @@
     ).astype(BF)
 
     hidden_cols = w_gate.shape[1]
-    share = hidden_cols // 2
+    share = -(-hidden_cols // 256) * 128
+    overlap = 2 * share - hidden_cols
     part = ((own & SPLIT_BIT) != 0).astype(jnp.int32)
-    gate_share = lax.dynamic_slice_in_dim(w_gate, part * share, share, 1)
-    up_share = lax.dynamic_slice_in_dim(w_up, part * share, share, 1)
-    down_share = lax.dynamic_slice_in_dim(w_down, part * share, share, 0)
+    begin = part * (hidden_cols - share)
+    gate_share = lax.dynamic_slice_in_dim(w_gate, begin, share, 1)
+    up_share = lax.dynamic_slice_in_dim(w_up, begin, share, 1)
+    down_share = lax.dynamic_slice_in_dim(w_down, begin, share, 0)
+    counted = (part == 0) | (jnp.arange(share) >= overlap)
+    down_share = jnp.where(counted[:, None], down_share, 0)
 
     kv_all = jnp.concatenate([earlier[d] for d in range(hops - 1, -1, -1)] + [kv_local], axis=1)
     key_total = kv_all.shape[1]
@@ -255,73 +421,60 @@
     middle = inputs + rms_forward(branch, gain_mid)
     ffn_in = rms_forward(middle, gain_ffn).astype(BF)
 
+    def core_blocks(block):
+        blocks = [block]
+        for mask in masks(cores):
+            together = jnp.concatenate(blocks, axis=0) if len(blocks) > 1 else blocks[0]
+            got = swap(together, "fsdp", mask)
+            blocks = blocks + [got[j * total : (j + 1) * total] for j in range(len(blocks))]
+        return blocks
+
+    def core_sum(keep, send):
+        steps = masks(cores)[::-1]
+        for mask in steps:
+            out = keep + swap(send, "fsdp", mask).astype(F32)
+            half = out.shape[0] // 2
+            keep, send = out[:half], out[half:].astype(BF)
+        return out
+
+    def sum_group(near_part, far_part):
+        got = swap(core_sum(*far_part).astype(BF), "seq", SPLIT_BIT)
+        return core_sum(*near_part) + got.astype(F32)
+
     far_in = swap(ffn_in, "seq", SPLIT_BIT)
-    near_all = gather_cores(ffn_in)
-    far_all = gather_cores(far_in)
-
-    def ffn_forward(rows_in):
-        gate = dot(rows_in, gate_share)
-        upward = dot(rows_in, up_share)
-        hid = (gelu_tanh(gate) * upward).astype(BF)
-        return gate, upward, hid, dot(hid, down_share)
-
-    near = ffn_forward(near_all)
-    far = ffn_forward(far_all)
-
-    def sum_group(near_part, far_part):
-        far_sum = sum_cores(far_part)
-        got = swap(far_sum.astype(BF), "seq", SPLIT_BIT)
-        return sum_cores(near_part) + got.astype(F32)
-
-    ffn_out = sum_group(near[3], far[3])
+    near_all = core_blocks(ffn_in)
+    far_all = core_blocks(far_in)
+    near = ffn_forward(near_all, gate_share, up_share, down_share)
+    far = ffn_forward(far_all, gate_share, up_share, down_share)
+    ffn_out = sum_group(near[3:], far[3:])
     result = middle + rms_forward(ffn_out, gain_top)
 
     grad_ffn_out, top_terms = rms_backward(ffn_out, gain_top, upstream)
     grad_low = grad_ffn_out.astype(BF)
     far_grad = swap(grad_low, "seq", SPLIT_BIT)
-    near_grads = gather_cores(grad_low)
-    far_grads = gather_cores(far_grad)
-
-    def ffn_backward(saved, grads):
-        gate, upward, hid, _ = saved
-        d_hidden = dot_nt(grads, down_share)
-        activated, pull = jax.vjp(gelu_tanh, gate)
-        d_gate = pull(d_hidden * upward)[0].astype(BF)
-        d_up = (d_hidden * activated).astype(BF)
-        return d_gate, d_up, dot_nt(d_gate, gate_share) + dot_nt(d_up, up_share)
-
-    near_back = ffn_backward(near, near_grads)
-    far_back = ffn_backward(far, far_grads)
-
-    grad_ffn_in = sum_group(near_back[2], far_back[2])
-
-    def weight_terms(left_near, left_far, right_near, right_far):
-        left = jnp.concatenate([left_near, left_far], axis=0)
-        right = jnp.concatenate([right_near, right_far], axis=0)
-        out = dot_tn(left, right).astype(BF)
-        return out.reshape(seq_count, width // seq_count, share)
+    near_grads = core_blocks(grad_low)
+    far_grads = core_blocks(far_grad)
+    near_back = ffn_backward(near_grads, near[1], near[2], gate_share, up_share, down_share)
+    far_back = ffn_backward(far_grads, far[1], far[2], gate_share, up_share, down_share)
+    grad_ffn_in = sum_group(near_back[2:], far_back[2:])
 
     others = [m for m in masks(seq_count) if m != SPLIT_BIT]
-
-    def owned(terms, order):
-        block = halve(terms, order, own)
-        mine = lax.dynamic_index_in_dim(block, part, 0, keepdims=False)
-        sent = lax.dynamic_index_in_dim(block, 1 - part, 0, keepdims=False)
-        got = swap(sent.astype(BF), "seq", SPLIT_BIT).astype(F32)
-        mine = mine.astype(F32)
-        return jnp.where(
-            part == 0,
-            jnp.concatenate([mine, got], axis=1),
-            jnp.concatenate([got, mine], axis=1),
+    swapped = [others[1], others[0]] + others[2:]
+
+    def owned(left, near_right, far_right, order):
+        first, rest = weight_terms(
+            own, seq_count, order + [SPLIT_BIT], left, near_right, far_right
         )
-
-    swapped = [others[1], others[0]] + others[2:]
-    down_terms = weight_terms(near_grads, far_grads, near[2], far[2])
-    down_grad = owned(down_terms, others).T
-    gate_terms = weight_terms(near_all, far_all, near_back[0], far_back[0])
-    gate_grad = owned(gate_terms, swapped)
-    up_terms = weight_terms(near_all, far_all, near_back[1], far_back[1])
-    up_grad = owned(up_terms, others)
+        block = halve(first, rest, order)
+        mine = block[1]
+        got = swap(block[0].astype(BF), "seq", SPLIT_BIT).astype(F32)
+        lower = jnp.where(part == 0, mine, got)
+        upper = jnp.where(part == 0, got, mine)
+        return jnp.concatenate([lower, upper[:, overlap:]], axis=1)
+
+    down_grad = owned(near_grads + far_grads, near[0], far[0], others).T
+    gate_grad = owned(near_all + far_all, near_back[0], far_back[0], swapped)
+    up_grad = owned(near_all + far_all, near_back[1], far_back[1], others)
 
     grad_middle_norm, ffn_terms = rms_backward(middle, gain_ffn, grad_ffn_in)
     grad_middle = upstream + grad_middle_norm
@@ -385,15 +538,14 @@
     narrow = width // cores
     out_terms = sum_cores(peer_terms(mixed_low, branch_peers).astype(BF)).astype(BF)
     query_terms_w = sum_cores(peer_terms(grad_query_low, in_peers).astype(BF)).astype(BF)
-    every = masks(seq_count)
-    out_grad = halve(
-        out_terms.reshape(seq_count, q_width // seq_count, narrow), every, own
-    ).reshape(q_width // seq_count, narrow)
-    query_grad = (
-        halve(query_terms_w.reshape(seq_count, q_width // seq_count, narrow), swapped + [SPLIT_BIT], own)
-        .reshape(q_width // seq_count, narrow)
-        .T
-    )
+    def rows_owned(terms, order):
+        terms = terms.reshape(seq_count, q_width // seq_count, narrow)
+        terms = jnp.take(terms, own ^ jnp.array(arrangement(order), jnp.int32), axis=0)
+        half = seq_count // 2
+        return halve(terms[:half], terms[half:], order)[0]
+
+    out_grad = rows_owned(out_terms, others + [SPLIT_BIT])
+    query_grad = rows_owned(query_terms_w, swapped + [SPLIT_BIT]).T
 
     kv_terms = sum_cores(peer_terms(grad_kv_low, in_peers).astype(BF)).astype(BF)
     kv_rows = HD // seq_count

time: 546 us -> 559 us (1.024)
  Pallas kernels: 0 us -> 98.6 us
  matrix products: 150 us -> 56.2 us
  local copies, waits for them, and re-layouts: 99.8 us -> 81.4 us
  waiting for transfers between devices: 141 us -> 159 us
  other arithmetic: 80.9 us -> 88.3 us
    pallas_call x0 -> x7, Pallas kernels: none -> 98.6 us  [the longest x3 34.5 us: weight_terms(): pl.pallas_call(functools.partial(weight_kernel, n, order), out_shape=[jax...]
    dot_general x9 -> x3, matrix products: 45.4 us -> 4.11 us  [dot_nt(): lax.dot_general(a, b, (((1,), (1,)), ((), ())), preferred_element_type=F32)]
    dot_general x9 -> x3, matrix products: 40 us -> 5.56 us  [dot(): return jnp.dot(a, b, preferred_element_type=F32)]
    convert_element_type x23 -> x5, other arithmetic: 27.1 us -> 4.75 us  [the longest x3 3.74 us: owned(): got = swap(block[0].astype(BF), 'seq', SPLIT_BIT).astype(F32)]
    dot_general x9 -> x6, matrix products: 30.5 us -> 11.1 us  [dot_tn(): lax.dot_general(a, b, (((0,), (0,)), ((), ())), preferred_element_type=F32)]
    convert_element_type x3, local copies, waits for them, and re-layouts: 19.4 us -> 2.32 us  [owned(): got = swap(block[0].astype(BF), 'seq', SPLIT_BIT).astype(F32)]
    another operation x2 -> x14, other arithmetic: 1.59 us -> 14.7 us
    ppermute x38, waiting for transfers between devices: 105 us -> 118 us  [swap(): return lax.ppermute(value, axis, [(i, i ^ mask) for i in range(count)])]
  transfers between devices with their start and end apart: 43 -> 43, of which waited for: 13 -> 14; matrix products, arithmetic and copies ran while one was open for 52% -> 33% of each run, Pallas kernels for 0% -> 18%
where the time goes in v2:
time: 559 us; the launch traced here: 550 us
  waiting for transfers between devices  159 us (28%)
  Pallas kernels  98.6 us (18%)
  other arithmetic  88.3 us (16%)
  local copies, waits for them, and re-layouts  81.4 us (15%)
  starting transfers between devices  62.7 us (11%)
  matrix products  56.2 us (10%)
    ppermute x38, waiting for transfers between devices, swap(): return lax.ppermute(value, axis, [(i, i ^ mask) for i in range(count)])  118 us
    ppermute x38, starting transfers between devices, swap(): return lax.ppermute(value, axis, [(i, i ^ mask) for i in range(count)])  34.9 us
    pallas_call x3, Pallas kernels, weight_terms(): pl.pallas_call(functools.partial(weight_kernel, n, order), out_shape=[jax...  34.5 us
    pallas_call x2, Pallas kernels, ffn_forward(): pl.pallas_call(functools.partial(ffn_forward_kernel, n), out_shape=[jax.S...  32.3 us
    pallas_call x2, Pallas kernels, ffn_backward(): pl.pallas_call(functools.partial(ffn_backward_kernel, n), out_shape=[jax....  31.9 us
    all_to_all x1, waiting for transfers between devices, shards(): lax.all_to_all(tail, 'seq', 0, 0, tiled=True).astype(F32)  22.3 us
    unnamed x252, local copies, waits for them, and re-layouts  19.4 us
    another operation x14, other arithmetic  14.7 us
  transfers between devices with their start and end apart: 43, of which 14 were waited for; matrix products, arithmetic and copies ran while one was open for 33% of the time, Pallas kernels for 18%

profile of v2, /device:TPU:0, one launch (start us, length us, event | category | flops | bytes accessed | tf_op | source)
XLA Modules:
  0.0 550.0 jit_solution(5293524466215673066)
XLA Ops:
  15.1 4.2 dynamic-slice_select_fusion.refs_4_.refs_6_
  19.2 1.8 pad_maximum_fusion
  21.0 2.4 maximum_select_fusion
  30.0 8.3 %all-to-all-start = ((bf16[16,16,512]{2,1,0:T(8,128)(2,1)}), bf16[16,16,512]{2,1,0:T(8,128)(2,1)S(1)}, u32[]{:S(2)}, u32[]{:S(2)}) async-start(bf16[16,16,512]{2,1,0:T(8,128)(2,1)} %pad_maximum_fusion.16), calls=%async_computation | async-start | bytes 524288 | tf_op jit(solution)/shard_map/all_to_all | solution.py:366
  38.3 1.9 pad_maximum_fusion.2
  40.2 1.9 bitcast_select_fusion
  42.1 6.3 %all-to-all-done = bf16[16,16,512]{2,1,0:T(8,128)(2,1)S(1)} async-done(((bf16[16,16,512]{2,1,0:T(8,128)(2,1)}), bf16[16,16,512]{2,1,0:T(8,128)(2,1)S(1)}, u32[]{:S(2)}, u32[]{:S(2)}) %all-to-all-start) | async-done | bytes 262176 | tf_op jit(solution)/shard_map/all_to_all | solution.py:366
  50.1 2.4 bitcast_select_fusion.1
  52.6 4.6 all-to-all-start.1
  60.3 2.5 copy.54
  62.8 2.6 multiply_reduce_fusion.11
  67.3 13.1 %all-to-all-done.1 = bf16[16,64,512]{2,1,0:T(8,128)(2,1)} async-done(((bf16[16,64,512]{2,1,0:T(8,128)(2,1)}), bf16[16,64,512]{2,1,0:T(8,128)(2,1)}, u32[]{:S(2)}, u32[]{:S(2)}) %all-to-all-start.1) | async-done | bytes 1048608 | tf_op jit(solution)/shard_map/all_to_all | solution.py:370
  82.8 3.2 fusion.121
  86.0 3.6 convolution_convert_fusion.6
  89.9 2.4 multiply_reduce_fusion.8
  95.2 3.1 collective-permute-start.4
  104.0 6.0 %collective-permute-done.4.refs_0_.refs_3_ = bf16[256,1152]{1,0:T(8,128)(2,1)} collective-permute-done((bf16[256,1152]{1,0:T(8,128)(2,1)S(1)}, bf16[256,1152]{1,0:T(8,128)(2,1)}, u32[]{:S(2)}, u32[]{:S(2)}) %collective-permute-start.4) | collective-permute-done | bytes 589856 | tf_op jit(solution)/shard_map/ppermute | solution.py:24
  110.0 7.3 %constant_dynamic-slice_fusion = (bf16[1152,1792]{1,0:T(8,128)(2,1)}, bf16[1152,1792]{1,0:T(8,128)(2,1)}) fusion(bf16[1152,3456]{1,0:T(8,128)(2,1)} %param.26, s32[]{:T(128)S(6)} %mul.733, bf16[1152,3456]{1,0:T(8,128)(2,1)} %param.25), kind=kLoop, calls=%fused_computation.270 | loop fusion | bytes 16515076 | tf_op jit(solution)/shard_map/dynamic_slice | solution.py:388
  118.5 15.9 %shard_map.231 = (bf16[512,1792]{1,0:T(8,128)(2,1)}, bf16[512,1792]{1,0:T(8,128)(2,1)}, bf16[512,1792]{1,0:T(8,128)(2,1)}, f32[256,1152]{1,0:T(8,128)}, bf16[256,1152]{1,0:T(8,128)(2,1)}) custom-call(bf16[256,1152]{1,0:T(8,128)(2,1)} %collective-permute-done.4.refs_0_.refs_3_, bf16[256,1152]{1,0:T(8,128)(2,1)} %copy-done.114, ...), custom_call_target="tpu_custom_call" | custom-call | flops 6341787648 | bytes 17891328 | tf_op jit(solution)/shard_map/pallas_call | solution.py:189
  135.3 16.4 %shard_map.230 = (bf16[512,1792]{1,0:T(8,128)(2,1)}, bf16[512,1792]{1,0:T(8,128)(2,1)}, bf16[512,1792]{1,0:T(8,128)(2,1)}, f32[256,1152]{1,0:T(8,128)}, bf16[256,1152]{1,0:T(8,128)(2,1)}) custom-call(bf16[256,1152]{1,0:T(8,128)(2,1)} %copy-done.54, bf16[256,1152]{1,0:T(8,128)(2,1)} %copy-done.115, bf16[1152,1792]{1,0:T(8,128)(2,1)} %get-tuple-element.157.refs_2_.refs_4_, ...), custom_call_target="tpu_custom_call" | custom-call | flops 6341787648 | bytes 17891328 | tf_op jit(solution)/shard_map/pallas_call | solution.py:189
  156.7 2.0 reshape.774
  158.8 3.3 copy.81
  165.9 2.8 collective-permute-done.7
  168.7 1.8 multiply_reduce_fusion.6
  176.1 11.3 %collective-permute-done.10.refs_0_.refs_3_ = bf16[256,1152]{1,0:T(8,128)(2,1)S(1)} collective-permute-done((bf16[256,1152]{1,0:T(8,128)(2,1)S(1)}, bf16[256,1152]{1,0:T(8,128)(2,1)S(1)}, u32[]{:S(2)}, u32[]{:S(2)}) %collective-permute-start.10) | collective-permute-done | bytes 589856 | tf_op jit(solution)/shard_map/ppermute | solution.py:24
  190.2 15.9 %shard_map.233 = (bf16[512,1792]{1,0:T(8,128)(2,1)}, bf16[512,1792]{1,0:T(8,128)(2,1)}, f32[256,1152]{1,0:T(8,128)}, bf16[256,1152]{1,0:T(8,128)(2,1)}) custom-call(bf16[256,1152]{1,0:T(8,128)(2,1)} %copy-done.116, bf16[256,1152]{1,0:T(8,128)(2,1)} %copy-done.117, bf16[512,1792]{1,0:T(8,128)(2,1)} %get-tuple-element.44.refs_2_, ...), custom_call_target="tpu_custom_call" | custom-call | flops 6341787648 | bytes 19726336 | tf_op jit(solution)/shard_map/pallas_call | solution.py:234
  207.1 15.9 %shard_map.232 = (bf16[512,1792]{1,0:T(8,128)(2,1)}, bf16[512,1792]{1,0:T(8,128)(2,1)}, f32[256,1152]{1,0:T(8,128)}, bf16[256,1152]{1,0:T(8,128)(2,1)}) custom-call(bf16[256,1152]{1,0:T(8,128)(2,1)} %copy-done.53, bf16[256,1152]{1,0:T(8,128)(2,1)} %copy-done.118, bf16[512,1792]{1,0:T(8,128)(2,1)} %get-tuple-element.40.refs_2_, ...), custom_call_target="tpu_custom_call" | custom-call | flops 6341787648 | bytes 19726336 | tf_op jit(solution)/shard_map/pallas_call | solution.py:234
  223.4 11.6 %shard_map.236 = (bf16[8,72,1792]{2,1,0:T(8,128)(2,1)}, bf16[8,72,1792]{2,1,0:T(8,128)(2,1)}) custom-call(s32[1]{0:T(128)} %bitcast.79.refs_0_, bf16[256,1152]{1,0:T(8,128)(2,1)} %copy-done.53, bf16[256,1152]{1,0:T(8,128)(2,1)} %copy-done.118, bf16[256,1152]{1,0:T(8,128)(2,1)} %copy-done.116, bf16[256,1152]{1,0:T(8,128)(2,1)} %copy-done.117, ...), custom_call_target="tpu_custom_call" | custom-call | flops 4227858432 | bytes 10158080 | tf_op jit(solution)/shard_map/pallas_call | solution.py:285
  235.5 1.8 collective-permute-start.13
  237.3 11.4 %shard_map.235 = (bf16[8,72,1792]{2,1,0:T(8,128)(2,1)}, bf16[8,72,1792]{2,1,0:T(8,128)(2,1)}) custom-call(s32[1]{0:T(128)} %bitcast.79.refs_0_, bf16[256,1152]{1,0:T(8,128)(2,1)} %copy-done.54, bf16[256,1152]{1,0:T(8,128)(2,1)} %copy-done.115, bf16[256,1152]{1,0:T(8,128)(2,1)} %collective-permute-done.4.refs_0_.refs_3_, bf16[256,1152]{1,0:T(8,128)(2,1)} %copy-done.114, ...), custom_call_target="tpu_custom_call" | custom-call | flops 4227858432 | bytes 10158080 | tf_op jit(solution)/shard_map/pallas_call | solution.py:285
  250.3 11.4 %shard_map.234 = (bf16[8,72,1792]{2,1,0:T(8,128)(2,1)}, bf16[8,72,1792]{2,1,0:T(8,128)(2,1)}) custom-call(s32[1]{0:T(128)} %bitcast.79.refs_0_, bf16[256,1152]{1,0:T(8,128)(2,1)} %copy-done.54, bf16[256,1152]{1,0:T(8,128)(2,1)} %copy-done.115, bf16[256,1152]{1,0:T(8,128)(2,1)} %collective-permute-done.4.refs_0_.refs_3_, bf16[256,1152]{1,0:T(8,128)(2,1)} %copy-done.114, ...), custom_call_target="tpu_custom_call" | custom-call | flops 4227858432 | bytes 10158080 | tf_op jit(solution)/shard_map/pallas_call | solution.py:285
  261.7 1.9 collective-permute-start.26
  267.9 2.5 fusion.23
  271.5 4.0 fusion.44
  275.5 3.8 fusion.53
  281.9 11.6 %fusion.9 = f32[2,640,256]{2,1,0:T(8,128)} fusion(f32[2,512,640]{2,1,0:T(8,128)} %fusion.53, bf16[2,512,128]{2,1,0:T(8,128)(2,1)S(1)} %bitcast.242, bf16[2,512,128]{2,1,0:T(8,128)(2,1)S(1)} %bitcast.238, f32[2,512,640]{2,1,0:T(8,128)} %get-tuple-element.148, f32[2,512]{1,0:T(2,128)S(1)} %copy-done.119), kind=kOutput, calls=%fused_computation.37 | convolution fusion | flops 341182080 | bytes 7081984 | tf_op jit(solution)/shard_map/xzo,xza->xoa/dot_general | solution.py:489
  296.2 4.7 all-to-all-start.2
  300.9 9.2 %fusion.12 = f32[2,512,256]{2,1,0:T(8,128)S(1)} fusion(f32[2,512,640]{2,1,0:T(8,128)} %fusion.53, bf16[2,640,512]{2,1,0:T(8,128)(2,1)S(1)} %copy-done.52, f32[2,512,640]{2,1,0:T(8,128)} %get-tuple-element.148, f32[2,512]{1,0:T(2,128)S(1)} %copy-done.119), kind=kOutput, calls=%fused_computation.38 | convolution fusion | flops 340133504 | bytes 12197888 | tf_op jit(solution)/shard_map/ajm,amn->ajn/dot_general | solution.py:488
  316.1 2.1 add_convert_fusion
  319.3 1.9 collective-permute-start.35
  321.2 14.6 %collective-permute-done.30 = bf16[8,72,1792]{2,1,0:T(8,128)(2,1)} collective-permute-done((bf16[8,72,1792]{2,1,0:T(8,128)(2,1)}, bf16[8,72,1792]{2,1,0:T(8,128)(2,1)}, u32[]{:S(2)}, u32[]{:S(2)}) %collective-permute-start.30) | collective-permute-done | bytes 2064416 | tf_op jit(solution)/shard_map/ppermute | solution.py:24
  335.7 2.1 add_convert_fusion.1
  340.2 2.0 collective-permute-start.31
  342.1 2.8 add_convert_fusion.3
  345.0 2.4 copy.75
  347.4 3.2 gather_fusion.5
  354.6 2.8 add_convert_fusion.4
  357.3 2.4 copy.71
  359.7 3.2 gather_fusion.4
  365.3 2.1 add_convert_fusion.2
  372.7 11.8 %collective-permute-done.15 = bf16[8,64,576]{2,1,0:T(8,128)(2,1)S(1)} collective-permute-done((bf16[8,64,576]{2,1,0:T(8,128)(2,1)S(1)}, bf16[8,64,576]{2,1,0:T(8,128)(2,1)S(1)}, u32[]{:S(2)}, u32[]{:S(2)}) %collective-permute-start.15) | collective-permute-done | bytes 589856 | tf_op jit(solution)/shard_map/ppermute | solution.py:24
  388.8 2.9 collective-permute-start.36
  396.2 2.9 collective-permute-start.28
  399.1 2.0 gather_fusion.3
  402.2 4.6 all-to-all-start.3
  408.0 2.9 collective-permute-start.24
  412.1 62.9 %collective-permute-done.24 = bf16[2,64,576]{2,1,0:T(8,128)(2,1)S(1)} collective-permute-done((bf16[2,64,576]{2,1,0:T(8,128)(2,1)S(1)}, bf16[2,64,576]{2,1,0:T(8,128)(2,1)S(1)}, u32[]{:S(2)}, u32[]{:S(2)}) %collective-permute-start.24) | collective-permute-done | bytes 147488 | tf_op jit(solution)/shard_map/ppermute | solution.py:24
  475.2 3.2 collective-permute-done.17
  480.7 2.2 collective-permute-done.18
  488.5 2.0 collective-permute-start.33
  505.3 1.8 broadcast_select_fusion.2
  515.1 5.7 %all-to-all-start.4 = ((bf16[16,50,576]{2,1,0:T(8,128)(2,1)}), bf16[16,50,576]{2,1,0:T(8,128)(2,1)S(1)}, u32[]{:S(2)}, u32[]{:S(2)}) async-start(bf16[16,50,576]{2,1,0:T(8,128)(2,1)} %pad_maximum_fusion.8), calls=%async_computation.4 | async-start | bytes 2293760 | tf_op jit(solution)/shard_map/all_to_all | solution.py:582
  520.9 2.1 pad_maximum_fusion.12
  525.1 22.3 %all-to-all-done.4 = bf16[16,50,576]{2,1,0:T(8,128)(2,1)S(1)} async-done(((bf16[16,50,576]{2,1,0:T(8,128)(2,1)}), bf16[16,50,576]{2,1,0:T(8,128)(2,1)S(1)}, u32[]{:S(2)}, u32[]{:S(2)}) %all-to-all-start.4) | async-done | bytes 921632 | tf_op jit(solution)/shard_map/all_to_all | solution.py:582
  (490 shorter events, 138.9 us)
Async XLA Ops:
  2.2 17.1 %collective-permute-start = (bf16[576,1536]{1,0:T(8,128)(2,1)S(1)}, bf16[576,1536]{1,0:T(8,128)(2,1)}, u32[]{:S(2)}, u32[]{:S(2)}) collective-permute-start(bf16[576,1536]{1,0:T(8,128)(2,1)S(1)} %constant_dynamic-update-slice_fusion), channel_id=1, source_target_pairs={{0,1},{1,0},{2,3},{3,2},{4,5},{5,4},{6,7},{7,6},{8,9},{9,8},{10,11... | collective-permute-start | bytes 5308424 | tf_op jit(solution)/shard_map/ppermute | solution.py:24
  2.7 35.6 %collective-permute-start.1 = (bf16[1024,576]{0,1:T(8,128)(2,1)}, bf16[1024,576]{0,1:T(8,128)(2,1)}, u32[]{:S(2)}, u32[]{:S(2)}) collective-permute-start(bf16[1024,576]{0,1:T(8,128)(2,1)} %param.24), channel_id=1, source_target_pairs={{0,1},{1,0},{2,3},{3,2},{4,5},{5,4},{6,7},{7,6},{8,9},{9,8},{10,11... | collective-permute-start | bytes 3538952 | tf_op jit(solution)/shard_map/ppermute | solution.py:24
  7.5 7.4 %copy-start.79 = (f32[256]{0:T(256)}, f32[256]{0:T(256)S(1)}, u32[]{:S(2)}) copy-start(f32[256]{0:T(256)S(1)} %get-tuple-element.142) | copy-start | bytes 3076
  8.1 19.2 %copy-start.90 = (f32[1,256]{1,0:T(1,128)}, f32[1,256]{1,0:T(1,128)S(1)}, u32[]{:S(2)}) copy-start(f32[1,256]{1,0:T(1,128)S(1)} %get-tuple-element.124) | copy-start | bytes 3076
  28.7 38.0 %copy-start.45 = (f32[2,128,128]{2,1,0:T(8,128)}, f32[2,128,128]{2,1,0:T(8,128)S(1)}, u32[]{:S(2)}) copy-start(f32[2,128,128]{2,1,0:T(8,128)S(1)} %get-tuple-element.129) | copy-start | bytes 393220
  30.0 18.4 %all-to-all-start = ((bf16[16,16,512]{2,1,0:T(8,128)(2,1)}), bf16[16,16,512]{2,1,0:T(8,128)(2,1)S(1)}, u32[]{:S(2)}, u32[]{:S(2)}) async-start(bf16[16,16,512]{2,1,0:T(8,128)(2,1)} %pad_maximum_fusion.16), calls=%async_computation | async-start | bytes 524288 | tf_op jit(solution)/shard_map/all_to_all | solution.py:366
  52.6 27.8 %all-to-all-start.1 = ((bf16[16,64,512]{2,1,0:T(8,128)(2,1)}), bf16[16,64,512]{2,1,0:T(8,128)(2,1)}, u32[]{:S(2)}, u32[]{:S(2)}) async-start(bf16[16,64,512]{2,1,0:T(8,128)(2,1)} %bitcast_select_fusion.1), calls=%async_computation.1 | async-start | bytes 2097152 | tf_op jit(solution)/shard_map/all_to_all | solution.py:370
  67.1 15.5 %copy-start.61 = (bf16[2,128,4,128]{3,2,1,0:T(4,128)(2,1)}, bf16[2,128,4,128]{3,2,1,0:T(4,128)(2,1)S(1)}, u32[]{:S(2)}) copy-start(bf16[2,128,4,128]{3,2,1,0:T(4,128)(2,1)S(1)} %copy.55) | copy-start | bytes 786436
  67.3 15.3 %copy-start.63 = (bf16[2,128,4,128]{3,2,1,0:T(4,128)(2,1)}, bf16[2,128,4,128]{3,2,1,0:T(4,128)(2,1)S(1)}, u32[]{:S(2)}) copy-start(bf16[2,128,4,128]{3,2,1,0:T(4,128)(2,1)S(1)} %copy.56) | copy-start | bytes 786436
  95.2 22.0 %copy-start.54 = (bf16[256,1152]{1,0:T(8,128)(2,1)}, bf16[256,1152]{1,0:T(8,128)(2,1)S(1)}, u32[]{:S(2)}) copy-start(bf16[256,1152]{1,0:T(8,128)(2,1)S(1)} %multiply_convert_fusion.2.refs_0_.refs_1_) | copy-start | bytes 1769476
  95.2 14.7 %collective-permute-start.4 = (bf16[256,1152]{1,0:T(8,128)(2,1)S(1)}, bf16[256,1152]{1,0:T(8,128)(2,1)}, u32[]{:S(2)}, u32[]{:S(2)}) collective-permute-start(bf16[256,1152]{1,0:T(8,128)(2,1)S(1)} %multiply_convert_fusion.2.refs_0_.refs_1_), channel_id=1, source_target_pairs={{0,8},{2,10},{4,12},{6,14},{8,0},{10,2},{12,4},{14,6},{16,24},{18,... | collective-permute-start | bytes 1769480 | tf_op jit(solution)/shard_map/ppermute | solution.py:24
  110.0 7.8 %collective-permute-start.5 = (bf16[256,1152]{1,0:T(8,128)(2,1)}, bf16[256,1152]{1,0:T(8,128)(2,1)S(1)}, u32[]{:S(2)}, u32[]{:S(2)}) collective-permute-start(bf16[256,1152]{1,0:T(8,128)(2,1)} %collective-permute-done.4.refs_0_.refs_3_), channel_id=1, source_target_pairs={{0,1},{1,0},{2,3},{3,2},{4,5},{5,4},{6,7},{7,6},{8,9},{9,8},{10,11... | collective-permute-start | bytes 1769480 | tf_op jit(solution)/shard_map/ppermute | solution.py:24
  117.2 17.2 %collective-permute-start.2 = (bf16[256,1152]{1,0:T(8,128)(2,1)S(1)}, bf16[256,1152]{1,0:T(8,128)(2,1)S(1)}, u32[]{:S(2)}, u32[]{:S(2)}) collective-permute-start(bf16[256,1152]{1,0:T(8,128)(2,1)S(1)} %multiply_convert_fusion.2.refs_0_.refs_1_), channel_id=1, source_target_pairs={{0,1},{1,0},{2,3},{3,2},{4,5},{5,4},{6,7},{7,6},{8,9},{9,8},{10,11... | collective-permute-start | bytes 1769480 | tf_op jit(solution)/shard_map/ppermute | solution.py:24
  134.4 17.8 %copy-start.48 = (f32[256,1152]{1,0:T(8,128)S(1)}, f32[256,1152]{1,0:T(8,128)}, u32[]{:S(2)}) copy-start(f32[256,1152]{1,0:T(8,128)} %get-tuple-element.38) | copy-start | bytes 3538948
  134.4 17.8 %collective-permute-start.6 = (bf16[256,1152]{1,0:T(8,128)(2,1)}, bf16[256,1152]{1,0:T(8,128)(2,1)S(1)}, u32[]{:S(2)}, u32[]{:S(2)}) collective-permute-start(bf16[256,1152]{1,0:T(8,128)(2,1)} %get-tuple-element.39), channel_id=1, source_target_pairs={{0,1},{1,0},{2,3},{3,2},{4,5},{5,4},{6,7},{7,6},{8,9},{9,8},{10,11... | collective-permute-start | bytes 1769480 | tf_op jit(solution)/shard_map/ppermute | solution.py:24
  151.7 14.2 %collective-permute-start.3 = (bf16[256,1152]{1,0:T(8,128)(2,1)}, bf16[256,1152]{1,0:T(8,128)(2,1)S(1)}, u32[]{:S(2)}, u32[]{:S(2)}) collective-permute-start(bf16[256,1152]{1,0:T(8,128)(2,1)} %get-tuple-element.37), channel_id=1, source_target_pairs={{0,1},{1,0},{2,3},{3,2},{4,5},{5,4},{6,7},{7,6},{8,9},{9,8},{10,11... | collective-permute-start | bytes 1769480 | tf_op jit(solution)/shard_map/ppermute | solution.py:24
  153.1 15.6 %collective-permute-start.7 = (bf16[256,1152]{1,0:T(8,128)(2,1)}, bf16[256,1152]{1,0:T(8,128)(2,1)}, u32[]{:S(2)}, u32[]{:S(2)}) collective-permute-start(bf16[256,1152]{1,0:T(8,128)(2,1)} %add_convert_fusion.12), channel_id=1, source_target_pairs={{0,8},{2,10},{4,12},{6,14},{8,0},{10,2},{12,4},{14,6},{16,24},{18,... | collective-permute-start | bytes 1769480 | tf_op jit(solution)/shard_map/ppermute | solution.py:24
  172.9 15.5 %copy-start.53 = (bf16[256,1152]{1,0:T(8,128)(2,1)}, bf16[256,1152]{1,0:T(8,128)(2,1)S(1)}, u32[]{:S(2)}) copy-start(bf16[256,1152]{1,0:T(8,128)(2,1)S(1)} %get-tuple-element.97.refs_0_.refs_1_) | copy-start | bytes 1769476
  172.9 14.4 %copy-start.105 = (s32[16]{0:T(128)S(1)}, s32[16]{0:T(128)}, u32[]{:S(2)}) copy-start(s32[16]{0:T(128)} %get-tuple-element.153) | copy-start | bytes 196
  172.9 14.4 %collective-permute-start.10 = (bf16[256,1152]{1,0:T(8,128)(2,1)S(1)}, bf16[256,1152]{1,0:T(8,128)(2,1)S(1)}, u32[]{:S(2)}, u32[]{:S(2)}) collective-permute-start(bf16[256,1152]{1,0:T(8,128)(2,1)S(1)} %get-tuple-element.97.refs_0_.refs_1_), channel_id=1, source_target_pairs={{0,8},{2,10},{4,12},{6,14},{8,0},{10,2},{12,4},{14,6},{16,24},{18,... | collective-permute-start | bytes 1769480 | tf_op jit(solution)/shard_map/ppermute | solution.py:24
  187.4 2.0 collective-permute-start.11
  188.4 17.8 %collective-permute-start.8 = (bf16[256,1152]{1,0:T(8,128)(2,1)S(1)}, bf16[256,1152]{1,0:T(8,128)(2,1)S(1)}, u32[]{:S(2)}, u32[]{:S(2)}) collective-permute-start(bf16[256,1152]{1,0:T(8,128)(2,1)S(1)} %get-tuple-element.97.refs_0_.refs_1_), channel_id=1, source_target_pairs={{0,1},{1,0},{2,3},{3,2},{4,5},{5,4},{6,7},{7,6},{8,9},{9,8},{10,11... | collective-permute-start | bytes 1769480 | tf_op jit(solution)/shard_map/ppermute | solution.py:24
  206.1 29.3 %collective-permute-start.12 = (bf16[256,1152]{1,0:T(8,128)(2,1)}, bf16[256,1152]{1,0:T(8,128)(2,1)S(1)}, u32[]{:S(2)}, u32[]{:S(2)}) collective-permute-start(bf16[256,1152]{1,0:T(8,128)(2,1)} %get-tuple-element.47), channel_id=1, source_target_pairs={{0,1},{1,0},{2,3},{3,2},{4,5},{5,4},{6,7},{7,6},{8,9},{9,8},{10,11... | collective-permute-start | bytes 1769480 | tf_op jit(solution)/shard_map/ppermute | solution.py:24
  223.0 40.7 %collective-permute-start.9 = (bf16[256,1152]{1,0:T(8,128)(2,1)}, bf16[256,1152]{1,0:T(8,128)(2,1)S(1)}, u32[]{:S(2)}, u32[]{:S(2)}) collective-permute-start(bf16[256,1152]{1,0:T(8,128)(2,1)} %get-tuple-element.43), channel_id=1, source_target_pairs={{0,1},{1,0},{2,3},{3,2},{4,5},{5,4},{6,7},{7,6},{8,9},{9,8},{10,11... | collective-permute-start | bytes 1769480 | tf_op jit(solution)/shard_map/ppermute | solution.py:24
  223.4 12.1 %copy-start.47 = (f32[256,1152]{1,0:T(8,128)S(1)}, f32[256,1152]{1,0:T(8,128)}, u32[]{:S(2)}) copy-start(f32[256,1152]{1,0:T(8,128)} %get-tuple-element.46) | copy-start | bytes 3538948
  235.0 81.1 %collective-permute-start.34 = (bf16[8,72,1792]{2,1,0:T(8,128)(2,1)}, bf16[8,72,1792]{2,1,0:T(8,128)(2,1)}, u32[]{:S(2)}, u32[]{:S(2)}) collective-permute-start(bf16[8,72,1792]{2,1,0:T(8,128)(2,1)} %get-tuple-element.59), channel_id=1, source_target_pairs={{0,2},{2,0},{4,6},{6,4},{8,10},{10,8},{12,14},{14,12},{16,18},{18,... | collective-permute-start | bytes 6193160 | tf_op jit(solution)/shard_map/ppermute | solution.py:24
  235.5 28.1 %collective-permute-start.13 = (bf16[256,1152]{1,0:T(8,128)(2,1)S(1)}, bf16[256,1152]{1,0:T(8,128)(2,1)S(1)}, u32[]{:S(2)}, u32[]{:S(2)}) collective-permute-start(bf16[256,1152]{1,0:T(8,128)(2,1)S(1)} %add_convert_fusion.11), channel_id=1, source_target_pairs={{0,8},{2,10},{4,12},{6,14},{8,0},{10,2},{12,4},{14,6},{16,24},{18,... | collective-permute-start | bytes 1769480 | tf_op jit(solution)/shard_map/ppermute | solution.py:24
  248.8 87.0 %collective-permute-start.30 = (bf16[8,72,1792]{2,1,0:T(8,128)(2,1)}, bf16[8,72,1792]{2,1,0:T(8,128)(2,1)}, u32[]{:S(2)}, u32[]{:S(2)}) collective-permute-start(bf16[8,72,1792]{2,1,0:T(8,128)(2,1)} %get-tuple-element.55), channel_id=1, source_target_pairs={{0,2},{2,0},{4,6},{6,4},{8,10},{10,8},{12,14},{14,12},{16,18},{18,... | collective-permute-start | bytes 6193160 | tf_op jit(solution)/shard_map/ppermute | solution.py:24
  250.3 13.4 %copy-start.20 = (f32[256,1152]{1,0:T(8,128)S(1)}, f32[256,1152]{1,0:T(8,128)}, u32[]{:S(2)}) copy-start(f32[256,1152]{1,0:T(8,128)} %get-tuple-element.42) | copy-start | bytes 3538948
  250.3 13.4 %copy-start.89 = (f32[256]{0:T(256)S(1)}, f32[256]{0:T(256)}, u32[]{:S(2)}) copy-start(f32[256]{0:T(256)} %copy-done.88) | copy-start | bytes 3076
  261.7 103.6 %collective-permute-start.26 = (bf16[8,72,1792]{2,1,0:T(8,128)(2,1)}, bf16[8,72,1792]{2,1,0:T(8,128)(2,1)}, u32[]{:S(2)}, u32[]{:S(2)}) collective-permute-start(bf16[8,72,1792]{2,1,0:T(8,128)(2,1)} %get-tuple-element.51), channel_id=1, source_target_pairs={{0,4},{2,6},{4,0},{6,2},{8,12},{10,14},{12,8},{14,10},{16,20},{18,... | collective-permute-start | bytes 6193160 | tf_op jit(solution)/shard_map/ppermute | solution.py:24
  275.5 18.0 %copy-start.12 = (f32[2,640,256]{2,1,0:T(8,128)}, f32[2,640,256]{2,1,0:T(8,128)S(1)}, u32[]{:S(2)}) copy-start(f32[2,640,256]{2,1,0:T(8,128)S(1)} %fusion.44) | copy-start | bytes 3932164
  281.9 60.2 %collective-permute-start.21 = (bf16[1024,576]{0,1:T(8,128)(2,1)}, bf16[1024,576]{0,1:T(8,128)(2,1)}, u32[]{:S(2)}, u32[]{:S(2)}) collective-permute-start(bf16[1024,576]{0,1:T(8,128)(2,1)} %convolution_convert_fusion), channel_id=1, source_target_pairs={{0,1},{1,0},{2,3},{3,2},{4,5},{5,4},{6,7},{7,6},{8,9},{9,8},{10,11... | collective-permute-start | bytes 3538952 | tf_op jit(solution)/shard_map/ppermute | solution.py:24
  296.2 102.9 %all-to-all-start.2 = ((bf16[16,64,512]{2,1,0:T(8,128)(2,1)}), bf16[16,64,512]{2,1,0:T(8,128)(2,1)}, u32[]{:S(2)}, u32[]{:S(2)}) async-start(bf16[16,64,512]{2,1,0:T(8,128)(2,1)} %bitcast.52), calls=%async_computation.2 | async-start | bytes 2097152 | tf_op jit(solution)/shard_map/all_to_all | solution.py:505
  315.6 39.0 %collective-permute-start.14 = (bf16[1024,576]{0,1:T(8,128)(2,1)}, bf16[1024,576]{0,1:T(8,128)(2,1)}, u32[]{:S(2)}, u32[]{:S(2)}) collective-permute-start(bf16[1024,576]{0,1:T(8,128)(2,1)} %convolution_convert_fusion.2), channel_id=1, source_target_pairs={{0,1},{1,0},{2,3},{3,2},{4,5},{5,4},{6,7},{7,6},{8,9},{9,8},{10,11... | collective-permute-start | bytes 3538952 | tf_op jit(solution)/shard_map/ppermute | solution.py:24
  318.2 17.5 %copy-start.38 = (bf16[8,72,1792]{2,1,0:T(8,128)(2,1)S(1)}, bf16[8,72,1792]{2,1,0:T(8,128)(2,1)}, u32[]{:S(2)}) copy-start(bf16[8,72,1792]{2,1,0:T(8,128)(2,1)} %get-tuple-element.54) | copy-start | bytes 6193156
  319.3 67.2 %collective-permute-start.35 = (bf16[4,72,1792]{2,1,0:T(8,128)(2,1)}, bf16[4,72,1792]{2,1,0:T(8,128)(2,1)}, u32[]{:S(2)}, u32[]{:S(2)}) collective-permute-start(bf16[4,72,1792]{2,1,0:T(8,128)(2,1)} %slice.505), channel_id=1, source_target_pairs={{0,4},{2,6},{4,0},{6,2},{8,12},{10,14},{12,8},{14,10},{16,20},{18,... | collective-permute-start | bytes 3096584 | tf_op jit(solution)/shard_map/ppermute | solution.py:24
  340.2 51.6 %collective-permute-start.31 = (bf16[4,72,1792]{2,1,0:T(8,128)(2,1)}, bf16[4,72,1792]{2,1,0:T(8,128)(2,1)}, u32[]{:S(2)}, u32[]{:S(2)}) collective-permute-start(bf16[4,72,1792]{2,1,0:T(8,128)(2,1)} %slice.497), channel_id=1, source_target_pairs={{0,4},{2,6},{4,0},{6,2},{8,12},{10,14},{12,8},{14,10},{16,20},{18,... | collective-permute-start | bytes 3096584 | tf_op jit(solution)/shard_map/ppermute | solution.py:24
  354.1 16.0 %collective-permute-start.22 = (bf16[8,64,576]{2,1,0:T(8,128)(2,1)}, bf16[8,64,576]{2,1,0:T(8,128)(2,1)}, u32[]{:S(2)}, u32[]{:S(2)}) collective-permute-start(bf16[8,64,576]{2,1,0:T(8,128)(2,1)} %slice.481), channel_id=1, source_target_pairs={{0,2},{2,0},{4,6},{6,4},{8,10},{10,8},{12,14},{14,12},{16,18},{18,... | collective-permute-start | bytes 1769480 | tf_op jit(solution)/shard_map/ppermute | solution.py:24
  364.7 19.7 %collective-permute-start.15 = (bf16[8,64,576]{2,1,0:T(8,128)(2,1)S(1)}, bf16[8,64,576]{2,1,0:T(8,128)(2,1)S(1)}, u32[]{:S(2)}, u32[]{:S(2)}) collective-permute-start(bf16[8,64,576]{2,1,0:T(8,128)(2,1)S(1)} %slice.467), channel_id=1, source_target_pairs={{0,4},{2,6},{4,0},{6,2},{8,12},{10,14},{12,8},{14,10},{16,20},{18,... | collective-permute-start | bytes 1769480 | tf_op jit(solution)/shard_map/ppermute | solution.py:24
  367.5 26.6 %collective-permute-start.27 = (bf16[4,72,1792]{2,1,0:T(8,128)(2,1)S(1)}, bf16[4,72,1792]{2,1,0:T(8,128)(2,1)S(1)}, u32[]{:S(2)}, u32[]{:S(2)}) collective-permute-start(bf16[4,72,1792]{2,1,0:T(8,128)(2,1)S(1)} %slice.489), channel_id=1, source_target_pairs={{0,2},{2,0},{4,6},{6,4},{8,10},{10,8},{12,14},{14,12},{16,18},{18,... | collective-permute-start | bytes 3096584 | tf_op jit(solution)/shard_map/ppermute | solution.py:24
  371.4 14.1 %copy-start.31 = (bf16[8,64,576]{2,1,0:T(8,128)(2,1)}, bf16[8,64,576]{2,1,0:T(8,128)(2,1)S(1)}, u32[]{:S(2)}) copy-start(bf16[8,64,576]{2,1,0:T(8,128)(2,1)S(1)} %add_convert_fusion.8) | copy-start | bytes 1769476
  372.2 34.5 %collective-permute-start.23 = (bf16[4,64,576]{2,1,0:T(8,128)(2,1)}, bf16[4,64,576]{2,1,0:T(8,128)(2,1)}, u32[]{:S(2)}, u32[]{:S(2)}) collective-permute-start(bf16[4,64,576]{2,1,0:T(8,128)(2,1)} %slice.483), channel_id=1, source_target_pairs={{0,4},{2,6},{4,0},{6,2},{8,12},{10,14},{12,8},{14,10},{16,20},{18,... | collective-permute-start | bytes 884744 | tf_op jit(solution)/shard_map/ppermute | solution.py:24
  385.5 6.3 %copy-start.10 = (bf16[8,72,1792]{2,1,0:T(8,128)(2,1)S(1)}, bf16[8,72,1792]{2,1,0:T(8,128)(2,1)}, u32[]{:S(2)}) copy-start(bf16[8,72,1792]{2,1,0:T(8,128)(2,1)} %copy-done.9) | copy-start | bytes 6193156
  385.5 25.4 %collective-permute-start.16 = (bf16[4,64,576]{2,1,0:T(8,128)(2,1)}, bf16[4,64,576]{2,1,0:T(8,128)(2,1)}, u32[]{:S(2)}, u32[]{:S(2)}) collective-permute-start(bf16[4,64,576]{2,1,0:T(8,128)(2,1)} %slice.469), channel_id=1, source_target_pairs={{0,2},{2,0},{4,6},{6,4},{8,10},{10,8},{12,14},{14,12},{16,18},{18,... | collective-permute-start | bytes 884744 | tf_op jit(solution)/shard_map/ppermute | solution.py:24
  388.8 94.8 %collective-permute-start.36 = (bf16[2,72,1792]{2,1,0:T(8,128)(2,1)}, bf16[2,72,1792]{2,1,0:T(8,128)(2,1)}, u32[]{:S(2)}, u32[]{:S(2)}) collective-permute-start(bf16[2,72,1792]{2,1,0:T(8,128)(2,1)} %slice.507), channel_id=1, source_target_pairs={{0,16},{2,18},{4,20},{6,22},{8,24},{10,26},{12,28},{14,30},{16,0},... | collective-permute-start | bytes 1548296 | tf_op jit(solution)/shard_map/ppermute | solution.py:24
  394.1 92.3 %collective-permute-start.32 = (bf16[2,72,1792]{2,1,0:T(8,128)(2,1)}, bf16[2,72,1792]{2,1,0:T(8,128)(2,1)}, u32[]{:S(2)}, u32[]{:S(2)}) collective-permute-start(bf16[2,72,1792]{2,1,0:T(8,128)(2,1)} %slice.499), channel_id=1, source_target_pairs={{0,16},{2,18},{4,20},{6,22},{8,24},{10,26},{12,28},{14,30},{16,0},... | collective-permute-start | bytes 1548296 | tf_op jit(solution)/shard_map/ppermute | solution.py:24
  395.3 5.7 %copy-start.77 = (f32[16,4]{1,0:T(8,128)S(1)}, f32[16,4]{1,0:T(8,128)}, u32[]{:S(2)}) copy-start(f32[16,4]{1,0:T(8,128)} %convert_convert_fusion) | copy-start | bytes 772
  395.3 5.7 %copy-start.97 = (pred[16,4]{1,0:T(8,128)(4,1)S(1)}, pred[16,4]{1,0:T(8,128)(4,1)}, u32[]{:S(2)}) copy-start(pred[16,4]{1,0:T(8,128)(4,1)} %compare_and_fusion) | copy-start | bytes 196
  396.2 95.1 %collective-permute-start.28 = (bf16[2,72,1792]{2,1,0:T(8,128)(2,1)}, bf16[2,72,1792]{2,1,0:T(8,128)(2,1)}, u32[]{:S(2)}, u32[]{:S(2)}) collective-permute-start(bf16[2,72,1792]{2,1,0:T(8,128)(2,1)} %slice.491), channel_id=1, source_target_pairs={{0,16},{2,18},{4,20},{6,22},{8,24},{10,26},{12,28},{14,30},{16,0},... | collective-permute-start | bytes 1548296 | tf_op jit(solution)/shard_map/ppermute | solution.py:24
  402.2 8.7 %copy-start.33 = (bf16[8,64,576]{2,1,0:T(8,128)(2,1)S(1)}, bf16[8,64,576]{2,1,0:T(8,128)(2,1)}, u32[]{:S(2)}) copy-start(bf16[8,64,576]{2,1,0:T(8,128)(2,1)} %copy-done.32) | copy-start | bytes 1769476
  402.2 92.0 %all-to-all-start.3 = ((bf16[16,16,512]{2,1,0:T(8,128)(2,1)}), bf16[16,16,512]{2,1,0:T(8,128)(2,1)}, u32[]{:S(2)}, u32[]{:S(2)}) async-start(bf16[16,16,512]{2,1,0:T(8,128)(2,1)} %multiply_reduce_fusion.1), calls=%async_computation.3 | async-start | bytes 524288 | tf_op jit(solution)/shard_map/all_to_all | solution.py:509
  408.0 67.1 %collective-permute-start.24 = (bf16[2,64,576]{2,1,0:T(8,128)(2,1)S(1)}, bf16[2,64,576]{2,1,0:T(8,128)(2,1)S(1)}, u32[]{:S(2)}, u32[]{:S(2)}) collective-permute-start(bf16[2,64,576]{2,1,0:T(8,128)(2,1)S(1)} %slice.485), channel_id=1, source_target_pairs={{0,16},{2,18},{4,20},{6,22},{8,24},{10,26},{12,28},{14,30},{16,0},... | collective-permute-start | bytes 442376 | tf_op jit(solution)/shard_map/ppermute | solution.py:24
  411.9 71.7 %copy-start.30 = (bf16[4,72,1792]{2,1,0:T(8,128)(2,1)S(1)}, bf16[4,72,1792]{2,1,0:T(8,128)(2,1)}, u32[]{:S(2)}) copy-start(bf16[4,72,1792]{2,1,0:T(8,128)(2,1)} %copy-done.29) | copy-start | bytes 3096580
  412.0 66.4 %collective-permute-start.17 = (bf16[2,64,576]{2,1,0:T(8,128)(2,1)S(1)}, bf16[2,64,576]{2,1,0:T(8,128)(2,1)S(1)}, u32[]{:S(2)}, u32[]{:S(2)}) collective-permute-start(bf16[2,64,576]{2,1,0:T(8,128)(2,1)S(1)} %slice.471), channel_id=1, source_target_pairs={{0,16},{2,18},{4,20},{6,22},{8,24},{10,26},{12,28},{14,30},{16,0},... | collective-permute-start | bytes 442376 | tf_op jit(solution)/shard_map/ppermute | solution.py:24
  475.1 4.9 collective-permute-start.25
  478.4 4.5 collective-permute-start.18
  485.6 16.6 %collective-permute-start.37 = (bf16[72,1792]{1,0:T(8,128)(2,1)}, bf16[72,1792]{1,0:T(8,128)(2,1)}, u32[]{:S(2)}, u32[]{:S(2)}) collective-permute-start(bf16[72,1792]{1,0:T(8,128)(2,1)} %fusion.63), channel_id=1, source_target_pairs={{0,8},{2,10},{4,12},{6,14},{8,0},{10,2},{12,4},{14,6},{16,24},{18,... | collective-permute-start | bytes 774152 | tf_op jit(solution)/shard_map/ppermute | solution.py:24
  488.5 16.9 %collective-permute-start.33 = (bf16[72,1792]{1,0:T(8,128)(2,1)}, bf16[72,1792]{1,0:T(8,128)(2,1)}, u32[]{:S(2)}, u32[]{:S(2)}) collective-permute-start(bf16[72,1792]{1,0:T(8,128)(2,1)} %fusion.62), channel_id=1, source_target_pairs={{0,8},{2,10},{4,12},{6,14},{8,0},{10,2},{12,4},{14,6},{16,24},{18,... | collective-permute-start | bytes 774152 | tf_op jit(solution)/shard_map/ppermute | solution.py:24
  493.3 15.8 %collective-permute-start.29 = (bf16[72,1792]{1,0:T(8,128)(2,1)}, bf16[72,1792]{1,0:T(8,128)(2,1)}, u32[]{:S(2)}, u32[]{:S(2)}) collective-permute-start(bf16[72,1792]{1,0:T(8,128)(2,1)} %fusion.61), channel_id=1, source_target_pairs={{0,8},{2,10},{4,12},{6,14},{8,0},{10,2},{12,4},{14,6},{16,24},{18,... | collective-permute-start | bytes 774152 | tf_op jit(solution)/shard_map/ppermute | solution.py:24
  498.2 13.5 %collective-permute-start.19 = (bf16[512,576]{0,1:T(8,128)(2,1)}, bf16[512,576]{0,1:T(8,128)(2,1)}, u32[]{:S(2)}, u32[]{:S(2)}) collective-permute-start(bf16[512,576]{0,1:T(8,128)(2,1)} %convolution_convert_fusion.4), channel_id=1, source_target_pairs={{0,1},{1,0},{2,3},{3,2},{4,5},{5,4},{6,7},{7,6},{8,9},{9,8},{10,11... | collective-permute-start | bytes 1769480 | tf_op jit(solution)/shard_map/ppermute | solution.py:24
  499.8 1.6 collective-permute-start.20
  515.1 5.7 %copy-start.39 = (f32[72,1792]{1,0:T(8,128)S(1)}, f32[72,1792]{1,0:T(8,128)}, u32[]{:S(2)}) copy-start(f32[72,1792]{1,0:T(8,128)} %broadcast_select_fusion.2) | copy-start | bytes 1548292
  515.1 32.3 %all-to-all-start.4 = ((bf16[16,50,576]{2,1,0:T(8,128)(2,1)}), bf16[16,50,576]{2,1,0:T(8,128)(2,1)S(1)}, u32[]{:S(2)}, u32[]{:S(2)}) async-start(bf16[16,50,576]{2,1,0:T(8,128)(2,1)} %pad_maximum_fusion.8), calls=%async_computation.4 | async-start | bytes 2293760 | tf_op jit(solution)/shard_map/all_to_all | solution.py:582
  (99 other events, 220.0 us)

commit v3 on v2

v3 whole, which is shorter than its diff:
```python
import functools
import math

import jax
import jax.numpy as jnp
from jax import lax
from jax.experimental import pallas as pl
from jax.experimental.pallas import tpu as pltpu
from jax.sharding import PartitionSpec as P

HQ = 4
HD = 256
W = 512
EPSILON = 1e-06
ROPE_BASE = 10000.0
SPLIT_BIT = 4

BF = jnp.bfloat16
F32 = jnp.float32


def swap(value, axis, mask):
    count = lax.axis_size(axis)
    return lax.ppermute(value, axis, [(i, i ^ mask) for i in range(count)])


def masks(count):
    return [1 << k for k in range(count.bit_length() - 1)]


def gather_cores(block):
    for mask in masks(lax.axis_size("fsdp")):
        block = jnp.concatenate([block, swap(block, "fsdp", mask)], axis=0)
    return block


def sum_cores(block):
    for mask in reversed(masks(lax.axis_size("fsdp"))):
        half = block.shape[0] // 2
        got = swap(block[half:].astype(BF), "fsdp", mask)
        block = block[:half].astype(F32) + got.astype(F32)
    return block


def flip(parts, index):
    count = parts.shape[0]
    for mask in masks(count):
        turned = jnp.stack([parts[j ^ mask] for j in range(count)])
        parts = jnp.where((index & mask) != 0, turned, parts)
    return parts


def rms_scale(values):
    return lax.rsqrt(jnp.mean(values * values, axis=-1, keepdims=True) + EPSILON)


def rms_forward(values, gain_vec):
    return values * rms_scale(values) * gain_vec


def rms_backward(values, gain_vec, grad_out):
    scale_rows = rms_scale(values)
    weighted = grad_out * gain_vec
    inner_mean = jnp.mean(weighted * values, axis=-1, keepdims=True)
    grad_in = scale_rows * weighted - values * (scale_rows * scale_rows * scale_rows) * inner_mean
    return (grad_in, grad_out * values * scale_rows)


def rope_tables(seq_pos, head_dim):
    half_dim = head_dim // 2
    frequency = jnp.exp(
        jnp.arange(half_dim, dtype=F32) * (-2.0 * math.log(ROPE_BASE) / head_dim)
    )
    angles = seq_pos.astype(F32)[..., None] * frequency
    return (jnp.cos(angles), jnp.sin(angles))


def rotate(values, cosine_table, sine_table):
    half_dim = values.shape[-1] // 2
    first_half = values[..., :half_dim]
    second_half = values[..., half_dim:]
    return jnp.concatenate(
        [
            first_half * cosine_table - second_half * sine_table,
            second_half * cosine_table + first_half * sine_table,
        ],
        axis=-1,
    )


def gelu_tanh(values):
    return jax.nn.gelu(values, approximate=True)


def sequence_info(lengths, stream_pos):
    seq_ends = jnp.cumsum(lengths, axis=-1)
    before = seq_ends[..., None, :] <= stream_pos[..., :, None]
    seq_ids = jnp.sum(before.astype(jnp.int32), axis=-1)
    starts = jnp.sum(jnp.where(before, lengths[..., None, :], 0), axis=-1)
    return (seq_ids, stream_pos - starts)


def dot(a, b):
    return jnp.dot(a, b, preferred_element_type=F32)


def dot_tn(a, b):
    return lax.dot_general(a, b, (((0,), (0,)), ((), ())), preferred_element_type=F32)


def dot_nt(a, b):
    return lax.dot_general(a, b, (((1,), (1,)), ((), ())), preferred_element_type=F32)


def pick(table, source):
    return jnp.take(source, table, axis=0)


def pick_sum(hops, table, valid, source):
    terms = jnp.take(source, table, axis=0).astype(F32) * valid.astype(F32)[:, None, None]
    count = table.shape[0] // hops
    return jnp.sum(terms.reshape((count, hops) + source.shape[1:]), axis=1).astype(source.dtype)


def arrangement(order):
    if not order:
        return [0]
    rest = arrangement(order[1:])
    return [j | order[0] for j in rest] + rest


def after(value, *others):
    return lax.optimization_barrier((value,) + others)[0]


class Turns:
    def __init__(self, token):
        self.token = token

    def wait(self, value):
        return after(value, self.token)

    def end(self, token):
        self.token = token


class Chain:
    def __init__(self, first, rest, order):
        self.rest, self.order = rest, list(order)
        self.got = swap(first, "seq", self.order[0])

    def step(self, turns):
        got = turns.wait(self.got)
        self.total = self.rest.astype(F32) + got.astype(F32)
        half = self.total.shape[0] // 2
        self.order.pop(0)
        if self.order:
            first, self.rest = self.total[:half].astype(BF), self.total[half:].astype(BF)
            self.got = swap(first, "seq", self.order[0])
            turns.end(first)
        else:
            turns.end(self.total)


def tiles(size):
    tile = 256 if size % 256 == 0 else 128
    return tile, size // tile


def column_tiles(size):
    return [(start, min(256, size - start)) for start in range(0, size, 256)]


COST = pl.CostEstimate(flops=1024, bytes_accessed=1024, transcendentals=0)
VMEM = pl.BlockSpec(memory_space=pltpu.VMEM)
SMEM = pl.BlockSpec(memory_space=pltpu.SMEM)
PARAMS = pltpu.CompilerParams(vmem_limit_bytes=56 * 1024 * 1024)
ROOT = math.sqrt(2.0 / math.pi)
CUBE = 0.044715


def ffn_forward_kernel(n, overlap, *refs):
    part, x_refs, (wg, wu, wd) = refs[0], refs[1 : n + 1], refs[n + 1 : n + 4]
    hid_out, act_out, slope_out, keep, send = refs[n + 4 : n + 9]
    x_all, wg_all, wu_all, wd_all, gate, hid, act, slope, load, store = refs[n + 9 :]
    rows = x_refs[0].shape[0]
    share = hid.shape[1]
    tile, count = tiles(share)
    begin = pl.multiple_of(part[0] * (wg.shape[1] - share), 128)
    down_begin = pl.multiple_of(part[0] * (wd.shape[0] - share), 16)
    loads = [
        pltpu.make_async_copy(wg.at[:, pl.ds(begin, share)], wg_all, load.at[0]),
        pltpu.make_async_copy(wu.at[:, pl.ds(begin, share)], wu_all, load.at[1]),
        pltpu.make_async_copy(wd.at[pl.ds(down_begin, share), :], wd_all, load.at[2]),
    ]
    for copy in loads:
        copy.start()
    for j in range(n):
        x_all[j * rows : (j + 1) * rows, :] = x_refs[j][...]
    parts = [slice(i * tile, (i + 1) * tile) for i in range(count)]
    loads[0].wait()
    for cols in parts:
        gate[:, cols] = dot(x_all[...], wg_all[:, cols])
    loads[1].wait()
    for i, cols in enumerate(parts):
        g, u = gate[:, cols], dot(x_all[...], wu_all[:, cols])
        square = g * g
        t = jnp.tanh(g * (ROOT + ROOT * CUBE * square))
        half = 0.5 * (1.0 + t)
        a = g * half
        d = half + a * (1.0 - t) * (ROOT + 3.0 * ROOT * CUBE * square)
        if i * tile < overlap:
            index = i * tile + lax.broadcasted_iota(jnp.int32, a.shape, 1)
            counted = index >= part[0] * overlap
            a, u = jnp.where(counted, a, 0.0), jnp.where(counted, u, 0.0)
        hid[:, cols] = (a * u).astype(BF)
        act[:, cols] = a.astype(BF)
        slope[:, cols] = (u * d).astype(BF)
    stores = [
        pltpu.make_async_copy(hid, hid_out, store.at[0]),
        pltpu.make_async_copy(act, act_out, store.at[1]),
        pltpu.make_async_copy(slope, slope_out, store.at[2]),
    ]
    for copy in stores:
        copy.start()
    loads[2].wait()
    for start, size in column_tiles(wd.shape[1]):
        out = dot(hid[...], wd_all[:, start : start + size])
        half = out.shape[0] // 2
        keep[:, start : start + size] = out[:half]
        send[:, start : start + size] = out[half:].astype(BF)
    for copy in stores:
        copy.wait()


ANY = pl.BlockSpec(memory_space=pl.ANY)


def ffn_forward(part, blocks, wg, wu, wd, share, overlap):
    n, (rows, width) = len(blocks), blocks[0].shape
    total = n * rows
    return pl.pallas_call(
        functools.partial(ffn_forward_kernel, n, overlap),
        out_shape=[jax.ShapeDtypeStruct((total, share), BF)] * 3
        + [
            jax.ShapeDtypeStruct((total // 2, width), F32),
            jax.ShapeDtypeStruct((total // 2, width), BF),
        ],
        in_specs=[SMEM] + [VMEM] * n + [ANY] * 3,
        out_specs=[ANY] * 3 + [VMEM] * 2,
        scratch_shapes=[pltpu.VMEM((total, width), BF)]
        + [pltpu.VMEM((width, share), BF)] * 2
        + [pltpu.VMEM((share, width), BF)]
        + [pltpu.VMEM((total, share), F32)]
        + [pltpu.VMEM((total, share), BF)] * 3
        + [pltpu.SemaphoreType.DMA((3,))] * 2,
        compiler_params=PARAMS,
        cost_estimate=COST,
    )(part, *blocks, wg, wu, wd)


def ffn_backward_kernel(n, *refs):
    part, g_refs, (act, slope, wg, wu, wd) = refs[0], refs[1 : n + 1], refs[n + 1 : n + 6]
    gate_out, up_out, keep, send = refs[n + 6 : n + 10]
    g_all, act_all, slope_all, wg_all, wu_all, wd_all, d_gate, d_up, load, store = refs[n + 10 :]
    rows = g_refs[0].shape[0]
    share = d_gate.shape[1]
    tile, count = tiles(share)
    down_begin = pl.multiple_of(part[0] * (wd.shape[0] - share), 16)
    begin = pl.multiple_of(part[0] * (wg.shape[1] - share), 128)
    loads = [
        pltpu.make_async_copy(wd.at[pl.ds(down_begin, share), :], wd_all, load.at[0]),
        pltpu.make_async_copy(act, act_all, load.at[1]),
        pltpu.make_async_copy(slope, slope_all, load.at[2]),
        pltpu.make_async_copy(wg.at[:, pl.ds(begin, share)], wg_all, load.at[3]),
        pltpu.make_async_copy(wu.at[:, pl.ds(begin, share)], wu_all, load.at[4]),
    ]
    for copy in loads:
        copy.start()
    for j in range(n):
        g_all[j * rows : (j + 1) * rows, :] = g_refs[j][...]
    for copy in loads[:3]:
        copy.wait()
    for i in range(count):
        cols = slice(i * tile, (i + 1) * tile)
        d = dot_nt(g_all[...], wd_all[cols, :])
        d_gate[:, cols] = (d * slope_all[:, cols].astype(F32)).astype(BF)
        d_up[:, cols] = (d * act_all[:, cols].astype(F32)).astype(BF)
    stores = [
        pltpu.make_async_copy(d_gate, gate_out, store.at[0]),
        pltpu.make_async_copy(d_up, up_out, store.at[1]),
    ]
    for copy in stores:
        copy.start()
    for copy in loads[3:]:
        copy.wait()
    for start, size in column_tiles(wg.shape[0]):
        out = dot_nt(d_gate[...], wg_all[start : start + size, :])
        out = out + dot_nt(d_up[...], wu_all[start : start + size, :])
        half = out.shape[0] // 2
        keep[:, start : start + size] = out[:half]
        send[:, start : start + size] = out[half:].astype(BF)
    for copy in stores:
        copy.wait()


def ffn_backward(part, blocks, act, slope, wg, wu, wd):
    n, (rows, width), share = len(blocks), blocks[0].shape, act.shape[1]
    total = n * rows
    return pl.pallas_call(
        functools.partial(ffn_backward_kernel, n),
        out_shape=[jax.ShapeDtypeStruct((total, share), BF)] * 2
        + [
            jax.ShapeDtypeStruct((total // 2, width), F32),
            jax.ShapeDtypeStruct((total // 2, width), BF),
        ],
        in_specs=[SMEM] + [VMEM] * n + [ANY] * 5,
        out_specs=[ANY] * 2 + [VMEM] * 2,
        scratch_shapes=[pltpu.VMEM((total, width), BF)]
        + [pltpu.VMEM((total, share), BF)] * 2
        + [pltpu.VMEM((width, share), BF)] * 2
        + [pltpu.VMEM((share, width), BF)]
        + [pltpu.VMEM((total, share), BF)] * 2
        + [pltpu.SemaphoreType.DMA((5,)), pltpu.SemaphoreType.DMA((2,))],
        compiler_params=PARAMS,
        cost_estimate=COST,
    )(part, *blocks, act, slope, wg, wu, wd)


def weight_kernel(n, pieces, *refs):
    own, left = refs[0], refs[1 : n + 1]
    outs, (turned, out, right, load) = refs[n + 3 : -4], refs[-4:]
    rows = left[0].shape[0]
    tile, count = tiles(right.shape[1])
    half = right.shape[0] // 2

    def copies(i):
        cols = pl.ds(pl.multiple_of(i * tile, tile), tile)
        return [
            pltpu.make_async_copy(
                refs[n + 1 + k].at[:, cols], right.at[k * half : (k + 1) * half, cols], load.at[k, i]
            )
            for k in range(2)
        ]

    for i in range(count):
        for copy in copies(i):
            copy.start()
    for j in range(n):
        turned[:, j * rows : (j + 1) * rows] = left[j][...].T
    me = own[0]
    begin = 0
    for p, (order, size) in enumerate(pieces):
        halves = outs[2 * p : 2 * p + 2]
        block = halves[0].shape[1]

        @pl.loop(0, size // tile)
        def _(i):
            cols = pl.ds(pl.multiple_of(begin + i * tile, tile), tile)
            into = pl.ds(pl.multiple_of(i * tile, tile), tile)
            for copy in copies(begin // tile + i):
                copy.wait()
            out[...] = dot(turned[...], right[:, cols])
            for k, j in enumerate(arrangement(order)):
                source = pl.multiple_of((me ^ j) * block, 8)
                top, k = divmod(k, halves[0].shape[0])
                halves[top][k, :, into] = out[pl.ds(source, block), :].astype(BF)

        begin = begin + size


def weight_terms(own, seq_count, pieces, left, near, far):
    width, share = left[0].shape[1], near.shape[1]
    block = width // seq_count
    half = seq_count // 2
    n = len(left)
    if block % 8:
        full = dot_tn(jnp.concatenate(left), jnp.concatenate([near, far])).astype(BF)
        full = full.reshape(seq_count, block, share)
        outs, begin = [], 0
        for order, size in pieces:
            piece = full[:, :, begin : begin + size]
            piece = jnp.take(piece, own ^ jnp.array(arrangement(order), jnp.int32), axis=0)
            outs += [piece[:half], piece[half:]]
            begin += size
        return outs
    tile, _ = tiles(share)
    return pl.pallas_call(
        functools.partial(weight_kernel, n, pieces),
        out_shape=[
            jax.ShapeDtypeStruct((half, block, size), BF) for _, size in pieces for _ in range(2)
        ],
        in_specs=[SMEM] + [VMEM] * n + [ANY] * 2,
        out_specs=[VMEM] * (2 * len(pieces)),
        scratch_shapes=[
            pltpu.VMEM((width, n * left[0].shape[0]), BF),
            pltpu.VMEM((width, tile), F32),
            pltpu.VMEM((n * left[0].shape[0], share), BF),
            pltpu.SemaphoreType.DMA((2, share // tile)),
        ],
        compiler_params=PARAMS,
        cost_estimate=COST,
    )(own.reshape(1), *left, near, far)


def window_size(width, cores):
    narrow = width // cores
    return max(-(-((c * narrow) % 128 + narrow) // 128) for c in range(cores)) * 128


def window_of(core, narrow, size):
    return pl.ds(pl.multiple_of(core * narrow // 128 * 128, 128), size)


def outer_kernel(cores, core, mixed, branch, query, attn_in, keep, send):
    size = keep.shape[1]
    split = mixed.shape[1]
    narrow = branch.shape[1] // cores
    for part, (left, right) in enumerate(((mixed, branch), (query, attn_in))):
        turned = left[...].T
        for j in range(cores):
            out = dot(turned, right[:, window_of(core[0] ^ j, narrow, size)])
            target, row = (keep, j) if j < cores // 2 else (send, j - cores // 2)
            row = (2 * row + part) * split
            target[row : row + split, :] = out.astype(target.dtype)


def outer_sum_kernel(order, own, keep, got, first, rest):
    me = own[0]
    half, two, _ = first.shape
    block = two // 2
    width = keep.shape[0] // 2
    for k, j in enumerate(arrangement(order)):
        target = first if k < half else rest
        for part in range(2):
            source = pl.ds(pl.multiple_of(part * width + (me ^ j) * block, 16), block)
            total = keep[source, :] + got[source, :].astype(F32)
            target[k % half, part * block : (part + 1) * block, :] = total.astype(BF)


def outer_begin(core, cores, mixed, branch, query, attn_in):
    width = mixed.shape[1]
    size = window_size(branch.shape[1], cores)
    return pl.pallas_call(
        functools.partial(outer_kernel, cores),
        out_shape=[
            jax.ShapeDtypeStruct((cores * width, size), F32),
            jax.ShapeDtypeStruct((cores * width, size), BF),
        ],
        in_specs=[SMEM] + [VMEM] * 4,
        out_specs=[VMEM] * 2,
        compiler_params=PARAMS,
        cost_estimate=COST,
    )(core, mixed, branch, query, attn_in)


def outer_end(own, seq_count, order, keep, got):
    total, size = keep.shape
    block = total // 2 // seq_count
    half = seq_count // 2
    return pl.pallas_call(
        functools.partial(outer_sum_kernel, order),
        out_shape=[jax.ShapeDtypeStruct((half, 2 * block, size), BF)] * 2,
        in_specs=[SMEM, VMEM, VMEM],
        out_specs=[VMEM] * 2,
        compiler_params=PARAMS,
        cost_estimate=COST,
    )(own, keep, got)


def whole_rows(core, peers, full):
    for j, peer in enumerate(peers):
        rows = peer.shape[0]
        full[pl.ds(pl.multiple_of((core[0] ^ j) * rows, 16), rows), :] = peer[...]


def key_value_kernel(n, core, tokens, *refs):
    peers, (gains, head_gains, cosine, sine) = refs[:n], refs[n : n + 4]
    attn_in, key_proj, kv_local, full = refs[n + 4 :]
    whole_rows(core, peers, full)
    normed = rms_forward(tokens[...].astype(F32), gains[0:1, :]).astype(BF)
    attn_in[...] = normed
    both = dot(normed, full[...])
    keys = both[:, :HD]
    key_proj[...] = keys
    turned = rotate(rms_forward(keys, head_gains[1:2, :]), cosine[...], sine[...])
    kv_local[:, :HD] = turned.astype(BF)
    kv_local[:, HD:] = both[:, HD:].astype(BF)


def key_value(core, tokens, peers, gains, head_gains, cosine, sine):
    total, width = tokens.shape
    return pl.pallas_call(
        functools.partial(key_value_kernel, len(peers)),
        out_shape=[
            jax.ShapeDtypeStruct((total, width), BF),
            jax.ShapeDtypeStruct((total, HD), F32),
            jax.ShapeDtypeStruct((total, 2 * HD), BF),
        ],
        in_specs=[SMEM] + [VMEM] * (len(peers) + 5),
        out_specs=[VMEM] * 3,
        scratch_shapes=[pltpu.VMEM((width, 2 * HD), BF)],
        compiler_params=PARAMS,
        cost_estimate=COST,
    )(core, tokens, *peers, gains, head_gains, cosine, sine)


def query_kernel(n, core, attn_in, *refs):
    peers, (head_gains, cosine, sine, proj, query, full) = refs[:n], refs[n:]
    whole_rows(core, peers, full)
    for h in range(HQ):
        cols = slice(h * HD, (h + 1) * HD)
        out = dot(attn_in[...], full[:, cols])
        proj[:, cols] = out
        turned = rotate(rms_forward(out, head_gains[0:1, :]), cosine[...], sine[...])
        query[:, cols] = turned.astype(BF)


def queries_of(core, attn_in, peers, head_gains, cosine, sine):
    total, width = attn_in.shape
    return pl.pallas_call(
        functools.partial(query_kernel, len(peers)),
        out_shape=[
            jax.ShapeDtypeStruct((total, HQ * HD), F32),
            jax.ShapeDtypeStruct((total, HQ * HD), BF),
        ],
        in_specs=[SMEM] + [VMEM] * (len(peers) + 4),
        out_specs=[VMEM] * 2,
        scratch_shapes=[pltpu.VMEM((width, HQ * HD), BF)],
        compiler_params=PARAMS,
        cost_estimate=COST,
    )(core, attn_in, *peers, head_gains, cosine, sine)


def last_kernel(n, core, *refs):
    q_peers, kv_peers = refs[:n], refs[n : 2 * n]
    (
        tokens, attn_in, grad_middle, grad_query, grad_kv, returned, key_proj, cosine, sine,
        gains, head_gains, grad_inputs, keep, send, in_terms, key_terms, q_full, kv_full,
    ) = refs[2 * n :]
    whole_rows(core, q_peers, q_full)
    whole_rows(core, kv_peers, kv_full)
    grads = grad_kv[...] + returned[...].astype(F32)
    normed = rotate(grads[:, :HD], cosine[...], -sine[...])
    d_key, terms = rms_backward(key_proj[...], head_gains[1:2, :], normed)
    key_terms[...] = jnp.broadcast_to(jnp.sum(terms, axis=0, keepdims=True), key_terms.shape)
    low = jnp.concatenate([d_key.astype(BF), grads[:, HD:].astype(BF)], axis=1)
    size = keep.shape[1]
    narrow = attn_in.shape[1] // n
    turned = low.T
    for j in range(n):
        out = dot(turned, attn_in[:, window_of(core[0] ^ j, narrow, size)])
        target, row = (keep, j) if j < n // 2 else (send, j - n // 2)
        row = row * 2 * HD
        target[row : row + 2 * HD, :] = out.astype(target.dtype)
    d_in = dot_nt(grad_query[...], q_full[...]) + dot_nt(low, kv_full[...])
    d_tokens, terms = rms_backward(tokens[...].astype(F32), gains[0:1, :], d_in)
    in_terms[...] = jnp.broadcast_to(jnp.sum(terms, axis=0, keepdims=True), in_terms.shape)
    grad_inputs[...] = grad_middle[...] + d_tokens


def last(core, q_peers, kv_peers, *rest):
    n = len(q_peers)
    total, width = rest[0].shape
    size = window_size(width, n)
    return pl.pallas_call(
        functools.partial(last_kernel, n),
        out_shape=[
            jax.ShapeDtypeStruct((total, width), F32),
            jax.ShapeDtypeStruct((n * HD, size), F32),
            jax.ShapeDtypeStruct((n * HD, size), BF),
            jax.ShapeDtypeStruct((8, width), F32),
            jax.ShapeDtypeStruct((8, HD), F32),
        ],
        in_specs=[SMEM] + [VMEM] * (2 * n + len(rest)),
        out_specs=[VMEM] * 5,
        scratch_shapes=[pltpu.VMEM((width, HQ * HD), BF), pltpu.VMEM((width, 2 * HD), BF)],
        compiler_params=PARAMS,
        cost_estimate=COST,
    )(core, *q_peers, *kv_peers, *rest)


SCALE = HD ** (-0.5)


def keys_of(lane, rows, hops, earlier, kv_local, keys):
    for d in range(1, hops + 1):
        keys[(hops - d) * rows : (hops - d + 1) * rows, :] = earlier[
            d - 1, lane * rows : (lane + 1) * rows, :
        ]
    keys[hops * rows :, :] = kv_local[lane * rows : (lane + 1) * rows, :]


def allowed_of(place, lengths, lane, rows, hops, window):
    first = place[0] * rows
    q_pos = first + lax.broadcasted_iota(jnp.int32, (rows, 1), 0)
    k_pos = first - hops * rows + lax.broadcasted_iota(jnp.int32, (1, (hops + 1) * rows), 1)
    q_id, k_id = jnp.zeros_like(q_pos), jnp.zeros_like(k_pos)
    end = jnp.int32(0)
    for j in range(lengths.shape[1]):
        end = end + lengths[lane, j]
        q_id = q_id + (end <= q_pos).astype(jnp.int32)
        k_id = k_id + (end <= k_pos).astype(jnp.int32)
    return (q_id == k_id) & (k_pos <= q_pos) & (q_pos - k_pos < window) & (k_pos >= 0)


def soft_of(query, keys, allowed):
    scores = jnp.where(allowed, dot_nt(query, keys) * SCALE, -1e30)
    grown = jnp.exp(scores - jnp.max(scores, axis=-1, keepdims=True))
    return grown * (1.0 / jnp.sum(grown, axis=-1, keepdims=True))


def attention_kernel(
    hops, place, lengths, query, kv_local, earlier, tokens, w_out, gains,
    mixed, branch, middle, ffn_in, keys,
):
    lanes = lengths.shape[0]
    rows = query.shape[0] // lanes
    for lane in range(lanes):
        span = slice(lane * rows, (lane + 1) * rows)
        keys_of(lane, rows, hops, earlier, kv_local, keys)
        allowed = allowed_of(place, lengths, lane, rows, hops, W)
        for h in range(HQ):
            cols = slice(h * HD, (h + 1) * HD)
            soft = soft_of(query[span, cols], keys[:, :HD], allowed)
            mixed[span, cols] = dot(soft.astype(BF), keys[:, HD:]).astype(BF)
        out = dot(mixed[span, :], w_out[...])
        branch[span, :] = out
        mid = tokens[span, :].astype(F32) + rms_forward(out, gains[1:2, :])
        middle[span, :] = mid
        ffn_in[span, :] = rms_forward(mid, gains[2:3, :]).astype(BF)


def attention(hops, place, lengths, query, kv_local, earlier, tokens, w_out, gains):
    total, width = tokens.shape
    lanes = lengths.shape[0]
    return pl.pallas_call(
        functools.partial(attention_kernel, hops),
        out_shape=[
            jax.ShapeDtypeStruct(query.shape, BF),
            jax.ShapeDtypeStruct((total, width), F32),
            jax.ShapeDtypeStruct((total, width), F32),
            jax.ShapeDtypeStruct((total, width), BF),
        ],
        in_specs=[SMEM, SMEM] + [VMEM] * 6,
        out_specs=[VMEM] * 4,
        scratch_shapes=[pltpu.VMEM(((hops + 1) * (total // lanes), 2 * HD), BF)],
        compiler_params=PARAMS,
        cost_estimate=COST,
    )(place, lengths, query, kv_local, earlier, tokens, w_out, gains)


def attention_back_kernel(
    hops, place, lengths, query, kv_local, earlier, upstream, w_out, gains, head_gains,
    branch, middle, keep, got, query_proj, cosine, sine,
    grad_middle, grad_branch, grad_query, grad_kv, grad_earlier, norm_terms, head_terms,
    keys, d_mixed, raws, softs, queries, mixes,
):
    lanes = lengths.shape[0]
    rows = query.shape[0] // lanes
    norm_terms[...] = jnp.zeros_like(norm_terms)
    head_terms[...] = jnp.zeros_like(head_terms)
    for lane in range(lanes):
        span = slice(lane * rows, (lane + 1) * rows)
        d_ffn_in = keep[span, :] + got[span, :].astype(F32)
        d_mid, ffn_terms = rms_backward(middle[span, :], gains[2:3, :], d_ffn_in)
        d_mid = d_mid + upstream[span, :].astype(F32)
        grad_middle[span, :] = d_mid
        d_branch, mid_terms = rms_backward(branch[span, :], gains[1:2, :], d_mid)
        norm_terms[0:1, :] += jnp.sum(mid_terms, axis=0, keepdims=True)
        norm_terms[1:2, :] += jnp.sum(ffn_terms, axis=0, keepdims=True)
        low = d_branch.astype(BF)
        grad_branch[span, :] = low
        d_mixed[...] = dot_nt(low, w_out[...]).astype(BF)
        keys_of(lane, rows, hops, earlier, kv_local, keys)
        allowed = allowed_of(place, lengths, lane, rows, hops, W)
        cos, sin = cosine[span, :], sine[span, :]
        for h in range(HQ):
            cols = slice(h * HD, (h + 1) * HD)
            stack = slice(h * rows, (h + 1) * rows)
            soft = soft_of(query[span, cols], keys[:, :HD], allowed)
            d_soft = dot_nt(d_mixed[:, cols], keys[:, HD:])
            inner = jnp.sum(soft * d_soft, axis=-1, keepdims=True)
            raw = (soft * (d_soft - inner) * SCALE).astype(BF)
            raws[stack, :] = raw
            softs[stack, :] = soft.astype(BF)
            queries[stack, :] = query[span, cols]
            mixes[stack, :] = d_mixed[:, cols]
            normed = rotate(dot(raw, keys[:, :HD]), cos, -sin)
            d_query, terms = rms_backward(query_proj[span, cols], head_gains[0:1, :], normed)
            grad_query[span, cols] = d_query.astype(BF)
            head_terms[0:1, :] += jnp.sum(terms, axis=0, keepdims=True)
        for part, (left, right) in enumerate(((raws, queries), (softs, mixes))):
            cols = slice(part * HD, (part + 1) * HD)
            out = dot_tn(left[...], right[...])
            for d in range(1, hops + 1):
                grad_earlier[d - 1, span, cols] = out[
                    (hops - d) * rows : (hops - d + 1) * rows
                ].astype(BF)
            grad_kv[span, cols] = out[hops * rows :]


def attention_back(
    hops, place, lengths, query, kv_local, earlier, upstream, w_out, gains, head_gains,
    branch, middle, keep, got, query_proj, cosine, sine,
):
    total, width = upstream.shape
    lanes = lengths.shape[0]
    rows = total // lanes
    span = (hops + 1) * rows
    return pl.pallas_call(
        functools.partial(attention_back_kernel, hops),
        out_shape=[
            jax.ShapeDtypeStruct((total, width), F32),
            jax.ShapeDtypeStruct((total, width), BF),
            jax.ShapeDtypeStruct(query.shape, BF),
            jax.ShapeDtypeStruct(kv_local.shape, F32),
            jax.ShapeDtypeStruct(earlier.shape, BF),
            jax.ShapeDtypeStruct((8, width), F32),
            jax.ShapeDtypeStruct((8, HD), F32),
        ],
        in_specs=[SMEM, SMEM] + [VMEM] * 14,
        out_specs=[VMEM] * 7,
        scratch_shapes=[
            pltpu.VMEM((span, 2 * HD), BF),
            pltpu.VMEM((rows, HQ * HD), BF),
            pltpu.VMEM((HQ * rows, span), BF),
            pltpu.VMEM((HQ * rows, span), BF),
            pltpu.VMEM((HQ * rows, HD), BF),
            pltpu.VMEM((HQ * rows, HD), BF),
        ],
        compiler_params=PARAMS,
        cost_estimate=COST,
    )(
        place, lengths, query, kv_local, earlier, upstream, w_out, gains, head_gains,
        branch, middle, keep, got, query_proj, cosine, sine,
    )


def shards(
    tokens,
    cotangent,
    lengths,
    deal_order,
    w_query,
    w_key,
    w_value,
    w_out,
    w_gate,
    w_up,
    w_down,
    norm_gains,
    head_gains,
):
    lanes, rows, width = tokens.shape[1:]
    total = lanes * rows
    seq_count = lax.axis_size("seq")
    cores = lax.axis_size("fsdp")
    own = lax.axis_index("seq")
    core = lax.axis_index("fsdp")
    window = W
    hops = (window - 1 + rows - 1) // rows
    chunk = total // seq_count

    deal = deal_order[0]
    places = jnp.arange(seq_count, dtype=jnp.int32)
    back = jnp.sum(jnp.where(deal[None, :] == places[:, None], places[None, :], 0), axis=1)
    place = deal[own]
    steps = jnp.arange(1, hops + 1, dtype=jnp.int32)
    wanted = deal[:, None] - steps[None, :]
    fetch_table = back[jnp.maximum(wanted, 0)].reshape(-1)
    readers = deal[:, None] + steps[None, :]
    reader_ok = (readers < seq_count).astype(jnp.int32).reshape(-1)
    reader_table = (
        back[jnp.minimum(readers, seq_count - 1)] * hops + (steps[None, :] - 1)
    ).reshape(-1)

    token_rows = tokens.reshape(total, width)
    upstream_rows = cotangent.reshape(total, width)
    q_width = HQ * HD
    narrow = width // cores
    core_ref, own_ref = core.reshape(1), own.reshape(1)

    def core_blocks(block):
        blocks = [block]
        for mask in masks(cores):
            together = jnp.concatenate(blocks, axis=0) if len(blocks) > 1 else blocks[0]
            got = swap(together, "fsdp", mask)
            size = block.shape[0]
            blocks = blocks + [got[j * size : (j + 1) * size] for j in range(len(blocks))]
        return blocks

    def core_sum(keep, send):
        steps = masks(cores)[::-1]
        for mask in steps:
            out = keep + swap(send, "fsdp", mask).astype(F32)
            half = out.shape[0] // 2
            keep, send = out[:half], out[half:].astype(BF)
        return out

    kv_peers = core_blocks(jnp.concatenate([w_key, w_value], axis=1))
    local_stream = place * rows + jnp.arange(rows, dtype=jnp.int32)
    positions = sequence_info(lengths[0], jnp.broadcast_to(local_stream, (lanes, rows)))[1]
    cosine, sine = rope_tables(positions.reshape(total), HD)
    attn_in, key_proj, kv_local = key_value(
        core_ref, token_rows, kv_peers, norm_gains, head_gains, cosine, sine
    )

    spread = lax.all_to_all(
        kv_local.reshape(seq_count, chunk, 2 * HD), "seq", 0, 0, tiled=True
    )
    picked = pick(fetch_table, spread).reshape(seq_count, hops * chunk, 2 * HD)
    arrived = lax.all_to_all(picked, "seq", 0, 0, tiled=True)
    earlier = (
        arrived.reshape(seq_count, hops, chunk, 2 * HD)
        .transpose(1, 0, 2, 3)
        .reshape(hops, total, 2 * HD)
    )

    w_query, w_out = lax.optimization_barrier((w_query, w_out, kv_local))[:2]
    query_peers = core_blocks(w_query)
    size = -(-narrow // 128) * 128
    peers_out = gather_cores(jnp.pad(w_out, ((0, 0), (0, size - narrow))))
    peers_out = flip(peers_out.reshape(cores, q_width, size), core)
    w_out_full = jnp.concatenate([peers_out[j, :, :narrow] for j in range(cores)], axis=1)
    query_proj, query_rot = queries_of(
        core_ref, attn_in, query_peers, head_gains, cosine, sine
    )

    hidden_cols = w_gate.shape[1]
    share = -(-hidden_cols // 256) * 128
    overlap = 2 * share - hidden_cols
    part = ((own & SPLIT_BIT) != 0).astype(jnp.int32)
    part_ref = part.reshape(1)
    if (hidden_cols - share) % 128:
        begin = part * (hidden_cols - share)
        w_gate = lax.dynamic_slice_in_dim(w_gate, begin, share, 1)
        w_up = lax.dynamic_slice_in_dim(w_up, begin, share, 1)
        w_down = lax.dynamic_slice_in_dim(w_down, begin, share, 0)

    earlier = after(earlier, query_rot, w_out_full)
    place_ref, lengths_ref = place.reshape(1), lengths[0]
    mixed_low, branch, middle, ffn_in = attention(
        hops, place_ref, lengths_ref, query_rot, kv_local, earlier, token_rows, w_out_full, norm_gains
    )

    def sum_group(near_part, far_part):
        got = swap(core_sum(*far_part).astype(BF), "seq", SPLIT_BIT)
        return core_sum(*near_part), got

    far_in = swap(ffn_in, "seq", SPLIT_BIT)
    near_all = core_blocks(ffn_in)
    near = ffn_forward(part_ref, near_all, w_gate, w_up, w_down, share, overlap)
    far_all = core_blocks(after(far_in, near[0]))
    far = ffn_forward(part_ref, far_all, w_gate, w_up, w_down, share, overlap)
    keep, got = sum_group(near[3:], far[3:])
    ffn_out = keep + got.astype(F32)
    result = middle + rms_forward(ffn_out, norm_gains[3])

    grad_ffn_out, top_terms = rms_backward(ffn_out, norm_gains[3], upstream_rows.astype(F32))
    top_terms = jnp.sum(top_terms, axis=0)
    grad_low = grad_ffn_out.astype(BF)
    far_grad = swap(grad_low, "seq", SPLIT_BIT)
    near_grads = core_blocks(grad_low)
    near_back = ffn_backward(part_ref, near_grads, near[1], near[2], w_gate, w_up, w_down)
    far_grads = core_blocks(after(far_grad, near_back[0]))
    others = [m for m in masks(seq_count) if m != SPLIT_BIT]
    swapped = [others[1], others[0]] + others[2:]

    def terms_of(left, right, pieces):
        pieces = [(order + [SPLIT_BIT], size) for order, size in pieces]
        return weight_terms(own, seq_count, pieces, left, *right)

    down_terms = terms_of(
        near_grads + far_grads,
        (near[0], far[0]),
        [(others, share)],
    )
    far_grads[0] = after(far_grads[0], *down_terms)
    far_back = ffn_backward(part_ref, far_grads, far[1], far[2], w_gate, w_up, w_down)
    keep, got = sum_group(near_back[2:], far_back[2:])

    gate_terms = terms_of(near_all + far_all, (near_back[0], far_back[0]), [(swapped, share)])
    up_terms = terms_of(
        near_all + far_all, (near_back[1], after(far_back[1], *gate_terms)), [(others, share)]
    )
    down_c = Chain(*down_terms, others)
    gate_c = Chain(*gate_terms, swapped)
    up_c = Chain(*up_terms, others)
    turns = Turns(up_terms[0])

    (
        grad_middle, grad_branch_low, grad_query_low, grad_kv, grad_earlier, norm_terms, head_terms
    ) = attention_back(
        hops, place_ref, lengths_ref, query_rot, kv_local, earlier, upstream_rows, w_out_full,
        norm_gains, head_gains, branch, middle, keep, turns.wait(got), query_proj, cosine, sine,
    )

    outward = (
        grad_earlier.reshape(hops, seq_count, chunk, 2 * HD)
        .transpose(1, 0, 2, 3)
        .reshape(seq_count, hops * chunk, 2 * HD)
    )
    collected = lax.all_to_all(outward, "seq", 0, 0, tiled=True)

    turns.end(outward)
    down_c.step(turns)
    outer_keep, outer_send = outer_begin(
        core_ref, cores, mixed_low, grad_branch_low, turns.wait(grad_query_low), attn_in
    )
    turns.end(outer_send)
    every = swapped + [SPLIT_BIT]
    if cores == 2:
        outer_got = swap(outer_send, "fsdp", 1)
    else:
        outer_keep = core_sum(outer_keep, outer_send)
        outer_got = jnp.zeros(outer_keep.shape, BF)
    gate_c.step(turns)
    attention_terms = outer_end(own_ref, seq_count, every, outer_keep, turns.wait(outer_got))
    turns.end(attention_terms[0])
    outer_c = Chain(*attention_terms, every)
    up_c.step(turns)
    down_c.step(turns)
    summed = pick_sum(
        hops,
        reader_table,
        reader_ok,
        turns.wait(collected).reshape(seq_count * hops, chunk, 2 * HD),
    )
    turns.end(summed)
    returned = lax.all_to_all(summed, "seq", 0, 0, tiled=True)
    gate_c.step(turns)
    down_c.step(turns)
    up_c.step(turns)
    outer_c.step(turns)
    returned = turns.wait(returned)

    grad_inputs, kv_keep, kv_send, in_terms, key_terms = last(
        core_ref, query_peers, kv_peers, token_rows, attn_in, grad_middle, grad_query_low, grad_kv,
        returned.reshape(total, 2 * HD), key_proj, cosine, sine, norm_gains, head_gains,
    )
    kv_terms = core_sum(kv_keep, kv_send).astype(BF)
    size = kv_terms.shape[1]
    kv_rows = HD // seq_count
    kv_terms = (
        kv_terms.reshape(2, seq_count, kv_rows, size)
        .transpose(1, 0, 2, 3)
        .reshape(seq_count, 2 * kv_rows, size)
    )
    gains = jnp.concatenate(
        [in_terms[0], norm_terms[0], norm_terms[1], top_terms, head_terms[0], key_terms[0]]
    )
    for mask in masks(cores):
        gains = gains + swap(gains, "fsdp", mask)
    gain_size = gains.shape[0]
    gain_rows = -(-gain_size // size)
    gains = jnp.pad(gains, (0, gain_rows * size - gain_size)).reshape(gain_rows, size)
    tail = jnp.concatenate(
        [kv_terms, jnp.broadcast_to(gains.astype(BF), (seq_count, gain_rows, size))], axis=1
    )
    ended = lax.all_to_all(tail, "seq", 0, 0, tiled=True)
    turns.end(tail)

    def exchanged(*chains):
        mine = jnp.concatenate([chain.total[1] for chain in chains], axis=1)
        sent = jnp.concatenate([chain.total[0].astype(BF) for chain in chains], axis=1)
        return mine, swap(sent, "seq", SPLIT_BIT)

    gate_c.step(turns)
    outer_c.step(turns)
    up_c.step(turns)
    ffn_mine, ffn_got = exchanged(down_c, gate_c, up_c)
    outer_c.step(turns)

    def own_columns(values):
        return lax.dynamic_slice_in_dim(values, core * narrow % 128, narrow, 1)

    ended = jnp.sum(turns.wait(ended).astype(F32), axis=0)
    key_grad = own_columns(ended[:kv_rows]).T
    value_grad = own_columns(ended[kv_rows : 2 * kv_rows]).T
    gains = ended[2 * kv_rows :].reshape(-1)[:gain_size]

    ffn_got = turns.wait(ffn_got).astype(F32)
    lower = jnp.where(part == 0, ffn_mine, ffn_got)
    upper = jnp.where(part == 0, ffn_got, ffn_mine)
    down_grad, gate_grad, up_grad = (
        jnp.concatenate(
            [
                lower[:, k * share : (k + 1) * share],
                upper[:, k * share + overlap : (k + 1) * share],
            ],
            axis=1,
        )
        for k in range(3)
    )
    down_grad = down_grad.T
    outer_c.step(turns)
    attention_grad = own_columns(outer_c.total[0])
    query_rows = q_width // seq_count
    out_grad = attention_grad[:query_rows]
    query_grad = attention_grad[query_rows:].T

    norm_total = gains[: 4 * width].reshape(4, width)
    head_total = gains[4 * width :].reshape(2, HD)

    return (
        result.reshape(1, lanes, rows, width),
        grad_inputs.reshape(1, lanes, rows, width),
        query_grad,
        key_grad,
        value_grad,
        out_grad,
        gate_grad,
        up_grad,
        down_grad,
        norm_total,
        head_total,
    )


def solution(mesh):
    in_specs = (
        P("fsdp", None, "seq", None),
        P("fsdp", None, "seq", None),
        P("fsdp", None, None),
        P("fsdp", None),
        P("fsdp", None),
        P("fsdp", None),
        P("fsdp", None),
        P(None, "fsdp"),
        P(None, "fsdp"),
        P(None, "fsdp"),
        P("fsdp", None),
        P(),
        P(),
    )
    out_specs = (
        P("fsdp", None, "seq", None),
        P("fsdp", None, "seq", None),
        P("fsdp", "seq"),
        P("fsdp", "seq"),
        P("fsdp", "seq"),
        P("seq", "fsdp"),
        P("seq", "fsdp"),
        P("seq", "fsdp"),
        P("fsdp", "seq"),
        P(),
        P(),
    )
    return jax.shard_map(shards, mesh=mesh, in_specs=in_specs, out_specs=out_specs, check_vma=False)
```

time: 559 us -> 442 us (0.79)
  matrix products: 56.2 us -> 0 us
  other arithmetic: 88.3 us -> 39.5 us
  Pallas kernels: 98.6 us -> 139 us
  local copies, waits for them, and re-layouts: 81.4 us -> 41.7 us
  starting transfers between devices: 62.7 us -> 50.8 us
    dot_general x17 -> x0, matrix products: 53 us -> none  [the longest x1 11.6 us: shards(): jnp.einsum('xzo,xza->xoa', grad_raw, flat_query, preferred_element_type=F32)]
    pallas_call x5 -> x12, Pallas kernels: 66.7 us -> 108 us  [the longest x3 32 us: weight_terms(): pl.pallas_call(functools.partial(weight_kernel, n, pieces), out_shape=[ja...]
    ppermute x38 -> x32, waiting for transfers between devices: 118 us -> 141 us  [swap(): return lax.ppermute(value, axis, [(i, i ^ mask) for i in range(count)])]
    all_to_all x1, waiting for transfers between devices: 22.3 us -> 0.01 us  [shards(): ended = lax.all_to_all(tail, 'seq', 0, 0, tiled=True)]
    select_n x9 -> x1, other arithmetic: 13.2 us -> 0.21 us  [shards(): lower = jnp.where(part == 0, ffn_mine, ffn_got)]
    convert_element_type x11 -> x4, local copies, waits for them, and re-layouts: 13.7 us -> 1.15 us  [the longest x3 1.13 us: exchanged(): chain.total[0].astype(BF)]
    ppermute x38 -> x32, starting transfers between devices: 34.9 us -> 24.4 us  [swap(): return lax.ppermute(value, axis, [(i, i ^ mask) for i in range(count)])]
    unnamed x252 -> x76, local copies, waits for them, and re-layouts: 19.4 us -> 11.6 us
  transfers between devices with their start and end apart: 43 -> 37, of which waited for: 14 -> 16; matrix products, arithmetic and copies ran while one was open for 33% -> 14% of each run, Pallas kernels for 18% -> 23%
where the time goes in v3:
time: 442 us; the launch traced here: 437 us
  waiting for transfers between devices  164 us (37%)
  Pallas kernels  139 us (31%)
  starting transfers between devices  50.8 us (11%)
  local copies, waits for them, and re-layouts  41.7 us (9%)
  other arithmetic  39.5 us (9%)
    ppermute x32, waiting for transfers between devices, swap(): return lax.ppermute(value, axis, [(i, i ^ mask) for i in range(count)])  141 us
    pallas_call x3, Pallas kernels, weight_terms(): pl.pallas_call(functools.partial(weight_kernel, n, pieces), out_shape=[ja...  32 us
    pallas_call x2, Pallas kernels, ffn_backward(): pl.pallas_call(functools.partial(ffn_backward_kernel, n), out_shape=[jax....  30.4 us
    pallas_call x2, Pallas kernels, ffn_forward(): pl.pallas_call(functools.partial(ffn_forward_kernel, n, overlap), out_sha...  28.4 us
    ppermute x32, starting transfers between devices, swap(): return lax.ppermute(value, axis, [(i, i ^ mask) for i in range(count)])  24.4 us
    all_to_all x1, waiting for transfers between devices, shards(): arrived = lax.all_to_all(picked, 'seq', 0, 0, tiled=True)  15.2 us
    pallas_call x1, Pallas kernels, attention_back(): pl.pallas_call(functools.partial(attention_back_kernel, hops), out_shape=...  13.2 us
    unnamed x76, local copies, waits for them, and re-layouts  11.6 us
  transfers between devices with their start and end apart: 37, of which 16 were waited for; matrix products, arithmetic and copies ran while one was open for 14% of the time, Pallas kernels for 23%

profile of v3, /device:TPU:0, one launch (start us, length us, event | category | flops | bytes accessed | tf_op | source)
XLA Modules:
  0.0 436.8 jit_solution(15930706764912188657)
XLA Ops:
  3.2 1.3 fusion.16
  9.0 1.2 multiply_sine_fusion
  11.1 3.0 shard_map.212
  14.1 7.9 %all-to-all-start = ((bf16[16,16,512]{2,1,0:T(8,128)(2,1)}), bf16[16,16,512]{2,1,0:T(8,128)(2,1)S(1)}, u32[]{:S(2)}, u32[]{:S(2)}) async-start(bf16[16,16,512]{2,1,0:T(8,128)(2,1)} %bitcast.94), calls=%async_computation | async-start | bytes 524288 | tf_op jit(solution)/shard_map/all_to_all | solution.py:809
  22.8 1.3 pad_bitcast_fusion
  24.8 7.7 %all-to-all-done = bf16[16,16,512]{2,1,0:T(8,128)(2,1)S(1)} async-done(((bf16[16,16,512]{2,1,0:T(8,128)(2,1)}), bf16[16,16,512]{2,1,0:T(8,128)(2,1)S(1)}, u32[]{:S(2)}, u32[]{:S(2)}) %all-to-all-start) | async-done | bytes 262176 | tf_op jit(solution)/shard_map/all_to_all | solution.py:809
  32.5 1.6 gather_fusion.1
  34.1 2.4 bitcast_select_fusion
  36.5 4.5 %all-to-all-start.1 = ((bf16[16,64,512]{2,1,0:T(8,128)(2,1)}), bf16[16,64,512]{2,1,0:T(8,128)(2,1)}, u32[]{:S(2)}, u32[]{:S(2)}) async-start(bf16[16,64,512]{2,1,0:T(8,128)(2,1)} %bitcast_select_fusion), calls=%async_computation.1 | async-start | bytes 2097152 | tf_op jit(solution)/shard_map/all_to_all | solution.py:813
  41.1 4.1 shard_map.213
  47.1 2.2 pad_maximum_fusion.1.w_out
  49.2 15.2 %all-to-all-done.1 = bf16[16,64,512]{2,1,0:T(8,128)(2,1)} async-done(((bf16[16,64,512]{2,1,0:T(8,128)(2,1)}), bf16[16,64,512]{2,1,0:T(8,128)(2,1)}, u32[]{:S(2)}, u32[]{:S(2)}) %all-to-all-start.1) | async-done | bytes 1048608 | tf_op jit(solution)/shard_map/all_to_all | solution.py:813
  64.4 2.3 copy.29
  66.7 9.2 %shard_map.214 = (bf16[256,1024]{1,0:T(8,128)(2,1)}, f32[256,1152]{1,0:T(8,128)}, f32[256,1152]{1,0:T(8,128)}, bf16[256,1152]{1,0:T(8,128)(2,1)}) custom-call(s32[1]{0:T(128)} %bitcast.place, s32[2,8]{1,0:T(2,128)} %bitcast.99, bf16[256,1024]{1,0:T(8,128)(2,1)} %get-tuple-element.90.query, bf16[256,512]{1,0:T(8,128)(2,1)} %get-tuple-element.88.kv_local, ...), custom_call_target="tpu_custom_call" | custom-call | flops 1024 | bytes 1024 | tf_op jit(solution)/shard_map/pallas_call | solution.py:637
  75.9 3.0 collective-permute-start.5
  79.7 14.4 %shard_map.215 = (bf16[512,1792]{1,0:T(8,128)(2,1)}, bf16[512,1792]{1,0:T(8,128)(2,1)}, bf16[512,1792]{1,0:T(8,128)(2,1)}, f32[256,1152]{1,0:T(8,128)}, bf16[256,1152]{1,0:T(8,128)(2,1)}) custom-call(s32[1]{0:T(128)} %bitcast.19.refs_0_, bf16[256,1152]{1,0:T(8,128)(2,1)} %get-tuple-element.94.refs_1_, bf16[256,1152]{1,0:T(8,128)(2,1)} %copy-done.4, ...), custom_call_target="tpu_custom_call" | custom-call | flops 1024 | bytes 1024 | tf_op jit(solution)/shard_map/pallas_call | solution.py:242
  94.4 1.8 collective-permute-done.6.refs_2_.refs_4_
  97.0 14.0 %shard_map.216 = (bf16[512,1792]{1,0:T(8,128)(2,1)}, bf16[512,1792]{1,0:T(8,128)(2,1)}, bf16[512,1792]{1,0:T(8,128)(2,1)}, f32[256,1152]{1,0:T(8,128)}, bf16[256,1152]{1,0:T(8,128)(2,1)}) custom-call(s32[1]{0:T(128)} %bitcast.19.refs_0_, bf16[256,1152]{1,0:T(8,128)(2,1)} %copy-done.5, bf16[256,1152]{1,0:T(8,128)(2,1)} %copy-done.6, ...), custom_call_target="tpu_custom_call" | custom-call | flops 1024 | bytes 1024 | tf_op jit(solution)/shard_map/pallas_call | solution.py:242
  111.6 1.7 collective-permute-done.7
  113.3 1.4 add_convert_fusion.10
  114.7 2.3 collective-permute-start.8
  117.7 12.9 %collective-permute-done.8 = bf16[256,1152]{1,0:T(8,128)(2,1)S(1)} collective-permute-done((bf16[256,1152]{1,0:T(8,128)(2,1)S(1)}, bf16[256,1152]{1,0:T(8,128)(2,1)S(1)}, u32[]{:S(2)}, u32[]{:S(2)}) %collective-permute-start.8) | collective-permute-done | bytes 589856 | tf_op jit(solution)/shard_map/ppermute | solution.py:24
  132.2 1.5 fusion.3
  133.7 1.7 collective-permute-start.11
  136.5 15.3 %shard_map.217 = (bf16[512,1792]{1,0:T(8,128)(2,1)}, bf16[512,1792]{1,0:T(8,128)(2,1)}, f32[256,1152]{1,0:T(8,128)}, bf16[256,1152]{1,0:T(8,128)(2,1)}) custom-call(s32[1]{0:T(128)} %bitcast.19.refs_0_, bf16[256,1152]{1,0:T(8,128)(2,1)} %copy-done.8, bf16[256,1152]{1,0:T(8,128)(2,1)} %copy-done.20, bf16[512,1792]{1,0:T(8,128)(2,1)} %get-tuple-element.102.refs_3_, ...), custom_call_target="tpu_custom_call" | custom-call | flops 1024 | bytes 1024 | tf_op jit(solution)/shard_map/pallas_call | solution.py:310
  152.0 1.9 collective-permute-done.12.refs_4_.refs_2_
  154.7 10.7 %shard_map.218 = (bf16[8,72,1792]{2,1,0:T(8,128)(2,1)}, bf16[8,72,1792]{2,1,0:T(8,128)(2,1)}) custom-call(s32[1]{0:T(128)} %bitcast.22.refs_0_.own, bf16[256,1152]{1,0:T(8,128)(2,1)} %copy-done.8, bf16[256,1152]{1,0:T(8,128)(2,1)} %copy-done.20, bf16[256,1152]{1,0:T(8,128)(2,1)} %copy-done.19, bf16[256,1152]{1,0:T(8,128)(2,1)} %copy-done.21, ...), custom_call_target="tpu_custom_call" | custom-call | flops 1024 | bytes 1024 | tf_op jit(solution)/shard_map/pallas_call | solution.py:388
  166.0 15.2 %shard_map.219 = (bf16[512,1792]{1,0:T(8,128)(2,1)}, bf16[512,1792]{1,0:T(8,128)(2,1)}, f32[256,1152]{1,0:T(8,128)}, bf16[256,1152]{1,0:T(8,128)(2,1)}) custom-call(s32[1]{0:T(128)} %bitcast.19.refs_0_, bf16[256,1152]{1,0:T(8,128)(2,1)} %copy-done.19, bf16[256,1152]{1,0:T(8,128)(2,1)} %copy-done.21, bf16[512,1792]{1,0:T(8,128)(2,1)} %get-tuple-element.112.refs_3_, ...), custom_call_target="tpu_custom_call" | custom-call | flops 1024 | bytes 1024 | tf_op jit(solution)/shard_map/pallas_call | solution.py:310
  181.8 1.7 collective-permute-done.13
  183.5 1.4 add_convert_fusion.9
  184.8 1.8 collective-permute-start.14
  186.6 10.6 %shard_map.220 = (bf16[8,72,1792]{2,1,0:T(8,128)(2,1)}, bf16[8,72,1792]{2,1,0:T(8,128)(2,1)}) custom-call(s32[1]{0:T(128)} %bitcast.22.refs_0_.own, bf16[256,1152]{1,0:T(8,128)(2,1)} %get-tuple-element.94.refs_1_, bf16[256,1152]{1,0:T(8,128)(2,1)} %copy-done.4, bf16[256,1152]{1,0:T(8,128)(2,1)} %copy-done.5, bf16[256,1152]{1,0:T(8,128)(2,1)} %copy-done.6, ...), custom_call_target="tpu_custom_call" | custom-call | flops 1024 | bytes 1024 | tf_op jit(solution)/shard_map/pallas_call | solution.py:388
  197.3 1.3 collective-permute-start.19
  198.6 10.8 %shard_map.221 = (bf16[8,72,1792]{2,1,0:T(8,128)(2,1)}, bf16[8,72,1792]{2,1,0:T(8,128)(2,1)}) custom-call(s32[1]{0:T(128)} %bitcast.22.refs_0_.own, bf16[256,1152]{1,0:T(8,128)(2,1)} %get-tuple-element.94.refs_1_, bf16[256,1152]{1,0:T(8,128)(2,1)} %copy-done.4, bf16[256,1152]{1,0:T(8,128)(2,1)} %copy-done.5, bf16[256,1152]{1,0:T(8,128)(2,1)} %copy-done.6, ...), custom_call_target="tpu_custom_call" | custom-call | flops 1024 | bytes 1024 | tf_op jit(solution)/shard_map/pallas_call | solution.py:388
  211.4 13.2 %shard_map.222 = (f32[256,1152]{1,0:T(8,128)}, bf16[256,1152]{1,0:T(8,128)(2,1)}, bf16[256,1024]{1,0:T(8,128)(2,1)}, f32[256,512]{1,0:T(8,128)}, bf16[4,256,512]...) custom-call(s32[1]{0:T(128)} %bitcast.place, s32[2,8]{1,0:T(2,128)} %bitcast.100, ...), custom_call_target="tpu_custom_call" | custom-call | flops 1024 | bytes 1024 | tf_op jit(solution)/shard_map/pallas_call | solution.py:711
  224.6 2.4 copy.31
  228.6 6.4 %shard_map.223 = (f32[2048,640]{1,0:T(8,128)}, bf16[2048,640]{1,0:T(8,128)(2,1)}) custom-call(s32[1]{0:T(128)} %bitcast.2.core, bf16[256,1024]{1,0:T(8,128)(2,1)} %get-tuple-element.131.mixed, bf16[256,1152]{1,0:T(8,128)(2,1)} %get-tuple-element.132.branch, bf16[256,1024]{1,0:T(8,128)(2,1)} %get-tuple-element.133.query.refs_7_, ...), custom_call_target="tpu_custom_call" | custom-call | flops 1024 | bytes 1024 | tf_op jit(solution)/shard_map/pallas_call | solution.py:444
  235.0 1.5 collective-permute-start.17
  236.5 4.0 all-to-all-start.2
  242.1 2.1 collective-permute-start.16
  244.2 2.6 collective-permute-done.19
  246.8 2.7 add_convert_fusion.1
  249.5 1.3 copy-done
  251.8 1.5 collective-permute-start.23
  253.3 5.3 %shard_map.224 = (bf16[8,128,640]{2,1,0:T(8,128)(2,1)}, bf16[8,128,640]{2,1,0:T(8,128)(2,1)}) custom-call(s32[1]{0:T(128)} %bitcast.22.refs_0_.own, f32[2048,640]{1,0:T(8,128)} %get-tuple-element.134.keep, bf16[2048,640]{1,0:T(8,128)(2,1)} %collective-permute-done.18.got), custom_call_target="tpu_custom_call" | custom-call | flops 1024 | bytes 1024 | tf_op jit(solution)/shard_map/pallas_call | solution.py:461
  258.7 32.8 %collective-permute-done.17 = bf16[8,72,1792]{2,1,0:T(8,128)(2,1)} collective-permute-done((bf16[8,72,1792]{2,1,0:T(8,128)(2,1)}, bf16[8,72,1792]{2,1,0:T(8,128)(2,1)}, u32[]{:S(2)}, u32[]{:S(2)}) %collective-permute-start.17) | collective-permute-done | bytes 2064416 | tf_op jit(solution)/shard_map/ppermute | solution.py:24
  291.5 2.1 add_convert_fusion
  298.9 2.0 gather_fusion.3
  302.0 4.9 %all-to-all-start.3 = ((bf16[16,16,512]{2,1,0:T(8,128)(2,1)}), bf16[16,16,512]{2,1,0:T(8,128)(2,1)S(1)}, u32[]{:S(2)}, u32[]{:S(2)}) async-start(bf16[16,16,512]{2,1,0:T(8,128)(2,1)} %multiply_reduce_fusion), calls=%async_computation.3 | async-start | bytes 524288 | tf_op jit(solution)/shard_map/all_to_all | solution.py:931
  306.9 10.9 %collective-permute-done.23 = bf16[4,72,1792]{2,1,0:T(8,128)(2,1)} collective-permute-done((bf16[4,72,1792]{2,1,0:T(8,128)(2,1)}, bf16[4,72,1792]{2,1,0:T(8,128)(2,1)}, u32[]{:S(2)}, u32[]{:S(2)}) %collective-permute-start.23) | collective-permute-done | bytes 1032224 | tf_op jit(solution)/shard_map/ppermute | solution.py:24
  317.8 1.5 add_convert_fusion.5
  320.1 1.3 collective-permute-start.25
  321.4 14.2 %collective-permute-done.22 = bf16[2,72,1792]{2,1,0:T(8,128)(2,1)} collective-permute-done((bf16[2,72,1792]{2,1,0:T(8,128)(2,1)}, bf16[2,72,1792]{2,1,0:T(8,128)(2,1)}, u32[]{:S(2)}, u32[]{:S(2)}) %collective-permute-start.22) | collective-permute-done | bytes 516128 | tf_op jit(solution)/shard_map/ppermute | solution.py:24
  337.9 1.6 add_convert_fusion.4
  340.4 1.7 add_convert_fusion.3
  343.7 6.4 %shard_map.225 = (f32[256,1152]{1,0:T(8,128)}, f32[512,640]{1,0:T(8,128)}, bf16[512,640]{1,0:T(8,128)(2,1)}, f32[8,1152]{1,0:T(8,128)}, f32[8,256]{1,0:T(8,128)}) custom-call(s32[1]{0:T(128)} %bitcast.2.core, bf16[576,1024]{1,0:T(8,128)(2,1)} %refs_0_.1, bf16[576,1024]{1,0:T(8,128)(2,1)} %collective-permute-done.1.refs_1_, bf16[576,512]{1,0:T(8,128)(2,1)} %copy-done.16, ...), custom_call_target="tpu_custom_call" | custom-call | flops 1024 | bytes 1024 | tf_op jit(solution)/shard_map/pallas_call | solution.py:566
  353.4 1.6 collective-permute-start.24
  355.0 1.4 add_convert_fusion.8
  357.5 5.1 %all-to-all-start.4 = ((bf16[16,40,640]{2,1,0:T(8,128)(2,1)}), bf16[16,40,640]{2,1,0:T(8,128)(2,1)}, u32[]{:S(2)}, u32[]{:S(2)}) async-start(bf16[16,40,640]{2,1,0:T(8,128)(2,1)} %pad_maximum_fusion.5), calls=%async_computation.4 | async-start | bytes 1638400 | tf_op jit(solution)/shard_map/all_to_all | solution.py:961
  363.8 9.8 %collective-permute-done.24 = bf16[4,128,640]{2,1,0:T(8,128)(2,1)} collective-permute-done((bf16[4,128,640]{2,1,0:T(8,128)(2,1)}, bf16[4,128,640]{2,1,0:T(8,128)(2,1)}, u32[]{:S(2)}, u32[]{:S(2)}) %collective-permute-start.24) | collective-permute-done | bytes 655392 | tf_op jit(solution)/shard_map/ppermute | solution.py:24
  375.5 19.3 %collective-permute-done.29 = bf16[2,72,1792]{2,1,0:T(8,128)(2,1)} collective-permute-done((bf16[2,72,1792]{2,1,0:T(8,128)(2,1)}, bf16[2,72,1792]{2,1,0:T(8,128)(2,1)}, u32[]{:S(2)}, u32[]{:S(2)}) %collective-permute-start.29) | collective-permute-done | bytes 516128 | tf_op jit(solution)/shard_map/ppermute | solution.py:24
  396.2 14.4 %collective-permute-done.28 = bf16[2,128,640]{2,1,0:T(8,128)(2,1)S(1)} collective-permute-done((bf16[2,128,640]{2,1,0:T(8,128)(2,1)S(1)}, bf16[2,128,640]{2,1,0:T(8,128)(2,1)S(1)}, u32[]{:S(2)}, u32[]{:S(2)}) %collective-permute-start.28) | collective-permute-done | bytes 327712 | tf_op jit(solution)/shard_map/ppermute | solution.py:24
  410.9 17.1 %collective-permute-done.30 = bf16[1,128,640]{2,1,0:T(8,128)(2,1)S(1)} collective-permute-done((bf16[1,128,640]{2,1,0:T(8,128)(2,1)S(1)}, bf16[1,128,640]{2,1,0:T(8,128)(2,1)S(1)}, u32[]{:S(2)}, u32[]{:S(2)}) %collective-permute-start.30) | collective-permute-done | bytes 163872 | tf_op jit(solution)/shard_map/ppermute | solution.py:24
  432.4 1.3 convert_reduce_fusion
  (207 shorter events, 53.6 us)
Async XLA Ops:
  2.6 4.2 copy-start.16
  2.6 7.6 %collective-permute-start = (bf16[576,512]{1,0:T(8,128)(2,1)S(1)}, bf16[576,512]{1,0:T(8,128)(2,1)S(1)}, u32[]{:S(2)}, u32[]{:S(2)}) collective-permute-start(bf16[576,512]{1,0:T(8,128)(2,1)S(1)} %constant_dynamic-update-slice_fusion.refs_0_.refs_2_), channel_id=1, source_target_pairs={{0,1},{1,0},{2,3},{3,2},{4,5},{5,4},{6,7},{7,6},{8,9},{9,8},{10,11... | collective-permute-start | bytes 1769480 | tf_op jit(solution)/shard_map/ppermute | solution.py:24
  6.0 1.8 copy-start.31
  8.8 13.3 %copy-start.26 = (bf16[1024,576]{0,1:T(8,128)(2,1)S(1)}, bf16[1024,576]{0,1:T(8,128)(2,1)}, u32[]{:S(2)}) copy-start(bf16[1024,576]{0,1:T(8,128)(2,1)} %param.20) | copy-start | bytes 3538948
  14.1 18.4 %all-to-all-start = ((bf16[16,16,512]{2,1,0:T(8,128)(2,1)}), bf16[16,16,512]{2,1,0:T(8,128)(2,1)S(1)}, u32[]{:S(2)}, u32[]{:S(2)}) async-start(bf16[16,16,512]{2,1,0:T(8,128)(2,1)} %bitcast.94), calls=%async_computation | async-start | bytes 524288 | tf_op jit(solution)/shard_map/all_to_all | solution.py:809
  24.1 21.1 %collective-permute-start.2 = (bf16[1024,640]{1,0:T(8,128)(2,1)S(1)}, bf16[1024,640]{1,0:T(8,128)(2,1)S(1)}, u32[]{:S(2)}, u32[]{:S(2)}) collective-permute-start(bf16[1024,640]{1,0:T(8,128)(2,1)S(1)} %get-tuple-element.180), channel_id=1, source_target_pairs={{0,1},{1,0},{2,3},{3,2},{4,5},{5,4},{6,7},{7,6},{8,9},{9,8},{10,11... | collective-permute-start | bytes 3932168 | tf_op jit(solution)/shard_map/ppermute | solution.py:24
  24.4 16.6 %collective-permute-start.1 = (bf16[576,1024]{1,0:T(8,128)(2,1)}, bf16[576,1024]{1,0:T(8,128)(2,1)}, u32[]{:S(2)}, u32[]{:S(2)}) collective-permute-start(bf16[576,1024]{1,0:T(8,128)(2,1)} %refs_0_.1), channel_id=1, source_target_pairs={{0,1},{1,0},{2,3},{3,2},{4,5},{5,4},{6,7},{7,6},{8,9},{9,8},{10,11... | collective-permute-start | bytes 3538952 | tf_op jit(solution)/shard_map/ppermute | solution.py:24
  36.5 27.9 %all-to-all-start.1 = ((bf16[16,64,512]{2,1,0:T(8,128)(2,1)}), bf16[16,64,512]{2,1,0:T(8,128)(2,1)}, u32[]{:S(2)}, u32[]{:S(2)}) async-start(bf16[16,64,512]{2,1,0:T(8,128)(2,1)} %bitcast_select_fusion), calls=%async_computation.1 | async-start | bytes 2097152 | tf_op jit(solution)/shard_map/all_to_all | solution.py:813
  45.2 1.3 copy-start.9
  75.9 3.0 collective-permute-start.3
  75.9 18.2 %collective-permute-start.5 = (bf16[256,1152]{1,0:T(8,128)(2,1)}, bf16[256,1152]{1,0:T(8,128)(2,1)S(1)}, u32[]{:S(2)}, u32[]{:S(2)}) collective-permute-start(bf16[256,1152]{1,0:T(8,128)(2,1)} %get-tuple-element.94.refs_1_), channel_id=1, source_target_pairs={{0,8},{2,10},{4,12},{6,14},{8,0},{10,2},{12,4},{14,6},{16,24},{18,... | collective-permute-start | bytes 1769480 | tf_op jit(solution)/shard_map/ppermute | solution.py:24
  94.1 2.1 copy-start.5
  94.1 17.2 %copy-start.34 = (bf16[256,1152]{1,0:T(8,128)(2,1)S(1)}, bf16[256,1152]{1,0:T(8,128)(2,1)}, u32[]{:S(2)}) copy-start(bf16[256,1152]{1,0:T(8,128)(2,1)} %get-tuple-element.96) | copy-start | bytes 1769476
  94.1 2.1 collective-permute-start.6
  111.0 19.6 %copy-start.28 = (f32[256,1152]{1,0:T(8,128)S(1)}, f32[256,1152]{1,0:T(8,128)}, u32[]{:S(2)}) copy-start(f32[256,1152]{1,0:T(8,128)} %get-tuple-element.95) | copy-start | bytes 3538948
  111.0 2.3 collective-permute-start.7
  111.3 6.4 %collective-permute-start.4 = (bf16[256,1152]{1,0:T(8,128)(2,1)S(1)}, bf16[256,1152]{1,0:T(8,128)(2,1)S(1)}, u32[]{:S(2)}, u32[]{:S(2)}) collective-permute-start(bf16[256,1152]{1,0:T(8,128)(2,1)S(1)} %copy-done.34), channel_id=1, source_target_pairs={{0,1},{1,0},{2,3},{3,2},{4,5},{5,4},{6,7},{7,6},{8,9},{9,8},{10,11... | collective-permute-start | bytes 1769480 | tf_op jit(solution)/shard_map/ppermute | solution.py:24
  114.7 15.9 %collective-permute-start.8 = (bf16[256,1152]{1,0:T(8,128)(2,1)S(1)}, bf16[256,1152]{1,0:T(8,128)(2,1)S(1)}, u32[]{:S(2)}, u32[]{:S(2)}) collective-permute-start(bf16[256,1152]{1,0:T(8,128)(2,1)S(1)} %add_convert_fusion.10), channel_id=1, source_target_pairs={{0,8},{2,10},{4,12},{6,14},{8,0},{10,2},{12,4},{14,6},{16,24},{18,... | collective-permute-start | bytes 1769480 | tf_op jit(solution)/shard_map/ppermute | solution.py:24
  130.6 1.1 copy-start.7
  130.9 1.3 copy-start.10
  133.7 2.0 copy-start.8
  133.7 2.0 collective-permute-start.9
  133.7 18.1 %collective-permute-start.11 = (bf16[256,1152]{1,0:T(8,128)(2,1)S(1)}, bf16[256,1152]{1,0:T(8,128)(2,1)S(1)}, u32[]{:S(2)}, u32[]{:S(2)}) collective-permute-start(bf16[256,1152]{1,0:T(8,128)(2,1)S(1)} %get-tuple-element.181.refs_1_), channel_id=1, source_target_pairs={{0,8},{2,10},{4,12},{6,14},{8,0},{10,2},{12,4},{14,6},{16,24},{18,... | collective-permute-start | bytes 1769480 | tf_op jit(solution)/shard_map/ppermute | solution.py:24
  151.8 2.1 copy-start.19
  151.8 2.1 collective-permute-start.12
  165.4 61.6 %collective-permute-start.15 = (bf16[8,72,1792]{2,1,0:T(8,128)(2,1)}, bf16[8,72,1792]{2,1,0:T(8,128)(2,1)S(1)}, u32[]{:S(2)}, u32[]{:S(2)}) collective-permute-start(bf16[8,72,1792]{2,1,0:T(8,128)(2,1)} %get-tuple-element.109), channel_id=1, source_target_pairs={{0,2},{2,0},{4,6},{6,4},{8,10},{10,8},{12,14},{14,12},{16,18},{18,... | collective-permute-start | bytes 6193160 | tf_op jit(solution)/shard_map/ppermute | solution.py:24
  166.0 15.3 %copy-start.33 = (bf16[256,1152]{1,0:T(8,128)(2,1)S(1)}, bf16[256,1152]{1,0:T(8,128)(2,1)}, u32[]{:S(2)}) copy-start(bf16[256,1152]{1,0:T(8,128)(2,1)} %get-tuple-element.105) | copy-start | bytes 1769476
  181.2 2.3 collective-permute-start.13
  181.3 28.1 %collective-permute-start.10 = (bf16[256,1152]{1,0:T(8,128)(2,1)S(1)}, bf16[256,1152]{1,0:T(8,128)(2,1)S(1)}, u32[]{:S(2)}, u32[]{:S(2)}) collective-permute-start(bf16[256,1152]{1,0:T(8,128)(2,1)S(1)} %copy-done.33), channel_id=1, source_target_pairs={{0,1},{1,0},{2,3},{3,2},{4,5},{5,4},{6,7},{7,6},{8,9},{9,8},{10,11... | collective-permute-start | bytes 1769480 | tf_op jit(solution)/shard_map/ppermute | solution.py:24
  184.8 25.7 %collective-permute-start.14 = (bf16[256,1152]{1,0:T(8,128)(2,1)S(1)}, bf16[256,1152]{1,0:T(8,128)(2,1)S(1)}, u32[]{:S(2)}, u32[]{:S(2)}) collective-permute-start(bf16[256,1152]{1,0:T(8,128)(2,1)S(1)} %add_convert_fusion.9), channel_id=1, source_target_pairs={{0,8},{2,10},{4,12},{6,14},{8,0},{10,2},{12,4},{14,6},{16,24},{18,... | collective-permute-start | bytes 1769480 | tf_op jit(solution)/shard_map/ppermute | solution.py:24
  197.3 49.5 %collective-permute-start.19 = (bf16[8,72,1792]{2,1,0:T(8,128)(2,1)}, bf16[8,72,1792]{2,1,0:T(8,128)(2,1)}, u32[]{:S(2)}, u32[]{:S(2)}) collective-permute-start(bf16[8,72,1792]{2,1,0:T(8,128)(2,1)} %get-tuple-element.119), channel_id=1, source_target_pairs={{0,4},{2,6},{4,0},{6,2},{8,12},{10,14},{12,8},{14,10},{16,20},{18,... | collective-permute-start | bytes 6193160 | tf_op jit(solution)/shard_map/ppermute | solution.py:24
  198.6 10.8 %copy-start.27 = (f32[256,1152]{1,0:T(8,128)S(1)}, f32[256,1152]{1,0:T(8,128)}, u32[]{:S(2)}) copy-start(f32[256,1152]{1,0:T(8,128)} %get-tuple-element.104) | copy-start | bytes 3538948
  224.6 2.4 copy-start.23
  235.0 5.5 %copy-start.32 = (s32[1,16]{1,0:T(1,128)S(1)}, s32[1,16]{1,0:T(1,128)}, u32[]{:S(2)}) copy-start(s32[1,16]{1,0:T(1,128)} %param.16) | copy-start | bytes 196
  235.0 18.3 %collective-permute-start.18 = (bf16[2048,640]{1,0:T(8,128)(2,1)}, bf16[2048,640]{1,0:T(8,128)(2,1)}, u32[]{:S(2)}, u32[]{:S(2)}) collective-permute-start(bf16[2048,640]{1,0:T(8,128)(2,1)} %get-tuple-element.135), channel_id=1, source_target_pairs={{0,1},{1,0},{2,3},{3,2},{4,5},{5,4},{6,7},{7,6},{8,9},{9,8},{10,11... | collective-permute-start | bytes 7864328 | tf_op jit(solution)/shard_map/ppermute | solution.py:24
  235.0 56.5 %collective-permute-start.17 = (bf16[8,72,1792]{2,1,0:T(8,128)(2,1)}, bf16[8,72,1792]{2,1,0:T(8,128)(2,1)}, u32[]{:S(2)}, u32[]{:S(2)}) collective-permute-start(bf16[8,72,1792]{2,1,0:T(8,128)(2,1)} %get-tuple-element.122), channel_id=1, source_target_pairs={{0,2},{2,0},{4,6},{6,4},{8,10},{10,8},{12,14},{14,12},{16,18},{18,... | collective-permute-start | bytes 6193160 | tf_op jit(solution)/shard_map/ppermute | solution.py:24
  236.5 61.4 %all-to-all-start.2 = ((bf16[16,64,512]{2,1,0:T(8,128)(2,1)}), bf16[16,64,512]{2,1,0:T(8,128)(2,1)S(1)}, u32[]{:S(2)}, u32[]{:S(2)}) async-start(bf16[16,64,512]{2,1,0:T(8,128)(2,1)} %bitcast.91), calls=%async_computation.2 | async-start | bytes 2097152 | tf_op jit(solution)/shard_map/all_to_all | solution.py:904
  242.1 53.3 %collective-permute-start.16 = (bf16[4,72,1792]{2,1,0:T(8,128)(2,1)}, bf16[4,72,1792]{2,1,0:T(8,128)(2,1)S(1)}, u32[]{:S(2)}, u32[]{:S(2)}) collective-permute-start(bf16[4,72,1792]{2,1,0:T(8,128)(2,1)} %slice.235), channel_id=1, source_target_pairs={{0,4},{2,6},{4,0},{6,2},{8,12},{10,14},{12,8},{14,10},{16,20},{18,... | collective-permute-start | bytes 3096584 | tf_op jit(solution)/shard_map/ppermute | solution.py:24
  249.5 1.3 copy-start
  251.8 66.0 %collective-permute-start.23 = (bf16[4,72,1792]{2,1,0:T(8,128)(2,1)}, bf16[4,72,1792]{2,1,0:T(8,128)(2,1)}, u32[]{:S(2)}, u32[]{:S(2)}) collective-permute-start(bf16[4,72,1792]{2,1,0:T(8,128)(2,1)} %slice.236), channel_id=1, source_target_pairs={{0,2},{2,0},{4,6},{6,4},{8,10},{10,8},{12,14},{14,12},{16,18},{18,... | collective-permute-start | bytes 3096584 | tf_op jit(solution)/shard_map/ppermute | solution.py:24
  253.3 38.2 %copy-start.22 = (bf16[8,72,1792]{2,1,0:T(8,128)(2,1)S(1)}, bf16[8,72,1792]{2,1,0:T(8,128)(2,1)}, u32[]{:S(2)}) copy-start(bf16[8,72,1792]{2,1,0:T(8,128)(2,1)} %get-tuple-element.130) | copy-start | bytes 6193156
  258.7 81.7 %collective-permute-start.20 = (bf16[8,128,640]{2,1,0:T(8,128)(2,1)}, bf16[8,128,640]{2,1,0:T(8,128)(2,1)}, u32[]{:S(2)}, u32[]{:S(2)}) collective-permute-start(bf16[8,128,640]{2,1,0:T(8,128)(2,1)} %get-tuple-element.138), channel_id=1, source_target_pairs={{0,4},{2,6},{4,0},{6,2},{8,12},{10,14},{12,8},{14,10},{16,20},{18,... | collective-permute-start | bytes 3932168 | tf_op jit(solution)/shard_map/ppermute | solution.py:24
  293.6 2.1 copy-start.2
  294.7 43.2 %collective-permute-start.21 = (bf16[4,72,1792]{2,1,0:T(8,128)(2,1)}, bf16[4,72,1792]{2,1,0:T(8,128)(2,1)}, u32[]{:S(2)}, u32[]{:S(2)}) collective-permute-start(bf16[4,72,1792]{2,1,0:T(8,128)(2,1)} %slice.237), channel_id=1, source_target_pairs={{0,4},{2,6},{4,0},{6,2},{8,12},{10,14},{12,8},{14,10},{16,20},{18,... | collective-permute-start | bytes 3096584 | tf_op jit(solution)/shard_map/ppermute | solution.py:24
  295.7 1.2 copy-start.14
  296.9 38.7 %collective-permute-start.22 = (bf16[2,72,1792]{2,1,0:T(8,128)(2,1)}, bf16[2,72,1792]{2,1,0:T(8,128)(2,1)}, u32[]{:S(2)}, u32[]{:S(2)}) collective-permute-start(bf16[2,72,1792]{2,1,0:T(8,128)(2,1)} %slice.238), channel_id=1, source_target_pairs={{0,16},{2,18},{4,20},{6,22},{8,24},{10,26},{12,28},{14,30},{16,0},... | collective-permute-start | bytes 1548296 | tf_op jit(solution)/shard_map/ppermute | solution.py:24
  298.9 18.9 %copy-start.1 = (bf16[8,72,1792]{2,1,0:T(8,128)(2,1)S(1)}, bf16[8,72,1792]{2,1,0:T(8,128)(2,1)}, u32[]{:S(2)}) copy-start(bf16[8,72,1792]{2,1,0:T(8,128)(2,1)} %copy-done) | copy-start | bytes 6193156
  302.0 41.0 %all-to-all-start.3 = ((bf16[16,16,512]{2,1,0:T(8,128)(2,1)}), bf16[16,16,512]{2,1,0:T(8,128)(2,1)S(1)}, u32[]{:S(2)}, u32[]{:S(2)}) async-start(bf16[16,16,512]{2,1,0:T(8,128)(2,1)} %multiply_reduce_fusion), calls=%async_computation.3 | async-start | bytes 524288 | tf_op jit(solution)/shard_map/all_to_all | solution.py:931
  306.9 28.7 %copy-start.15 = (bf16[4,72,1792]{2,1,0:T(8,128)(2,1)S(1)}, bf16[4,72,1792]{2,1,0:T(8,128)(2,1)}, u32[]{:S(2)}) copy-start(bf16[4,72,1792]{2,1,0:T(8,128)(2,1)} %copy-done.14) | copy-start | bytes 3096580
  320.1 17.8 %copy-start.3 = (bf16[8,72,1792]{2,1,0:T(8,128)(2,1)S(1)}, bf16[8,72,1792]{2,1,0:T(8,128)(2,1)}, u32[]{:S(2)}) copy-start(bf16[8,72,1792]{2,1,0:T(8,128)(2,1)} %copy-done.2) | copy-start | bytes 6193156
  320.1 42.5 %collective-permute-start.25 = (bf16[2,72,1792]{2,1,0:T(8,128)(2,1)}, bf16[2,72,1792]{2,1,0:T(8,128)(2,1)}, u32[]{:S(2)}, u32[]{:S(2)}) collective-permute-start(bf16[2,72,1792]{2,1,0:T(8,128)(2,1)} %slice.242), channel_id=1, source_target_pairs={{0,16},{2,18},{4,20},{6,22},{8,24},{10,26},{12,28},{14,30},{16,0},... | collective-permute-start | bytes 1548296 | tf_op jit(solution)/shard_map/ppermute | solution.py:24
  336.8 1.1 copy-start.17
  337.9 2.5 copy-start.25
  339.5 2.6 copy-start.12
  351.7 3.3 collective-permute-start.27
  351.7 3.2 collective-permute-start.26
  353.3 41.5 %collective-permute-start.29 = (bf16[2,72,1792]{2,1,0:T(8,128)(2,1)}, bf16[2,72,1792]{2,1,0:T(8,128)(2,1)}, u32[]{:S(2)}, u32[]{:S(2)}) collective-permute-start(bf16[2,72,1792]{2,1,0:T(8,128)(2,1)} %slice.243), channel_id=1, source_target_pairs={{0,16},{2,18},{4,20},{6,22},{8,24},{10,26},{12,28},{14,30},{16,0},... | collective-permute-start | bytes 1548296 | tf_op jit(solution)/shard_map/ppermute | solution.py:24
  353.4 20.2 %collective-permute-start.24 = (bf16[4,128,640]{2,1,0:T(8,128)(2,1)}, bf16[4,128,640]{2,1,0:T(8,128)(2,1)}, u32[]{:S(2)}, u32[]{:S(2)}) collective-permute-start(bf16[4,128,640]{2,1,0:T(8,128)(2,1)} %slice.244), channel_id=1, source_target_pairs={{0,2},{2,0},{4,6},{6,4},{8,10},{10,8},{12,14},{14,12},{16,18},{18,... | collective-permute-start | bytes 1966088 | tf_op jit(solution)/shard_map/ppermute | solution.py:24
  357.5 74.9 %all-to-all-start.4 = ((bf16[16,40,640]{2,1,0:T(8,128)(2,1)}), bf16[16,40,640]{2,1,0:T(8,128)(2,1)}, u32[]{:S(2)}, u32[]{:S(2)}) async-start(bf16[16,40,640]{2,1,0:T(8,128)(2,1)} %pad_maximum_fusion.5), calls=%async_computation.4 | async-start | bytes 1638400 | tf_op jit(solution)/shard_map/all_to_all | solution.py:961
  363.8 31.1 %copy-start.13 = (bf16[4,72,1792]{2,1,0:T(8,128)(2,1)S(1)}, bf16[4,72,1792]{2,1,0:T(8,128)(2,1)}, u32[]{:S(2)}) copy-start(bf16[4,72,1792]{2,1,0:T(8,128)(2,1)} %copy-done.12) | copy-start | bytes 3096580
  374.8 35.8 %collective-permute-start.28 = (bf16[2,128,640]{2,1,0:T(8,128)(2,1)S(1)}, bf16[2,128,640]{2,1,0:T(8,128)(2,1)S(1)}, u32[]{:S(2)}, u32[]{:S(2)}) collective-permute-start(bf16[2,128,640]{2,1,0:T(8,128)(2,1)S(1)} %slice.248), channel_id=1, source_target_pairs={{0,16},{2,18},{4,20},{6,22},{8,24},{10,26},{12,28},{14,30},{16,0},... | collective-permute-start | bytes 983048 | tf_op jit(solution)/shard_map/ppermute | solution.py:24
  396.1 32.8 %collective-permute-start.31 = (bf16[72,5376]{1,0:T(8,128)(2,1)S(1)}, bf16[72,5376]{1,0:T(8,128)(2,1)S(1)}, u32[]{:S(2)}, u32[]{:S(2)}) collective-permute-start(bf16[72,5376]{1,0:T(8,128)(2,1)S(1)} %pad_maximum_fusion.6), channel_id=1, source_target_pairs={{0,8},{2,10},{4,12},{6,14},{8,0},{10,2},{12,4},{14,6},{16,24},{18,... | collective-permute-start | bytes 2322440 | tf_op jit(solution)/shard_map/ppermute | solution.py:24
  410.7 18.2 %copy-start.24 = (f32[72,1792]{1,0:T(8,128)S(1)}, f32[72,1792]{1,0:T(8,128)}, u32[]{:S(2)}) copy-start(f32[72,1792]{1,0:T(8,128)} %slice_bitcast_fusion.4) | copy-start | bytes 1548292
  410.8 17.3 %collective-permute-start.30 = (bf16[1,128,640]{2,1,0:T(8,128)(2,1)S(1)}, bf16[1,128,640]{2,1,0:T(8,128)(2,1)S(1)}, u32[]{:S(2)}, u32[]{:S(2)}) collective-permute-start(bf16[1,128,640]{2,1,0:T(8,128)(2,1)S(1)} %get-tuple-element.186), channel_id=1, source_target_pairs={{0,8},{2,10},{4,12},{6,14},{8,0},{10,2},{12,4},{14,6},{16,24},{18,... | collective-permute-start | bytes 491528 | tf_op jit(solution)/shard_map/ppermute | solution.py:24
  (8 other events, 6.7 us)

commit v4 on v3

--- a/solution.py
+++ b/solution.py
@@ -113,13 +113,30 @@
 
 
 def pick(table, source):
-    return jnp.take(source, table, axis=0)
+    return jnp.take(source, table, axis=0, mode="clip")
 
 
 def pick_sum(hops, table, valid, source):
-    terms = jnp.take(source, table, axis=0).astype(F32) * valid.astype(F32)[:, None, None]
+    terms = jnp.take(source, table, axis=0, mode="clip").astype(F32) * valid.astype(F32)[:, None, None]
     count = table.shape[0] // hops
     return jnp.sum(terms.reshape((count, hops) + source.shape[1:]), axis=1).astype(source.dtype)
+
+
+QUAD = 4
+
+
+def quads(count):
+    return [[base + q for q in range(QUAD)] for base in range(0, count, QUAD)]
+
+
+def quad_arrangement(order):
+    return [(q, j) for q in range(QUAD) for j in arrangement(order)]
+
+
+def places_of(order, quad):
+    if quad:
+        return [lambda me, q=q, j=j: ((me & ~(QUAD - 1)) ^ j) + q for q, j in quad_arrangement(order)]
+    return [lambda me, j=j: me ^ j for j in arrangement(order)]
 
 
 def arrangement(order):
@@ -144,6 +161,48 @@
         self.token = token
 
 
+def step_kernel(rest, got, *outs):
+    count = rest.shape[0]
+    for k in range(count):
+        total = rest[k].astype(F32) + got[k].astype(F32)
+        top, row = divmod(k, outs[0].shape[0])
+        outs[top][row] = total.astype(outs[top].dtype)
+
+
+def step_of(rest, got, final):
+    count = rest.shape[0]
+    parts, kind = (1, F32) if final else (2, BF)
+    shape = jax.ShapeDtypeStruct((count // parts,) + rest.shape[1:], kind)
+    return pl.pallas_call(
+        step_kernel,
+        out_shape=[shape] * parts,
+        in_specs=[VMEM] * 2,
+        out_specs=[VMEM] * parts,
+        compiler_params=PARAMS,
+        cost_estimate=COST,
+    )(rest, got)
+
+
+def quad_kernel(got, *outs):
+    count = got.shape[0] // QUAD
+    for k in range(count):
+        total = sum(got[q * count + k].astype(F32) for q in range(QUAD))
+        top, row = divmod(k, outs[0].shape[0])
+        outs[top][row] = total.astype(BF)
+
+
+def quad_sum(got):
+    shape = jax.ShapeDtypeStruct((got.shape[0] // QUAD // 2,) + got.shape[1:], BF)
+    return pl.pallas_call(
+        quad_kernel,
+        out_shape=[shape] * 2,
+        in_specs=[VMEM],
+        out_specs=[VMEM] * 2,
+        compiler_params=PARAMS,
+        cost_estimate=COST,
+    )(got)
+
+
 class Chain:
     def __init__(self, first, rest, order):
         self.rest, self.order = rest, list(order)
@@ -151,14 +210,13 @@
 
     def step(self, turns):
         got = turns.wait(self.got)
-        self.total = self.rest.astype(F32) + got.astype(F32)
-        half = self.total.shape[0] // 2
         self.order.pop(0)
         if self.order:
-            first, self.rest = self.total[:half].astype(BF), self.total[half:].astype(BF)
+            first, self.rest = step_of(self.rest, got, False)
             self.got = swap(first, "seq", self.order[0])
             turns.end(first)
         else:
+            (self.total,) = step_of(self.rest, got, True)
             turns.end(self.total)
 
 
@@ -350,8 +408,8 @@
         turned[:, j * rows : (j + 1) * rows] = left[j][...].T
     me = own[0]
     begin = 0
-    for p, (order, size) in enumerate(pieces):
-        halves = outs[2 * p : 2 * p + 2]
+    for order, size, quad in pieces:
+        halves, outs = (outs[:1], outs[1:]) if quad else (outs[:2], outs[2:])
         block = halves[0].shape[1]
 
         @pl.loop(0, size // tile)
@@ -361,8 +419,8 @@
             for copy in copies(begin // tile + i):
                 copy.wait()
             out[...] = dot(turned[...], right[:, cols])
-            for k, j in enumerate(arrangement(order)):
-                source = pl.multiple_of((me ^ j) * block, 8)
+            for k, owner in enumerate(places_of(order, quad)):
+                source = pl.multiple_of(owner(me) * block, 8)
                 top, k = divmod(k, halves[0].shape[0])
                 halves[top][k, :, into] = out[pl.ds(source, block), :].astype(BF)
 
@@ -378,20 +436,23 @@
         full = dot_tn(jnp.concatenate(left), jnp.concatenate([near, far])).astype(BF)
         full = full.reshape(seq_count, block, share)
         outs, begin = [], 0
-        for order, size in pieces:
+        for order, size, quad in pieces:
             piece = full[:, :, begin : begin + size]
-            piece = jnp.take(piece, own ^ jnp.array(arrangement(order), jnp.int32), axis=0)
-            outs += [piece[:half], piece[half:]]
+            owners = jnp.stack([owner(own) for owner in places_of(order, quad)])
+            piece = jnp.take(piece, owners, axis=0, mode="clip")
+            outs += [piece] if quad else [piece[:half], piece[half:]]
             begin += size
         return outs
     tile, _ = tiles(share)
     return pl.pallas_call(
         functools.partial(weight_kernel, n, pieces),
         out_shape=[
-            jax.ShapeDtypeStruct((half, block, size), BF) for _, size in pieces for _ in range(2)
+            jax.ShapeDtypeStruct((seq_count if quad else half, block, size), BF)
+            for _, size, quad in pieces
+            for _ in range(1 if quad else 2)
         ],
         in_specs=[SMEM] + [VMEM] * n + [ANY] * 2,
-        out_specs=[VMEM] * (2 * len(pieces)),
+        out_specs=[VMEM] * sum(1 if quad else 2 for _, _, quad in pieces),
         scratch_shapes=[
             pltpu.VMEM((width, n * left[0].shape[0]), BF),
             pltpu.VMEM((width, tile), F32),
@@ -427,15 +488,17 @@
 
 def outer_sum_kernel(order, own, keep, got, first, rest):
     me = own[0]
-    half, two, _ = first.shape
-    block = two // 2
+    half, padded, two = first.shape
+    size = two // 2
     width = keep.shape[0] // 2
+    block = width // (2 * half)
     for k, j in enumerate(arrangement(order)):
         target = first if k < half else rest
         for part in range(2):
             source = pl.ds(pl.multiple_of(part * width + (me ^ j) * block, 16), block)
             total = keep[source, :] + got[source, :].astype(F32)
-            target[k % half, part * block : (part + 1) * block, :] = total.astype(BF)
+            total = jnp.concatenate([total, jnp.zeros((padded - block, size), F32)], axis=0)
+            target[k % half, :, part * size : (part + 1) * size] = total.astype(BF)
 
 
 def outer_begin(core, cores, mixed, branch, query, attn_in):
@@ -454,18 +517,64 @@
     )(core, mixed, branch, query, attn_in)
 
 
-def outer_end(own, seq_count, order, keep, got):
+def outer_end(own, seq_count, order, keep, got, padded):
     total, size = keep.shape
-    block = total // 2 // seq_count
     half = seq_count // 2
     return pl.pallas_call(
         functools.partial(outer_sum_kernel, order),
-        out_shape=[jax.ShapeDtypeStruct((half, 2 * block, size), BF)] * 2,
+        out_shape=[jax.ShapeDtypeStruct((half, padded, 2 * size), BF)] * 2,
         in_specs=[SMEM, VMEM, VMEM],
         out_specs=[VMEM] * 2,
         compiler_params=PARAMS,
         cost_estimate=COST,
     )(own, keep, got)
+
+
+def outer_pair_kernel(
+    order, own, core, mixed, mixed_peer, branch, query, late, attn_in, attn_peer,
+    first, rest, left, right, total,
+):
+    me = own[0]
+    half, padded, two = first.shape
+    size = two // 2
+    rows, width = mixed.shape
+    block = width // (2 * half)
+    window = window_of(core[0], branch.shape[1] // 2, size)
+    for part, (mine, peer, other, other_peer) in enumerate(
+        (
+            (mixed, mixed_peer, branch, late[:, width:]),
+            (query, late.at[:, :width], attn_in, attn_peer[...]),
+        )
+    ):
+        left[:rows, :] = mine[...]
+        left[rows:, :] = peer[...]
+        right[:rows, :] = other[:, window]
+        right[rows:, :] = other_peer
+        total[part] = dot_tn(left[...], right[...])
+        for k, j in enumerate(arrangement(order)):
+            target = first if k < half else rest
+            value = total[part, pl.ds(pl.multiple_of((me ^ j) * block, 16), block), :]
+            value = jnp.concatenate([value, jnp.zeros((padded - block, size), F32)], axis=0)
+            target[k % half, :, part * size : (part + 1) * size] = value.astype(BF)
+
+
+def outer_pair(own, core, seq_count, order, padded, mixed, *rest):
+    rows, width = mixed.shape
+    size = rest[-1].shape[1]
+    half = seq_count // 2
+    return pl.pallas_call(
+        functools.partial(outer_pair_kernel, order),
+        out_shape=[jax.ShapeDtypeStruct((half, padded, 2 * size), BF)] * 2,
+        in_specs=[SMEM, SMEM] + [VMEM] * (1 + len(rest)),
+        out_specs=[VMEM] * 2,
+        scratch_shapes=[
+            pltpu.VMEM((2 * rows, width), BF),
+            pltpu.VMEM((2 * rows, size), BF),
+            pltpu.VMEM((2, width, size), F32),
+        ],
+        compiler_params=PARAMS,
+        cost_estimate=COST,
+    )(own, core, mixed, *rest)
 
 
 def whole_rows(core, peers, full):
@@ -532,18 +641,25 @@
     )(core, attn_in, *peers, head_gains, cosine, sine)
 
 
+GAIN_ROWS = 16
+
+
+def gain_starts(width, size):
+    return [min(start, width - size) for start in range(0, width, size)]
+
+
 def last_kernel(n, core, *refs):
     q_peers, kv_peers = refs[:n], refs[n : 2 * n]
     (
         tokens, attn_in, grad_middle, grad_query, grad_kv, returned, key_proj, cosine, sine,
-        gains, head_gains, grad_inputs, keep, send, in_terms, key_terms, q_full, kv_full,
+        gains, head_gains, norm_terms, head_terms, top_terms,
+        grad_inputs, keep, send, gain_terms, q_full, kv_full,
     ) = refs[2 * n :]
     whole_rows(core, q_peers, q_full)
     whole_rows(core, kv_peers, kv_full)
     grads = grad_kv[...] + returned[...].astype(F32)
     normed = rotate(grads[:, :HD], cosine[...], -sine[...])
-    d_key, terms = rms_backward(key_proj[...], head_gains[1:2, :], normed)
-    key_terms[...] = jnp.broadcast_to(jnp.sum(terms, axis=0, keepdims=True), key_terms.shape)
+    d_key, key_terms = rms_backward(key_proj[...], head_gains[1:2, :], normed)
     low = jnp.concatenate([d_key.astype(BF), grads[:, HD:].astype(BF)], axis=1)
     size = keep.shape[1]
     narrow = attn_in.shape[1] // n
@@ -554,9 +670,14 @@
         row = row * 2 * HD
         target[row : row + 2 * HD, :] = out.astype(target.dtype)
     d_in = dot_nt(grad_query[...], q_full[...]) + dot_nt(low, kv_full[...])
-    d_tokens, terms = rms_backward(tokens[...].astype(F32), gains[0:1, :], d_in)
-    in_terms[...] = jnp.broadcast_to(jnp.sum(terms, axis=0, keepdims=True), in_terms.shape)
+    d_tokens, in_terms = rms_backward(tokens[...].astype(F32), gains[0:1, :], d_in)
     grad_inputs[...] = grad_middle[...] + d_tokens
+    gain_terms[...] = jnp.zeros_like(gain_terms)
+    gain_terms[0:1, :] = jnp.sum(in_terms, axis=0, keepdims=True)
+    gain_terms[1:3, :] = norm_terms[0:2, :]
+    gain_terms[3:4, :] = top_terms[...]
+    gain_terms[4:5, :HD] = head_terms[0:1, :]
+    gain_terms[5:6, :HD] = jnp.sum(key_terms, axis=0, keepdims=True)
 
 
 def last(core, q_peers, kv_peers, *rest):
@@ -569,25 +690,135 @@
             jax.ShapeDtypeStruct((total, width), F32),
             jax.ShapeDtypeStruct((n * HD, size), F32),
             jax.ShapeDtypeStruct((n * HD, size), BF),
-            jax.ShapeDtypeStruct((8, width), F32),
-            jax.ShapeDtypeStruct((8, HD), F32),
+            jax.ShapeDtypeStruct((GAIN_ROWS, width), F32),
         ],
         in_specs=[SMEM] + [VMEM] * (2 * n + len(rest)),
-        out_specs=[VMEM] * 5,
+        out_specs=[VMEM] * 4,
         scratch_shapes=[pltpu.VMEM((width, HQ * HD), BF), pltpu.VMEM((width, 2 * HD), BF)],
         compiler_params=PARAMS,
         cost_estimate=COST,
     )(core, *q_peers, *kv_peers, *rest)
 
 
+def tail_kernel(order, count, own, keep, got, gains, gains_got, out):
+    me = own[0]
+    size = keep.shape[1]
+    block = keep.shape[0] // 2 // count
+    places = places_of(order, True)
+    part = len(places) // QUAD
+    starts = gain_starts(gains.shape[1], size)
+    rows = part * 2 * block + len(starts) * GAIN_ROWS
+    summed = (gains[...] + gains_got[...]).astype(BF)
+    for k, owner in enumerate(places):
+        q, k = divmod(k, part)
+        for half in range(2):
+            source = pl.ds(pl.multiple_of((half * count + owner(me)) * block, 16), block)
+            row = q * rows + (2 * k + half) * block
+            out[row : row + block, :] = (keep[source, :] + got[source, :].astype(F32)).astype(BF)
+    for q in range(QUAD):
+        row = (q + 1) * rows - len(starts) * GAIN_ROWS
+        for k, start in enumerate(starts):
+            at = row + k * GAIN_ROWS
+            out[at : at + GAIN_ROWS, :] = summed[:, start : start + size]
+
+
+def tail_begin(own, order, count, keep, got, gains, gains_got):
+    rows, size = keep.shape
+    extra = len(gain_starts(gains.shape[1], size)) * GAIN_ROWS
+    return pl.pallas_call(
+        functools.partial(tail_kernel, order, count),
+        out_shape=jax.ShapeDtypeStruct((rows + QUAD * extra, size), BF),
+        in_specs=[SMEM] + [VMEM] * 4,
+        out_specs=VMEM,
+        compiler_params=PARAMS,
+        cost_estimate=COST,
+    )(own, keep, got, gains, gains_got)
+
+
+def tail_step_kernel(ways, extra, final, *refs):
+    parts, outs = refs[:ways], refs[ways:]
+    total = sum(part[...].astype(F32) for part in parts)
+    if final:
+        outs[0][...] = total
+        return
+    low = total.astype(BF)
+    body = low.shape[0] - extra
+    half = body // 2
+    send, keep = outs
+    send[:half, :] = low[:half]
+    keep[:half, :] = low[half:body]
+    send[half:, :] = low[body:]
+    keep[half:, :] = low[body:]
+
+
+def tail_step(parts, extra, final):
+    rows, size = parts[0].shape
+    if final:
+        shapes = [jax.ShapeDtypeStruct((rows, size), F32)]
+    else:
+        half = (rows - extra) // 2 + extra
+        shapes = [jax.ShapeDtypeStruct((half, size), BF)] * 2
+    return pl.pallas_call(
+        functools.partial(tail_step_kernel, len(parts), extra, final),
+        out_shape=shapes,
+        in_specs=[VMEM] * len(parts),
+        out_specs=[VMEM] * len(shapes),
+        compiler_params=PARAMS,
+        cost_estimate=COST,
+    )(*parts)
+
+
+def tail_end_kernel(core, kept, got, key_grad, value_grad, norm_total, head_total):
+    total = kept[...].astype(F32) + got[...].astype(F32)
+    rows, size = total.shape
+    width = norm_total.shape[1]
+    block, narrow = key_grad.shape
+    starts = gain_starts(width, size)
+    for k, target in enumerate((key_grad, value_grad)):
+        rows_of = total[k * block : (k + 1) * block]
+        start = narrow % 128
+        target[...] = jnp.where(
+            core[0] == 0, rows_of[:, :narrow], rows_of[:, start : start + narrow]
+        )
+    first = rows - len(starts) * GAIN_ROWS
+    for k, begin in enumerate(starts):
+        row = first + k * GAIN_ROWS
+        norm_total[:, begin : begin + size] = total[row : row + 4]
+    head_total[...] = total[first + 4 : first + 6, :HD]
+
+
+def tail_end(core, width, block, parts):
+    narrow, size = width // 2, parts[0].shape[1]
+    return pl.pallas_call(
+        tail_end_kernel,
+        out_shape=[
+            jax.ShapeDtypeStruct((block, narrow), F32),
+            jax.ShapeDtypeStruct((block, narrow), F32),
+            jax.ShapeDtypeStruct((4, width), F32),
+            jax.ShapeDtypeStruct((2, HD), F32),
+        ],
+        in_specs=[SMEM, VMEM, VMEM],
+        out_specs=[VMEM] * 4,
+        compiler_params=PARAMS,
+        cost_estimate=COST,
+    )(core, *parts)
+
+
 SCALE = HD ** (-0.5)
 
 
-def keys_of(lane, rows, hops, earlier, kv_local, keys):
+def pieces_of(lane, rows, hops, chunk, d):
+    size = min(chunk, rows)
+    for start in range(0, rows, size):
+        row = lane * rows + start
+        yield start, size, (row // chunk * hops + d - 1) * chunk + row % chunk
+
+
+def keys_of(lane, rows, hops, chunk, earlier, kv_local, keys):
     for d in range(1, hops + 1):
-        keys[(hops - d) * rows : (hops - d + 1) * rows, :] = earlier[
-            d - 1, lane * rows : (lane + 1) * rows, :
-        ]
+        for start, size, source in pieces_of(lane, rows, hops, chunk, d):
+            target = (hops - d) * rows + start
+            keys[target : target + size, :] = earlier[source : source + size, :]
     keys[hops * rows :, :] = kv_local[lane * rows : (lane + 1) * rows, :]
 
 
@@ -611,14 +842,14 @@
 
 
 def attention_kernel(
-    hops, place, lengths, query, kv_local, earlier, tokens, w_out, gains,
+    hops, chunk, place, lengths, query, kv_local, earlier, tokens, w_out, gains,
     mixed, branch, middle, ffn_in, keys,
 ):
     lanes = lengths.shape[0]
     rows = query.shape[0] // lanes
     for lane in range(lanes):
         span = slice(lane * rows, (lane + 1) * rows)
-        keys_of(lane, rows, hops, earlier, kv_local, keys)
+        keys_of(lane, rows, hops, chunk, earlier, kv_local, keys)
         allowed = allowed_of(place, lengths, lane, rows, hops, W)
         for h in range(HQ):
             cols = slice(h * HD, (h + 1) * HD)
@@ -631,11 +862,11 @@
         ffn_in[span, :] = rms_forward(mid, gains[2:3, :]).astype(BF)
 
 
-def attention(hops, place, lengths, query, kv_local, earlier, tokens, w_out, gains):
+def attention(hops, chunk, place, lengths, query, kv_local, earlier, tokens, w_out, gains):
     total, width = tokens.shape
     lanes = lengths.shape[0]
     return pl.pallas_call(
-        functools.partial(attention_kernel, hops),
+        functools.partial(attention_kernel, hops, chunk),
         out_shape=[
             jax.ShapeDtypeStruct(query.shape, BF),
             jax.ShapeDtypeStruct((total, width), F32),
@@ -651,13 +882,13 @@
 
 
 def attention_back_kernel(
-    hops, place, lengths, query, kv_local, earlier, upstream, w_out, gains, head_gains,
-    branch, middle, keep, got, query_proj, cosine, sine,
-    grad_middle, grad_branch, grad_query, grad_kv, grad_earlier, norm_terms, head_terms,
+    hops, chunk, cores, core, place, lengths, query, kv_local, earlier, upstream, w_out, gains,
+    head_gains, branch, middle, keep, got, query_proj, cosine, sine, late, grad_middle, grad_branch, grad_query, grad_kv, grad_earlier, norm_terms, head_terms,
     keys, d_mixed, raws, softs, queries, mixes,
 ):
     lanes = lengths.shape[0]
     rows = query.shape[0] // lanes
+    width = upstream.shape[1]
     norm_terms[...] = jnp.zeros_like(norm_terms)
     head_terms[...] = jnp.zeros_like(head_terms)
     for lane in range(lanes):
@@ -671,8 +902,12 @@
         norm_terms[1:2, :] += jnp.sum(ffn_terms, axis=0, keepdims=True)
         low = d_branch.astype(BF)
         grad_branch[span, :] = low
+        if cores == 2:
+            size = late.shape[1] - HQ * HD
+            window = window_of(core[0] ^ 1, width // 2, size)
+            late[span, HQ * HD :] = grad_branch[span, window]
         d_mixed[...] = dot_nt(low, w_out[...]).astype(BF)
-        keys_of(lane, rows, hops, earlier, kv_local, keys)
+        keys_of(lane, rows, hops, chunk, earlier, kv_local, keys)
         allowed = allowed_of(place, lengths, lane, rows, hops, W)
         cos, sin = cosine[span, :], sine[span, :]
         for h in range(HQ):
@@ -689,19 +924,23 @@
             normed = rotate(dot(raw, keys[:, :HD]), cos, -sin)
             d_query, terms = rms_backward(query_proj[span, cols], head_gains[0:1, :], normed)
             grad_query[span, cols] = d_query.astype(BF)
+            if cores == 2:
+                late[span, cols] = d_query.astype(BF)
             head_terms[0:1, :] += jnp.sum(terms, axis=0, keepdims=True)
         for part, (left, right) in enumerate(((raws, queries), (softs, mixes))):
             cols = slice(part * HD, (part + 1) * HD)
             out = dot_tn(left[...], right[...])
             for d in range(1, hops + 1):
-                grad_earlier[d - 1, span, cols] = out[
-                    (hops - d) * rows : (hops - d + 1) * rows
-                ].astype(BF)
+                for start, size, target in pieces_of(lane, rows, hops, chunk, d):
+                    source = (hops - d) * rows + start
+                    grad_earlier[target : target + size, cols] = out[
+                        source : source + size
+                    ].astype(BF)
             grad_kv[span, cols] = out[hops * rows :]
 
 
 def attention_back(
-    hops, place, lengths, query, kv_local, earlier, upstream, w_out, gains, head_gains,
+    hops, chunk, cores, core, place, lengths, query, kv_local, earlier, upstream, w_out, gains, head_gains,
     branch, middle, keep, got, query_proj, cosine, sine,
 ):
     total, width = upstream.shape
@@ -709,8 +948,9 @@
     rows = total // lanes
     span = (hops + 1) * rows
     return pl.pallas_call(
-        functools.partial(attention_back_kernel, hops),
+        functools.partial(attention_back_kernel, hops, chunk, cores),
         out_shape=[
+            jax.ShapeDtypeStruct((total, HQ * HD + window_size(width, cores)), BF),
             jax.ShapeDtypeStruct((total, width), F32),
             jax.ShapeDtypeStruct((total, width), BF),
             jax.ShapeDtypeStruct(query.shape, BF),
@@ -719,8 +959,8 @@
             jax.ShapeDtypeStruct((8, width), F32),
             jax.ShapeDtypeStruct((8, HD), F32),
         ],
-        in_specs=[SMEM, SMEM] + [VMEM] * 14,
-        out_specs=[VMEM] * 7,
+        in_specs=[SMEM] * 3 + [VMEM] * 14,
+        out_specs=[VMEM] * 8,
         scratch_shapes=[
             pltpu.VMEM((span, 2 * HD), BF),
             pltpu.VMEM((rows, HQ * HD), BF),
@@ -732,7 +972,7 @@
         compiler_params=PARAMS,
         cost_estimate=COST,
     )(
-        place, lengths, query, kv_local, earlier, upstream, w_out, gains, head_gains,
+        core, place, lengths, query, kv_local, earlier, upstream, w_out, gains, head_gains,
         branch, middle, keep, got, query_proj, cosine, sine,
     )
 
@@ -811,11 +1051,11 @@
     )
     picked = pick(fetch_table, spread).reshape(seq_count, hops * chunk, 2 * HD)
     arrived = lax.all_to_all(picked, "seq", 0, 0, tiled=True)
-    earlier = (
-        arrived.reshape(seq_count, hops, chunk, 2 * HD)
-        .transpose(1, 0, 2, 3)
-        .reshape(hops, total, 2 * HD)
-    )
+    run = chunk
+    if chunk % 16:
+        run = total
+        arrived = arrived.reshape(seq_count, hops, chunk, 2 * HD).transpose(1, 0, 2, 3)
+    earlier = arrived.reshape(hops * total, 2 * HD)
 
     w_query, w_out = lax.optimization_barrier((w_query, w_out, kv_local))[:2]
     query_peers = core_blocks(w_query)
@@ -826,6 +1066,12 @@
     query_proj, query_rot = queries_of(
         core_ref, attn_in, query_peers, head_gains, cosine, sine
     )
+
+    size = window_size(width, cores)
+
+    def peer_window(values):
+        start = (core ^ 1) * narrow // 128 * 128
+        return lax.dynamic_slice_in_dim(values, start, size, 1)
 
     hidden_cols = w_gate.shape[1]
     share = -(-hidden_cols // 256) * 128
@@ -841,8 +1087,15 @@
     earlier = after(earlier, query_rot, w_out_full)
     place_ref, lengths_ref = place.reshape(1), lengths[0]
     mixed_low, branch, middle, ffn_in = attention(
-        hops, place_ref, lengths_ref, query_rot, kv_local, earlier, token_rows, w_out_full, norm_gains
-    )
+        hops, run, place_ref, lengths_ref, query_rot, kv_local, earlier, token_rows, w_out_full, norm_gains
+    )
+
+    if cores == 2:
+        mixed_peer = swap(mixed_low, "fsdp", 1)
+        attn_peer = swap(peer_window(attn_in), "fsdp", 1)
+        early = (mixed_peer, attn_peer)
+    else:
+        early = ()
 
     def sum_group(near_part, far_part):
         got = swap(core_sum(*far_part).astype(BF), "seq", SPLIT_BIT)
@@ -851,76 +1104,96 @@
     far_in = swap(ffn_in, "seq", SPLIT_BIT)
     near_all = core_blocks(ffn_in)
     near = ffn_forward(part_ref, near_all, w_gate, w_up, w_down, share, overlap)
-    far_all = core_blocks(after(far_in, near[0]))
+    far_all = core_blocks(after(far_in, near[0], *early))
     far = ffn_forward(part_ref, far_all, w_gate, w_up, w_down, share, overlap)
     keep, got = sum_group(near[3:], far[3:])
     ffn_out = keep + got.astype(F32)
     result = middle + rms_forward(ffn_out, norm_gains[3])
 
     grad_ffn_out, top_terms = rms_backward(ffn_out, norm_gains[3], upstream_rows.astype(F32))
-    top_terms = jnp.sum(top_terms, axis=0)
+    top_terms = jnp.sum(top_terms, axis=0, keepdims=True)
     grad_low = grad_ffn_out.astype(BF)
     far_grad = swap(grad_low, "seq", SPLIT_BIT)
     near_grads = core_blocks(grad_low)
     near_back = ffn_backward(part_ref, near_grads, near[1], near[2], w_gate, w_up, w_down)
     far_grads = core_blocks(after(far_grad, near_back[0]))
     others = [m for m in masks(seq_count) if m != SPLIT_BIT]
-    swapped = [others[1], others[0]] + others[2:]
-
-    def terms_of(left, right, pieces):
-        pieces = [(order + [SPLIT_BIT], size) for order, size in pieces]
+    swapped, beyond = [others[1], others[0]] + others[2:], others[2:]
+
+    def terms_of(left, right, *pieces):
+        pieces = [(order + [SPLIT_BIT], size, quad) for order, size, quad in pieces]
         return weight_terms(own, seq_count, pieces, left, *right)
+
+    tile, count = tiles(share)
+    minor = max(1, count * 2 // 7) * tile
+    outward_first = beyond[:1] + others[:2] + beyond[1:]
 
     down_terms = terms_of(
         near_grads + far_grads,
         (near[0], far[0]),
-        [(others, share)],
+        (beyond, share - minor, True),
+        (outward_first, minor, False),
+    )
+    down_b = Chain(*down_terms[1:], outward_first)
+    down_quad = lax.all_to_all(
+        down_terms[0], "seq", 0, 0, tiled=True, axis_index_groups=quads(seq_count)
     )
     far_grads[0] = after(far_grads[0], *down_terms)
     far_back = ffn_backward(part_ref, far_grads, far[1], far[2], w_gate, w_up, w_down)
-    keep, got = sum_group(near_back[2:], far_back[2:])
-
-    gate_terms = terms_of(near_all + far_all, (near_back[0], far_back[0]), [(swapped, share)])
+    far_sum = core_sum(*far_back[2:]).astype(BF)
+    got = swap(far_sum, "seq", SPLIT_BIT)
+    keep = core_sum(*near_back[2:])
+
+    gate_terms = terms_of(
+        near_all + far_all, (near_back[0], after(far_back[0], far_sum)), (swapped, share, False)
+    )
     up_terms = terms_of(
-        near_all + far_all, (near_back[1], after(far_back[1], *gate_terms)), [(others, share)]
-    )
-    down_c = Chain(*down_terms, others)
+        near_all + far_all, (near_back[1], after(far_back[1], *gate_terms)), (others, share, False)
+    )
     gate_c = Chain(*gate_terms, swapped)
     up_c = Chain(*up_terms, others)
     turns = Turns(up_terms[0])
 
+    down_b.step(turns)
+    down_first, down_rest = quad_sum(turns.wait(down_quad))
+    turns.end(down_first)
+    down_a = Chain(down_first, down_rest, beyond)
+
     (
-        grad_middle, grad_branch_low, grad_query_low, grad_kv, grad_earlier, norm_terms, head_terms
+        late, grad_middle, grad_branch_low, grad_query_low, grad_kv, grad_earlier, norm_terms,
+        head_terms,
     ) = attention_back(
-        hops, place_ref, lengths_ref, query_rot, kv_local, earlier, upstream_rows, w_out_full,
+        hops, run, cores, core_ref, place_ref, lengths_ref, query_rot, kv_local, earlier, upstream_rows, w_out_full,
         norm_gains, head_gains, branch, middle, keep, turns.wait(got), query_proj, cosine, sine,
     )
 
-    outward = (
-        grad_earlier.reshape(hops, seq_count, chunk, 2 * HD)
-        .transpose(1, 0, 2, 3)
-        .reshape(seq_count, hops * chunk, 2 * HD)
-    )
+    outward = grad_earlier
+    if chunk % 16:
+        outward = outward.reshape(hops, seq_count, chunk, 2 * HD).transpose(1, 0, 2, 3)
+    outward = outward.reshape(seq_count, hops * chunk, 2 * HD)
     collected = lax.all_to_all(outward, "seq", 0, 0, tiled=True)
 
     turns.end(outward)
-    down_c.step(turns)
-    outer_keep, outer_send = outer_begin(
-        core_ref, cores, mixed_low, grad_branch_low, turns.wait(grad_query_low), attn_in
-    )
-    turns.end(outer_send)
     every = swapped + [SPLIT_BIT]
+    padded = width // seq_count
     if cores == 2:
-        outer_got = swap(outer_send, "fsdp", 1)
+        late = swap(late, "fsdp", 1)
+        attention_terms = outer_pair(
+            own_ref, core_ref, seq_count, every, padded, mixed_low, mixed_peer, grad_branch_low,
+            grad_query_low, turns.wait(late), attn_in, attn_peer,
+        )
     else:
+        outer_keep, outer_send = outer_begin(
+            core_ref, cores, mixed_low, grad_branch_low, turns.wait(grad_query_low), attn_in
+        )
         outer_keep = core_sum(outer_keep, outer_send)
         outer_got = jnp.zeros(outer_keep.shape, BF)
+        attention_terms = outer_end(own_ref, seq_count, every, outer_keep, outer_got, padded)
+    turns.end(attention_terms[0])
+    outer_c = Chain(*attention_terms, swapped)
     gate_c.step(turns)
-    attention_terms = outer_end(own_ref, seq_count, every, outer_keep, turns.wait(outer_got))
-    turns.end(attention_terms[0])
-    outer_c = Chain(*attention_terms, every)
     up_c.step(turns)
-    down_c.step(turns)
+    down_b.step(turns)
     summed = pick_sum(
         hops,
         reader_table,
@@ -929,36 +1202,47 @@
     )
     turns.end(summed)
     returned = lax.all_to_all(summed, "seq", 0, 0, tiled=True)
+    while down_a.order:
+        down_a.step(turns)
     gate_c.step(turns)
-    down_c.step(turns)
     up_c.step(turns)
     outer_c.step(turns)
+    while down_b.order:
+        down_b.step(turns)
     returned = turns.wait(returned)
 
-    grad_inputs, kv_keep, kv_send, in_terms, key_terms = last(
+    grad_inputs, kv_keep, kv_send, gain_terms = last(
         core_ref, query_peers, kv_peers, token_rows, attn_in, grad_middle, grad_query_low, grad_kv,
-        returned.reshape(total, 2 * HD), key_proj, cosine, sine, norm_gains, head_gains,
-    )
-    kv_terms = core_sum(kv_keep, kv_send).astype(BF)
-    size = kv_terms.shape[1]
+        returned.reshape(total, 2 * HD), key_proj, cosine, sine, norm_gains, head_gains, norm_terms,
+        head_terms, top_terms,
+    )
     kv_rows = HD // seq_count
-    kv_terms = (
-        kv_terms.reshape(2, seq_count, kv_rows, size)
-        .transpose(1, 0, 2, 3)
-        .reshape(seq_count, 2 * kv_rows, size)
-    )
-    gains = jnp.concatenate(
-        [in_terms[0], norm_terms[0], norm_terms[1], top_terms, head_terms[0], key_terms[0]]
-    )
-    for mask in masks(cores):
-        gains = gains + swap(gains, "fsdp", mask)
-    gain_size = gains.shape[0]
-    gain_rows = -(-gain_size // size)
-    gains = jnp.pad(gains, (0, gain_rows * size - gain_size)).reshape(gain_rows, size)
-    tail = jnp.concatenate(
-        [kv_terms, jnp.broadcast_to(gains.astype(BF), (seq_count, gain_rows, size))], axis=1
-    )
-    ended = lax.all_to_all(tail, "seq", 0, 0, tiled=True)
+    tail_order = beyond + [SPLIT_BIT]
+    size = kv_keep.shape[1]
+    starts = gain_starts(width, size)
+    extra = len(starts) * GAIN_ROWS
+    if cores == 2:
+        kv_got, gains_got = swap(kv_send, "fsdp", 1), swap(gain_terms, "fsdp", 1)
+    else:
+        kv_keep = core_sum(kv_keep, kv_send)
+        kv_got = jnp.zeros(kv_keep.shape, BF)
+        for mask in masks(cores)[1:]:
+            gain_terms = gain_terms + swap(gain_terms, "fsdp", mask)
+        gains_got = swap(gain_terms, "fsdp", 1)
+    if kv_rows % 16:
+        gains = (gain_terms + gains_got).astype(BF)
+        owners = jnp.stack([owner(own) for owner in places_of(tail_order, True)])
+        tail = (kv_keep + kv_got.astype(F32)).astype(BF).reshape(2, seq_count, kv_rows, size)
+        tail = jnp.take(tail, owners, axis=1, mode="clip").transpose(1, 0, 2, 3)
+        tail = tail.reshape(QUAD, -1, size)
+        gains = jnp.concatenate([gains[:, start : start + size] for start in starts], axis=0)
+        gains = jnp.broadcast_to(gains, (QUAD,) + gains.shape)
+        tail = jnp.concatenate([tail, gains], axis=1).reshape(-1, size)
+    else:
+        tail = tail_begin(own_ref, tail_order, seq_count, kv_keep, kv_got, gain_terms, gains_got)
+    ended = lax.all_to_all(
+        tail, "seq", 0, 0, tiled=True, axis_index_groups=quads(seq_count)
+    )
     turns.end(tail)
 
     def exchanged(*chains):
@@ -966,23 +1250,48 @@
         sent = jnp.concatenate([chain.total[0].astype(BF) for chain in chains], axis=1)
         return mine, swap(sent, "seq", SPLIT_BIT)
 
-    gate_c.step(turns)
+    down_pair = exchanged(down_a, down_b)
+    while gate_c.order:
+        gate_c.step(turns)
     outer_c.step(turns)
-    up_c.step(turns)
-    ffn_mine, ffn_got = exchanged(down_c, gate_c, up_c)
-    outer_c.step(turns)
+    ended = turns.wait(ended).reshape(QUAD, -1, size)
+    parts = [ended[q] for q in range(QUAD)]
+    for mask in tail_order:
+        sent, kept = tail_step(parts, extra, False)
+        turns.end(sent)
+        got = swap(sent, "seq", mask)
+        if mask == tail_order[0]:
+            while up_c.order:
+                up_c.step(turns)
+            gate_pair = exchanged(gate_c, up_c)
+        if mask == tail_order[-1]:
+            while outer_c.order:
+                outer_c.step(turns)
+            outer_mine, outer_got = exchanged(outer_c)
+            pair_got = turns.wait(gate_pair[1])
+            turns.end(pair_got)
+        parts = [kept, turns.wait(got)]
 
     def own_columns(values):
         return lax.dynamic_slice_in_dim(values, core * narrow % 128, narrow, 1)
 
-    ended = jnp.sum(turns.wait(ended).astype(F32), axis=0)
-    key_grad = own_columns(ended[:kv_rows]).T
-    value_grad = own_columns(ended[kv_rows : 2 * kv_rows]).T
-    gains = ended[2 * kv_rows :].reshape(-1)[:gain_size]
-
-    ffn_got = turns.wait(ffn_got).astype(F32)
-    lower = jnp.where(part == 0, ffn_mine, ffn_got)
-    upper = jnp.where(part == 0, ffn_got, ffn_mine)
+    if kv_rows % 16 or cores != 2:
+        (ended,) = tail_step(parts, extra, True)
+        key_grad = own_columns(ended[:kv_rows]).T
+        value_grad = own_columns(ended[kv_rows : 2 * kv_rows]).T
+        windows = ended[-extra:].reshape(len(starts), GAIN_ROWS, size)
+        gains = jnp.concatenate(
+            [windows[k][:, k * size - start :] for k, start in enumerate(starts)], axis=1
+        )
+        norm_total, head_total = gains[:4], gains[4:6, :HD]
+    else:
+        key_grad, value_grad, norm_total, head_total = tail_end(core_ref, width, kv_rows, parts)
+        key_grad, value_grad = key_grad.T, value_grad.T
+
+    mine, got = down_pair
+    mine = jnp.concatenate([mine, gate_pair[0]], axis=1)
+    got = jnp.concatenate([turns.wait(got), pair_got], axis=1).astype(F32)
+    lower, upper = jnp.where(part == 0, mine, got), jnp.where(part == 0, got, mine)
     down_grad, gate_grad, up_grad = (
         jnp.concatenate(
             [
@@ -994,14 +1303,12 @@
         for k in range(3)
     )
     down_grad = down_grad.T
-    outer_c.step(turns)
-    attention_grad = own_columns(outer_c.total[0])
+    attention_grad = outer_mine + turns.wait(outer_got).astype(F32)
     query_rows = q_width // seq_count
-    out_grad = attention_grad[:query_rows]
-    query_grad = attention_grad[query_rows:].T
-
-    norm_total = gains[: 4 * width].reshape(4, width)
-    head_total = gains[4 * width :].reshape(2, HD)
+    size = attention_grad.shape[1] // 2
+    out_grad = own_columns(attention_grad[:query_rows, :size])
+    query_grad = own_columns(attention_grad[:query_rows, size:]).T
+
 
     return (
         result.reshape(1, lanes, rows, width),

time: 442 us -> 401 us (0.907)
  waiting for transfers between devices: 164 us -> 97.2 us
  Pallas kernels: 139 us -> 177 us
  other arithmetic: 39.5 us -> 23.5 us
  starting transfers between devices: 50.8 us -> 61.4 us
  local copies, waits for them, and re-layouts: 41.7 us -> 35.5 us
    ppermute x32 -> x38, waiting for transfers between devices: 141 us -> 74.4 us  [swap(): return lax.ppermute(value, axis, [(i, i ^ mask) for i in range(count)])]
    pallas_call x4 -> x21, Pallas kernels: 34.1 us -> 71.9 us  [the longest x13 32.5 us: step_of(): pl.pallas_call(step_kernel, out_shape=[shape] * parts, in_specs=[VMEM] *...]
    another operation x9 -> x0, other arithmetic: 11.5 us -> none
    slice x18 -> x2, local copies, waits for them, and re-layouts: 11.3 us -> 0.93 us  [the longest x1 0.9 us: shards(): parts = [ended[q] for q in range(QUAD)]]
    ppermute x32 -> x38, starting transfers between devices: 24.4 us -> 33.1 us  [swap(): return lax.ppermute(value, axis, [(i, i ^ mask) for i in range(count)])]
    unnamed x76 -> x91, local copies, waits for them, and re-layouts: 11.6 us -> 17.6 us
  transfers between devices with their start and end apart: 37 -> 44, of which waited for: 16 -> 20; matrix products, arithmetic and copies ran while one was open for 14% -> 9% of each run, Pallas kernels for 23% -> 35%
where the time goes in v4:
time: 401 us; the launch traced here: 396 us
  Pallas kernels  177 us (44%)
  waiting for transfers between devices  97.2 us (24%)
  starting transfers between devices  61.4 us (15%)
  local copies, waits for them, and re-layouts  35.5 us (9%)
  other arithmetic  23.5 us (6%)
    ppermute x38, waiting for transfers between devices, swap(): return lax.ppermute(value, axis, [(i, i ^ mask) for i in range(count)])  74.4 us
    ppermute x38, starting transfers between devices, swap(): return lax.ppermute(value, axis, [(i, i ^ mask) for i in range(count)])  33.1 us
    pallas_call x13, Pallas kernels, step_of(): pl.pallas_call(step_kernel, out_shape=[shape] * parts, in_specs=[VMEM] *...  32.5 us
    pallas_call x3, Pallas kernels, weight_terms(): pl.pallas_call(functools.partial(weight_kernel, n, pieces), out_shape=[ja...  32.3 us
    pallas_call x2, Pallas kernels, ffn_backward(): pl.pallas_call(functools.partial(ffn_backward_kernel, n), out_shape=[jax....  30.4 us
    pallas_call x2, Pallas kernels, ffn_forward(): pl.pallas_call(functools.partial(ffn_forward_kernel, n, overlap), out_sha...  28.4 us
    unnamed x91, local copies, waits for them, and re-layouts  17.6 us
    all_to_all x1, waiting for transfers between devices, shards(): arrived = lax.all_to_all(picked, 'seq', 0, 0, tiled=True)  13.6 us
  transfers between devices with their start and end apart: 44, of which 20 were waited for; matrix products, arithmetic and copies ran while one was open for 9% of the time, Pallas kernels for 35%

profile of v4, /device:TPU:0, one launch (start us, length us, event | category | flops | bytes accessed | tf_op | source)
XLA Modules:
  0.0 395.9 jit_solution(15860326176758562458)
XLA Ops:
  10.5 3.0 shard_map.212
  13.6 8.3 %all-to-all-start = ((bf16[16,16,512]{2,1,0:T(8,128)(2,1)}), bf16[16,16,512]{2,1,0:T(8,128)(2,1)S(1)}, u32[]{:S(2)}, u32[]{:S(2)}) async-start(bf16[16,16,512]{2,1,0:T(8,128)(2,1)} %bitcast.78), calls=%async_computation | async-start | bytes 524288 | tf_op jit(solution)/shard_map/all_to_all | solution.py:1049
  25.1 6.9 %all-to-all-done = bf16[16,16,512]{2,1,0:T(8,128)(2,1)S(1)} async-done(((bf16[16,16,512]{2,1,0:T(8,128)(2,1)}), bf16[16,16,512]{2,1,0:T(8,128)(2,1)S(1)}, u32[]{:S(2)}, u32[]{:S(2)}) %all-to-all-start) | async-done | bytes 262176 | tf_op jit(solution)/shard_map/all_to_all | solution.py:1049
  32.0 1.6 gather_fusion.1
  33.5 3.9 all-to-all-start.1
  37.4 4.1 %shard_map.213 = (f32[256,1024]{1,0:T(8,128)}, bf16[256,1024]{1,0:T(8,128)(2,1)}) custom-call(s32[1]{0:T(128)} %bitcast.2.core, bf16[256,1152]{1,0:T(8,128)(2,1)} %get-tuple-element.117.attn_in.refs_5_, bf16[576,1024]{1,0:T(8,128)(2,1)} %refs_0_.1, bf16[576,1024]{1,0:T(8,128)(2,1)} %collective-permute-done.1.refs_1_, f32[2,256]{1,0:T(2,128)} %refs_14_.1, ...), custom_call_target="tpu_custom_call" | custom-call | flops 1024 | bytes 1024 | tf_op jit(solution)/shard_map/pallas_call | solution.py:630
  41.5 1.6 pad_maximum_fusion
  43.2 1.7 maximum_select_fusion
  45.1 2.2 pad_maximum_fusion.1.w_out
  47.4 13.6 %all-to-all-done.1 = bf16[16,64,512]{2,1,0:T(8,128)(2,1)S(1)} async-done(((bf16[16,64,512]{2,1,0:T(8,128)(2,1)}), bf16[16,64,512]{2,1,0:T(8,128)(2,1)S(1)}, u32[]{:S(2)}, u32[]{:S(2)}) %all-to-all-start.1) | async-done | bytes 1048608 | tf_op jit(solution)/shard_map/all_to_all | solution.py:1053
  62.0 9.2 %shard_map.214 = (bf16[256,1024]{1,0:T(8,128)(2,1)}, f32[256,1152]{1,0:T(8,128)}, f32[256,1152]{1,0:T(8,128)}, bf16[256,1152]{1,0:T(8,128)(2,1)}) custom-call(s32[1]{0:T(128)} %bitcast.place, s32[2,8]{1,0:T(2,128)} %bitcast.83, bf16[256,1024]{1,0:T(8,128)(2,1)} %get-tuple-element.120.query, bf16[256,512]{1,0:T(8,128)(2,1)} %get-tuple-element.118.kv_local, ...), custom_call_target="tpu_custom_call" | custom-call | flops 1024 | bytes 1024 | tf_op jit(solution)/shard_map/pallas_call | solution.py:868
  71.2 3.0 collective-permute-start.5
  75.7 14.4 %shard_map.215 = (bf16[512,1792]{1,0:T(8,128)(2,1)}, bf16[512,1792]{1,0:T(8,128)(2,1)}, bf16[512,1792]{1,0:T(8,128)(2,1)}, f32[256,1152]{1,0:T(8,128)}, bf16[256,1152]{1,0:T(8,128)(2,1)}) custom-call(s32[1]{0:T(128)} %bitcast.15.refs_0_, bf16[256,1152]{1,0:T(8,128)(2,1)} %get-tuple-element.124.refs_1_, bf16[256,1152]{1,0:T(8,128)(2,1)} %copy-done.3, ...), custom_call_target="tpu_custom_call" | custom-call | flops 1024 | bytes 1024 | tf_op jit(solution)/shard_map/pallas_call | solution.py:300
  90.5 1.8 collective-permute-done.8.refs_2_.refs_4_
  93.1 14.0 %shard_map.216 = (bf16[512,1792]{1,0:T(8,128)(2,1)}, bf16[512,1792]{1,0:T(8,128)(2,1)}, bf16[512,1792]{1,0:T(8,128)(2,1)}, f32[256,1152]{1,0:T(8,128)}, bf16[256,1152]{1,0:T(8,128)(2,1)}) custom-call(s32[1]{0:T(128)} %bitcast.15.refs_0_, bf16[256,1152]{1,0:T(8,128)(2,1)} %copy-done.4, bf16[256,1152]{1,0:T(8,128)(2,1)} %copy-done.5, ...), custom_call_target="tpu_custom_call" | custom-call | flops 1024 | bytes 1024 | tf_op jit(solution)/shard_map/pallas_call | solution.py:300
  107.7 1.7 collective-permute-done.9
  110.8 1.7 collective-permute-start.10
  113.2 13.1 %collective-permute-done.10 = bf16[256,1152]{1,0:T(8,128)(2,1)S(1)} collective-permute-done((bf16[256,1152]{1,0:T(8,128)(2,1)S(1)}, bf16[256,1152]{1,0:T(8,128)(2,1)S(1)}, u32[]{:S(2)}, u32[]{:S(2)}) %collective-permute-start.10) | collective-permute-done | bytes 589856 | tf_op jit(solution)/shard_map/ppermute | solution.py:24
  132.3 15.2 %shard_map.217 = (bf16[512,1792]{1,0:T(8,128)(2,1)}, bf16[512,1792]{1,0:T(8,128)(2,1)}, f32[256,1152]{1,0:T(8,128)}, bf16[256,1152]{1,0:T(8,128)(2,1)}) custom-call(s32[1]{0:T(128)} %bitcast.15.refs_0_, bf16[256,1152]{1,0:T(8,128)(2,1)} %copy-done.7, bf16[256,1152]{1,0:T(8,128)(2,1)} %copy-done.14, bf16[512,1792]{1,0:T(8,128)(2,1)} %get-tuple-element.133.refs_3_, ...), custom_call_target="tpu_custom_call" | custom-call | flops 1024 | bytes 1024 | tf_op jit(solution)/shard_map/pallas_call | solution.py:368
  147.7 1.9 collective-permute-done.14.refs_4_.refs_2_
  150.4 10.7 %shard_map.218 = (bf16[16,72,1280]{2,1,0:T(8,128)(2,1)}, bf16[8,72,512]{2,1,0:T(8,128)(2,1)}, bf16[8,72,512]{2,1,0:T(8,128)(2,1)}) custom-call(s32[1]{0:T(128)} %bitcast.18.refs_0_.own, bf16[256,1152]{1,0:T(8,128)(2,1)} %copy-done.7, bf16[256,1152]{1,0:T(8,128)(2,1)} %copy-done.14, bf16[256,1152]{1,0:T(8,128)(2,1)} %copy-done.13, ...), custom_call_target="tpu_custom_call" | custom-call | flops 1024 | bytes 1024 | tf_op jit(solution)/shard_map/pallas_call | solution.py:447
  161.1 3.7 all-to-all-start.2
  164.8 15.2 %shard_map.219 = (bf16[512,1792]{1,0:T(8,128)(2,1)}, bf16[512,1792]{1,0:T(8,128)(2,1)}, f32[256,1152]{1,0:T(8,128)}, bf16[256,1152]{1,0:T(8,128)(2,1)}) custom-call(s32[1]{0:T(128)} %bitcast.15.refs_0_, bf16[256,1152]{1,0:T(8,128)(2,1)} %copy-done.13, bf16[256,1152]{1,0:T(8,128)(2,1)} %copy-done.15, bf16[512,1792]{1,0:T(8,128)(2,1)} %get-tuple-element.144.refs_3_, ...), custom_call_target="tpu_custom_call" | custom-call | flops 1024 | bytes 1024 | tf_op jit(solution)/shard_map/pallas_call | solution.py:368
  185.3 10.7 %shard_map.220 = (bf16[8,72,1792]{2,1,0:T(8,128)(2,1)}, bf16[8,72,1792]{2,1,0:T(8,128)(2,1)}) custom-call(s32[1]{0:T(128)} %bitcast.18.refs_0_.own, bf16[256,1152]{1,0:T(8,128)(2,1)} %get-tuple-element.124.refs_1_, bf16[256,1152]{1,0:T(8,128)(2,1)} %copy-done.3, bf16[256,1152]{1,0:T(8,128)(2,1)} %copy-done.4, bf16[256,1152]{1,0:T(8,128)(2,1)} %copy-done.5, ...), custom_call_target="tpu_custom_call" | custom-call | flops 1024 | bytes 1024 | tf_op jit(solution)/shard_map/pallas_call | solution.py:447
  195.9 2.0 collective-permute-start.20
  198.0 11.0 %shard_map.221 = (bf16[8,72,1792]{2,1,0:T(8,128)(2,1)}, bf16[8,72,1792]{2,1,0:T(8,128)(2,1)}) custom-call(s32[1]{0:T(128)} %bitcast.18.refs_0_.own, bf16[256,1152]{1,0:T(8,128)(2,1)} %get-tuple-element.124.refs_1_, bf16[256,1152]{1,0:T(8,128)(2,1)} %copy-done.3, bf16[256,1152]{1,0:T(8,128)(2,1)} %copy-done.4, bf16[256,1152]{1,0:T(8,128)(2,1)} %copy-done.5, ...), custom_call_target="tpu_custom_call" | custom-call | flops 1024 | bytes 1024 | tf_op jit(solution)/shard_map/pallas_call | solution.py:447
  212.4 2.1 shard_map.222
  214.6 1.7 copy-done
  216.2 2.9 shard_map.223
  219.2 13.5 %shard_map.224 = (bf16[256,1664]{1,0:T(8,128)(2,1)}, f32[256,1152]{1,0:T(8,128)}, bf16[256,1152]{1,0:T(8,128)(2,1)}, bf16[256,1024]{1,0:T(8,128)(2,1)}, f32[256,...) custom-call(s32[1]{0:T(128)} %bitcast.2.core, s32[1]{0:T(128)} %bitcast.place, ...), custom_call_target="tpu_custom_call" | custom-call | flops 1024 | bytes 1024 | tf_op jit(solution)/shard_map/pallas_call | solution.py:950
  232.7 3.8 all-to-all-start.3
  236.6 2.4 collective-permute-done.21.late
  239.9 5.8 %shard_map.225 = (bf16[8,72,1280]{2,1,0:T(8,128)(2,1)}, bf16[8,72,1280]{2,1,0:T(8,128)(2,1)}) custom-call(s32[1]{0:T(128)} %bitcast.18.refs_0_.own, s32[1]{0:T(128)} %bitcast.2.core, bf16[256,1024]{1,0:T(8,128)(2,1)} %get-tuple-element.128.mixed, bf16[256,1024]{1,0:T(8,128)(2,1)} %copy-done.27, bf16[256,1152]{1,0:T(8,128)(2,1)} %get-tuple-element.168.branch, ...), custom_call_target="tpu_custom_call" | custom-call | flops 1024 | bytes 1024 | tf_op jit(solution)/shard_map/pallas_call | solution.py:565
  245.7 1.8 collective-permute-start.23
  249.0 2.4 collective-permute-start.26
  252.1 3.8 shard_map.226
  256.5 7.4 %collective-permute-done.19.got = bf16[8,72,1792]{2,1,0:T(8,128)(2,1)} collective-permute-done((bf16[8,72,1792]{2,1,0:T(8,128)(2,1)}, bf16[8,72,1792]{2,1,0:T(8,128)(2,1)}, u32[]{:S(2)}, u32[]{:S(2)}) %collective-permute-start.19) | collective-permute-done | bytes 2064416 | tf_op jit(solution)/shard_map/ppermute | solution.py:24
  263.8 3.8 shard_map.227
  267.6 7.0 %collective-permute-done.18.got = bf16[4,72,512]{2,1,0:T(8,128)(2,1)S(1)} collective-permute-done((bf16[4,72,512]{2,1,0:T(8,128)(2,1)S(1)}, bf16[4,72,512]{2,1,0:T(8,128)(2,1)S(1)}, u32[]{:S(2)}, u32[]{:S(2)}) %collective-permute-start.18) | collective-permute-done | bytes 294944 | tf_op jit(solution)/shard_map/ppermute | solution.py:24
  275.3 1.8 shard_map.228
  278.9 5.2 %all-to-all-start.4 = ((bf16[16,16,512]{2,1,0:T(8,128)(2,1)}), bf16[16,16,512]{2,1,0:T(8,128)(2,1)S(1)}, u32[]{:S(2)}, u32[]{:S(2)}) async-start(bf16[16,16,512]{2,1,0:T(8,128)(2,1)} %fusion), calls=%async_computation.4 | async-start | bytes 524288 | tf_op jit(solution)/shard_map/all_to_all | solution.py:1204
  284.9 2.0 shard_map.229
  288.9 8.8 %collective-permute-done.25.got = bf16[4,72,1792]{2,1,0:T(8,128)(2,1)S(1)} collective-permute-done((bf16[4,72,1792]{2,1,0:T(8,128)(2,1)}, bf16[4,72,1792]{2,1,0:T(8,128)(2,1)S(1)}, u32[]{:S(2)}, u32[]{:S(2)}) %collective-permute-start.25) | collective-permute-done | bytes 1032224 | tf_op jit(solution)/shard_map/ppermute | solution.py:24
  298.7 2.6 shard_map.230
  302.2 9.3 %collective-permute-done.24.got = bf16[4,72,1792]{2,1,0:T(8,128)(2,1)} collective-permute-done((bf16[4,72,1792]{2,1,0:T(8,128)(2,1)}, bf16[4,72,1792]{2,1,0:T(8,128)(2,1)}, u32[]{:S(2)}, u32[]{:S(2)}) %collective-permute-start.24) | collective-permute-done | bytes 1032224 | tf_op jit(solution)/shard_map/ppermute | solution.py:24
  311.5 2.6 shard_map.231
  314.1 3.1 collective-permute-start.33
  317.2 3.1 shard_map.232
  321.6 1.7 shard_map.233
  324.1 6.5 %shard_map.234 = (f32[256,1152]{1,0:T(8,128)}, f32[512,640]{1,0:T(8,128)}, bf16[512,640]{1,0:T(8,128)(2,1)}, f32[16,1152]{1,0:T(8,128)}) custom-call(s32[1]{0:T(128)} %bitcast.2.core, bf16[576,1024]{1,0:T(8,128)(2,1)} %refs_0_.1, bf16[576,1024]{1,0:T(8,128)(2,1)} %collective-permute-done.1.refs_1_, bf16[576,512]{1,0:T(8,128)(2,1)} %copy-done.10, ...), custom_call_target="tpu_custom_call" | custom-call | flops 1024 | bytes 1024 | tf_op jit(solution)/shard_map/pallas_call | solution.py:687
  333.9 2.6 shard_map.235
  336.8 3.5 all-to-all-start.5
  340.3 2.3 shard_map.236
  344.5 2.3 shard_map.237
  349.3 2.4 all-to-all-done.5
  352.6 2.0 shard_map.238
  356.9 2.3 shard_map.239
  360.7 10.9 %collective-permute-done.32.refs_1_ = bf16[96,640]{1,0:T(8,128)(2,1)S(1)} collective-permute-done((bf16[96,640]{1,0:T(8,128)(2,1)}, bf16[96,640]{1,0:T(8,128)(2,1)S(1)}, u32[]{:S(2)}, u32[]{:S(2)}) %collective-permute-start.32) | collective-permute-done | bytes 122912 | tf_op jit(solution)/shard_map/ppermute | solution.py:24
  372.2 1.6 shard_map.240
  374.6 2.1 shard_map.241
  377.9 2.1 collective-permute-start.36
  380.0 2.7 collective-permute-done.35
  382.7 3.9 collective-permute-done.34
  390.8 1.6 shard_map.242
  (212 shorter events, 70.7 us)
Async XLA Ops:
  2.6 5.7 %copy-start.10 = (bf16[576,512]{1,0:T(8,128)(2,1)}, bf16[576,512]{1,0:T(8,128)(2,1)S(1)}, u32[]{:S(2)}) copy-start(bf16[576,512]{1,0:T(8,128)(2,1)S(1)} %constant_dynamic-update-slice_fusion.refs_0_.refs_2_) | copy-start | bytes 1769476
  2.6 7.0 %collective-permute-start = (bf16[576,512]{1,0:T(8,128)(2,1)S(1)}, bf16[576,512]{1,0:T(8,128)(2,1)S(1)}, u32[]{:S(2)}, u32[]{:S(2)}) collective-permute-start(bf16[576,512]{1,0:T(8,128)(2,1)S(1)} %constant_dynamic-update-slice_fusion.refs_0_.refs_2_), channel_id=1, source_target_pairs={{0,1},{1,0},{2,3},{3,2},{4,5},{5,4},{6,7},{7,6},{8,9},{9,8},{10,11... | collective-permute-start | bytes 1769480 | tf_op jit(solution)/shard_map/ppermute | solution.py:24
  9.7 12.2 %copy-start.17 = (bf16[1024,576]{0,1:T(8,128)(2,1)S(1)}, bf16[1024,576]{0,1:T(8,128)(2,1)}, u32[]{:S(2)}) copy-start(bf16[1024,576]{0,1:T(8,128)(2,1)} %param.20) | copy-start | bytes 3538948
  13.5 23.9 %collective-permute-start.1 = (bf16[576,1024]{1,0:T(8,128)(2,1)}, bf16[576,1024]{1,0:T(8,128)(2,1)}, u32[]{:S(2)}, u32[]{:S(2)}) collective-permute-start(bf16[576,1024]{1,0:T(8,128)(2,1)} %refs_0_.1), channel_id=1, source_target_pairs={{0,1},{1,0},{2,3},{3,2},{4,5},{5,4},{6,7},{7,6},{8,9},{9,8},{10,11... | collective-permute-start | bytes 3538952 | tf_op jit(solution)/shard_map/ppermute | solution.py:24
  13.6 18.4 %all-to-all-start = ((bf16[16,16,512]{2,1,0:T(8,128)(2,1)}), bf16[16,16,512]{2,1,0:T(8,128)(2,1)S(1)}, u32[]{:S(2)}, u32[]{:S(2)}) async-start(bf16[16,16,512]{2,1,0:T(8,128)(2,1)} %bitcast.78), calls=%async_computation | async-start | bytes 524288 | tf_op jit(solution)/shard_map/all_to_all | solution.py:1049
  24.0 17.6 %collective-permute-start.2 = (bf16[1024,640]{1,0:T(8,128)(2,1)S(1)}, bf16[1024,640]{1,0:T(8,128)(2,1)}, u32[]{:S(2)}, u32[]{:S(2)}) collective-permute-start(bf16[1024,640]{1,0:T(8,128)(2,1)S(1)} %get-tuple-element.238), channel_id=1, source_target_pairs={{0,1},{1,0},{2,3},{3,2},{4,5},{5,4},{6,7},{7,6},{8,9},{9,8},{10,11... | collective-permute-start | bytes 3932168 | tf_op jit(solution)/shard_map/ppermute | solution.py:24
  33.5 27.5 %all-to-all-start.1 = ((bf16[16,64,512]{2,1,0:T(8,128)(2,1)}), bf16[16,64,512]{2,1,0:T(8,128)(2,1)S(1)}, u32[]{:S(2)}, u32[]{:S(2)}) async-start(bf16[16,64,512]{2,1,0:T(8,128)(2,1)} %bitcast.75), calls=%async_computation.1 | async-start | bytes 2097152 | tf_op jit(solution)/shard_map/all_to_all | solution.py:1053
  62.0 12.5 %copy-start.2 = (bf16[256,1152]{1,0:T(8,128)(2,1)S(1)}, bf16[256,1152]{1,0:T(8,128)(2,1)}, u32[]{:S(2)}) copy-start(bf16[256,1152]{1,0:T(8,128)(2,1)} %get-tuple-element.117.attn_in.refs_5_) | copy-start | bytes 1769476
  71.2 3.6 collective-permute-start.3
  71.2 19.0 %collective-permute-start.5 = (bf16[256,1152]{1,0:T(8,128)(2,1)}, bf16[256,1152]{1,0:T(8,128)(2,1)S(1)}, u32[]{:S(2)}, u32[]{:S(2)}) collective-permute-start(bf16[256,1152]{1,0:T(8,128)(2,1)} %get-tuple-element.124.refs_1_), channel_id=1, source_target_pairs={{0,8},{2,10},{4,12},{6,14},{8,0},{10,2},{12,4},{14,6},{16,24},{18,... | collective-permute-start | bytes 1769480 | tf_op jit(solution)/shard_map/ppermute | solution.py:24
  74.2 15.9 %collective-permute-start.6 = (bf16[256,1024]{1,0:T(8,128)(2,1)}, bf16[256,1024]{1,0:T(8,128)(2,1)S(1)}, u32[]{:S(2)}, u32[]{:S(2)}) collective-permute-start(bf16[256,1024]{1,0:T(8,128)(2,1)} %get-tuple-element.128.mixed), channel_id=1, source_target_pairs={{0,1},{1,0},{2,3},{3,2},{4,5},{5,4},{6,7},{7,6},{8,9},{9,8},{10,11... | collective-permute-start | bytes 1572872 | tf_op jit(solution)/shard_map/ppermute | solution.py:24
  74.5 15.7 %collective-permute-start.7 = (bf16[256,640]{1,0:T(8,128)(2,1)S(1)}, bf16[256,640]{1,0:T(8,128)(2,1)S(1)}, u32[]{:S(2)}, u32[]{:S(2)}) collective-permute-start(bf16[256,640]{1,0:T(8,128)(2,1)S(1)} %constant_dynamic-slice_fusion.1), channel_id=1, source_target_pairs={{0,1},{1,0},{2,3},{3,2},{4,5},{5,4},{6,7},{7,6},{8,9},{9,8},{10,11... | collective-permute-start | bytes 983048 | tf_op jit(solution)/shard_map/ppermute | solution.py:24
  90.2 16.9 %copy-start.32 = (bf16[256,640]{1,0:T(8,128)(2,1)}, bf16[256,640]{1,0:T(8,128)(2,1)S(1)}, u32[]{:S(2)}) copy-start(bf16[256,640]{1,0:T(8,128)(2,1)S(1)} %collective-permute-done.7.attn_peer) | copy-start | bytes 983044
  90.2 16.9 %copy-start.27 = (bf16[256,1024]{1,0:T(8,128)(2,1)}, bf16[256,1024]{1,0:T(8,128)(2,1)S(1)}, u32[]{:S(2)}) copy-start(bf16[256,1024]{1,0:T(8,128)(2,1)S(1)} %collective-permute-done.6.mixed_peer) | copy-start | bytes 1572868
  90.2 2.1 copy-start.4
  90.2 17.2 %copy-start.42 = (bf16[256,1152]{1,0:T(8,128)(2,1)S(1)}, bf16[256,1152]{1,0:T(8,128)(2,1)}, u32[]{:S(2)}) copy-start(bf16[256,1152]{1,0:T(8,128)(2,1)} %get-tuple-element.126) | copy-start | bytes 1769476
  90.2 2.1 collective-permute-start.8
  107.1 19.2 %copy-start.19 = (f32[256,1152]{1,0:T(8,128)S(1)}, f32[256,1152]{1,0:T(8,128)}, u32[]{:S(2)}) copy-start(f32[256,1152]{1,0:T(8,128)} %get-tuple-element.125) | copy-start | bytes 3538948
  107.1 2.3 collective-permute-start.9
  107.4 5.8 %collective-permute-start.4 = (bf16[256,1152]{1,0:T(8,128)(2,1)S(1)}, bf16[256,1152]{1,0:T(8,128)(2,1)S(1)}, u32[]{:S(2)}, u32[]{:S(2)}) collective-permute-start(bf16[256,1152]{1,0:T(8,128)(2,1)S(1)} %copy-done.42), channel_id=1, source_target_pairs={{0,1},{1,0},{2,3},{3,2},{4,5},{5,4},{6,7},{7,6},{8,9},{9,8},{10,11... | collective-permute-start | bytes 1769480 | tf_op jit(solution)/shard_map/ppermute | solution.py:24
  110.8 15.5 %collective-permute-start.10 = (bf16[256,1152]{1,0:T(8,128)(2,1)S(1)}, bf16[256,1152]{1,0:T(8,128)(2,1)S(1)}, u32[]{:S(2)}, u32[]{:S(2)}) collective-permute-start(bf16[256,1152]{1,0:T(8,128)(2,1)S(1)} %add_convert_fusion.1), channel_id=1, source_target_pairs={{0,8},{2,10},{4,12},{6,14},{8,0},{10,2},{12,4},{14,6},{16,24},{18,... | collective-permute-start | bytes 1769480 | tf_op jit(solution)/shard_map/ppermute | solution.py:24
  129.4 2.0 collective-permute-start.11
  129.4 18.1 %collective-permute-start.13 = (bf16[256,1152]{1,0:T(8,128)(2,1)S(1)}, bf16[256,1152]{1,0:T(8,128)(2,1)S(1)}, u32[]{:S(2)}, u32[]{:S(2)}) collective-permute-start(bf16[256,1152]{1,0:T(8,128)(2,1)S(1)} %get-tuple-element.239.refs_1_), channel_id=1, source_target_pairs={{0,8},{2,10},{4,12},{6,14},{8,0},{10,2},{12,4},{14,6},{16,24},{18,... | collective-permute-start | bytes 1769480 | tf_op jit(solution)/shard_map/ppermute | solution.py:24
  147.5 2.1 collective-permute-start.14
  161.1 53.4 %all-to-all-start.2 = ((bf16[16,72,1280]{2,1,0:T(8,128)(2,1)}), bf16[16,72,1280]{2,1,0:T(8,128)(2,1)S(1)}, u32[]{:S(2)}, u32[]{:S(2)}) async-start(bf16[16,72,1280]{2,1,0:T(8,128)(2,1)} %get-tuple-element.140), calls=%async_computation.2 | async-start | bytes 5898240 | tf_op jit(solution)/shard_map/all_to_all | solution.py:1138
  164.8 15.4 %copy-start.40 = (bf16[256,1152]{1,0:T(8,128)(2,1)S(1)}, bf16[256,1152]{1,0:T(8,128)(2,1)}, u32[]{:S(2)}) copy-start(bf16[256,1152]{1,0:T(8,128)(2,1)} %get-tuple-element.136) | copy-start | bytes 1769476
  164.8 15.8 %copy-start.41 = (bf16[8,72,512]{2,1,0:T(8,128)(2,1)S(1)}, bf16[8,72,512]{2,1,0:T(8,128)(2,1)}, u32[]{:S(2)}) copy-start(bf16[8,72,512]{2,1,0:T(8,128)(2,1)} %get-tuple-element.141) | copy-start | bytes 1769476
  180.0 2.3 collective-permute-start.15
  180.2 30.2 %collective-permute-start.12 = (bf16[256,1152]{1,0:T(8,128)(2,1)S(1)}, bf16[256,1152]{1,0:T(8,128)(2,1)S(1)}, u32[]{:S(2)}, u32[]{:S(2)}) collective-permute-start(bf16[256,1152]{1,0:T(8,128)(2,1)S(1)} %copy-done.40), channel_id=1, source_target_pairs={{0,1},{1,0},{2,3},{3,2},{4,5},{5,4},{6,7},{7,6},{8,9},{9,8},{10,11... | collective-permute-start | bytes 1769480 | tf_op jit(solution)/shard_map/ppermute | solution.py:24
  180.6 31.0 %collective-permute-start.17 = (bf16[8,72,512]{2,1,0:T(8,128)(2,1)S(1)}, bf16[8,72,512]{2,1,0:T(8,128)(2,1)S(1)}, u32[]{:S(2)}, u32[]{:S(2)}) collective-permute-start(bf16[8,72,512]{2,1,0:T(8,128)(2,1)S(1)} %copy-done.41), channel_id=1, source_target_pairs={{0,16},{2,18},{4,20},{6,22},{8,24},{10,26},{12,28},{14,30},{16,0},... | collective-permute-start | bytes 1769480 | tf_op jit(solution)/shard_map/ppermute | solution.py:24
  183.7 35.5 %collective-permute-start.16 = (bf16[256,1152]{1,0:T(8,128)(2,1)S(1)}, bf16[256,1152]{1,0:T(8,128)(2,1)}, u32[]{:S(2)}, u32[]{:S(2)}) collective-permute-start(bf16[256,1152]{1,0:T(8,128)(2,1)S(1)} %add_convert_fusion), channel_id=1, source_target_pairs={{0,8},{2,10},{4,12},{6,14},{8,0},{10,2},{12,4},{14,6},{16,24},{18,... | collective-permute-start | bytes 1769480 | tf_op jit(solution)/shard_map/ppermute | solution.py:24
  195.9 56.2 %collective-permute-start.20 = (bf16[8,72,1792]{2,1,0:T(8,128)(2,1)}, bf16[8,72,1792]{2,1,0:T(8,128)(2,1)}, u32[]{:S(2)}, u32[]{:S(2)}) collective-permute-start(bf16[8,72,1792]{2,1,0:T(8,128)(2,1)} %get-tuple-element.152), channel_id=1, source_target_pairs={{0,4},{2,6},{4,0},{6,2},{8,12},{10,14},{12,8},{14,10},{16,20},{18,... | collective-permute-start | bytes 6193160 | tf_op jit(solution)/shard_map/ppermute | solution.py:24
  198.0 12.5 %copy-start.18 = (f32[256,1152]{1,0:T(8,128)S(1)}, f32[256,1152]{1,0:T(8,128)}, u32[]{:S(2)}) copy-start(f32[256,1152]{1,0:T(8,128)} %get-tuple-element.135) | copy-start | bytes 3538948
  208.9 54.9 %collective-permute-start.19 = (bf16[8,72,1792]{2,1,0:T(8,128)(2,1)}, bf16[8,72,1792]{2,1,0:T(8,128)(2,1)}, u32[]{:S(2)}, u32[]{:S(2)}) collective-permute-start(bf16[8,72,1792]{2,1,0:T(8,128)(2,1)} %get-tuple-element.155), channel_id=1, source_target_pairs={{0,2},{2,0},{4,6},{6,4},{8,10},{10,8},{12,14},{14,12},{16,18},{18,... | collective-permute-start | bytes 6193160 | tf_op jit(solution)/shard_map/ppermute | solution.py:24
  232.7 3.8 copy-start.39
  232.7 44.4 %all-to-all-start.3 = ((bf16[16,64,512]{2,1,0:T(8,128)(2,1)}), bf16[16,64,512]{2,1,0:T(8,128)(2,1)S(1)}, u32[]{:S(2)}, u32[]{:S(2)}) async-start(bf16[16,64,512]{2,1,0:T(8,128)(2,1)} %bitcast.80), calls=%async_computation.3 | async-start | bytes 2097152 | tf_op jit(solution)/shard_map/all_to_all | solution.py:1174
  236.5 2.4 collective-permute-start.21
  239.9 7.6 %copy-start.43 = (bf16[4,72,512]{2,1,0:T(8,128)(2,1)S(1)}, bf16[4,72,512]{2,1,0:T(8,128)(2,1)}, u32[]{:S(2)}) copy-start(bf16[4,72,512]{2,1,0:T(8,128)(2,1)} %get-tuple-element.157) | copy-start | bytes 884740
  239.9 11.5 %copy-start.38 = (s32[1,16]{1,0:T(1,128)S(1)}, s32[1,16]{1,0:T(1,128)}, u32[]{:S(2)}) copy-start(s32[1,16]{1,0:T(1,128)} %param.16) | copy-start | bytes 196
  245.7 71.6 %collective-permute-start.23 = (bf16[8,72,1280]{2,1,0:T(8,128)(2,1)}, bf16[8,72,1280]{2,1,0:T(8,128)(2,1)}, u32[]{:S(2)}, u32[]{:S(2)}) collective-permute-start(bf16[8,72,1280]{2,1,0:T(8,128)(2,1)} %get-tuple-element.171), channel_id=1, source_target_pairs={{0,4},{2,6},{4,0},{6,2},{8,12},{10,14},{12,8},{14,10},{16,20},{18,... | collective-permute-start | bytes 4423688 | tf_op jit(solution)/shard_map/ppermute | solution.py:24
  247.5 27.1 %collective-permute-start.18 = (bf16[4,72,512]{2,1,0:T(8,128)(2,1)S(1)}, bf16[4,72,512]{2,1,0:T(8,128)(2,1)S(1)}, u32[]{:S(2)}, u32[]{:S(2)}) collective-permute-start(bf16[4,72,512]{2,1,0:T(8,128)(2,1)S(1)} %copy-done.43), channel_id=1, source_target_pairs={{0,2},{2,0},{4,6},{6,4},{8,10},{10,8},{12,14},{14,12},{16,18},{18,... | collective-permute-start | bytes 884744 | tf_op jit(solution)/shard_map/ppermute | solution.py:24
  249.0 35.2 %collective-permute-start.26 = (bf16[2,72,1280]{2,1,0:T(8,128)(2,1)}, bf16[2,72,1280]{2,1,0:T(8,128)(2,1)S(1)}, u32[]{:S(2)}, u32[]{:S(2)}) collective-permute-start(bf16[2,72,1280]{2,1,0:T(8,128)(2,1)} %get-tuple-element.159), channel_id=1, source_target_pairs={{0,16},{2,18},{4,20},{6,22},{8,24},{10,26},{12,28},{14,30},{16,0},... | collective-permute-start | bytes 1105928 | tf_op jit(solution)/shard_map/ppermute | solution.py:24
  255.9 41.8 %collective-permute-start.25 = (bf16[4,72,1792]{2,1,0:T(8,128)(2,1)}, bf16[4,72,1792]{2,1,0:T(8,128)(2,1)S(1)}, u32[]{:S(2)}, u32[]{:S(2)}) collective-permute-start(bf16[4,72,1792]{2,1,0:T(8,128)(2,1)} %get-tuple-element.173), channel_id=1, source_target_pairs={{0,2},{2,0},{4,6},{6,4},{8,10},{10,8},{12,14},{14,12},{16,18},{18,... | collective-permute-start | bytes 3096584 | tf_op jit(solution)/shard_map/ppermute | solution.py:24
  267.6 43.9 %collective-permute-start.24 = (bf16[4,72,1792]{2,1,0:T(8,128)(2,1)}, bf16[4,72,1792]{2,1,0:T(8,128)(2,1)}, u32[]{:S(2)}, u32[]{:S(2)}) collective-permute-start(bf16[4,72,1792]{2,1,0:T(8,128)(2,1)} %get-tuple-element.175), channel_id=1, source_target_pairs={{0,4},{2,6},{4,0},{6,2},{8,12},{10,14},{12,8},{14,10},{16,20},{18,... | collective-permute-start | bytes 3096584 | tf_op jit(solution)/shard_map/ppermute | solution.py:24
  277.1 44.5 %collective-permute-start.22 = (bf16[2,72,512]{2,1,0:T(8,128)(2,1)}, bf16[2,72,512]{2,1,0:T(8,128)(2,1)}, u32[]{:S(2)}, u32[]{:S(2)}) collective-permute-start(bf16[2,72,512]{2,1,0:T(8,128)(2,1)} %get-tuple-element.177), channel_id=1, source_target_pairs={{0,4},{2,6},{4,0},{6,2},{8,12},{10,14},{12,8},{14,10},{16,20},{18,... | collective-permute-start | bytes 442376 | tf_op jit(solution)/shard_map/ppermute | solution.py:24
  278.9 44.4 %all-to-all-start.4 = ((bf16[16,16,512]{2,1,0:T(8,128)(2,1)}), bf16[16,16,512]{2,1,0:T(8,128)(2,1)S(1)}, u32[]{:S(2)}, u32[]{:S(2)}) async-start(bf16[16,16,512]{2,1,0:T(8,128)(2,1)} %fusion), calls=%async_computation.4 | async-start | bytes 524288 | tf_op jit(solution)/shard_map/all_to_all | solution.py:1204
  301.4 35.4 %collective-permute-start.28 = (bf16[2,72,1792]{2,1,0:T(8,128)(2,1)}, bf16[2,72,1792]{2,1,0:T(8,128)(2,1)S(1)}, u32[]{:S(2)}, u32[]{:S(2)}) collective-permute-start(bf16[2,72,1792]{2,1,0:T(8,128)(2,1)} %get-tuple-element.186), channel_id=1, source_target_pairs={{0,16},{2,18},{4,20},{6,22},{8,24},{10,26},{12,28},{14,30},{16,0},... | collective-permute-start | bytes 1548296 | tf_op jit(solution)/shard_map/ppermute | solution.py:24
  314.1 42.0 %collective-permute-start.33 = (bf16[2,72,1792]{2,1,0:T(8,128)(2,1)}, bf16[2,72,1792]{2,1,0:T(8,128)(2,1)S(1)}, u32[]{:S(2)}, u32[]{:S(2)}) collective-permute-start(bf16[2,72,1792]{2,1,0:T(8,128)(2,1)} %get-tuple-element.188), channel_id=1, source_target_pairs={{0,16},{2,18},{4,20},{6,22},{8,24},{10,26},{12,28},{14,30},{16,0},... | collective-permute-start | bytes 1548296 | tf_op jit(solution)/shard_map/ppermute | solution.py:24
  320.3 23.3 %collective-permute-start.27 = (bf16[4,72,1280]{2,1,0:T(8,128)(2,1)}, bf16[4,72,1280]{2,1,0:T(8,128)(2,1)S(1)}, u32[]{:S(2)}, u32[]{:S(2)}) collective-permute-start(bf16[4,72,1280]{2,1,0:T(8,128)(2,1)} %get-tuple-element.190), channel_id=1, source_target_pairs={{0,2},{2,0},{4,6},{6,4},{8,10},{10,8},{12,14},{14,12},{16,18},{18,... | collective-permute-start | bytes 2211848 | tf_op jit(solution)/shard_map/ppermute | solution.py:24
  324.1 6.5 %copy-start.22 = (f32[2,72,512]{2,1,0:T(8,128)S(1)}, f32[2,72,512]{2,1,0:T(8,128)}, u32[]{:S(2)}) copy-start(f32[2,72,512]{2,1,0:T(8,128)} %shard_map.233) | copy-start | bytes 884740
  330.5 2.5 collective-permute-start.29
  330.6 2.4 collective-permute-start.30
  333.0 56.4 %collective-permute-start.37 = (bf16[72,1792]{1,0:T(8,128)(2,1)}, bf16[72,1792]{1,0:T(8,128)(2,1)}, u32[]{:S(2)}, u32[]{:S(2)}) collective-permute-start(bf16[72,1792]{1,0:T(8,128)(2,1)} %pad_maximum_fusion.7), channel_id=1, source_target_pairs={{0,8},{2,10},{4,12},{6,14},{8,0},{10,2},{12,4},{14,6},{16,24},{18,... | collective-permute-start | bytes 774152 | tf_op jit(solution)/shard_map/ppermute | solution.py:24
  336.8 3.5 copy-start.29
  336.8 14.9 %all-to-all-start.5 = ((bf16[4,160,640]{2,1,0:T(8,128)(2,1)}), bf16[4,160,640]{2,1,0:T(8,128)(2,1)S(1)}, u32[]{:S(2)}, u32[]{:S(2)}) async-start(bf16[4,160,640]{2,1,0:T(8,128)(2,1)} %bitcast.76), calls=%async_computation.5 | async-start | bytes 1638400 | tf_op jit(solution)/shard_map/all_to_all | solution.py:1243
  346.8 27.1 %collective-permute-start.31 = (bf16[2,72,1280]{2,1,0:T(8,128)(2,1)}, bf16[2,72,1280]{2,1,0:T(8,128)(2,1)S(1)}, u32[]{:S(2)}, u32[]{:S(2)}) collective-permute-start(bf16[2,72,1280]{2,1,0:T(8,128)(2,1)} %get-tuple-element.205), channel_id=1, source_target_pairs={{0,16},{2,18},{4,20},{6,22},{8,24},{10,26},{12,28},{14,30},{16,0},... | collective-permute-start | bytes 1105928 | tf_op jit(solution)/shard_map/ppermute | solution.py:24
  354.6 16.9 %collective-permute-start.32 = (bf16[96,640]{1,0:T(8,128)(2,1)}, bf16[96,640]{1,0:T(8,128)(2,1)S(1)}, u32[]{:S(2)}, u32[]{:S(2)}) collective-permute-start(bf16[96,640]{1,0:T(8,128)(2,1)} %get-tuple-element.208), channel_id=1, source_target_pairs={{0,16},{2,18},{4,20},{6,22},{8,24},{10,26},{12,28},{14,30},{16,0},... | collective-permute-start | bytes 368648 | tf_op jit(solution)/shard_map/ppermute | solution.py:24
  360.2 17.6 %copy-start.11 = (f32[2,72,1792]{2,1,0:T(8,128)S(1)}, f32[2,72,1792]{2,1,0:T(8,128)}, u32[]{:S(2)}) copy-start(f32[2,72,1792]{2,1,0:T(8,128)} %shard_map.239) | copy-start | bytes 3096580
  360.3 22.4 %collective-permute-start.35 = (bf16[72,3584]{1,0:T(8,128)(2,1)S(1)}, bf16[72,3584]{1,0:T(8,128)(2,1)S(1)}, u32[]{:S(2)}, u32[]{:S(2)}) collective-permute-start(bf16[72,3584]{1,0:T(8,128)(2,1)S(1)} %pad_maximum_fusion.6), channel_id=1, source_target_pairs={{0,8},{2,10},{4,12},{6,14},{8,0},{10,2},{12,4},{14,6},{16,24},{18,... | collective-permute-start | bytes 1548296 | tf_op jit(solution)/shard_map/ppermute | solution.py:24
  374.6 3.3 copy-start.44
  376.7 10.0 %copy-start.16 = (f32[2,72,1280]{2,1,0:T(8,128)S(1)}, f32[2,72,1280]{2,1,0:T(8,128)}, u32[]{:S(2)}) copy-start(f32[2,72,1280]{2,1,0:T(8,128)} %shard_map.241) | copy-start | bytes 2211844
  377.8 8.9 %collective-permute-start.34 = (bf16[72,1280]{1,0:T(8,128)(2,1)S(1)}, bf16[72,1280]{1,0:T(8,128)(2,1)S(1)}, u32[]{:S(2)}, u32[]{:S(2)}) collective-permute-start(bf16[72,1280]{1,0:T(8,128)(2,1)S(1)} %fusion.11), channel_id=1, source_target_pairs={{0,8},{2,10},{4,12},{6,14},{8,0},{10,2},{12,4},{14,6},{16,24},{18,... | collective-permute-start | bytes 552968 | tf_op jit(solution)/shard_map/ppermute | solution.py:24
  377.9 9.9 %collective-permute-start.36 = (bf16[64,640]{1,0:T(8,128)(2,1)S(1)}, bf16[64,640]{1,0:T(8,128)(2,1)S(1)}, u32[]{:S(2)}, u32[]{:S(2)}) collective-permute-start(bf16[64,640]{1,0:T(8,128)(2,1)S(1)} %copy-done.44), channel_id=1, source_target_pairs={{0,8},{2,10},{4,12},{6,14},{8,0},{10,2},{12,4},{14,6},{16,24},{18,... | collective-permute-start | bytes 245768 | tf_op jit(solution)/shard_map/ppermute | solution.py:24
  387.9 2.7 copy-start.35
  (25 other events, 25.1 us)

commit v5 on v4

--- a/solution.py
+++ b/solution.py
@@ -581,6 +581,29 @@
     for j, peer in enumerate(peers):
         rows = peer.shape[0]
         full[pl.ds(pl.multiple_of((core[0] ^ j) * rows, 16), rows), :] = peer[...]
+
+
+def angle_kernel(rows, own, deal, lengths, frequency, angles):
+    place = deal[own[0]] * rows + lax.broadcasted_iota(jnp.int32, (rows, 1), 0)
+    for lane in range(lengths.shape[0]):
+        start, end = jnp.zeros_like(place), jnp.int32(0)
+        for j in range(lengths.shape[1]):
+            end = end + lengths[lane, j]
+            start = start + jnp.where(end <= place, lengths[lane, j], 0)
+        angles[lane * rows : (lane + 1) * rows, :] = (place - start).astype(F32) * frequency[...]
+
+
+def angles_of(own, deal, lengths, rows):
+    half = HD // 2
+    frequency = jnp.exp(jnp.arange(half, dtype=F32) * (-2.0 * math.log(ROPE_BASE) / HD))
+    return pl.pallas_call(
+        functools.partial(angle_kernel, rows),
+        out_shape=jax.ShapeDtypeStruct((lengths.shape[0] * rows, half), F32),
+        in_specs=[SMEM] * 3 + [VMEM],
+        out_specs=VMEM,
+        compiler_params=PARAMS,
+        cost_estimate=COST,
+    )(own, deal, lengths, frequency.reshape(1, half))
 
 
 def key_value_kernel(n, core, tokens, *refs):
@@ -1039,9 +1062,8 @@
         return out
 
     kv_peers = core_blocks(jnp.concatenate([w_key, w_value], axis=1))
-    local_stream = place * rows + jnp.arange(rows, dtype=jnp.int32)
-    positions = sequence_info(lengths[0], jnp.broadcast_to(local_stream, (lanes, rows)))[1]
-    cosine, sine = rope_tables(positions.reshape(total), HD)
+    angles = angles_of(own_ref, deal, lengths[0], rows)
+    cosine, sine = jnp.cos(angles), jnp.sin(angles)
     attn_in, key_proj, kv_local = key_value(
         core_ref, token_rows, kv_peers, norm_gains, head_gains, cosine, sine
     )

time: 401 us -> 399 us (level)
  other arithmetic: 23.5 us -> 18.5 us
    unnamed x91 -> x95, local copies, waits for them, and re-layouts: 17.6 us -> 17.7 us
  transfers between devices with their start and end apart: 44 -> 44, of which waited for: 20 -> 20; matrix products, arithmetic and copies ran while one was open for 9% -> 8% of each run, Pallas kernels for 35% -> 35%
where the time goes in v5:
time: 399 us; the launch traced here: 394 us
  Pallas kernels  178 us (45%)
  waiting for transfers between devices  96.8 us (24%)
  starting transfers between devices  61.4 us (15%)
  local copies, waits for them, and re-layouts  37.4 us (9%)
  other arithmetic  18.5 us (5%)
    ppermute x38, waiting for transfers between devices, swap(): return lax.ppermute(value, axis, [(i, i ^ mask) for i in range(count)])  74.3 us
    ppermute x38, starting transfers between devices, swap(): return lax.ppermute(value, axis, [(i, i ^ mask) for i in range(count)])  33.1 us
    pallas_call x13, Pallas kernels, step_of(): pl.pallas_call(step_kernel, out_shape=[shape] * parts, in_specs=[VMEM] *...  32.6 us
    pallas_call x3, Pallas kernels, weight_terms(): pl.pallas_call(functools.partial(weight_kernel, n, pieces), out_shape=[ja...  32.3 us
    pallas_call x2, Pallas kernels, ffn_backward(): pl.pallas_call(functools.partial(ffn_backward_kernel, n), out_shape=[jax....  30.5 us
    pallas_call x2, Pallas kernels, ffn_forward(): pl.pallas_call(functools.partial(ffn_forward_kernel, n, overlap), out_sha...  28.4 us
    unnamed x95, local copies, waits for them, and re-layouts  17.7 us
    pallas_call x1, Pallas kernels, attention_back(): pl.pallas_call(functools.partial(attention_back_kernel, hops, chunk, core...  13.5 us
  transfers between devices with their start and end apart: 44, of which 20 were waited for; matrix products, arithmetic and copies ran while one was open for 8% of the time, Pallas kernels for 35%

profile of v5, /device:TPU:0, one launch (start us, length us, event | category | flops | bytes accessed | tf_op | source)
XLA Modules:
  0.0 394.1 jit_solution(10059698334580660471)
XLA Ops:
  8.4 3.0 shard_map.213
  11.5 8.3 %all-to-all-start = ((bf16[16,16,512]{2,1,0:T(8,128)(2,1)}), bf16[16,16,512]{2,1,0:T(8,128)(2,1)S(1)}, u32[]{:S(2)}, u32[]{:S(2)}) async-start(bf16[16,16,512]{2,1,0:T(8,128)(2,1)} %bitcast.75), calls=%async_computation | async-start | bytes 524288 | tf_op jit(solution)/shard_map/all_to_all | solution.py:1071
  23.0 6.9 %all-to-all-done = bf16[16,16,512]{2,1,0:T(8,128)(2,1)S(1)} async-done(((bf16[16,16,512]{2,1,0:T(8,128)(2,1)}), bf16[16,16,512]{2,1,0:T(8,128)(2,1)S(1)}, u32[]{:S(2)}, u32[]{:S(2)}) %all-to-all-start) | async-done | bytes 262176 | tf_op jit(solution)/shard_map/all_to_all | solution.py:1071
  29.9 1.6 gather_fusion.1
  31.5 3.9 all-to-all-start.1
  36.0 4.1 %shard_map.214 = (f32[256,1024]{1,0:T(8,128)}, bf16[256,1024]{1,0:T(8,128)(2,1)}) custom-call(s32[1]{0:T(128)} %bitcast.2.core, bf16[256,1152]{1,0:T(8,128)(2,1)} %get-tuple-element.117.attn_in.refs_5_, bf16[576,1024]{1,0:T(8,128)(2,1)} %refs_0_.1, bf16[576,1024]{1,0:T(8,128)(2,1)} %collective-permute-done.1.refs_1_, f32[2,256]{1,0:T(2,128)} %refs_14_.1, ...), custom_call_target="tpu_custom_call" | custom-call | flops 1024 | bytes 1024 | tf_op jit(solution)/shard_map/pallas_call | solution.py:653
  40.0 1.6 pad_maximum_fusion
  41.7 1.7 maximum_select_fusion
  43.6 2.2 pad_maximum_fusion.1.w_out
  45.8 13.1 %all-to-all-done.1 = bf16[16,64,512]{2,1,0:T(8,128)(2,1)S(1)} async-done(((bf16[16,64,512]{2,1,0:T(8,128)(2,1)}), bf16[16,64,512]{2,1,0:T(8,128)(2,1)S(1)}, u32[]{:S(2)}, u32[]{:S(2)}) %all-to-all-start.1) | async-done | bytes 1048608 | tf_op jit(solution)/shard_map/all_to_all | solution.py:1075
  59.9 9.2 %shard_map.215 = (bf16[256,1024]{1,0:T(8,128)(2,1)}, f32[256,1152]{1,0:T(8,128)}, f32[256,1152]{1,0:T(8,128)}, bf16[256,1152]{1,0:T(8,128)(2,1)}) custom-call(s32[1]{0:T(128)} %bitcast.place, s32[2,8]{1,0:T(2,128)} %bitcast.80, bf16[256,1024]{1,0:T(8,128)(2,1)} %get-tuple-element.120.query, bf16[256,512]{1,0:T(8,128)(2,1)} %get-tuple-element.118.kv_local, ...), custom_call_target="tpu_custom_call" | custom-call | flops 1024 | bytes 1024 | tf_op jit(solution)/shard_map/pallas_call | solution.py:891
  69.2 3.0 collective-permute-start.5
  73.7 14.5 %shard_map.216 = (bf16[512,1792]{1,0:T(8,128)(2,1)}, bf16[512,1792]{1,0:T(8,128)(2,1)}, bf16[512,1792]{1,0:T(8,128)(2,1)}, f32[256,1152]{1,0:T(8,128)}, bf16[256,1152]{1,0:T(8,128)(2,1)}) custom-call(s32[1]{0:T(128)} %bitcast.14.refs_0_, bf16[256,1152]{1,0:T(8,128)(2,1)} %get-tuple-element.124.refs_1_, bf16[256,1152]{1,0:T(8,128)(2,1)} %copy-done.3, ...), custom_call_target="tpu_custom_call" | custom-call | flops 1024 | bytes 1024 | tf_op jit(solution)/shard_map/pallas_call | solution.py:300
  88.5 1.8 collective-permute-done.8.refs_2_.refs_4_
  91.1 14.0 %shard_map.217 = (bf16[512,1792]{1,0:T(8,128)(2,1)}, bf16[512,1792]{1,0:T(8,128)(2,1)}, bf16[512,1792]{1,0:T(8,128)(2,1)}, f32[256,1152]{1,0:T(8,128)}, bf16[256,1152]{1,0:T(8,128)(2,1)}) custom-call(s32[1]{0:T(128)} %bitcast.14.refs_0_, bf16[256,1152]{1,0:T(8,128)(2,1)} %copy-done.4, bf16[256,1152]{1,0:T(8,128)(2,1)} %copy-done.5, ...), custom_call_target="tpu_custom_call" | custom-call | flops 1024 | bytes 1024 | tf_op jit(solution)/shard_map/pallas_call | solution.py:300
  105.7 1.7 collective-permute-done.9
  108.8 1.7 collective-permute-start.10
  111.2 13.1 %collective-permute-done.10 = bf16[256,1152]{1,0:T(8,128)(2,1)S(1)} collective-permute-done((bf16[256,1152]{1,0:T(8,128)(2,1)S(1)}, bf16[256,1152]{1,0:T(8,128)(2,1)S(1)}, u32[]{:S(2)}, u32[]{:S(2)}) %collective-permute-start.10) | collective-permute-done | bytes 589856 | tf_op jit(solution)/shard_map/ppermute | solution.py:24
  130.3 15.3 %shard_map.218 = (bf16[512,1792]{1,0:T(8,128)(2,1)}, bf16[512,1792]{1,0:T(8,128)(2,1)}, f32[256,1152]{1,0:T(8,128)}, bf16[256,1152]{1,0:T(8,128)(2,1)}) custom-call(s32[1]{0:T(128)} %bitcast.14.refs_0_, bf16[256,1152]{1,0:T(8,128)(2,1)} %copy-done.7, bf16[256,1152]{1,0:T(8,128)(2,1)} %copy-done.14, bf16[512,1792]{1,0:T(8,128)(2,1)} %get-tuple-element.133.refs_3_, ...), custom_call_target="tpu_custom_call" | custom-call | flops 1024 | bytes 1024 | tf_op jit(solution)/shard_map/pallas_call | solution.py:368
  145.8 1.9 collective-permute-done.14.refs_4_.refs_2_
  148.5 10.7 %shard_map.219 = (bf16[16,72,1280]{2,1,0:T(8,128)(2,1)}, bf16[8,72,512]{2,1,0:T(8,128)(2,1)}, bf16[8,72,512]{2,1,0:T(8,128)(2,1)}) custom-call(s32[1]{0:T(128)} %bitcast.4.own.refs_0_, bf16[256,1152]{1,0:T(8,128)(2,1)} %copy-done.7, bf16[256,1152]{1,0:T(8,128)(2,1)} %copy-done.14, bf16[256,1152]{1,0:T(8,128)(2,1)} %copy-done.13, ...), custom_call_target="tpu_custom_call" | custom-call | flops 1024 | bytes 1024 | tf_op jit(solution)/shard_map/pallas_call | solution.py:447
  159.2 3.7 all-to-all-start.2
  162.9 15.2 %shard_map.220 = (bf16[512,1792]{1,0:T(8,128)(2,1)}, bf16[512,1792]{1,0:T(8,128)(2,1)}, f32[256,1152]{1,0:T(8,128)}, bf16[256,1152]{1,0:T(8,128)(2,1)}) custom-call(s32[1]{0:T(128)} %bitcast.14.refs_0_, bf16[256,1152]{1,0:T(8,128)(2,1)} %copy-done.13, bf16[256,1152]{1,0:T(8,128)(2,1)} %copy-done.15, bf16[512,1792]{1,0:T(8,128)(2,1)} %get-tuple-element.144.refs_3_, ...), custom_call_target="tpu_custom_call" | custom-call | flops 1024 | bytes 1024 | tf_op jit(solution)/shard_map/pallas_call | solution.py:368
  183.3 10.7 %shard_map.221 = (bf16[8,72,1792]{2,1,0:T(8,128)(2,1)}, bf16[8,72,1792]{2,1,0:T(8,128)(2,1)}) custom-call(s32[1]{0:T(128)} %bitcast.4.own.refs_0_, bf16[256,1152]{1,0:T(8,128)(2,1)} %get-tuple-element.124.refs_1_, bf16[256,1152]{1,0:T(8,128)(2,1)} %copy-done.3, bf16[256,1152]{1,0:T(8,128)(2,1)} %copy-done.4, bf16[256,1152]{1,0:T(8,128)(2,1)} %copy-done.5, ...), custom_call_target="tpu_custom_call" | custom-call | flops 1024 | bytes 1024 | tf_op jit(solution)/shard_map/pallas_call | solution.py:447
  194.0 2.0 collective-permute-start.20
  196.0 11.0 %shard_map.222 = (bf16[8,72,1792]{2,1,0:T(8,128)(2,1)}, bf16[8,72,1792]{2,1,0:T(8,128)(2,1)}) custom-call(s32[1]{0:T(128)} %bitcast.4.own.refs_0_, bf16[256,1152]{1,0:T(8,128)(2,1)} %get-tuple-element.124.refs_1_, bf16[256,1152]{1,0:T(8,128)(2,1)} %copy-done.3, bf16[256,1152]{1,0:T(8,128)(2,1)} %copy-done.4, bf16[256,1152]{1,0:T(8,128)(2,1)} %copy-done.5, ...), custom_call_target="tpu_custom_call" | custom-call | flops 1024 | bytes 1024 | tf_op jit(solution)/shard_map/pallas_call | solution.py:447
  210.5 2.1 shard_map.223
  212.6 1.7 copy-done
  214.3 2.9 shard_map.224
  217.3 13.5 %shard_map.225 = (bf16[256,1664]{1,0:T(8,128)(2,1)}, f32[256,1152]{1,0:T(8,128)}, bf16[256,1152]{1,0:T(8,128)(2,1)}, bf16[256,1024]{1,0:T(8,128)(2,1)}, f32[256,...) custom-call(s32[1]{0:T(128)} %bitcast.2.core, s32[1]{0:T(128)} %bitcast.place, ...), custom_call_target="tpu_custom_call" | custom-call | flops 1024 | bytes 1024 | tf_op jit(solution)/shard_map/pallas_call | solution.py:973
  230.8 3.8 all-to-all-start.3
  234.7 2.4 collective-permute-done.21.late
  238.0 5.8 %shard_map.226 = (bf16[8,72,1280]{2,1,0:T(8,128)(2,1)}, bf16[8,72,1280]{2,1,0:T(8,128)(2,1)}) custom-call(s32[1]{0:T(128)} %bitcast.4.own.refs_0_, s32[1]{0:T(128)} %bitcast.2.core, bf16[256,1024]{1,0:T(8,128)(2,1)} %get-tuple-element.128.mixed, bf16[256,1024]{1,0:T(8,128)(2,1)} %copy-done.27, bf16[256,1152]{1,0:T(8,128)(2,1)} %get-tuple-element.168.branch, ...), custom_call_target="tpu_custom_call" | custom-call | flops 1024 | bytes 1024 | tf_op jit(solution)/shard_map/pallas_call | solution.py:565
  243.8 1.8 collective-permute-start.23
  247.1 2.4 collective-permute-start.26
  250.2 3.8 shard_map.227
  254.5 7.3 %collective-permute-done.19.got = bf16[8,72,1792]{2,1,0:T(8,128)(2,1)} collective-permute-done((bf16[8,72,1792]{2,1,0:T(8,128)(2,1)}, bf16[8,72,1792]{2,1,0:T(8,128)(2,1)}, u32[]{:S(2)}, u32[]{:S(2)}) %collective-permute-start.19) | collective-permute-done | bytes 2064416 | tf_op jit(solution)/shard_map/ppermute | solution.py:24
  261.9 3.8 shard_map.228
  265.7 7.0 %collective-permute-done.18.got = bf16[4,72,512]{2,1,0:T(8,128)(2,1)S(1)} collective-permute-done((bf16[4,72,512]{2,1,0:T(8,128)(2,1)S(1)}, bf16[4,72,512]{2,1,0:T(8,128)(2,1)S(1)}, u32[]{:S(2)}, u32[]{:S(2)}) %collective-permute-start.18) | collective-permute-done | bytes 294944 | tf_op jit(solution)/shard_map/ppermute | solution.py:24
  273.4 1.8 shard_map.229
  277.0 5.2 %all-to-all-start.4 = ((bf16[16,16,512]{2,1,0:T(8,128)(2,1)}), bf16[16,16,512]{2,1,0:T(8,128)(2,1)S(1)}, u32[]{:S(2)}, u32[]{:S(2)}) async-start(bf16[16,16,512]{2,1,0:T(8,128)(2,1)} %fusion), calls=%async_computation.4 | async-start | bytes 524288 | tf_op jit(solution)/shard_map/all_to_all | solution.py:1226
  282.9 2.0 shard_map.230
  287.0 8.8 %collective-permute-done.25.got = bf16[4,72,1792]{2,1,0:T(8,128)(2,1)S(1)} collective-permute-done((bf16[4,72,1792]{2,1,0:T(8,128)(2,1)}, bf16[4,72,1792]{2,1,0:T(8,128)(2,1)S(1)}, u32[]{:S(2)}, u32[]{:S(2)}) %collective-permute-start.25) | collective-permute-done | bytes 1032224 | tf_op jit(solution)/shard_map/ppermute | solution.py:24
  296.8 2.7 shard_map.231
  300.4 9.2 %collective-permute-done.24.got = bf16[4,72,1792]{2,1,0:T(8,128)(2,1)} collective-permute-done((bf16[4,72,1792]{2,1,0:T(8,128)(2,1)}, bf16[4,72,1792]{2,1,0:T(8,128)(2,1)}, u32[]{:S(2)}, u32[]{:S(2)}) %collective-permute-start.24) | collective-permute-done | bytes 1032224 | tf_op jit(solution)/shard_map/ppermute | solution.py:24
  309.5 2.6 shard_map.232
  312.2 3.2 collective-permute-start.33
  315.3 3.1 shard_map.233
  319.7 1.8 shard_map.234
  322.2 6.5 %shard_map.235 = (f32[256,1152]{1,0:T(8,128)}, f32[512,640]{1,0:T(8,128)}, bf16[512,640]{1,0:T(8,128)(2,1)}, f32[16,1152]{1,0:T(8,128)}) custom-call(s32[1]{0:T(128)} %bitcast.2.core, bf16[576,1024]{1,0:T(8,128)(2,1)} %refs_0_.1, bf16[576,1024]{1,0:T(8,128)(2,1)} %collective-permute-done.1.refs_1_, bf16[576,512]{1,0:T(8,128)(2,1)} %copy-done.10, ...), custom_call_target="tpu_custom_call" | custom-call | flops 1024 | bytes 1024 | tf_op jit(solution)/shard_map/pallas_call | solution.py:710
  332.0 2.6 shard_map.236
  334.9 3.5 all-to-all-start.5
  338.4 2.3 shard_map.237
  342.6 2.3 shard_map.238
  347.5 2.4 all-to-all-done.5
  350.7 2.0 shard_map.239
  355.0 2.3 shard_map.240
  358.8 10.9 %collective-permute-done.32.refs_1_ = bf16[96,640]{1,0:T(8,128)(2,1)S(1)} collective-permute-done((bf16[96,640]{1,0:T(8,128)(2,1)}, bf16[96,640]{1,0:T(8,128)(2,1)S(1)}, u32[]{:S(2)}, u32[]{:S(2)}) %collective-permute-start.32) | collective-permute-done | bytes 122912 | tf_op jit(solution)/shard_map/ppermute | solution.py:24
  370.4 1.6 shard_map.241
  372.7 2.1 shard_map.242
  376.0 2.1 collective-permute-start.36
  378.1 2.7 collective-permute-done.35
  380.8 3.9 %collective-permute-done.34 = bf16[72,1280]{1,0:T(8,128)(2,1)S(1)} collective-permute-done((bf16[72,1280]{1,0:T(8,128)(2,1)S(1)}, bf16[72,1280]{1,0:T(8,128)(2,1)S(1)}, u32[]{:S(2)}, u32[]{:S(2)}) %collective-permute-start.34) | collective-permute-done | bytes 184352 | tf_op jit(solution)/shard_map/ppermute | solution.py:24
  388.9 1.6 shard_map.243
  (213 shorter events, 69.2 us)
Async XLA Ops:
  0.6 4.5 %copy-start.38 = (s32[1,16]{1,0:T(1,128)S(1)}, s32[1,16]{1,0:T(1,128)}, u32[]{:S(2)}) copy-start(s32[1,16]{1,0:T(1,128)} %param.16) | copy-start | bytes 196
  2.6 3.6 copy-start.10
  2.6 4.9 %collective-permute-start = (bf16[576,512]{1,0:T(8,128)(2,1)S(1)}, bf16[576,512]{1,0:T(8,128)(2,1)S(1)}, u32[]{:S(2)}, u32[]{:S(2)}) collective-permute-start(bf16[576,512]{1,0:T(8,128)(2,1)S(1)} %constant_dynamic-update-slice_fusion.refs_0_.refs_2_), channel_id=1, source_target_pairs={{0,1},{1,0},{2,3},{3,2},{4,5},{5,4},{6,7},{7,6},{8,9},{9,8},{10,11... | collective-permute-start | bytes 1769480 | tf_op jit(solution)/shard_map/ppermute | solution.py:24
  7.6 12.2 %copy-start.17 = (bf16[1024,576]{0,1:T(8,128)(2,1)S(1)}, bf16[1024,576]{0,1:T(8,128)(2,1)}, u32[]{:S(2)}) copy-start(bf16[1024,576]{0,1:T(8,128)(2,1)} %param.20) | copy-start | bytes 3538948
  11.4 24.6 %collective-permute-start.1 = (bf16[576,1024]{1,0:T(8,128)(2,1)}, bf16[576,1024]{1,0:T(8,128)(2,1)}, u32[]{:S(2)}, u32[]{:S(2)}) collective-permute-start(bf16[576,1024]{1,0:T(8,128)(2,1)} %refs_0_.1), channel_id=1, source_target_pairs={{0,1},{1,0},{2,3},{3,2},{4,5},{5,4},{6,7},{7,6},{8,9},{9,8},{10,11... | collective-permute-start | bytes 3538952 | tf_op jit(solution)/shard_map/ppermute | solution.py:24
  11.5 18.4 %all-to-all-start = ((bf16[16,16,512]{2,1,0:T(8,128)(2,1)}), bf16[16,16,512]{2,1,0:T(8,128)(2,1)S(1)}, u32[]{:S(2)}, u32[]{:S(2)}) async-start(bf16[16,16,512]{2,1,0:T(8,128)(2,1)} %bitcast.75), calls=%async_computation | async-start | bytes 524288 | tf_op jit(solution)/shard_map/all_to_all | solution.py:1071
  21.9 18.1 %collective-permute-start.2 = (bf16[1024,640]{1,0:T(8,128)(2,1)S(1)}, bf16[1024,640]{1,0:T(8,128)(2,1)}, u32[]{:S(2)}, u32[]{:S(2)}) collective-permute-start(bf16[1024,640]{1,0:T(8,128)(2,1)S(1)} %get-tuple-element.238), channel_id=1, source_target_pairs={{0,1},{1,0},{2,3},{3,2},{4,5},{5,4},{6,7},{7,6},{8,9},{9,8},{10,11... | collective-permute-start | bytes 3932168 | tf_op jit(solution)/shard_map/ppermute | solution.py:24
  31.5 27.5 %all-to-all-start.1 = ((bf16[16,64,512]{2,1,0:T(8,128)(2,1)}), bf16[16,64,512]{2,1,0:T(8,128)(2,1)S(1)}, u32[]{:S(2)}, u32[]{:S(2)}) async-start(bf16[16,64,512]{2,1,0:T(8,128)(2,1)} %bitcast.72), calls=%async_computation.1 | async-start | bytes 2097152 | tf_op jit(solution)/shard_map/all_to_all | solution.py:1075
  59.9 12.5 %copy-start.2 = (bf16[256,1152]{1,0:T(8,128)(2,1)S(1)}, bf16[256,1152]{1,0:T(8,128)(2,1)}, u32[]{:S(2)}) copy-start(bf16[256,1152]{1,0:T(8,128)(2,1)} %get-tuple-element.117.attn_in.refs_5_) | copy-start | bytes 1769476
  69.2 3.6 collective-permute-start.3
  69.2 19.0 %collective-permute-start.5 = (bf16[256,1152]{1,0:T(8,128)(2,1)}, bf16[256,1152]{1,0:T(8,128)(2,1)S(1)}, u32[]{:S(2)}, u32[]{:S(2)}) collective-permute-start(bf16[256,1152]{1,0:T(8,128)(2,1)} %get-tuple-element.124.refs_1_), channel_id=1, source_target_pairs={{0,8},{2,10},{4,12},{6,14},{8,0},{10,2},{12,4},{14,6},{16,24},{18,... | collective-permute-start | bytes 1769480 | tf_op jit(solution)/shard_map/ppermute | solution.py:24
  72.2 16.0 %collective-permute-start.6 = (bf16[256,1024]{1,0:T(8,128)(2,1)}, bf16[256,1024]{1,0:T(8,128)(2,1)S(1)}, u32[]{:S(2)}, u32[]{:S(2)}) collective-permute-start(bf16[256,1024]{1,0:T(8,128)(2,1)} %get-tuple-element.128.mixed), channel_id=1, source_target_pairs={{0,1},{1,0},{2,3},{3,2},{4,5},{5,4},{6,7},{7,6},{8,9},{9,8},{10,11... | collective-permute-start | bytes 1572872 | tf_op jit(solution)/shard_map/ppermute | solution.py:24
  72.5 15.7 %collective-permute-start.7 = (bf16[256,640]{1,0:T(8,128)(2,1)S(1)}, bf16[256,640]{1,0:T(8,128)(2,1)S(1)}, u32[]{:S(2)}, u32[]{:S(2)}) collective-permute-start(bf16[256,640]{1,0:T(8,128)(2,1)S(1)} %constant_dynamic-slice_fusion.1), channel_id=1, source_target_pairs={{0,1},{1,0},{2,3},{3,2},{4,5},{5,4},{6,7},{7,6},{8,9},{9,8},{10,11... | collective-permute-start | bytes 983048 | tf_op jit(solution)/shard_map/ppermute | solution.py:24
  88.2 16.9 %copy-start.33 = (bf16[256,640]{1,0:T(8,128)(2,1)}, bf16[256,640]{1,0:T(8,128)(2,1)S(1)}, u32[]{:S(2)}) copy-start(bf16[256,640]{1,0:T(8,128)(2,1)S(1)} %collective-permute-done.7.attn_peer) | copy-start | bytes 983044
  88.2 16.9 %copy-start.27 = (bf16[256,1024]{1,0:T(8,128)(2,1)}, bf16[256,1024]{1,0:T(8,128)(2,1)S(1)}, u32[]{:S(2)}) copy-start(bf16[256,1024]{1,0:T(8,128)(2,1)S(1)} %collective-permute-done.6.mixed_peer) | copy-start | bytes 1572868
  88.2 17.2 %copy-start.44 = (bf16[256,1152]{1,0:T(8,128)(2,1)S(1)}, bf16[256,1152]{1,0:T(8,128)(2,1)}, u32[]{:S(2)}) copy-start(bf16[256,1152]{1,0:T(8,128)(2,1)} %get-tuple-element.126) | copy-start | bytes 1769476
  88.2 2.1 collective-permute-start.8
  105.1 19.2 %copy-start.19 = (f32[256,1152]{1,0:T(8,128)S(1)}, f32[256,1152]{1,0:T(8,128)}, u32[]{:S(2)}) copy-start(f32[256,1152]{1,0:T(8,128)} %get-tuple-element.125) | copy-start | bytes 3538948
  105.1 2.3 collective-permute-start.9
  105.4 5.8 %collective-permute-start.4 = (bf16[256,1152]{1,0:T(8,128)(2,1)S(1)}, bf16[256,1152]{1,0:T(8,128)(2,1)S(1)}, u32[]{:S(2)}, u32[]{:S(2)}) collective-permute-start(bf16[256,1152]{1,0:T(8,128)(2,1)S(1)} %copy-done.44), channel_id=1, source_target_pairs={{0,1},{1,0},{2,3},{3,2},{4,5},{5,4},{6,7},{7,6},{8,9},{9,8},{10,11... | collective-permute-start | bytes 1769480 | tf_op jit(solution)/shard_map/ppermute | solution.py:24
  108.8 15.5 %collective-permute-start.10 = (bf16[256,1152]{1,0:T(8,128)(2,1)S(1)}, bf16[256,1152]{1,0:T(8,128)(2,1)S(1)}, u32[]{:S(2)}, u32[]{:S(2)}) collective-permute-start(bf16[256,1152]{1,0:T(8,128)(2,1)S(1)} %add_convert_fusion.1), channel_id=1, source_target_pairs={{0,8},{2,10},{4,12},{6,14},{8,0},{10,2},{12,4},{14,6},{16,24},{18,... | collective-permute-start | bytes 1769480 | tf_op jit(solution)/shard_map/ppermute | solution.py:24
  127.4 2.0 collective-permute-start.11
  127.4 18.1 %collective-permute-start.13 = (bf16[256,1152]{1,0:T(8,128)(2,1)S(1)}, bf16[256,1152]{1,0:T(8,128)(2,1)S(1)}, u32[]{:S(2)}, u32[]{:S(2)}) collective-permute-start(bf16[256,1152]{1,0:T(8,128)(2,1)S(1)} %get-tuple-element.239.refs_1_), channel_id=1, source_target_pairs={{0,8},{2,10},{4,12},{6,14},{8,0},{10,2},{12,4},{14,6},{16,24},{18,... | collective-permute-start | bytes 1769480 | tf_op jit(solution)/shard_map/ppermute | solution.py:24
  145.6 2.1 collective-permute-start.14
  159.2 53.5 %all-to-all-start.2 = ((bf16[16,72,1280]{2,1,0:T(8,128)(2,1)}), bf16[16,72,1280]{2,1,0:T(8,128)(2,1)S(1)}, u32[]{:S(2)}, u32[]{:S(2)}) async-start(bf16[16,72,1280]{2,1,0:T(8,128)(2,1)} %get-tuple-element.140), calls=%async_computation.2 | async-start | bytes 5898240 | tf_op jit(solution)/shard_map/all_to_all | solution.py:1160
  162.9 15.4 %copy-start.42 = (bf16[256,1152]{1,0:T(8,128)(2,1)S(1)}, bf16[256,1152]{1,0:T(8,128)(2,1)}, u32[]{:S(2)}) copy-start(bf16[256,1152]{1,0:T(8,128)(2,1)} %get-tuple-element.136) | copy-start | bytes 1769476
  162.9 15.8 %copy-start.43 = (bf16[8,72,512]{2,1,0:T(8,128)(2,1)S(1)}, bf16[8,72,512]{2,1,0:T(8,128)(2,1)}, u32[]{:S(2)}) copy-start(bf16[8,72,512]{2,1,0:T(8,128)(2,1)} %get-tuple-element.141) | copy-start | bytes 1769476
  178.1 2.3 collective-permute-start.15
  178.3 30.2 %collective-permute-start.12 = (bf16[256,1152]{1,0:T(8,128)(2,1)S(1)}, bf16[256,1152]{1,0:T(8,128)(2,1)S(1)}, u32[]{:S(2)}, u32[]{:S(2)}) collective-permute-start(bf16[256,1152]{1,0:T(8,128)(2,1)S(1)} %copy-done.42), channel_id=1, source_target_pairs={{0,1},{1,0},{2,3},{3,2},{4,5},{5,4},{6,7},{7,6},{8,9},{9,8},{10,11... | collective-permute-start | bytes 1769480 | tf_op jit(solution)/shard_map/ppermute | solution.py:24
  178.7 31.0 %collective-permute-start.17 = (bf16[8,72,512]{2,1,0:T(8,128)(2,1)S(1)}, bf16[8,72,512]{2,1,0:T(8,128)(2,1)S(1)}, u32[]{:S(2)}, u32[]{:S(2)}) collective-permute-start(bf16[8,72,512]{2,1,0:T(8,128)(2,1)S(1)} %copy-done.43), channel_id=1, source_target_pairs={{0,16},{2,18},{4,20},{6,22},{8,24},{10,26},{12,28},{14,30},{16,0},... | collective-permute-start | bytes 1769480 | tf_op jit(solution)/shard_map/ppermute | solution.py:24
  181.7 35.5 %collective-permute-start.16 = (bf16[256,1152]{1,0:T(8,128)(2,1)S(1)}, bf16[256,1152]{1,0:T(8,128)(2,1)}, u32[]{:S(2)}, u32[]{:S(2)}) collective-permute-start(bf16[256,1152]{1,0:T(8,128)(2,1)S(1)} %add_convert_fusion), channel_id=1, source_target_pairs={{0,8},{2,10},{4,12},{6,14},{8,0},{10,2},{12,4},{14,6},{16,24},{18,... | collective-permute-start | bytes 1769480 | tf_op jit(solution)/shard_map/ppermute | solution.py:24
  194.0 56.3 %collective-permute-start.20 = (bf16[8,72,1792]{2,1,0:T(8,128)(2,1)}, bf16[8,72,1792]{2,1,0:T(8,128)(2,1)}, u32[]{:S(2)}, u32[]{:S(2)}) collective-permute-start(bf16[8,72,1792]{2,1,0:T(8,128)(2,1)} %get-tuple-element.152), channel_id=1, source_target_pairs={{0,4},{2,6},{4,0},{6,2},{8,12},{10,14},{12,8},{14,10},{16,20},{18,... | collective-permute-start | bytes 6193160 | tf_op jit(solution)/shard_map/ppermute | solution.py:24
  196.0 12.5 %copy-start.18 = (f32[256,1152]{1,0:T(8,128)S(1)}, f32[256,1152]{1,0:T(8,128)}, u32[]{:S(2)}) copy-start(f32[256,1152]{1,0:T(8,128)} %get-tuple-element.135) | copy-start | bytes 3538948
  207.0 54.9 %collective-permute-start.19 = (bf16[8,72,1792]{2,1,0:T(8,128)(2,1)}, bf16[8,72,1792]{2,1,0:T(8,128)(2,1)}, u32[]{:S(2)}, u32[]{:S(2)}) collective-permute-start(bf16[8,72,1792]{2,1,0:T(8,128)(2,1)} %get-tuple-element.155), channel_id=1, source_target_pairs={{0,2},{2,0},{4,6},{6,4},{8,10},{10,8},{12,14},{14,12},{16,18},{18,... | collective-permute-start | bytes 6193160 | tf_op jit(solution)/shard_map/ppermute | solution.py:24
  230.8 3.8 copy-start.41
  230.8 44.4 %all-to-all-start.3 = ((bf16[16,64,512]{2,1,0:T(8,128)(2,1)}), bf16[16,64,512]{2,1,0:T(8,128)(2,1)S(1)}, u32[]{:S(2)}, u32[]{:S(2)}) async-start(bf16[16,64,512]{2,1,0:T(8,128)(2,1)} %bitcast.77), calls=%async_computation.3 | async-start | bytes 2097152 | tf_op jit(solution)/shard_map/all_to_all | solution.py:1196
  234.6 2.4 collective-permute-start.21
  238.0 7.6 %copy-start.45 = (bf16[4,72,512]{2,1,0:T(8,128)(2,1)S(1)}, bf16[4,72,512]{2,1,0:T(8,128)(2,1)}, u32[]{:S(2)}) copy-start(bf16[4,72,512]{2,1,0:T(8,128)(2,1)} %get-tuple-element.157) | copy-start | bytes 884740
  238.0 11.5 %copy-start.40 = (s32[4]{0:T(128)S(1)}, s32[4]{0:T(128)}, u32[]{:S(2)}) copy-start(s32[4]{0:T(128)} %copy-done.39) | copy-start | bytes 52
  243.8 71.6 %collective-permute-start.23 = (bf16[8,72,1280]{2,1,0:T(8,128)(2,1)}, bf16[8,72,1280]{2,1,0:T(8,128)(2,1)}, u32[]{:S(2)}, u32[]{:S(2)}) collective-permute-start(bf16[8,72,1280]{2,1,0:T(8,128)(2,1)} %get-tuple-element.171), channel_id=1, source_target_pairs={{0,4},{2,6},{4,0},{6,2},{8,12},{10,14},{12,8},{14,10},{16,20},{18,... | collective-permute-start | bytes 4423688 | tf_op jit(solution)/shard_map/ppermute | solution.py:24
  245.6 27.1 %collective-permute-start.18 = (bf16[4,72,512]{2,1,0:T(8,128)(2,1)S(1)}, bf16[4,72,512]{2,1,0:T(8,128)(2,1)S(1)}, u32[]{:S(2)}, u32[]{:S(2)}) collective-permute-start(bf16[4,72,512]{2,1,0:T(8,128)(2,1)S(1)} %copy-done.45), channel_id=1, source_target_pairs={{0,2},{2,0},{4,6},{6,4},{8,10},{10,8},{12,14},{14,12},{16,18},{18,... | collective-permute-start | bytes 884744 | tf_op jit(solution)/shard_map/ppermute | solution.py:24
  247.1 35.1 %collective-permute-start.26 = (bf16[2,72,1280]{2,1,0:T(8,128)(2,1)}, bf16[2,72,1280]{2,1,0:T(8,128)(2,1)S(1)}, u32[]{:S(2)}, u32[]{:S(2)}) collective-permute-start(bf16[2,72,1280]{2,1,0:T(8,128)(2,1)} %get-tuple-element.159), channel_id=1, source_target_pairs={{0,16},{2,18},{4,20},{6,22},{8,24},{10,26},{12,28},{14,30},{16,0},... | collective-permute-start | bytes 1105928 | tf_op jit(solution)/shard_map/ppermute | solution.py:24
  254.0 41.9 %collective-permute-start.25 = (bf16[4,72,1792]{2,1,0:T(8,128)(2,1)}, bf16[4,72,1792]{2,1,0:T(8,128)(2,1)S(1)}, u32[]{:S(2)}, u32[]{:S(2)}) collective-permute-start(bf16[4,72,1792]{2,1,0:T(8,128)(2,1)} %get-tuple-element.173), channel_id=1, source_target_pairs={{0,2},{2,0},{4,6},{6,4},{8,10},{10,8},{12,14},{14,12},{16,18},{18,... | collective-permute-start | bytes 3096584 | tf_op jit(solution)/shard_map/ppermute | solution.py:24
  265.7 43.9 %collective-permute-start.24 = (bf16[4,72,1792]{2,1,0:T(8,128)(2,1)}, bf16[4,72,1792]{2,1,0:T(8,128)(2,1)}, u32[]{:S(2)}, u32[]{:S(2)}) collective-permute-start(bf16[4,72,1792]{2,1,0:T(8,128)(2,1)} %get-tuple-element.175), channel_id=1, source_target_pairs={{0,4},{2,6},{4,0},{6,2},{8,12},{10,14},{12,8},{14,10},{16,20},{18,... | collective-permute-start | bytes 3096584 | tf_op jit(solution)/shard_map/ppermute | solution.py:24
  275.2 44.5 %collective-permute-start.22 = (bf16[2,72,512]{2,1,0:T(8,128)(2,1)}, bf16[2,72,512]{2,1,0:T(8,128)(2,1)}, u32[]{:S(2)}, u32[]{:S(2)}) collective-permute-start(bf16[2,72,512]{2,1,0:T(8,128)(2,1)} %get-tuple-element.177), channel_id=1, source_target_pairs={{0,4},{2,6},{4,0},{6,2},{8,12},{10,14},{12,8},{14,10},{16,20},{18,... | collective-permute-start | bytes 442376 | tf_op jit(solution)/shard_map/ppermute | solution.py:24
  277.0 44.5 %all-to-all-start.4 = ((bf16[16,16,512]{2,1,0:T(8,128)(2,1)}), bf16[16,16,512]{2,1,0:T(8,128)(2,1)S(1)}, u32[]{:S(2)}, u32[]{:S(2)}) async-start(bf16[16,16,512]{2,1,0:T(8,128)(2,1)} %fusion), calls=%async_computation.4 | async-start | bytes 524288 | tf_op jit(solution)/shard_map/all_to_all | solution.py:1226
  299.5 35.4 %collective-permute-start.28 = (bf16[2,72,1792]{2,1,0:T(8,128)(2,1)}, bf16[2,72,1792]{2,1,0:T(8,128)(2,1)S(1)}, u32[]{:S(2)}, u32[]{:S(2)}) collective-permute-start(bf16[2,72,1792]{2,1,0:T(8,128)(2,1)} %get-tuple-element.186), channel_id=1, source_target_pairs={{0,16},{2,18},{4,20},{6,22},{8,24},{10,26},{12,28},{14,30},{16,0},... | collective-permute-start | bytes 1548296 | tf_op jit(solution)/shard_map/ppermute | solution.py:24
  312.2 42.0 %collective-permute-start.33 = (bf16[2,72,1792]{2,1,0:T(8,128)(2,1)}, bf16[2,72,1792]{2,1,0:T(8,128)(2,1)S(1)}, u32[]{:S(2)}, u32[]{:S(2)}) collective-permute-start(bf16[2,72,1792]{2,1,0:T(8,128)(2,1)} %get-tuple-element.188), channel_id=1, source_target_pairs={{0,16},{2,18},{4,20},{6,22},{8,24},{10,26},{12,28},{14,30},{16,0},... | collective-permute-start | bytes 1548296 | tf_op jit(solution)/shard_map/ppermute | solution.py:24
  318.4 23.3 %collective-permute-start.27 = (bf16[4,72,1280]{2,1,0:T(8,128)(2,1)}, bf16[4,72,1280]{2,1,0:T(8,128)(2,1)S(1)}, u32[]{:S(2)}, u32[]{:S(2)}) collective-permute-start(bf16[4,72,1280]{2,1,0:T(8,128)(2,1)} %get-tuple-element.190), channel_id=1, source_target_pairs={{0,2},{2,0},{4,6},{6,4},{8,10},{10,8},{12,14},{14,12},{16,18},{18,... | collective-permute-start | bytes 2211848 | tf_op jit(solution)/shard_map/ppermute | solution.py:24
  322.2 6.5 %copy-start.22 = (f32[2,72,512]{2,1,0:T(8,128)S(1)}, f32[2,72,512]{2,1,0:T(8,128)}, u32[]{:S(2)}) copy-start(f32[2,72,512]{2,1,0:T(8,128)} %shard_map.234) | copy-start | bytes 884740
  328.6 2.5 collective-permute-start.29
  328.7 2.4 collective-permute-start.30
  331.1 56.5 %collective-permute-start.37 = (bf16[72,1792]{1,0:T(8,128)(2,1)}, bf16[72,1792]{1,0:T(8,128)(2,1)}, u32[]{:S(2)}, u32[]{:S(2)}) collective-permute-start(bf16[72,1792]{1,0:T(8,128)(2,1)} %pad_maximum_fusion.7), channel_id=1, source_target_pairs={{0,8},{2,10},{4,12},{6,14},{8,0},{10,2},{12,4},{14,6},{16,24},{18,... | collective-permute-start | bytes 774152 | tf_op jit(solution)/shard_map/ppermute | solution.py:24
  334.9 3.5 copy-start.30
  334.9 14.9 %all-to-all-start.5 = ((bf16[4,160,640]{2,1,0:T(8,128)(2,1)}), bf16[4,160,640]{2,1,0:T(8,128)(2,1)S(1)}, u32[]{:S(2)}, u32[]{:S(2)}) async-start(bf16[4,160,640]{2,1,0:T(8,128)(2,1)} %bitcast.73), calls=%async_computation.5 | async-start | bytes 1638400 | tf_op jit(solution)/shard_map/all_to_all | solution.py:1265
  344.9 27.1 %collective-permute-start.31 = (bf16[2,72,1280]{2,1,0:T(8,128)(2,1)}, bf16[2,72,1280]{2,1,0:T(8,128)(2,1)S(1)}, u32[]{:S(2)}, u32[]{:S(2)}) collective-permute-start(bf16[2,72,1280]{2,1,0:T(8,128)(2,1)} %get-tuple-element.205), channel_id=1, source_target_pairs={{0,16},{2,18},{4,20},{6,22},{8,24},{10,26},{12,28},{14,30},{16,0},... | collective-permute-start | bytes 1105928 | tf_op jit(solution)/shard_map/ppermute | solution.py:24
  352.8 16.9 %collective-permute-start.32 = (bf16[96,640]{1,0:T(8,128)(2,1)}, bf16[96,640]{1,0:T(8,128)(2,1)S(1)}, u32[]{:S(2)}, u32[]{:S(2)}) collective-permute-start(bf16[96,640]{1,0:T(8,128)(2,1)} %get-tuple-element.208), channel_id=1, source_target_pairs={{0,16},{2,18},{4,20},{6,22},{8,24},{10,26},{12,28},{14,30},{16,0},... | collective-permute-start | bytes 368648 | tf_op jit(solution)/shard_map/ppermute | solution.py:24
  358.4 17.6 %copy-start.11 = (f32[2,72,1792]{2,1,0:T(8,128)S(1)}, f32[2,72,1792]{2,1,0:T(8,128)}, u32[]{:S(2)}) copy-start(f32[2,72,1792]{2,1,0:T(8,128)} %shard_map.240) | copy-start | bytes 3096580
  358.4 22.4 %collective-permute-start.35 = (bf16[72,3584]{1,0:T(8,128)(2,1)S(1)}, bf16[72,3584]{1,0:T(8,128)(2,1)S(1)}, u32[]{:S(2)}, u32[]{:S(2)}) collective-permute-start(bf16[72,3584]{1,0:T(8,128)(2,1)S(1)} %pad_maximum_fusion.6), channel_id=1, source_target_pairs={{0,8},{2,10},{4,12},{6,14},{8,0},{10,2},{12,4},{14,6},{16,24},{18,... | collective-permute-start | bytes 1548296 | tf_op jit(solution)/shard_map/ppermute | solution.py:24
  372.7 3.3 copy-start.46
  374.8 10.0 %copy-start.16 = (f32[2,72,1280]{2,1,0:T(8,128)S(1)}, f32[2,72,1280]{2,1,0:T(8,128)}, u32[]{:S(2)}) copy-start(f32[2,72,1280]{2,1,0:T(8,128)} %shard_map.242) | copy-start | bytes 2211844
  375.9 8.9 %collective-permute-start.34 = (bf16[72,1280]{1,0:T(8,128)(2,1)S(1)}, bf16[72,1280]{1,0:T(8,128)(2,1)S(1)}, u32[]{:S(2)}, u32[]{:S(2)}) collective-permute-start(bf16[72,1280]{1,0:T(8,128)(2,1)S(1)} %fusion.11), channel_id=1, source_target_pairs={{0,8},{2,10},{4,12},{6,14},{8,0},{10,2},{12,4},{14,6},{16,24},{18,... | collective-permute-start | bytes 552968 | tf_op jit(solution)/shard_map/ppermute | solution.py:24
  376.0 10.0 %collective-permute-start.36 = (bf16[64,640]{1,0:T(8,128)(2,1)S(1)}, bf16[64,640]{1,0:T(8,128)(2,1)S(1)}, u32[]{:S(2)}, u32[]{:S(2)}) collective-permute-start(bf16[64,640]{1,0:T(8,128)(2,1)S(1)} %copy-done.46), channel_id=1, source_target_pairs={{0,8},{2,10},{4,12},{6,14},{8,0},{10,2},{12,4},{14,6},{16,24},{18,... | collective-permute-start | bytes 245768 | tf_op jit(solution)/shard_map/ppermute | solution.py:24
  386.0 2.7 copy-start.36
  (27 other events, 29.0 us)

commit v6 on v5

--- a/solution.py
+++ b/solution.py
@@ -1177,10 +1177,6 @@
     turns = Turns(up_terms[0])
 
     down_b.step(turns)
-    down_first, down_rest = quad_sum(turns.wait(down_quad))
-    turns.end(down_first)
-    down_a = Chain(down_first, down_rest, beyond)
-
     (
         late, grad_middle, grad_branch_low, grad_query_low, grad_kv, grad_earlier, norm_terms,
         head_terms,
@@ -1196,6 +1192,9 @@
     collected = lax.all_to_all(outward, "seq", 0, 0, tiled=True)
 
     turns.end(outward)
+    down_first, down_rest = quad_sum(turns.wait(down_quad))
+    turns.end(down_first)
+    down_a = Chain(down_first, down_rest, beyond)
     every = swapped + [SPLIT_BIT]
     padded = width // seq_count
     if cores == 2:

time: 399 us -> 400 us (level)
    unnamed x95 -> x93, local copies, waits for them, and re-layouts: 17.7 us -> 17.7 us
  transfers between devices with their start and end apart: 44 -> 44, of which waited for: 20 -> 19; matrix products, arithmetic and copies ran while one was open for 8% -> 8% of each run, Pallas kernels for 35% -> 35%
where the time goes in v6:
time: 400 us; the launch traced here: 395 us
  Pallas kernels  178 us (44%)
  waiting for transfers between devices  93.6 us (23%)
  starting transfers between devices  63.9 us (16%)
  local copies, waits for them, and re-layouts  38.7 us (10%)
  other arithmetic  19.2 us (5%)
    ppermute x38, waiting for transfers between devices, swap(): return lax.ppermute(value, axis, [(i, i ^ mask) for i in range(count)])  71.9 us
    ppermute x38, starting transfers between devices, swap(): return lax.ppermute(value, axis, [(i, i ^ mask) for i in range(count)])  35 us
    pallas_call x13, Pallas kernels, step_of(): pl.pallas_call(step_kernel, out_shape=[shape] * parts, in_specs=[VMEM] *...  32.7 us
    pallas_call x3, Pallas kernels, weight_terms(): pl.pallas_call(functools.partial(weight_kernel, n, pieces), out_shape=[ja...  32.3 us
    pallas_call x2, Pallas kernels, ffn_backward(): pl.pallas_call(functools.partial(ffn_backward_kernel, n), out_shape=[jax....  30.4 us
    pallas_call x2, Pallas kernels, ffn_forward(): pl.pallas_call(functools.partial(ffn_forward_kernel, n, overlap), out_sha...  28.4 us
    unnamed x93, local copies, waits for them, and re-layouts  17.7 us
    pallas_call x1, Pallas kernels, attention_back(): pl.pallas_call(functools.partial(attention_back_kernel, hops, chunk, core...  13.5 us
  transfers between devices with their start and end apart: 44, of which 19 were waited for; matrix products, arithmetic and copies ran while one was open for 8% of the time, Pallas kernels for 35%

profile of v6, /device:TPU:0, one launch (start us, length us, event | category | flops | bytes accessed | tf_op | source)
XLA Modules:
  0.0 395.3 jit_solution(5037799298861863446)
XLA Ops:
  8.4 3.0 shard_map.213
  11.5 8.3 %all-to-all-start = ((bf16[16,16,512]{2,1,0:T(8,128)(2,1)}), bf16[16,16,512]{2,1,0:T(8,128)(2,1)S(1)}, u32[]{:S(2)}, u32[]{:S(2)}) async-start(bf16[16,16,512]{2,1,0:T(8,128)(2,1)} %bitcast.74), calls=%async_computation | async-start | bytes 524288 | tf_op jit(solution)/shard_map/all_to_all | solution.py:1071
  23.6 6.3 %all-to-all-done = bf16[16,16,512]{2,1,0:T(8,128)(2,1)S(1)} async-done(((bf16[16,16,512]{2,1,0:T(8,128)(2,1)}), bf16[16,16,512]{2,1,0:T(8,128)(2,1)S(1)}, u32[]{:S(2)}, u32[]{:S(2)}) %all-to-all-start) | async-done | bytes 262176 | tf_op jit(solution)/shard_map/all_to_all | solution.py:1071
  31.5 3.9 all-to-all-start.1
  36.0 4.1 %shard_map.214 = (f32[256,1024]{1,0:T(8,128)}, bf16[256,1024]{1,0:T(8,128)(2,1)}) custom-call(s32[1]{0:T(128)} %bitcast.2.core, bf16[256,1152]{1,0:T(8,128)(2,1)} %get-tuple-element.117.attn_in.refs_5_, bf16[576,1024]{1,0:T(8,128)(2,1)} %refs_0_.1, bf16[576,1024]{1,0:T(8,128)(2,1)} %collective-permute-done.1.refs_1_, f32[2,256]{1,0:T(2,128)} %refs_14_.1, ...), custom_call_target="tpu_custom_call" | custom-call | flops 1024 | bytes 1024 | tf_op jit(solution)/shard_map/pallas_call | solution.py:653
  40.0 1.6 pad_maximum_fusion
  41.7 1.7 maximum_select_fusion
  43.6 2.2 pad_maximum_fusion.1.w_out
  45.9 13.1 %all-to-all-done.1 = bf16[16,64,512]{2,1,0:T(8,128)(2,1)S(1)} async-done(((bf16[16,64,512]{2,1,0:T(8,128)(2,1)}), bf16[16,64,512]{2,1,0:T(8,128)(2,1)S(1)}, u32[]{:S(2)}, u32[]{:S(2)}) %all-to-all-start.1) | async-done | bytes 1048608 | tf_op jit(solution)/shard_map/all_to_all | solution.py:1075
  60.0 9.3 %shard_map.215 = (bf16[256,1024]{1,0:T(8,128)(2,1)}, f32[256,1152]{1,0:T(8,128)}, f32[256,1152]{1,0:T(8,128)}, bf16[256,1152]{1,0:T(8,128)(2,1)}) custom-call(s32[1]{0:T(128)} %bitcast.place, s32[2,8]{1,0:T(2,128)} %bitcast.79, bf16[256,1024]{1,0:T(8,128)(2,1)} %get-tuple-element.120.query, bf16[256,512]{1,0:T(8,128)(2,1)} %get-tuple-element.118.kv_local, ...), custom_call_target="tpu_custom_call" | custom-call | flops 1024 | bytes 1024 | tf_op jit(solution)/shard_map/pallas_call | solution.py:891
  69.3 3.0 collective-permute-start.5
  73.7 14.5 %shard_map.216 = (bf16[512,1792]{1,0:T(8,128)(2,1)}, bf16[512,1792]{1,0:T(8,128)(2,1)}, bf16[512,1792]{1,0:T(8,128)(2,1)}, f32[256,1152]{1,0:T(8,128)}, bf16[256,1152]{1,0:T(8,128)(2,1)}) custom-call(s32[1]{0:T(128)} %bitcast.14.refs_0_, bf16[256,1152]{1,0:T(8,128)(2,1)} %get-tuple-element.124.refs_1_, bf16[256,1152]{1,0:T(8,128)(2,1)} %copy-done.3, ...), custom_call_target="tpu_custom_call" | custom-call | flops 1024 | bytes 1024 | tf_op jit(solution)/shard_map/pallas_call | solution.py:300
  88.6 1.8 collective-permute-done.8.refs_2_.refs_4_
  91.2 14.0 %shard_map.217 = (bf16[512,1792]{1,0:T(8,128)(2,1)}, bf16[512,1792]{1,0:T(8,128)(2,1)}, bf16[512,1792]{1,0:T(8,128)(2,1)}, f32[256,1152]{1,0:T(8,128)}, bf16[256,1152]{1,0:T(8,128)(2,1)}) custom-call(s32[1]{0:T(128)} %bitcast.14.refs_0_, bf16[256,1152]{1,0:T(8,128)(2,1)} %copy-done.4, bf16[256,1152]{1,0:T(8,128)(2,1)} %copy-done.5, ...), custom_call_target="tpu_custom_call" | custom-call | flops 1024 | bytes 1024 | tf_op jit(solution)/shard_map/pallas_call | solution.py:300
  105.8 1.7 collective-permute-done.9
  108.8 1.7 collective-permute-start.10
  111.2 13.1 %collective-permute-done.10 = bf16[256,1152]{1,0:T(8,128)(2,1)S(1)} collective-permute-done((bf16[256,1152]{1,0:T(8,128)(2,1)S(1)}, bf16[256,1152]{1,0:T(8,128)(2,1)S(1)}, u32[]{:S(2)}, u32[]{:S(2)}) %collective-permute-start.10) | collective-permute-done | bytes 589856 | tf_op jit(solution)/shard_map/ppermute | solution.py:24
  130.3 15.3 %shard_map.218 = (bf16[512,1792]{1,0:T(8,128)(2,1)}, bf16[512,1792]{1,0:T(8,128)(2,1)}, f32[256,1152]{1,0:T(8,128)}, bf16[256,1152]{1,0:T(8,128)(2,1)}) custom-call(s32[1]{0:T(128)} %bitcast.14.refs_0_, bf16[256,1152]{1,0:T(8,128)(2,1)} %copy-done.7, bf16[256,1152]{1,0:T(8,128)(2,1)} %copy-done.14, bf16[512,1792]{1,0:T(8,128)(2,1)} %get-tuple-element.133.refs_3_, ...), custom_call_target="tpu_custom_call" | custom-call | flops 1024 | bytes 1024 | tf_op jit(solution)/shard_map/pallas_call | solution.py:368
  145.8 1.9 collective-permute-done.14.refs_4_.refs_2_
  148.5 10.6 %shard_map.219 = (bf16[16,72,1280]{2,1,0:T(8,128)(2,1)}, bf16[8,72,512]{2,1,0:T(8,128)(2,1)}, bf16[8,72,512]{2,1,0:T(8,128)(2,1)}) custom-call(s32[1]{0:T(128)} %bitcast.4.own.refs_0_, bf16[256,1152]{1,0:T(8,128)(2,1)} %copy-done.7, bf16[256,1152]{1,0:T(8,128)(2,1)} %copy-done.14, bf16[256,1152]{1,0:T(8,128)(2,1)} %copy-done.13, ...), custom_call_target="tpu_custom_call" | custom-call | flops 1024 | bytes 1024 | tf_op jit(solution)/shard_map/pallas_call | solution.py:447
  159.1 3.7 all-to-all-start.3
  162.8 15.2 %shard_map.220 = (bf16[512,1792]{1,0:T(8,128)(2,1)}, bf16[512,1792]{1,0:T(8,128)(2,1)}, f32[256,1152]{1,0:T(8,128)}, bf16[256,1152]{1,0:T(8,128)(2,1)}) custom-call(s32[1]{0:T(128)} %bitcast.14.refs_0_, bf16[256,1152]{1,0:T(8,128)(2,1)} %copy-done.13, bf16[256,1152]{1,0:T(8,128)(2,1)} %copy-done.15, bf16[512,1792]{1,0:T(8,128)(2,1)} %get-tuple-element.144.refs_3_, ...), custom_call_target="tpu_custom_call" | custom-call | flops 1024 | bytes 1024 | tf_op jit(solution)/shard_map/pallas_call | solution.py:368
  183.2 10.8 %shard_map.221 = (bf16[8,72,1792]{2,1,0:T(8,128)(2,1)}, bf16[8,72,1792]{2,1,0:T(8,128)(2,1)}) custom-call(s32[1]{0:T(128)} %bitcast.4.own.refs_0_, bf16[256,1152]{1,0:T(8,128)(2,1)} %get-tuple-element.124.refs_1_, bf16[256,1152]{1,0:T(8,128)(2,1)} %copy-done.3, bf16[256,1152]{1,0:T(8,128)(2,1)} %copy-done.4, bf16[256,1152]{1,0:T(8,128)(2,1)} %copy-done.5, ...), custom_call_target="tpu_custom_call" | custom-call | flops 1024 | bytes 1024 | tf_op jit(solution)/shard_map/pallas_call | solution.py:447
  194.1 2.0 collective-permute-start.20
  196.1 10.9 %shard_map.222 = (bf16[8,72,1792]{2,1,0:T(8,128)(2,1)}, bf16[8,72,1792]{2,1,0:T(8,128)(2,1)}) custom-call(s32[1]{0:T(128)} %bitcast.4.own.refs_0_, bf16[256,1152]{1,0:T(8,128)(2,1)} %get-tuple-element.124.refs_1_, bf16[256,1152]{1,0:T(8,128)(2,1)} %copy-done.3, bf16[256,1152]{1,0:T(8,128)(2,1)} %copy-done.4, bf16[256,1152]{1,0:T(8,128)(2,1)} %copy-done.5, ...), custom_call_target="tpu_custom_call" | custom-call | flops 1024 | bytes 1024 | tf_op jit(solution)/shard_map/pallas_call | solution.py:447
  210.5 2.1 shard_map.223
  213.4 13.5 %shard_map.224 = (bf16[256,1664]{1,0:T(8,128)(2,1)}, f32[256,1152]{1,0:T(8,128)}, bf16[256,1152]{1,0:T(8,128)(2,1)}, bf16[256,1024]{1,0:T(8,128)(2,1)}, f32[256,...) custom-call(s32[1]{0:T(128)} %bitcast.2.core, s32[1]{0:T(128)} %bitcast.place, ...), custom_call_target="tpu_custom_call" | custom-call | flops 1024 | bytes 1024 | tf_op jit(solution)/shard_map/pallas_call | solution.py:973
  227.0 4.4 %all-to-all-start.2 = ((bf16[16,64,512]{2,1,0:T(8,128)(2,1)}), bf16[16,64,512]{2,1,0:T(8,128)(2,1)}, u32[]{:S(2)}, u32[]{:S(2)}) async-start(bf16[16,64,512]{2,1,0:T(8,128)(2,1)} %bitcast.76), calls=%async_computation.2 | async-start | bytes 2097152 | tf_op jit(solution)/shard_map/all_to_all | solution.py:1192
  231.4 2.9 shard_map.225
  235.3 5.7 %shard_map.226 = (bf16[8,72,1280]{2,1,0:T(8,128)(2,1)}, bf16[8,72,1280]{2,1,0:T(8,128)(2,1)}) custom-call(s32[1]{0:T(128)} %bitcast.4.own.refs_0_, s32[1]{0:T(128)} %bitcast.2.core, bf16[256,1024]{1,0:T(8,128)(2,1)} %get-tuple-element.128.mixed, bf16[256,1024]{1,0:T(8,128)(2,1)} %copy-done.28, bf16[256,1152]{1,0:T(8,128)(2,1)} %get-tuple-element.166.branch, ...), custom_call_target="tpu_custom_call" | custom-call | flops 1024 | bytes 1024 | tf_op jit(solution)/shard_map/pallas_call | solution.py:565
  241.0 1.7 collective-permute-start.23
  244.2 2.4 collective-permute-start.26
  248.6 3.8 shard_map.227
  254.1 9.4 %collective-permute-done.19.got = bf16[8,72,1792]{2,1,0:T(8,128)(2,1)} collective-permute-done((bf16[8,72,1792]{2,1,0:T(8,128)(2,1)}, bf16[8,72,1792]{2,1,0:T(8,128)(2,1)}, u32[]{:S(2)}, u32[]{:S(2)}) %collective-permute-start.19) | collective-permute-done | bytes 2064416 | tf_op jit(solution)/shard_map/ppermute | solution.py:24
  263.5 3.9 shard_map.228
  267.4 5.3 %collective-permute-done.18.got = bf16[4,72,512]{2,1,0:T(8,128)(2,1)S(1)} collective-permute-done((bf16[4,72,512]{2,1,0:T(8,128)(2,1)S(1)}, bf16[4,72,512]{2,1,0:T(8,128)(2,1)S(1)}, u32[]{:S(2)}, u32[]{:S(2)}) %collective-permute-start.18) | collective-permute-done | bytes 294944 | tf_op jit(solution)/shard_map/ppermute | solution.py:24
  273.4 1.8 shard_map.229
  275.2 2.0 gather_fusion.3
  278.3 5.2 %all-to-all-start.4 = ((bf16[16,16,512]{2,1,0:T(8,128)(2,1)}), bf16[16,16,512]{2,1,0:T(8,128)(2,1)S(1)}, u32[]{:S(2)}, u32[]{:S(2)}) async-start(bf16[16,16,512]{2,1,0:T(8,128)(2,1)} %fusion), calls=%async_computation.4 | async-start | bytes 524288 | tf_op jit(solution)/shard_map/all_to_all | solution.py:1225
  284.3 2.0 shard_map.230
  288.4 7.6 %collective-permute-done.25.got = bf16[4,72,1792]{2,1,0:T(8,128)(2,1)} collective-permute-done((bf16[4,72,1792]{2,1,0:T(8,128)(2,1)}, bf16[4,72,1792]{2,1,0:T(8,128)(2,1)}, u32[]{:S(2)}, u32[]{:S(2)}) %collective-permute-start.25) | collective-permute-done | bytes 1032224 | tf_op jit(solution)/shard_map/ppermute | solution.py:24
  295.9 2.7 shard_map.231
  299.5 10.2 %collective-permute-done.24.got = bf16[4,72,1792]{2,1,0:T(8,128)(2,1)} collective-permute-done((bf16[4,72,1792]{2,1,0:T(8,128)(2,1)}, bf16[4,72,1792]{2,1,0:T(8,128)(2,1)}, u32[]{:S(2)}, u32[]{:S(2)}) %collective-permute-start.24) | collective-permute-done | bytes 1032224 | tf_op jit(solution)/shard_map/ppermute | solution.py:24
  309.6 2.6 shard_map.232
  314.7 3.1 shard_map.233
  317.8 1.9 collective-permute-start.27
  320.4 1.7 shard_map.234
  322.9 6.5 %shard_map.235 = (f32[256,1152]{1,0:T(8,128)}, f32[512,640]{1,0:T(8,128)}, bf16[512,640]{1,0:T(8,128)(2,1)}, f32[16,1152]{1,0:T(8,128)}) custom-call(s32[1]{0:T(128)} %bitcast.2.core, bf16[576,1024]{1,0:T(8,128)(2,1)} %refs_0_.1, bf16[576,1024]{1,0:T(8,128)(2,1)} %collective-permute-done.1.refs_1_, bf16[576,512]{1,0:T(8,128)(2,1)} %copy-done.10, ...), custom_call_target="tpu_custom_call" | custom-call | flops 1024 | bytes 1024 | tf_op jit(solution)/shard_map/pallas_call | solution.py:710
  333.2 2.6 shard_map.236
  335.8 3.5 all-to-all-start.5
  339.3 2.3 shard_map.237
  344.6 2.3 shard_map.238
  346.9 1.6 collective-permute-start.31
  348.5 2.2 all-to-all-done.5
  351.6 2.0 shard_map.239
  353.7 1.6 collective-permute-start.32
  356.1 2.3 shard_map.240
  361.1 10.6 %collective-permute-done.32.refs_1_ = bf16[96,640]{1,0:T(8,128)(2,1)S(1)} collective-permute-done((bf16[96,640]{1,0:T(8,128)(2,1)}, bf16[96,640]{1,0:T(8,128)(2,1)S(1)}, u32[]{:S(2)}, u32[]{:S(2)}) %collective-permute-start.32) | collective-permute-done | bytes 122912 | tf_op jit(solution)/shard_map/ppermute | solution.py:24
  372.3 1.6 shard_map.241
  374.7 2.1 shard_map.242
  378.0 2.1 collective-permute-start.36
  380.0 2.7 collective-permute-done.35
  382.7 3.6 collective-permute-done.34
  390.1 1.6 shard_map.243
  (211 shorter events, 72.9 us)
Async XLA Ops:
  0.6 4.5 %copy-start.39 = (s32[1,16]{1,0:T(1,128)S(1)}, s32[1,16]{1,0:T(1,128)}, u32[]{:S(2)}) copy-start(s32[1,16]{1,0:T(1,128)} %param.16) | copy-start | bytes 196
  2.6 3.6 copy-start.10
  2.6 4.9 %collective-permute-start = (bf16[576,512]{1,0:T(8,128)(2,1)S(1)}, bf16[576,512]{1,0:T(8,128)(2,1)S(1)}, u32[]{:S(2)}, u32[]{:S(2)}) collective-permute-start(bf16[576,512]{1,0:T(8,128)(2,1)S(1)} %constant_dynamic-update-slice_fusion.refs_0_.refs_2_), channel_id=1, source_target_pairs={{0,1},{1,0},{2,3},{3,2},{4,5},{5,4},{6,7},{7,6},{8,9},{9,8},{10,11... | collective-permute-start | bytes 1769480 | tf_op jit(solution)/shard_map/ppermute | solution.py:24
  7.6 12.2 %copy-start.18 = (bf16[1024,576]{0,1:T(8,128)(2,1)S(1)}, bf16[1024,576]{0,1:T(8,128)(2,1)}, u32[]{:S(2)}) copy-start(bf16[1024,576]{0,1:T(8,128)(2,1)} %param.20) | copy-start | bytes 3538948
  11.4 24.6 %collective-permute-start.1 = (bf16[576,1024]{1,0:T(8,128)(2,1)}, bf16[576,1024]{1,0:T(8,128)(2,1)}, u32[]{:S(2)}, u32[]{:S(2)}) collective-permute-start(bf16[576,1024]{1,0:T(8,128)(2,1)} %refs_0_.1), channel_id=1, source_target_pairs={{0,1},{1,0},{2,3},{3,2},{4,5},{5,4},{6,7},{7,6},{8,9},{9,8},{10,11... | collective-permute-start | bytes 3538952 | tf_op jit(solution)/shard_map/ppermute | solution.py:24
  11.5 18.4 %all-to-all-start = ((bf16[16,16,512]{2,1,0:T(8,128)(2,1)}), bf16[16,16,512]{2,1,0:T(8,128)(2,1)S(1)}, u32[]{:S(2)}, u32[]{:S(2)}) async-start(bf16[16,16,512]{2,1,0:T(8,128)(2,1)} %bitcast.74), calls=%async_computation | async-start | bytes 524288 | tf_op jit(solution)/shard_map/all_to_all | solution.py:1071
  21.9 18.1 %collective-permute-start.2 = (bf16[1024,640]{1,0:T(8,128)(2,1)S(1)}, bf16[1024,640]{1,0:T(8,128)(2,1)}, u32[]{:S(2)}, u32[]{:S(2)}) collective-permute-start(bf16[1024,640]{1,0:T(8,128)(2,1)S(1)} %get-tuple-element.238), channel_id=1, source_target_pairs={{0,1},{1,0},{2,3},{3,2},{4,5},{5,4},{6,7},{7,6},{8,9},{9,8},{10,11... | collective-permute-start | bytes 3932168 | tf_op jit(solution)/shard_map/ppermute | solution.py:24
  31.5 27.5 %all-to-all-start.1 = ((bf16[16,64,512]{2,1,0:T(8,128)(2,1)}), bf16[16,64,512]{2,1,0:T(8,128)(2,1)S(1)}, u32[]{:S(2)}, u32[]{:S(2)}) async-start(bf16[16,64,512]{2,1,0:T(8,128)(2,1)} %bitcast.71), calls=%async_computation.1 | async-start | bytes 2097152 | tf_op jit(solution)/shard_map/all_to_all | solution.py:1075
  60.0 12.5 %copy-start.2 = (bf16[256,1152]{1,0:T(8,128)(2,1)S(1)}, bf16[256,1152]{1,0:T(8,128)(2,1)}, u32[]{:S(2)}) copy-start(bf16[256,1152]{1,0:T(8,128)(2,1)} %get-tuple-element.117.attn_in.refs_5_) | copy-start | bytes 1769476
  69.3 3.6 collective-permute-start.3
  69.3 19.0 %collective-permute-start.5 = (bf16[256,1152]{1,0:T(8,128)(2,1)}, bf16[256,1152]{1,0:T(8,128)(2,1)S(1)}, u32[]{:S(2)}, u32[]{:S(2)}) collective-permute-start(bf16[256,1152]{1,0:T(8,128)(2,1)} %get-tuple-element.124.refs_1_), channel_id=1, source_target_pairs={{0,8},{2,10},{4,12},{6,14},{8,0},{10,2},{12,4},{14,6},{16,24},{18,... | collective-permute-start | bytes 1769480 | tf_op jit(solution)/shard_map/ppermute | solution.py:24
  72.3 15.9 %collective-permute-start.6 = (bf16[256,1024]{1,0:T(8,128)(2,1)}, bf16[256,1024]{1,0:T(8,128)(2,1)S(1)}, u32[]{:S(2)}, u32[]{:S(2)}) collective-permute-start(bf16[256,1024]{1,0:T(8,128)(2,1)} %get-tuple-element.128.mixed), channel_id=1, source_target_pairs={{0,1},{1,0},{2,3},{3,2},{4,5},{5,4},{6,7},{7,6},{8,9},{9,8},{10,11... | collective-permute-start | bytes 1572872 | tf_op jit(solution)/shard_map/ppermute | solution.py:24
  72.5 15.7 %collective-permute-start.7 = (bf16[256,640]{1,0:T(8,128)(2,1)S(1)}, bf16[256,640]{1,0:T(8,128)(2,1)S(1)}, u32[]{:S(2)}, u32[]{:S(2)}) collective-permute-start(bf16[256,640]{1,0:T(8,128)(2,1)S(1)} %constant_dynamic-slice_fusion.1), channel_id=1, source_target_pairs={{0,1},{1,0},{2,3},{3,2},{4,5},{5,4},{6,7},{7,6},{8,9},{9,8},{10,11... | collective-permute-start | bytes 983048 | tf_op jit(solution)/shard_map/ppermute | solution.py:24
  88.2 16.9 %copy-start.33 = (bf16[256,640]{1,0:T(8,128)(2,1)}, bf16[256,640]{1,0:T(8,128)(2,1)S(1)}, u32[]{:S(2)}) copy-start(bf16[256,640]{1,0:T(8,128)(2,1)S(1)} %collective-permute-done.7.attn_peer) | copy-start | bytes 983044
  88.2 16.9 %copy-start.28 = (bf16[256,1024]{1,0:T(8,128)(2,1)}, bf16[256,1024]{1,0:T(8,128)(2,1)S(1)}, u32[]{:S(2)}) copy-start(bf16[256,1024]{1,0:T(8,128)(2,1)S(1)} %collective-permute-done.6.mixed_peer) | copy-start | bytes 1572868
  88.3 2.1 copy-start.4
  88.3 17.2 %copy-start.42 = (bf16[256,1152]{1,0:T(8,128)(2,1)S(1)}, bf16[256,1152]{1,0:T(8,128)(2,1)}, u32[]{:S(2)}) copy-start(bf16[256,1152]{1,0:T(8,128)(2,1)} %get-tuple-element.126) | copy-start | bytes 1769476
  88.3 2.1 collective-permute-start.8
  105.2 19.2 %copy-start.20 = (f32[256,1152]{1,0:T(8,128)S(1)}, f32[256,1152]{1,0:T(8,128)}, u32[]{:S(2)}) copy-start(f32[256,1152]{1,0:T(8,128)} %get-tuple-element.125) | copy-start | bytes 3538948
  105.2 2.3 collective-permute-start.9
  105.5 5.8 %collective-permute-start.4 = (bf16[256,1152]{1,0:T(8,128)(2,1)S(1)}, bf16[256,1152]{1,0:T(8,128)(2,1)S(1)}, u32[]{:S(2)}, u32[]{:S(2)}) collective-permute-start(bf16[256,1152]{1,0:T(8,128)(2,1)S(1)} %copy-done.42), channel_id=1, source_target_pairs={{0,1},{1,0},{2,3},{3,2},{4,5},{5,4},{6,7},{7,6},{8,9},{9,8},{10,11... | collective-permute-start | bytes 1769480 | tf_op jit(solution)/shard_map/ppermute | solution.py:24
  108.8 15.5 %collective-permute-start.10 = (bf16[256,1152]{1,0:T(8,128)(2,1)S(1)}, bf16[256,1152]{1,0:T(8,128)(2,1)S(1)}, u32[]{:S(2)}, u32[]{:S(2)}) collective-permute-start(bf16[256,1152]{1,0:T(8,128)(2,1)S(1)} %add_convert_fusion.1), channel_id=1, source_target_pairs={{0,8},{2,10},{4,12},{6,14},{8,0},{10,2},{12,4},{14,6},{16,24},{18,... | collective-permute-start | bytes 1769480 | tf_op jit(solution)/shard_map/ppermute | solution.py:24
  127.5 2.0 collective-permute-start.11
  127.5 18.1 %collective-permute-start.13 = (bf16[256,1152]{1,0:T(8,128)(2,1)S(1)}, bf16[256,1152]{1,0:T(8,128)(2,1)S(1)}, u32[]{:S(2)}, u32[]{:S(2)}) collective-permute-start(bf16[256,1152]{1,0:T(8,128)(2,1)S(1)} %get-tuple-element.239.refs_1_), channel_id=1, source_target_pairs={{0,8},{2,10},{4,12},{6,14},{8,0},{10,2},{12,4},{14,6},{16,24},{18,... | collective-permute-start | bytes 1769480 | tf_op jit(solution)/shard_map/ppermute | solution.py:24
  145.6 2.1 collective-permute-start.14
  159.1 67.9 %all-to-all-start.3 = ((bf16[16,72,1280]{2,1,0:T(8,128)(2,1)}), bf16[16,72,1280]{2,1,0:T(8,128)(2,1)S(1)}, u32[]{:S(2)}, u32[]{:S(2)}) async-start(bf16[16,72,1280]{2,1,0:T(8,128)(2,1)} %get-tuple-element.140), calls=%async_computation.3 | async-start | bytes 5898240 | tf_op jit(solution)/shard_map/all_to_all | solution.py:1160
  162.8 15.4 %copy-start.40 = (bf16[256,1152]{1,0:T(8,128)(2,1)S(1)}, bf16[256,1152]{1,0:T(8,128)(2,1)}, u32[]{:S(2)}) copy-start(bf16[256,1152]{1,0:T(8,128)(2,1)} %get-tuple-element.136) | copy-start | bytes 1769476
  162.8 15.8 %copy-start.41 = (bf16[8,72,512]{2,1,0:T(8,128)(2,1)S(1)}, bf16[8,72,512]{2,1,0:T(8,128)(2,1)}, u32[]{:S(2)}) copy-start(bf16[8,72,512]{2,1,0:T(8,128)(2,1)} %get-tuple-element.141) | copy-start | bytes 1769476
  178.0 2.3 collective-permute-start.15
  178.2 30.3 %collective-permute-start.12 = (bf16[256,1152]{1,0:T(8,128)(2,1)S(1)}, bf16[256,1152]{1,0:T(8,128)(2,1)S(1)}, u32[]{:S(2)}, u32[]{:S(2)}) collective-permute-start(bf16[256,1152]{1,0:T(8,128)(2,1)S(1)} %copy-done.40), channel_id=1, source_target_pairs={{0,1},{1,0},{2,3},{3,2},{4,5},{5,4},{6,7},{7,6},{8,9},{9,8},{10,11... | collective-permute-start | bytes 1769480 | tf_op jit(solution)/shard_map/ppermute | solution.py:24
  178.6 31.1 %collective-permute-start.17 = (bf16[8,72,512]{2,1,0:T(8,128)(2,1)S(1)}, bf16[8,72,512]{2,1,0:T(8,128)(2,1)S(1)}, u32[]{:S(2)}, u32[]{:S(2)}) collective-permute-start(bf16[8,72,512]{2,1,0:T(8,128)(2,1)S(1)} %copy-done.41), channel_id=1, source_target_pairs={{0,16},{2,18},{4,20},{6,22},{8,24},{10,26},{12,28},{14,30},{16,0},... | collective-permute-start | bytes 1769480 | tf_op jit(solution)/shard_map/ppermute | solution.py:24
  181.7 30.9 %collective-permute-start.16 = (bf16[256,1152]{1,0:T(8,128)(2,1)S(1)}, bf16[256,1152]{1,0:T(8,128)(2,1)S(1)}, u32[]{:S(2)}, u32[]{:S(2)}) collective-permute-start(bf16[256,1152]{1,0:T(8,128)(2,1)S(1)} %add_convert_fusion), channel_id=1, source_target_pairs={{0,8},{2,10},{4,12},{6,14},{8,0},{10,2},{12,4},{14,6},{16,24},{18,... | collective-permute-start | bytes 1769480 | tf_op jit(solution)/shard_map/ppermute | solution.py:24
  194.1 54.6 %collective-permute-start.20 = (bf16[8,72,1792]{2,1,0:T(8,128)(2,1)}, bf16[8,72,1792]{2,1,0:T(8,128)(2,1)}, u32[]{:S(2)}, u32[]{:S(2)}) collective-permute-start(bf16[8,72,1792]{2,1,0:T(8,128)(2,1)} %get-tuple-element.152), channel_id=1, source_target_pairs={{0,4},{2,6},{4,0},{6,2},{8,12},{10,14},{12,8},{14,10},{16,20},{18,... | collective-permute-start | bytes 6193160 | tf_op jit(solution)/shard_map/ppermute | solution.py:24
  196.1 12.4 %copy-start.19 = (f32[256,1152]{1,0:T(8,128)S(1)}, f32[256,1152]{1,0:T(8,128)}, u32[]{:S(2)}) copy-start(f32[256,1152]{1,0:T(8,128)} %get-tuple-element.135) | copy-start | bytes 3538948
  207.0 56.5 %collective-permute-start.19 = (bf16[8,72,1792]{2,1,0:T(8,128)(2,1)}, bf16[8,72,1792]{2,1,0:T(8,128)(2,1)}, u32[]{:S(2)}, u32[]{:S(2)}) collective-permute-start(bf16[8,72,1792]{2,1,0:T(8,128)(2,1)} %get-tuple-element.155), channel_id=1, source_target_pairs={{0,2},{2,0},{4,6},{6,4},{8,10},{10,8},{12,14},{14,12},{16,18},{18,... | collective-permute-start | bytes 6193160 | tf_op jit(solution)/shard_map/ppermute | solution.py:24
  227.0 4.5 %copy-start = (bf16[16,72,1280]{2,1,0:T(8,128)(2,1)}, bf16[16,72,1280]{2,1,0:T(8,128)(2,1)S(1)}, u32[]{:S(2)}) copy-start(bf16[16,72,1280]{2,1,0:T(8,128)(2,1)S(1)} %all-to-all-done.3.got) | copy-start | bytes 8847364
  227.0 48.2 %all-to-all-start.2 = ((bf16[16,64,512]{2,1,0:T(8,128)(2,1)}), bf16[16,64,512]{2,1,0:T(8,128)(2,1)}, u32[]{:S(2)}, u32[]{:S(2)}) async-start(bf16[16,64,512]{2,1,0:T(8,128)(2,1)} %bitcast.76), calls=%async_computation.2 | async-start | bytes 2097152 | tf_op jit(solution)/shard_map/all_to_all | solution.py:1192
  231.3 3.0 collective-permute-start.21
  235.3 7.4 %copy-start.44 = (bf16[4,72,512]{2,1,0:T(8,128)(2,1)S(1)}, bf16[4,72,512]{2,1,0:T(8,128)(2,1)}, u32[]{:S(2)}) copy-start(bf16[4,72,512]{2,1,0:T(8,128)(2,1)} %get-tuple-element.157) | copy-start | bytes 884740
  235.3 8.9 %copy-start.43 = (bf16[2,72,1280]{2,1,0:T(8,128)(2,1)S(1)}, bf16[2,72,1280]{2,1,0:T(8,128)(2,1)}, u32[]{:S(2)}) copy-start(bf16[2,72,1280]{2,1,0:T(8,128)(2,1)} %get-tuple-element.169) | copy-start | bytes 1105924
  241.0 72.6 %collective-permute-start.23 = (bf16[8,72,1280]{2,1,0:T(8,128)(2,1)}, bf16[8,72,1280]{2,1,0:T(8,128)(2,1)S(1)}, u32[]{:S(2)}, u32[]{:S(2)}) collective-permute-start(bf16[8,72,1280]{2,1,0:T(8,128)(2,1)} %get-tuple-element.171), channel_id=1, source_target_pairs={{0,4},{2,6},{4,0},{6,2},{8,12},{10,14},{12,8},{14,10},{16,20},{18,... | collective-permute-start | bytes 4423688 | tf_op jit(solution)/shard_map/ppermute | solution.py:24
  242.7 30.0 %collective-permute-start.18 = (bf16[4,72,512]{2,1,0:T(8,128)(2,1)S(1)}, bf16[4,72,512]{2,1,0:T(8,128)(2,1)S(1)}, u32[]{:S(2)}, u32[]{:S(2)}) collective-permute-start(bf16[4,72,512]{2,1,0:T(8,128)(2,1)S(1)} %copy-done.44), channel_id=1, source_target_pairs={{0,2},{2,0},{4,6},{6,4},{8,10},{10,8},{12,14},{14,12},{16,18},{18,... | collective-permute-start | bytes 884744 | tf_op jit(solution)/shard_map/ppermute | solution.py:24
  244.2 39.4 %collective-permute-start.26 = (bf16[2,72,1280]{2,1,0:T(8,128)(2,1)S(1)}, bf16[2,72,1280]{2,1,0:T(8,128)(2,1)S(1)}, u32[]{:S(2)}, u32[]{:S(2)}) collective-permute-start(bf16[2,72,1280]{2,1,0:T(8,128)(2,1)S(1)} %copy-done.43), channel_id=1, source_target_pairs={{0,16},{2,18},{4,20},{6,22},{8,24},{10,26},{12,28},{14,30},{16,0},... | collective-permute-start | bytes 1105928 | tf_op jit(solution)/shard_map/ppermute | solution.py:24
  252.5 43.4 %collective-permute-start.25 = (bf16[4,72,1792]{2,1,0:T(8,128)(2,1)}, bf16[4,72,1792]{2,1,0:T(8,128)(2,1)}, u32[]{:S(2)}, u32[]{:S(2)}) collective-permute-start(bf16[4,72,1792]{2,1,0:T(8,128)(2,1)} %get-tuple-element.173), channel_id=1, source_target_pairs={{0,2},{2,0},{4,6},{6,4},{8,10},{10,8},{12,14},{14,12},{16,18},{18,... | collective-permute-start | bytes 3096584 | tf_op jit(solution)/shard_map/ppermute | solution.py:24
  267.4 42.3 %collective-permute-start.24 = (bf16[4,72,1792]{2,1,0:T(8,128)(2,1)}, bf16[4,72,1792]{2,1,0:T(8,128)(2,1)}, u32[]{:S(2)}, u32[]{:S(2)}) collective-permute-start(bf16[4,72,1792]{2,1,0:T(8,128)(2,1)} %get-tuple-element.175), channel_id=1, source_target_pairs={{0,4},{2,6},{4,0},{6,2},{8,12},{10,14},{12,8},{14,10},{16,20},{18,... | collective-permute-start | bytes 3096584 | tf_op jit(solution)/shard_map/ppermute | solution.py:24
  275.2 44.6 %collective-permute-start.22 = (bf16[2,72,512]{2,1,0:T(8,128)(2,1)}, bf16[2,72,512]{2,1,0:T(8,128)(2,1)S(1)}, u32[]{:S(2)}, u32[]{:S(2)}) collective-permute-start(bf16[2,72,512]{2,1,0:T(8,128)(2,1)} %get-tuple-element.177), channel_id=1, source_target_pairs={{0,4},{2,6},{4,0},{6,2},{8,12},{10,14},{12,8},{14,10},{16,20},{18,... | collective-permute-start | bytes 442376 | tf_op jit(solution)/shard_map/ppermute | solution.py:24
  278.3 43.9 %all-to-all-start.4 = ((bf16[16,16,512]{2,1,0:T(8,128)(2,1)}), bf16[16,16,512]{2,1,0:T(8,128)(2,1)S(1)}, u32[]{:S(2)}, u32[]{:S(2)}) async-start(bf16[16,16,512]{2,1,0:T(8,128)(2,1)} %fusion), calls=%async_computation.4 | async-start | bytes 524288 | tf_op jit(solution)/shard_map/all_to_all | solution.py:1225
  298.6 37.2 %collective-permute-start.28 = (bf16[2,72,1792]{2,1,0:T(8,128)(2,1)}, bf16[2,72,1792]{2,1,0:T(8,128)(2,1)}, u32[]{:S(2)}, u32[]{:S(2)}) collective-permute-start(bf16[2,72,1792]{2,1,0:T(8,128)(2,1)} %get-tuple-element.186), channel_id=1, source_target_pairs={{0,16},{2,18},{4,20},{6,22},{8,24},{10,26},{12,28},{14,30},{16,0},... | collective-permute-start | bytes 1548296 | tf_op jit(solution)/shard_map/ppermute | solution.py:24
  312.3 43.0 %collective-permute-start.33 = (bf16[2,72,1792]{2,1,0:T(8,128)(2,1)}, bf16[2,72,1792]{2,1,0:T(8,128)(2,1)S(1)}, u32[]{:S(2)}, u32[]{:S(2)}) collective-permute-start(bf16[2,72,1792]{2,1,0:T(8,128)(2,1)} %get-tuple-element.188), channel_id=1, source_target_pairs={{0,16},{2,18},{4,20},{6,22},{8,24},{10,26},{12,28},{14,30},{16,0},... | collective-permute-start | bytes 1548296 | tf_op jit(solution)/shard_map/ppermute | solution.py:24
  317.8 25.9 %collective-permute-start.27 = (bf16[4,72,1280]{2,1,0:T(8,128)(2,1)}, bf16[4,72,1280]{2,1,0:T(8,128)(2,1)S(1)}, u32[]{:S(2)}, u32[]{:S(2)}) collective-permute-start(bf16[4,72,1280]{2,1,0:T(8,128)(2,1)} %get-tuple-element.190), channel_id=1, source_target_pairs={{0,2},{2,0},{4,6},{6,4},{8,10},{10,8},{12,14},{14,12},{16,18},{18,... | collective-permute-start | bytes 2211848 | tf_op jit(solution)/shard_map/ppermute | solution.py:24
  322.9 6.5 %copy-start.22 = (f32[2,72,512]{2,1,0:T(8,128)S(1)}, f32[2,72,512]{2,1,0:T(8,128)}, u32[]{:S(2)}) copy-start(f32[2,72,512]{2,1,0:T(8,128)} %shard_map.234) | copy-start | bytes 884740
  329.3 3.0 collective-permute-start.29
  329.5 2.4 collective-permute-start.30
  331.8 56.9 %collective-permute-start.37 = (bf16[72,1792]{1,0:T(8,128)(2,1)}, bf16[72,1792]{1,0:T(8,128)(2,1)}, u32[]{:S(2)}, u32[]{:S(2)}) collective-permute-start(bf16[72,1792]{1,0:T(8,128)(2,1)} %pad_maximum_fusion.7), channel_id=1, source_target_pairs={{0,8},{2,10},{4,12},{6,14},{8,0},{10,2},{12,4},{14,6},{16,24},{18,... | collective-permute-start | bytes 774152 | tf_op jit(solution)/shard_map/ppermute | solution.py:24
  335.8 14.9 %all-to-all-start.5 = ((bf16[4,160,640]{2,1,0:T(8,128)(2,1)}), bf16[4,160,640]{2,1,0:T(8,128)(2,1)S(1)}, u32[]{:S(2)}, u32[]{:S(2)}) async-start(bf16[4,160,640]{2,1,0:T(8,128)(2,1)} %bitcast.72), calls=%async_computation.5 | async-start | bytes 1638400 | tf_op jit(solution)/shard_map/all_to_all | solution.py:1264
  346.9 27.0 %collective-permute-start.31 = (bf16[2,72,1280]{2,1,0:T(8,128)(2,1)}, bf16[2,72,1280]{2,1,0:T(8,128)(2,1)S(1)}, u32[]{:S(2)}, u32[]{:S(2)}) collective-permute-start(bf16[2,72,1280]{2,1,0:T(8,128)(2,1)} %get-tuple-element.205), channel_id=1, source_target_pairs={{0,16},{2,18},{4,20},{6,22},{8,24},{10,26},{12,28},{14,30},{16,0},... | collective-permute-start | bytes 1105928 | tf_op jit(solution)/shard_map/ppermute | solution.py:24
  353.7 18.0 %collective-permute-start.32 = (bf16[96,640]{1,0:T(8,128)(2,1)}, bf16[96,640]{1,0:T(8,128)(2,1)S(1)}, u32[]{:S(2)}, u32[]{:S(2)}) collective-permute-start(bf16[96,640]{1,0:T(8,128)(2,1)} %get-tuple-element.208), channel_id=1, source_target_pairs={{0,16},{2,18},{4,20},{6,22},{8,24},{10,26},{12,28},{14,30},{16,0},... | collective-permute-start | bytes 368648 | tf_op jit(solution)/shard_map/ppermute | solution.py:24
  359.4 18.5 %copy-start.11 = (f32[2,72,1792]{2,1,0:T(8,128)S(1)}, f32[2,72,1792]{2,1,0:T(8,128)}, u32[]{:S(2)}) copy-start(f32[2,72,1792]{2,1,0:T(8,128)} %shard_map.240) | copy-start | bytes 3096580
  359.5 23.3 %collective-permute-start.35 = (bf16[72,3584]{1,0:T(8,128)(2,1)S(1)}, bf16[72,3584]{1,0:T(8,128)(2,1)S(1)}, u32[]{:S(2)}, u32[]{:S(2)}) collective-permute-start(bf16[72,3584]{1,0:T(8,128)(2,1)S(1)} %pad_maximum_fusion.6), channel_id=1, source_target_pairs={{0,8},{2,10},{4,12},{6,14},{8,0},{10,2},{12,4},{14,6},{16,24},{18,... | collective-permute-start | bytes 1548296 | tf_op jit(solution)/shard_map/ppermute | solution.py:24
  374.7 3.3 copy-start.45
  376.7 9.6 %copy-start.16 = (f32[2,72,1280]{2,1,0:T(8,128)S(1)}, f32[2,72,1280]{2,1,0:T(8,128)}, u32[]{:S(2)}) copy-start(f32[2,72,1280]{2,1,0:T(8,128)} %shard_map.242) | copy-start | bytes 2211844
  377.8 8.5 %collective-permute-start.34 = (bf16[72,1280]{1,0:T(8,128)(2,1)S(1)}, bf16[72,1280]{1,0:T(8,128)(2,1)S(1)}, u32[]{:S(2)}, u32[]{:S(2)}) collective-permute-start(bf16[72,1280]{1,0:T(8,128)(2,1)S(1)} %fusion.11), channel_id=1, source_target_pairs={{0,8},{2,10},{4,12},{6,14},{8,0},{10,2},{12,4},{14,6},{16,24},{18,... | collective-permute-start | bytes 552968 | tf_op jit(solution)/shard_map/ppermute | solution.py:24
  378.0 9.2 %collective-permute-start.36 = (bf16[64,640]{1,0:T(8,128)(2,1)S(1)}, bf16[64,640]{1,0:T(8,128)(2,1)S(1)}, u32[]{:S(2)}, u32[]{:S(2)}) collective-permute-start(bf16[64,640]{1,0:T(8,128)(2,1)S(1)} %copy-done.45), channel_id=1, source_target_pairs={{0,8},{2,10},{4,12},{6,14},{8,0},{10,2},{12,4},{14,6},{16,24},{18,... | collective-permute-start | bytes 245768 | tf_op jit(solution)/shard_map/ppermute | solution.py:24
  387.2 2.7 copy-start.37
  (26 other events, 25.3 us)
